TPU v7x, 32 devices: a whole 2x2x4 slice. The times are simulated.
32 devices in a mesh: group: 2 (over y), adapter: 4 (over z), tensor: 4 (over x, core).
Axes of the slice: x: 2, y: 2, z: 4, core: 2. Of those that a mesh axis runs over, the one named last changes fastest.
Arguments:
- normed_hidden_rows: bfloat16 [24576, 8192], P(('group', 'adapter'), 'tensor'), parts along dimension 0, may hold values from -6 to 6
- key_value_weight: bfloat16 [8192, 2, 1024], P('tensor'), may hold values from -0.0625 to 0.0625
- adapter_down_maps: bfloat16 [24, 8192, 128], P(('group', 'adapter'), 'tensor'), parts along dimension 0, may hold values from -0.0625 to 0.0625
- adapter_up_maps: bfloat16 [24, 2, 64, 1024], P(('group', 'adapter'), None, None, 'tensor'), parts along dimension 0, may hold values from -0.75 to 0.75
- storage_row_table: int32 [24], P('group'), parts along dimension 0, may hold values from 0 to 11, as said below
- adapter_of_request: int32 [96], P(('group', 'adapter')), parts along dimension 0, may hold values from 0 to 11, as said below
- request_token_length: int32 [96], P(('group', 'adapter')), parts along dimension 0, may hold values from 1 to 256, 7680 in all
Outputs:
- kv_states: bfloat16 [24576, 2, 1024], P(('group', 'adapter'), None, 'tensor'), parts along dimension 0
There are 2 independent parts, one for each index of `group`. A program takes and returns all parts, laid end to end along the dimension named above; an argument that names none is the same for every part. Nothing has to cross between parts.
Inputs may be any that keep to these rules, and one draw needn't show every extreme that they name: A permutation: adapter a is stored in row storage_row_table[a] of adapter_down_maps and adapter_up_maps, which lies on index storage_row_table[a] // 3 of adapter. `adapter_of_request`: in each aligned block of 12 requests (those of one index of adapter) the requests fall into groups of exactly 3, only the last group smaller when 3 does not divide 12; the adapters of one group are all stored on one index of adapter, different groups on different indices; requests may share an adapter.
All inputs are finite; a program needn't handle non-finite values. No bound on the sum of `request_token_length` on one device may be relied on, other than what follows from the above.
Results may differ from a plain program's by a relative error of at most 0.013.
Values may be sent and summed in bfloat16 or wider, within the bound.
No kernel may reach another device: no remote copies, remote signals or barrier semaphores. Data moves between devices by JAX's collectives and lax.ppermute only.
A program may use at most 128 MiB of HBM per device.

v0:
```python
import jax
import jax.numpy as jnp
from jax import lax
from jax.sharding import PartitionSpec as P


def per_device(
    normed_hidden_rows,
    key_value_weight,
    adapter_down_maps,
    adapter_up_maps,
    storage_row_table,
    adapter_of_request,
    request_token_length,
):
    requests = adapter_of_request.shape[0]
    tok_rows = normed_hidden_rows.shape[0]
    prefill = tok_rows // requests
    feature_cols = normed_hidden_rows.shape[1]
    rank_span_width = adapter_up_maps.shape[2]
    head_columns = adapter_up_maps.shape[3]
    all_rows = storage_row_table.shape[0]
    matches = adapter_of_request[:, None] == jnp.arange(all_rows, dtype=jnp.int32)[None, :]
    slot_of = jnp.sum(jnp.where(matches, storage_row_table[None, :], 0), axis=1)
    partial_kv = jnp.einsum(
        "td,dsk->tsk", normed_hidden_rows, key_value_weight, preferred_element_type=jnp.float32
    )
    base_term = lax.psum_scatter(
        partial_kv.astype(jnp.bfloat16), "tensor", scatter_dimension=2, tiled=True
    ).astype(jnp.float32)
    down_segment = lax.all_gather(adapter_down_maps, "adapter", axis=0, tiled=True)
    up_segment = lax.all_gather(adapter_up_maps, "adapter", axis=0, tiled=True)
    piece_rows = down_segment.shape[0]
    wanted_rows = jnp.arange(piece_rows, dtype=jnp.int32)
    selector = (slot_of[:, None] == wanted_rows[None, :]).astype(jnp.bfloat16)
    down_pick = jnp.einsum(
        "rn,nde->rde", selector, down_segment, preferred_element_type=jnp.float32
    )
    up_pick = jnp.einsum("rn,nsak->rsak", selector, up_segment, preferred_element_type=jnp.float32)
    down_req = down_pick.astype(jnp.bfloat16)
    up_req = up_pick.astype(jnp.bfloat16)
    token_blocks = normed_hidden_rows.reshape(requests, prefill, feature_cols)
    rank_part = jnp.einsum(
        "rcd,rde->rce", token_blocks, down_req, preferred_element_type=jnp.float32
    )
    rank_products = lax.psum(rank_part.astype(jnp.bfloat16), "tensor")
    rank_bf = rank_products.reshape(requests, prefill, 2, rank_span_width)
    adapter_term = jnp.einsum(
        "rcsa,rsak->rcsk", rank_bf, up_req, preferred_element_type=jnp.float32
    )
    live_mask = (
        jnp.arange(prefill, dtype=jnp.int32)[None, :] < request_token_length[:, None]
    ).astype(jnp.float32)
    mixed = (base_term.reshape(requests, prefill, 2, head_columns) + adapter_term) * live_mask[
        :, :, None, None
    ]
    return mixed.reshape(tok_rows, 2, head_columns).astype(jnp.bfloat16)


def solution(mesh):
    in_specs = (
        P(("group", "adapter"), "tensor"),
        P("tensor", None, None),
        P(("group", "adapter"), "tensor", None),
        P(("group", "adapter"), None, None, "tensor"),
        P("group"),
        P(("group", "adapter")),
        P(("group", "adapter")),
    )
    out_specs = P(("group", "adapter"), None, "tensor")
    return jax.shard_map(
        per_device, mesh=mesh, in_specs=in_specs, out_specs=out_specs, check_vma=False
    )
```

profile of v0, /device:TPU:0, one launch (start us, length us, event | category | flops | bytes accessed | tf_op | source)
XLA Modules:
  0.0 319.1 jit_solution(275372055177232231)
XLA Ops:
  6.5 0.0 all-gather.2.cloned.1.call-start
  6.5 0.7 all-gather.2.cloned.1.call-update
  7.3 0.0 all-reduce.2.cloned.1.call-start
  7.3 0.9 select_reduce_fusion
  8.2 118.9 %all-gather.2.cloned.1.call-done = bf16[12,2048,128]{2,1,0:T(8,128)(2,1)} async-done(((bf16[3,2048,128]{2,1,0:T(8,128)(2,1)}), bf16[12,2048,128]{2,1,0:T(8,128)(2,1)}) %all-gather.2.cloned.1.call-update) | async-done | bytes 6291472 | tf_op jit(solution)/shard_map/all_gather | solution.py:31
  127.0 10.4 %fusion.10 = bf16[12,2048,128]{2,0,1:T(8,128)(2,1)} fusion(bf16[12,2048,128]{2,1,0:T(8,128)(2,1)} %all-gather.2.cloned.1.call-done, s32[12]{0:T(128)S(1)} %select_reduce_fusion), kind=kOutput, calls=%fused_computation.6 | convolution fusion | flops 78643344 | bytes 12582960 | tf_op jit(solution)/shard_map/rn,nde->rde/dot_general | solution.py:36
  137.4 15.7 %fusion.17 = bf16[12,128,256]{2,1,0:T(8,128)(2,1)} fusion(bf16[12,256,2048]{2,1,0:T(8,128)(2,1)} %bitcast.31, bf16[12,2048,128]{2,0,1:T(8,128)(2,1)} %fusion.10), kind=kOutput, calls=%fused_computation.13 | convolution fusion | flops 1611005952 | bytes 19660800 | tf_op jit(solution)/shard_map/rcd,rde->rce/dot_general | solution.py:43
  153.1 0.0 all-reduce.2.cloned.1.call-update
  153.2 0.2 reduce-scatter.2.cloned.1.call-start
  153.4 33.1 %fusion.5 = bf16[3072,2,1024]{2,0,1:T(8,128)(2,1)} fusion(bf16[2048,2,1024]{2,1,0:T(2,128)(2,1)} %param.8, bf16[3072,2048]{1,0:T(8,128)(2,1)} %param.7), kind=kOutput, calls=%fused_computation.5 | convolution fusion | flops 25776095232 | bytes 33554432 | tf_op jit(solution)/shard_map/td,dsk->tsk/dot_general | solution.py:25
  186.5 0.0 copy-start.1
  186.5 0.0 copy-start
  186.5 0.0 reduce-scatter.2.cloned.1.call-update
  186.6 0.6 copy-done.1
  187.2 0.1 fusion.22
  187.3 0.2 copy-done
  187.5 17.8 %all_gather.6 = bf16[12,2,64,256]{3,2,1,0:T(8,128)(2,1)S(1)} all-gather(bf16[3,2,64,256]{3,2,1,0:T(8,128)(2,1)S(1)} %copy-done), channel_id=1, replica_groups=mesh['group'=2,'adapter'=4,'tensor'=4] {'adapter'}, dimensions={0}, use_global_device_ids=true | all-gather | bytes 983040 | tf_op jit(solution)/shard_map/all_gather | solution.py:32
  205.2 0.6 convolution_convert_fusion
  205.9 0.0 all-reduce.2.cloned.1.call-done
  205.9 82.0 %reduce-scatter.2.cloned.1.call-done = bf16[3072,2,256]{2,0,1:T(8,128)(2,1)} async-done(((bf16[3072,2,1024]{2,0,1:T(8,128)(2,1)}), bf16[3072,2,256]{2,0,1:T(8,128)(2,1)}) %reduce-scatter.2.cloned.1.call-update) | async-done | bytes 3145744 | tf_op jit(solution)/shard_map/reduce_scatter | solution.py:28
  287.9 3.8 %fusion.14 = bf16[12,256,2,256]{3,1,2,0:T(8,128)(2,1)S(1)} fusion(f32[12,256]{1,0:T(8,128)S(1)} %fusion.22, bf16[12,256,2,64]{1,3,2,0:T(8,128)(2,1)} %all-reduce.2.cloned.1.call-done, bf16[12,2,64,256]{3,0,2,1:T(8,128)(2,1)S(1)} %convolution_convert_fusion, bf16[12,256,2,256]{3,1,0,2:T(8,128)(2,1)} %bitcast.29), kind=kOutput, calls=%fused_computation.9 | convolution fusion | flops 207618048 | bytes 7876608 | tf_op jit(solution)/shard_map/rcsa,rsak->rcsk/dot_general | solution.py:48
  291.7 0.3 copy.28
  292.0 20.6 %copy.29 = bf16[3072,2,256]{2,1,0:T(2,128)(2,1)} copy(bf16[3072,2,256]{2,0,1:T(8,128)(2,1)S(1)} %bitcast.28) | data formatting | bytes 6291456 | tf_op jit(solution)/shard_map/convert_element_type | solution.py:57
Async XLA Ops:
  6.5 120.5 %all-gather.2.cloned.1.call-start = ((), (), s32[]{:S(2)}) async-start(), calls=%async_computation.2 | async-start | bytes 7864320 | tf_op jit(solution)/shard_map/all_gather | solution.py:31
  7.3 198.6 %all-reduce.2.cloned.1.call-start = ((), (), s32[]{:S(2)}) async-start(), calls=%async_computation.3 | async-start | bytes 1572864 | tf_op jit(solution)/shard_map/psum | solution.py:46
  153.2 134.7 %reduce-scatter.2.cloned.1.call-start = ((), (), s32[]{:S(2)}) async-start(), calls=%async_computation.1 | async-start | bytes 15728640 | tf_op jit(solution)/shard_map/reduce_scatter | solution.py:28
  186.5 0.7 copy-start.1
  186.5 0.9 copy-start
Sparse Core Ops, SparseCore 0:
  8.9 118.0 all-gather.1
  153.3 32.8 all-reduce.1
  188.8 99.0 reduce-scatter.1
where the time goes:
time: 319 us
  waiting for transfers between devices  202 us (63%)
  matrix products  63.6 us (20%)
  local copies, waits for them, and re-layouts  21.7 us (7%)
  blocking collectives  17.8 us (6%)
  between operations  13.1 us (4%)
    all_gather x1, waiting for transfers between devices, per_device(): lax.all_gather(adapter_down_maps, 'adapter', axis=0, tiled=True)  119 us
    reduce_scatter x1, waiting for transfers between devices, per_device(): lax.psum_scatter(partial_kv.astype(jnp.bfloat16), 'tensor', scatter_dimen...  82 us
    dot_general x1, matrix products, per_device(): jnp.einsum('td,dsk->tsk', normed_hidden_rows, key_value_weight, preferred...  33.1 us
    convert_element_type x2, local copies, waits for them, and re-layouts, per_device(): return mixed.reshape(tok_rows, 2, head_columns).astype(jnp.bfloat16)  20.9 us
    all_gather x1, blocking collectives, per_device(): up_segment = lax.all_gather(adapter_up_maps, 'adapter', axis=0, tiled=True)  17.8 us
    dot_general x1, matrix products, per_device(): jnp.einsum('rcd,rde->rce', token_blocks, down_req, preferred_element_type...  15.7 us
    dot_general x1, matrix products, per_device(): jnp.einsum('rn,nde->rde', selector, down_segment, preferred_element_type=...  10.4 us
  transfers between devices with their start and end apart: 3, of which 2 were waited for; matrix products, arithmetic and copies ran while one was open for 11% of the time, Pallas kernels for 0%

commit v1 on v0

v1 whole, which is shorter than its diff:
```python
import jax
import jax.numpy as jnp
from jax import lax
from jax.experimental import pallas as pl
from jax.experimental.pallas import tpu as pltpu
from jax.sharding import PartitionSpec as P

BF = jnp.bfloat16
F32 = jnp.float32
CHUNKS = 4
SMEM = pltpu.SMEM
ORDER, SOURCE, ROW, LENGTH, KEYS = 0, 32, 64, 96, 128
PLAN = 256


def params(mib, **more):
    return pltpu.CompilerParams(vmem_limit_bytes=mib * 1024 * 1024, **more)


def plan_requests(table, adapters, lengths, here, n_z, stored):
    requests = adapters.shape[0]

    def body(table_ref, adapter_ref, length_ref, here_ref, plan_ref):
        me = here_ref[0]

        def key_of(r, carry):
            owner = table_ref[adapter_ref[r]] // stored
            distance = jnp.abs(owner - me)
            plan_ref[KEYS + r] = distance * requests + r
            return carry

        lax.fori_loop(0, requests, key_of, 0)

        def place(r, carry):
            mine = plan_ref[KEYS + r]
            position = lax.fori_loop(
                0,
                requests,
                lambda q, n: n + jnp.where(plan_ref[KEYS + q] < mine, 1, 0),
                jnp.int32(0),
            )
            row = table_ref[adapter_ref[r]]
            owner = row // stored
            source = jnp.where(owner >= me, owner - me, n_z - 1 + me - owner)
            plan_ref[ORDER + position] = r
            plan_ref[SOURCE + position] = source
            plan_ref[ROW + position] = row - owner * stored
            plan_ref[LENGTH + position] = length_ref[r]
            return carry

        lax.fori_loop(0, requests, place, 0)

    return pl.pallas_call(
        body,
        out_shape=jax.ShapeDtypeStruct((PLAN,), jnp.int32),
        in_specs=[pl.BlockSpec(memory_space=SMEM)] * 4,
        out_specs=pl.BlockSpec(memory_space=SMEM),
        name="plan_requests",
    )(table, adapters, lengths, here)


def split_weight(weight, slots):
    features, _, columns = weight.shape
    n_t = slots.shape[0]
    width = columns // n_t
    rows, half = 256, 128

    def body(slot_ref, w_ref, o_ref):
        out_row = lax.broadcasted_iota(jnp.int32, (2 * half, 2 * half), 0)
        in_row = lax.broadcasted_iota(jnp.int32, (2 * half, 2 * half), 1)
        pick = in_row == 2 * (out_row % half) + out_row // half
        pick = pick.astype(F32).astype(BF)
        for b in range(rows // half):
            mixed = w_ref[b * half : (b + 1) * half].reshape(2 * half, columns)
            apart = jnp.dot(pick, mixed, preferred_element_type=F32).astype(BF)
            for t in range(n_t):
                for s in range(2):
                    o_ref[
                        slot_ref[t],
                        b * half : (b + 1) * half,
                        s * width : (s + 1) * width,
                    ] = apart[s * half : (s + 1) * half, t * width : (t + 1) * width]

    return pl.pallas_call(
        body,
        out_shape=jax.ShapeDtypeStruct((n_t, features, 2 * width), BF),
        grid_spec=pltpu.PrefetchScalarGridSpec(
            num_scalar_prefetch=1,
            grid=(features // rows,),
            in_specs=[pl.BlockSpec((rows, 2, columns), lambda i, s: (i, 0, 0))],
            out_specs=pl.BlockSpec((n_t, rows, 2 * width), lambda i, s: (0, i, 0)),
        ),
        compiler_params=params(32),
        cost_estimate=pl.CostEstimate(
            flops=4 * half * features * 2 * columns // 2,
            bytes_accessed=8 * features * columns,
            transcendentals=0,
        ),
        name="split_weight",
    )(slots, weight)


def base_products(plan, hidden, weight, chunk, count, prefill):
    n_t, features, width = weight.shape
    n_x = n_t // 2
    first = chunk * count
    short = prefill // 2

    def body(plan_ref, x_ref, w_ref, send_ref, keep_ref):
        live = plan_ref[LENGTH + first + pl.program_id(0)]

        def products(rows):
            for j in range(n_t):
                out = send_ref if j < n_x else keep_ref
                out[j % n_x, :rows] = jnp.dot(
                    x_ref[:rows], w_ref[j], preferred_element_type=F32
                ).astype(BF)
                if rows < prefill:
                    out[j % n_x, rows:] = jnp.zeros((prefill - rows, width), BF)

        @pl.when(live > short)
        def _():
            products(prefill)

        @pl.when(live <= short)
        def _():
            products(short)

    out = jax.ShapeDtypeStruct((n_x, count * prefill, width), BF)
    block = pl.BlockSpec((n_x, prefill, width), lambda i, p: (0, i, 0))
    return pl.pallas_call(
        body,
        out_shape=(out, out),
        grid_spec=pltpu.PrefetchScalarGridSpec(
            num_scalar_prefetch=1,
            grid=(count,),
            in_specs=[
                pl.BlockSpec(
                    (prefill, features), lambda i, p: (p[ORDER + first + i], 0)
                ),
                pl.BlockSpec((n_t, features, width), lambda i, p: (0, 0, 0)),
            ],
            out_specs=(block, block),
        ),
        compiler_params=params(40),
        cost_estimate=pl.CostEstimate(
            flops=2 * count * prefill * features * width * n_t,
            bytes_accessed=2 * (count * prefill * (features + n_t * width))
            + 2 * n_t * features * width,
            transcendentals=0,
        ),
        name="base_products",
    )(plan, hidden, weight)


def fetch(refs, source, row, target, sem):
    for k, ref in enumerate(refs):

        @pl.when(source == k)
        def _():
            pltpu.make_async_copy(ref.at[row], target, sem).start()


def rank_products(plan, hidden, maps, chunk, count, prefill):
    _, features, ranks = maps[0].shape
    first = chunk * count

    def body(plan_ref, x_ref, *rest):
        refs, (o_ref, held, sems) = rest[: len(maps)], rest[len(maps) :]
        step = pl.program_id(0)

        @pl.when(step == 0)
        def _():
            for i in range(count):
                fetch(
                    refs,
                    plan_ref[SOURCE + first + i],
                    plan_ref[ROW + first + i],
                    held.at[i],
                    sems.at[i],
                )

        pltpu.make_async_copy(refs[0].at[0], held.at[step], sems.at[step]).wait()
        o_ref[...] = jnp.dot(
            x_ref[...], held[step], preferred_element_type=F32
        ).astype(BF)

    return pl.pallas_call(
        body,
        out_shape=jax.ShapeDtypeStruct((count * prefill, ranks), BF),
        grid_spec=pltpu.PrefetchScalarGridSpec(
            num_scalar_prefetch=1,
            grid=(count,),
            in_specs=[
                pl.BlockSpec(
                    (prefill, features), lambda i, p: (p[ORDER + first + i], 0)
                )
            ]
            + [pl.BlockSpec(memory_space=pl.ANY)] * len(maps),
            out_specs=pl.BlockSpec((prefill, ranks), lambda i, p: (i, 0)),
            scratch_shapes=[
                pltpu.VMEM((count, features, ranks), BF),
                pltpu.SemaphoreType.DMA((count,)),
            ],
        ),
        compiler_params=params(32),
        cost_estimate=pl.CostEstimate(
            flops=2 * count * prefill * features * ranks,
            bytes_accessed=2 * count * features * (prefill + ranks),
            transcendentals=0,
        ),
        name="rank_products",
    )(plan, hidden, *maps)


def finish(plan, bases, ranks, maps, before, chunk, count, prefill, shape):
    first = chunk * count
    _, _, depth, columns = maps[0].shape
    half = prefill // 2
    n_base, n_rank, n_map = len(bases), len(ranks), len(maps)

    def body(plan_ref, *rest):
        base_refs, rest = rest[:n_base], rest[n_base:]
        rank_refs, rest = rest[:n_rank], rest[n_rank:]
        map_refs, rest = rest[:n_map], rest[n_map:]
        o_ref, held, sems = rest[-3:]
        step = pl.program_id(0)

        @pl.when(step == 0)
        def _():
            for i in range(count):
                fetch(
                    map_refs,
                    plan_ref[SOURCE + first + i],
                    plan_ref[ROW + first + i],
                    held.at[i],
                    sems.at[i],
                )

        pltpu.make_async_copy(map_refs[0].at[0], held.at[step], sems.at[step]).wait()
        live = plan_ref[LENGTH + first + step]
        up = held[step].reshape(2 * depth, columns)
        mix_row = lax.broadcasted_iota(jnp.int32, (2 * half, 2 * half), 0)
        mix_column = lax.broadcasted_iota(jnp.int32, (2 * half, 2 * half), 1)
        mix = mix_column == mix_row // 2 + half * (mix_row % 2)
        mix = mix.astype(F32).astype(BF)
        twice_row = lax.broadcasted_iota(jnp.int32, (2 * half, half), 0)
        twice_column = lax.broadcasted_iota(jnp.int32, (2 * half, half), 1)
        twice = (twice_column == twice_row // 2).astype(F32).astype(BF)
        lane = lax.broadcasted_iota(jnp.int32, (2 * half, 2 * depth), 1)
        side = lax.broadcasted_iota(jnp.int32, (2 * half, 2 * depth), 0) % 2
        own_side = lane // depth == side
        token = lax.broadcasted_iota(jnp.int32, (2 * half, columns), 0) // 2
        for b in range(2):
            rows = slice(b * half, (b + 1) * half)
            total = jnp.zeros((2 * half, columns), F32)
            for ref in base_refs:
                piece = ref[0, rows] if len(ref.shape) == 3 else ref[rows]
                piece = jnp.concatenate([piece[:, :columns], piece[:, columns:]], 0)
                total += jnp.dot(mix, piece, preferred_element_type=F32)
            rank = rank_refs[0][rows].astype(F32)
            for ref in rank_refs[1:]:
                rank += ref[rows].astype(F32)
            rank = jnp.dot(twice, rank.astype(BF), preferred_element_type=F32)
            rank = jnp.where(own_side, rank, 0.0).astype(BF)
            total += jnp.dot(rank, up, preferred_element_type=F32)
            total = jnp.where(token + b * half < live, total, 0.0)
            o_ref[rows] = total.astype(BF).reshape(half, 2, columns)

    base_specs = [
        pl.BlockSpec((1, prefill, 2 * columns), lambda i, p: (0, i, 0))
        if a.ndim == 3
        else pl.BlockSpec((prefill, 2 * columns), lambda i, p: (i, 0))
        for a in bases
    ]
    operands = [plan, *bases, *ranks, *maps]
    specs = (
        base_specs
        + [pl.BlockSpec((prefill, 2 * depth), lambda i, p: (i, 0))] * n_rank
        + [pl.BlockSpec(memory_space=pl.ANY)] * n_map
    )
    aliases = {}
    if before is not None:
        aliases = {len(operands): 0}
        operands.append(before)
        specs.append(pl.BlockSpec(memory_space=pl.ANY))
    return pl.pallas_call(
        body,
        out_shape=jax.ShapeDtypeStruct(shape, BF),
        grid_spec=pltpu.PrefetchScalarGridSpec(
            num_scalar_prefetch=1,
            grid=(count,),
            in_specs=specs,
            out_specs=pl.BlockSpec(
                (prefill, 2, columns), lambda i, p: (p[ORDER + first + i], 0, 0)
            ),
            scratch_shapes=[
                pltpu.VMEM((count, 2, depth, columns), BF),
                pltpu.SemaphoreType.DMA((count,)),
            ],
        ),
        input_output_aliases=aliases,
        compiler_params=params(32),
        cost_estimate=pl.CostEstimate(
            flops=8 * count * prefill * prefill * 2 * columns,
            bytes_accessed=10 * count * prefill * columns * 2,
            transcendentals=0,
        ),
        name="finish",
    )(*operands)


def solution(mesh):
    n_z, n_t = mesh.shape["adapter"], mesh.shape["tensor"]
    n_x = n_t // 2

    def core_swap(a):
        return lax.ppermute(a, "tensor", [(t, t ^ 1) for t in range(n_t)])

    def chip_shift(a, k):
        return lax.ppermute(
            a,
            "tensor",
            [(2 * x + c, 2 * ((x + k) % n_x) + c) for x in range(n_x) for c in (0, 1)],
        )

    def down_line(a):
        return lax.ppermute(a, "adapter", [(z, z - 1) for z in range(1, n_z)])

    def up_line(a):
        return lax.ppermute(a, "adapter", [(z - 1, z) for z in range(1, n_z)])

    def per_device(hidden, weight, down, up, table, adapters, lengths):
        requests = adapters.shape[0]
        prefill = hidden.shape[0] // requests
        stored = down.shape[0]
        columns = up.shape[3]
        count = requests // CHUNKS
        by_distance = n_z == CHUNKS
        z, t = lax.axis_index("adapter"), lax.axis_index("tensor")
        plan = plan_requests(
            table, adapters, lengths, jnp.reshape(z, (1,)), n_z, stored
        )

        near_down, near_up = [(down, up)], [(down, up)]
        for _ in range(n_z - 1):
            d, u = near_down[-1]
            near_down.append((down_line(d), down_line(u)))
            d, u = near_up[-1]
            near_up.append((up_line(d), up_line(u)))

        def arrived(step, which):
            held = [own[which] for own in near_down[: step + 1]]
            held += [down if which == 0 else up] * (n_z - 1 - step)
            held += [own[which] for own in near_up[1 : step + 1]]
            return held

        dest = jnp.arange(n_t, dtype=jnp.int32)
        away = (dest // 2 - t // 2 + n_x) % n_x
        slots = jnp.where(dest % 2 == t % 2, n_x + away, away)
        split = split_weight(weight, slots)

        shape = (requests * prefill, 2, columns)
        out = None
        bases = []
        for chunk in range(CHUNKS):
            send, keep = base_products(plan, hidden, split, chunk, count, prefill)
            got = core_swap(send)
            pieces = [keep, got]
            for k in range(1, n_x):
                pair = keep[k].astype(F32) + got[k].astype(F32)
                pieces.append(chip_shift(pair.astype(BF), k))
            bases.append(pieces)
        for chunk in range(CHUNKS):
            step = chunk if by_distance else n_z - 1
            part = rank_products(
                plan, hidden, arrived(step, 0), chunk, count, prefill
            )
            pair = part.astype(F32) + core_swap(part).astype(F32)
            pair = pair.astype(BF)
            ranks = [pair] + [chip_shift(pair, k) for k in range(1, n_x)]
            out = finish(
                plan,
                bases[chunk],
                ranks,
                arrived(step, 1),
                out,
                chunk,
                count,
                prefill,
                shape,
            )
        return out

    return jax.shard_map(
        per_device,
        mesh=mesh,
        in_specs=(
            P(("group", "adapter"), "tensor"),
            P("tensor", None, None),
            P(("group", "adapter"), "tensor", None),
            P(("group", "adapter"), None, None, "tensor"),
            P("group"),
            P(("group", "adapter")),
            P(("group", "adapter")),
        ),
        out_specs=P(("group", "adapter"), None, "tensor"),
        check_vma=False,
    )
```

time: 319 us -> 229 us (0.72)
  waiting for transfers between devices: 202 us -> 77.4 us
  Pallas kernels: 0 us -> 74.9 us
  matrix products: 63.6 us -> 0 us
  starting transfers between devices: 0.26 us -> 42.4 us
  blocking collectives: 17.8 us -> 0 us
  between operations: 13.1 us -> 0.85 us
  other arithmetic: 0.93 us -> 7.5 us
    all_gather x1 -> x0, waiting for transfers between devices: 119 us -> none  [per_device(): lax.all_gather(adapter_down_maps, 'adapter', axis=0, tiled=True)]
    reduce_scatter x1 -> x0, waiting for transfers between devices: 82 us -> none  [per_device(): lax.psum_scatter(partial_kv.astype(jnp.bfloat16), 'tensor', scatter_dimen...]
    ppermute x0 -> x28, waiting for transfers between devices: none -> 77.4 us  [the longest x8 45 us: chip_shift(): lax.ppermute(a, 'tensor', [(2 * x + c, 2 * ((x + k) % n_x) + c) for x in...]
    pallas_call x0 -> x14, Pallas kernels: none -> 74.9 us  [the longest x4 37.4 us: base_products(): pl.pallas_call(body, out_shape=(out, out), grid_spec=pltpu.PrefetchScalar...]
    dot_general x5 -> x0, matrix products: 63.6 us -> none  [the longest x1 33.1 us: per_device(): jnp.einsum('td,dsk->tsk', normed_hidden_rows, key_value_weight, preferred...]
    ppermute x0 -> x28, starting transfers between devices: none -> 42.4 us  [the longest x6 26.1 us: up_line(): return lax.ppermute(a, 'adapter', [(z - 1, z) for z in range(1, n_z)])]
    unnamed x4 -> x98, local copies, waits for them, and re-layouts: 0.84 us -> 24.8 us
    convert_element_type x2 -> x0, local copies, waits for them, and re-layouts: 20.9 us -> none  [per_device(): return mixed.reshape(tok_rows, 2, head_columns).astype(jnp.bfloat16)]
  transfers between devices with their start and end apart: 3 -> 28, of which waited for: 2 -> 9; matrix products, arithmetic and copies ran while one was open for 11% -> 3% of each run, Pallas kernels for 0% -> 31%
where the time goes in v1:
time: 229 us; the launch traced here: 228 us
  waiting for transfers between devices  77.4 us (34%)
  Pallas kernels  74.9 us (33%)
  starting transfers between devices  42.4 us (19%)
  local copies, waits for them, and re-layouts  24.8 us (11%)
  other arithmetic  7.5 us (3%)
    ppermute x8, waiting for transfers between devices, chip_shift(): lax.ppermute(a, 'tensor', [(2 * x + c, 2 * ((x + k) % n_x) + c) for x in...  45 us
    pallas_call x4, Pallas kernels, base_products(): pl.pallas_call(body, out_shape=(out, out), grid_spec=pltpu.PrefetchScalar...  37.4 us
    ppermute x6, starting transfers between devices, up_line(): return lax.ppermute(a, 'adapter', [(z - 1, z) for z in range(1, n_z)])  26.1 us
    unnamed x98, local copies, waits for them, and re-layouts  24.8 us
    ppermute x6, waiting for transfers between devices, up_line(): return lax.ppermute(a, 'adapter', [(z - 1, z) for z in range(1, n_z)])  20.6 us
    pallas_call x4, Pallas kernels, finish(): pl.pallas_call(body, out_shape=jax.ShapeDtypeStruct(shape, BF), grid_spec...  17.7 us
    pallas_call x4, Pallas kernels, rank_products(): pl.pallas_call(body, out_shape=jax.ShapeDtypeStruct((count * prefill, ran...  12.1 us
    ppermute x6, waiting for transfers between devices, down_line(): return lax.ppermute(a, 'adapter', [(z, z - 1) for z in range(1, n_z)])  10.6 us
  transfers between devices with their start and end apart: 28, of which 9 were waited for; matrix products, arithmetic and copies ran while one was open for 3% of the time, Pallas kernels for 31%

profile of v1, /device:TPU:0, one launch (start us, length us, event | category | flops | bytes accessed | tf_op | source)
XLA Modules:
  0.0 227.8 jit_solution(2150570899938053717)
XLA Ops:
  0.0 6.1 %collective-permute-start.5 = (bf16[3,2048,128]{2,1,0:T(8,128)(2,1)}, bf16[3,2048,128]{2,1,0:T(8,128)(2,1)}, u32[]{:S(2)}, u32[]{:S(2)}) collective-permute-start(bf16[3,2048,128]{2,1,0:T(8,128)(2,1)} %rest_3_.5), channel_id=1, source_target_pairs={{0,4},{4,8},{8,12},{1,5},{5,9},{9,13},{2,6},{6,10},{10,14},{3,7},{... | collective-permute-start | bytes 4718600 | tf_op jit(solution)/shard_map/ppermute | solution.py:331
  7.4 2.7 %plan_requests.1.plan_ref = s32[256]{0:T(256)} custom-call(s32[12]{0:T(128)} %table_ref.1, s32[12]{0:T(128)} %adapter_ref.1, s32[12]{0:T(128)} %length_ref.1, s32[1]{0:T(128)} %bitcast.here_ref), custom_call_target="tpu_custom_call" | custom-call | tf_op jit(solution)/shard_map/plan_requests/pallas_call | solution.py:53
  10.1 4.6 %copy-done = bf16[3072,2048]{1,0:T(8,128)(2,1)S(1)} copy-done((bf16[3072,2048]{1,0:T(8,128)(2,1)S(1)}, bf16[3072,2048]{1,0:T(8,128)(2,1)}, u32[]{:S(2)}) %copy-start) | copy-done | bytes 12582936
  19.0 4.6 %collective-permute-start.13 = (bf16[3,2,64,256]{3,2,1,0:T(8,128)(2,1)S(1)}, bf16[3,2,64,256]{3,2,1,0:T(8,128)(2,1)S(1)}, u32[]{:S(2)}, u32[]{:S(2)}) collective-permute-start(bf16[3,2,64,256]{3,2,1,0:T(8,128)(2,1)S(1)} %copy-done.4), channel_id=1, source_target_pairs={{0,4},{4,8},{8,12},{1,5},{5,9},{9,13},{2,6},{6,10},{10,14},{3,7},{... | collective-permute-start | bytes 589832 | tf_op jit(solution)/shard_map/ppermute | solution.py:331
  23.6 3.4 %copy-done.5 = bf16[2048,2,1024]{2,1,0:T(2,128)(2,1)S(1)} copy-done((bf16[2048,2,1024]{2,1,0:T(2,128)(2,1)S(1)}, bf16[2048,2,1024]{2,1,0:T(2,128)(2,1)}, u32[]{:S(2)}) %copy-start.5) | copy-done | bytes 8388632
  26.9 5.0 %split_weight.1.w_ref = bf16[4,2048,512]{2,1,0:T(8,128)(2,1)S(1)} custom-call(s32[4]{0:T(128)S(1)} %compare_select_fusion.2.slot_ref, bf16[2048,2,1024]{2,1,0:T(2,128)(2,1)S(1)} %copy-done.5), custom_call_target="tpu_custom_call" | custom-call | flops 1073741824 | bytes 16777216 | tf_op jit(solution)/shard_map/split_weight/pallas_call | solution.py:84
  32.0 8.7 %base_products.7 = (bf16[2,768,512]{2,1,0:T(8,128)(2,1)}, bf16[2,768,512]{2,1,0:T(8,128)(2,1)S(1)}) custom-call(s32[256]{0:T(256)S(1)} %copy-done.45, bf16[3072,2048]{1,0:T(8,128)(2,1)} %x_ref.15, bf16[4,2048,512]{2,1,0:T(8,128)(2,1)S(1)} %split_weight.1.w_ref), custom_call_target="tpu_custom_call" | custom-call | flops 6442450944 | bytes 14680064 | tf_op jit(solution)/shard_map/base_products/pallas_call | solution.py:131
  42.0 4.6 %collective-permute-start.6 = (bf16[3,2048,128]{2,1,0:T(8,128)(2,1)}, bf16[3,2048,128]{2,1,0:T(8,128)(2,1)}, u32[]{:S(2)}, u32[]{:S(2)}) collective-permute-start(bf16[3,2048,128]{2,1,0:T(8,128)(2,1)} %collective-permute-done.5.rest_4_), channel_id=1, source_target_pairs={{0,4},{4,8},{8,12},{1,5},{5,9},{9,13},{2,6},{6,10},{10,14},{3,7},{... | collective-permute-start | bytes 4718600 | tf_op jit(solution)/shard_map/ppermute | solution.py:331
  46.6 9.0 %base_products.6 = (bf16[2,768,512]{2,1,0:T(8,128)(2,1)}, bf16[2,768,512]{2,1,0:T(8,128)(2,1)S(1)}) custom-call(s32[256]{0:T(256)S(1)} %copy-done.45, bf16[3072,2048]{1,0:T(8,128)(2,1)} %x_ref.15, bf16[4,2048,512]{2,1,0:T(8,128)(2,1)S(1)} %split_weight.1.w_ref), custom_call_target="tpu_custom_call" | custom-call | flops 6442450944 | bytes 14680064 | tf_op jit(solution)/shard_map/base_products/pallas_call | solution.py:131
  59.6 6.7 %collective-permute-done.10.rest_6_ = bf16[3,2,64,256]{3,2,1,0:T(8,128)(2,1)S(1)} collective-permute-done((bf16[3,2,64,256]{3,2,1,0:T(8,128)(2,1)S(1)}, bf16[3,2,64,256]{3,2,1,0:T(8,128)(2,1)S(1)}, u32[]{:S(2)}, u32[]{:S(2)}) %collective-permute-start.10) | collective-permute-done | bytes 196640 | tf_op jit(solution)/shard_map/ppermute | solution.py:328
  67.8 10.0 %base_products.5 = (bf16[2,768,512]{2,1,0:T(8,128)(2,1)}, bf16[2,768,512]{2,1,0:T(8,128)(2,1)S(1)}) custom-call(s32[256]{0:T(256)S(1)} %copy-done.45, bf16[3072,2048]{1,0:T(8,128)(2,1)} %x_ref.15, bf16[4,2048,512]{2,1,0:T(8,128)(2,1)S(1)} %split_weight.1.w_ref), custom_call_target="tpu_custom_call" | custom-call | flops 6442450944 | bytes 14680064 | tf_op jit(solution)/shard_map/base_products/pallas_call | solution.py:131
  79.7 3.5 %copy-done.7 = bf16[4,2048,512]{2,1,0:T(8,128)(2,1)S(1)} copy-done((bf16[4,2048,512]{2,1,0:T(8,128)(2,1)S(1)}, bf16[4,2048,512]{2,1,0:T(8,128)(2,1)}, u32[]{:S(2)}) %copy-start.7) | copy-done | bytes 8388632
  83.2 9.7 %base_products.4 = (bf16[2,768,512]{2,1,0:T(8,128)(2,1)}, bf16[2,768,512]{2,1,0:T(8,128)(2,1)S(1)}) custom-call(s32[256]{0:T(256)S(1)} %copy-done.45, bf16[3072,2048]{1,0:T(8,128)(2,1)} %x_ref.15, bf16[4,2048,512]{2,1,0:T(8,128)(2,1)S(1)} %copy-done.7), custom_call_target="tpu_custom_call" | custom-call | flops 6442450944 | bytes 14680064 | tf_op jit(solution)/shard_map/base_products/pallas_call | solution.py:131
  94.4 2.5 %collective-permute-start.7 = (bf16[3,2048,128]{2,1,0:T(8,128)(2,1)}, bf16[3,2048,128]{2,1,0:T(8,128)(2,1)S(1)}, u32[]{:S(2)}, u32[]{:S(2)}) collective-permute-start(bf16[3,2048,128]{2,1,0:T(8,128)(2,1)} %collective-permute-done.6.rest_5_), channel_id=1, source_target_pairs={{0,4},{4,8},{8,12},{1,5},{5,9},{9,13},{2,6},{6,10},{10,14},{3,7},{... | collective-permute-start | bytes 4718600 | tf_op jit(solution)/shard_map/ppermute | solution.py:331
  96.9 2.3 %collective-permute-done.3.rest_2_ = bf16[3,2048,128]{2,1,0:T(8,128)(2,1)} collective-permute-done((bf16[3,2048,128]{2,1,0:T(8,128)(2,1)}, bf16[3,2048,128]{2,1,0:T(8,128)(2,1)}, u32[]{:S(2)}, u32[]{:S(2)}) %collective-permute-start.3) | collective-permute-done | bytes 1572896 | tf_op jit(solution)/shard_map/ppermute | solution.py:328
  101.9 3.0 %rank_products.6 = bf16[768,128]{1,0:T(8,128)(2,1)S(1)} custom-call(s32[256]{0:T(256)S(1)} %copy-done.45, bf16[3072,2048]{1,0:T(8,128)(2,1)S(1)} %bitcast.10, bf16[3,2048,128]{2,1,0:T(8,128)(2,1)S(1)} %copy-done.2, bf16[3,2048,128]{2,1,0:T(8,128)(2,1)} %collective-permute-done.2.rest_1_, bf16[3,2048,128]{2,1,0:T(8,128)(2,1)S(1)} %copy-done.2, ...), custom_call_target="tpu_custom_call" | custom-call | flops 402653184 | bytes 4718592 | tf_op jit(solution)/shard_map/rank_products/pallas_call | solution.py:188
  104.9 2.3 %fusion.3 = bf16[768,512]{1,0:T(8,128)(2,1)} fusion(bf16[2,768,512]{2,1,0:T(8,128)(2,1)} %collective-permute-done.24.rest_1_, bf16[2,768,512]{2,1,0:T(8,128)(2,1)S(1)} %copy-done.9), kind=kLoop, calls=%fused_computation.7 | loop fusion | flops 1572864 | bytes 2359296 | tf_op jit(solution)/shard_map/convert_element_type | solution.py:372
  107.4 2.4 %fusion.2 = bf16[768,512]{1,0:T(8,128)(2,1)} fusion(bf16[2,768,512]{2,1,0:T(8,128)(2,1)} %collective-permute-done.20.rest_1_, bf16[2,768,512]{2,1,0:T(8,128)(2,1)S(1)} %copy-done.12), kind=kLoop, calls=%fused_computation.6 | loop fusion | flops 1572864 | bytes 2359296 | tf_op jit(solution)/shard_map/convert_element_type | solution.py:372
  109.8 4.7 %collective-permute-start.14 = (bf16[3,2,64,256]{3,2,1,0:T(8,128)(2,1)S(1)}, bf16[3,2,64,256]{3,2,1,0:T(8,128)(2,1)S(1)}, u32[]{:S(2)}, u32[]{:S(2)}) collective-permute-start(bf16[3,2,64,256]{3,2,1,0:T(8,128)(2,1)S(1)} %copy-done.23), channel_id=1, source_target_pairs={{0,4},{4,8},{8,12},{1,5},{5,9},{9,13},{2,6},{6,10},{10,14},{3,7},{... | collective-permute-start | bytes 589832 | tf_op jit(solution)/shard_map/ppermute | solution.py:331
  114.6 20.6 %collective-permute-done.14.rest_10_ = bf16[3,2,64,256]{3,2,1,0:T(8,128)(2,1)S(1)} collective-permute-done((bf16[3,2,64,256]{3,2,1,0:T(8,128)(2,1)S(1)}, bf16[3,2,64,256]{3,2,1,0:T(8,128)(2,1)S(1)}, u32[]{:S(2)}, u32[]{:S(2)}) %collective-permute-start.14) | collective-permute-done | bytes 196640 | tf_op jit(solution)/shard_map/ppermute | solution.py:331
  137.1 2.2 fusion.1
  139.4 3.0 %rank_products.5 = bf16[768,128]{1,0:T(8,128)(2,1)S(1)} custom-call(s32[256]{0:T(256)S(1)} %copy-done.45, bf16[3072,2048]{1,0:T(8,128)(2,1)S(1)} %bitcast.10, bf16[3,2048,128]{2,1,0:T(8,128)(2,1)S(1)} %copy-done.3, bf16[3,2048,128]{2,1,0:T(8,128)(2,1)} %collective-permute-done.2.rest_1_, bf16[3,2048,128]{2,1,0:T(8,128)(2,1)} %collective-permute-done.3.rest_2_, ...), custom_call_target="tpu_custom_call" | custom-call | flops 402653184 | bytes 4718592 | tf_op jit(solution)/shard_map/rank_products/pallas_call | solution.py:188
  152.9 4.1 %rank_products.4 = bf16[768,128]{1,0:T(8,128)(2,1)S(1)} custom-call(s32[256]{0:T(256)S(1)} %copy-done.45, bf16[3072,2048]{1,0:T(8,128)(2,1)} %x_ref.15, bf16[3,2048,128]{2,1,0:T(8,128)(2,1)S(1)} %copy-done.3, bf16[3,2048,128]{2,1,0:T(8,128)(2,1)} %collective-permute-done.2.rest_1_, bf16[3,2048,128]{2,1,0:T(8,128)(2,1)} %collective-permute-done.3.rest_2_, ...), custom_call_target="tpu_custom_call" | custom-call | flops 402653184 | bytes 4718592 | tf_op jit(solution)/shard_map/rank_products/pallas_call | solution.py:188
  159.1 5.6 %collective-permute-done.25.rest_2_ = bf16[768,512]{1,0:T(8,128)(2,1)S(1)} collective-permute-done((bf16[768,512]{1,0:T(8,128)(2,1)}, bf16[768,512]{1,0:T(8,128)(2,1)S(1)}, u32[]{:S(2)}, u32[]{:S(2)}) %collective-permute-start.25) | collective-permute-done | bytes 786464 | tf_op jit(solution)/shard_map/ppermute | solution.py:321
  164.7 3.6 %collective-permute-start.15 = (bf16[3,2,64,256]{3,2,1,0:T(8,128)(2,1)S(1)}, bf16[3,2,64,256]{3,2,1,0:T(8,128)(2,1)S(1)}, u32[]{:S(2)}, u32[]{:S(2)}) collective-permute-start(bf16[3,2,64,256]{3,2,1,0:T(8,128)(2,1)S(1)} %copy-done.37), channel_id=1, source_target_pairs={{0,4},{4,8},{8,12},{1,5},{5,9},{9,13},{2,6},{6,10},{10,14},{3,7},{... | collective-permute-start | bytes 589832 | tf_op jit(solution)/shard_map/ppermute | solution.py:331
  168.4 13.2 %collective-permute-done.21.rest_2_ = bf16[768,512]{1,0:T(8,128)(2,1)S(1)} collective-permute-done((bf16[768,512]{1,0:T(8,128)(2,1)}, bf16[768,512]{1,0:T(8,128)(2,1)S(1)}, u32[]{:S(2)}, u32[]{:S(2)}) %collective-permute-start.21) | collective-permute-done | bytes 786464 | tf_op jit(solution)/shard_map/ppermute | solution.py:321
  183.1 15.3 %collective-permute-done.17.rest_2_ = bf16[768,512]{1,0:T(8,128)(2,1)S(1)} collective-permute-done((bf16[768,512]{1,0:T(8,128)(2,1)}, bf16[768,512]{1,0:T(8,128)(2,1)S(1)}, u32[]{:S(2)}, u32[]{:S(2)}) %collective-permute-start.17) | collective-permute-done | bytes 786464 | tf_op jit(solution)/shard_map/ppermute | solution.py:321
  199.0 4.7 %finish.4.rest_10_ = bf16[3072,2,256]{2,1,0:T(2,128)(2,1)} custom-call(s32[256]{0:T(256)S(1)} %copy-done.45, bf16[2,768,512]{2,1,0:T(8,128)(2,1)S(1)} %copy-done.10, bf16[2,768,512]{2,1,0:T(8,128)(2,1)} %collective-permute-done.24.rest_1_, bf16[768,512]{1,0:T(8,128)(2,1)S(1)} %collective-permute-done.25.rest_2_, bf16[768,128]{1,0:T(8,128)(2,1)S(1)} %copy-done.33, ...), custom_call_target="tpu_custom_call" | custom-call | flops 805306368 | bytes 3932160 | tf_op jit(solution)/shard_map/finish/pallas_call | solution.py:287
  203.7 4.7 %finish.5.rest_11_ = bf16[3072,2,256]{2,1,0:T(2,128)(2,1)} custom-call(s32[256]{0:T(256)S(1)} %copy-done.45, bf16[2,768,512]{2,1,0:T(8,128)(2,1)S(1)} %copy-done.13, bf16[2,768,512]{2,1,0:T(8,128)(2,1)} %collective-permute-done.20.rest_1_, bf16[768,512]{1,0:T(8,128)(2,1)S(1)} %collective-permute-done.21.rest_2_, ...), custom_call_target="tpu_custom_call", output_to_operand_aliasing={{}: (11, {})} | custom-call | flops 805306368 | bytes 3932160 | tf_op jit(solution)/shard_map/finish/pallas_call | solution.py:287
  208.5 10.8 %collective-permute-done.19.rest_4_ = bf16[768,128]{1,0:T(8,128)(2,1)S(1)} collective-permute-done((bf16[768,128]{1,0:T(8,128)(2,1)S(1)}, bf16[768,128]{1,0:T(8,128)(2,1)S(1)}, u32[]{:S(2)}, u32[]{:S(2)}) %collective-permute-start.19) | collective-permute-done | bytes 196640 | tf_op jit(solution)/shard_map/ppermute | solution.py:321
  219.3 4.7 %finish.6.rest_12_ = bf16[3072,2,256]{2,1,0:T(2,128)(2,1)} custom-call(s32[256]{0:T(256)S(1)} %copy-done.45, bf16[2,768,512]{2,1,0:T(8,128)(2,1)S(1)} %copy-done.21, bf16[2,768,512]{2,1,0:T(8,128)(2,1)} %collective-permute-done.16.rest_1_, bf16[768,512]{1,0:T(8,128)(2,1)S(1)} %collective-permute-done.17.rest_2_, ...), custom_call_target="tpu_custom_call", output_to_operand_aliasing={{}: (12, {})} | custom-call | flops 805306368 | bytes 3932160 | tf_op jit(solution)/shard_map/finish/pallas_call | solution.py:287
  224.1 3.5 %finish.7 = bf16[3072,2,256]{2,1,0:T(2,128)(2,1)} custom-call(s32[256]{0:T(256)S(1)} %copy-done.45, bf16[2,768,512]{2,1,0:T(8,128)(2,1)S(1)} %copy-done.16, bf16[2,768,512]{2,1,0:T(8,128)(2,1)S(1)} %copy-done.18, bf16[768,512]{1,0:T(8,128)(2,1)S(1)} %collective-permute-done.1.rest_2_, ...), custom_call_target="tpu_custom_call", output_to_operand_aliasing={{}: (13, {})} | custom-call | flops 805306368 | bytes 3932160 | tf_op jit(solution)/shard_map/finish/pallas_call | solution.py:287
  (146 shorter events, 35.1 us)
Async XLA Ops:
  0.0 42.0 %collective-permute-start.5 = (bf16[3,2048,128]{2,1,0:T(8,128)(2,1)}, bf16[3,2048,128]{2,1,0:T(8,128)(2,1)}, u32[]{:S(2)}, u32[]{:S(2)}) collective-permute-start(bf16[3,2048,128]{2,1,0:T(8,128)(2,1)} %rest_3_.5), channel_id=1, source_target_pairs={{0,4},{4,8},{8,12},{1,5},{5,9},{9,13},{2,6},{6,10},{10,14},{3,7},{... | collective-permute-start | bytes 4718600 | tf_op jit(solution)/shard_map/ppermute | solution.py:331
  6.1 51.9 %collective-permute-start.2 = (bf16[3,2048,128]{2,1,0:T(8,128)(2,1)}, bf16[3,2048,128]{2,1,0:T(8,128)(2,1)}, u32[]{:S(2)}, u32[]{:S(2)}) collective-permute-start(bf16[3,2048,128]{2,1,0:T(8,128)(2,1)} %rest_3_.5), channel_id=1, source_target_pairs={{4,0},{8,4},{12,8},{5,1},{9,5},{13,9},{6,2},{10,6},{14,10},{7,3},{... | collective-permute-start | bytes 4718600 | tf_op jit(solution)/shard_map/ppermute | solution.py:328
  18.9 37.8 %collective-permute-start.26 = (bf16[768,128]{1,0:T(8,128)(2,1)S(1)}, bf16[768,128]{1,0:T(8,128)(2,1)S(1)}, u32[]{:S(2)}, u32[]{:S(2)}) collective-permute-start(bf16[768,128]{1,0:T(8,128)(2,1)S(1)} %rank_products.7), channel_id=1, source_target_pairs={{0,1},{1,0},{2,3},{3,2},{4,5},{5,4},{6,7},{7,6},{8,9},{9,8},{10,11... | collective-permute-start | bytes 589832 | tf_op jit(solution)/shard_map/ppermute | solution.py:318
  19.0 40.6 %collective-permute-start.13 = (bf16[3,2,64,256]{3,2,1,0:T(8,128)(2,1)S(1)}, bf16[3,2,64,256]{3,2,1,0:T(8,128)(2,1)S(1)}, u32[]{:S(2)}, u32[]{:S(2)}) collective-permute-start(bf16[3,2,64,256]{3,2,1,0:T(8,128)(2,1)S(1)} %copy-done.4), channel_id=1, source_target_pairs={{0,4},{4,8},{8,12},{1,5},{5,9},{9,13},{2,6},{6,10},{10,14},{3,7},{... | collective-permute-start | bytes 589832 | tf_op jit(solution)/shard_map/ppermute | solution.py:331
  41.8 52.3 %collective-permute-start.24 = (bf16[2,768,512]{2,1,0:T(8,128)(2,1)}, bf16[2,768,512]{2,1,0:T(8,128)(2,1)}, u32[]{:S(2)}, u32[]{:S(2)}) collective-permute-start(bf16[2,768,512]{2,1,0:T(8,128)(2,1)} %get-tuple-element.20), channel_id=1, source_target_pairs={{0,1},{1,0},{2,3},{3,2},{4,5},{5,4},{6,7},{7,6},{8,9},{9,8},{10,11... | collective-permute-start | bytes 4718600 | tf_op jit(solution)/shard_map/ppermute | solution.py:318
  42.0 52.4 %collective-permute-start.6 = (bf16[3,2048,128]{2,1,0:T(8,128)(2,1)}, bf16[3,2048,128]{2,1,0:T(8,128)(2,1)}, u32[]{:S(2)}, u32[]{:S(2)}) collective-permute-start(bf16[3,2048,128]{2,1,0:T(8,128)(2,1)} %collective-permute-done.5.rest_4_), channel_id=1, source_target_pairs={{0,4},{4,8},{8,12},{1,5},{5,9},{9,13},{2,6},{6,10},{10,14},{3,7},{... | collective-permute-start | bytes 4718600 | tf_op jit(solution)/shard_map/ppermute | solution.py:331
  56.7 9.6 %collective-permute-start.10 = (bf16[3,2,64,256]{3,2,1,0:T(8,128)(2,1)S(1)}, bf16[3,2,64,256]{3,2,1,0:T(8,128)(2,1)S(1)}, u32[]{:S(2)}, u32[]{:S(2)}) collective-permute-start(bf16[3,2,64,256]{3,2,1,0:T(8,128)(2,1)S(1)} %copy-done.4), channel_id=1, source_target_pairs={{4,0},{8,4},{12,8},{5,1},{9,5},{13,9},{6,2},{10,6},{14,10},{7,3},{... | collective-permute-start | bytes 589832 | tf_op jit(solution)/shard_map/ppermute | solution.py:328
  58.0 41.2 %collective-permute-start.3 = (bf16[3,2048,128]{2,1,0:T(8,128)(2,1)}, bf16[3,2048,128]{2,1,0:T(8,128)(2,1)}, u32[]{:S(2)}, u32[]{:S(2)}) collective-permute-start(bf16[3,2048,128]{2,1,0:T(8,128)(2,1)} %collective-permute-done.2.rest_1_), channel_id=1, source_target_pairs={{4,0},{8,4},{12,8},{5,1},{9,5},{13,9},{6,2},{10,6},{14,10},{7,3},{... | collective-permute-start | bytes 4718600 | tf_op jit(solution)/shard_map/ppermute | solution.py:328
  59.5 47.7 %collective-permute-start.20 = (bf16[2,768,512]{2,1,0:T(8,128)(2,1)}, bf16[2,768,512]{2,1,0:T(8,128)(2,1)}, u32[]{:S(2)}, u32[]{:S(2)}) collective-permute-start(bf16[2,768,512]{2,1,0:T(8,128)(2,1)} %get-tuple-element.18), channel_id=1, source_target_pairs={{0,1},{1,0},{2,3},{3,2},{4,5},{5,4},{6,7},{7,6},{8,9},{9,8},{10,11... | collective-permute-start | bytes 4718600 | tf_op jit(solution)/shard_map/ppermute | solution.py:318
  66.3 12.7 %collective-permute-start.27 = (bf16[768,128]{1,0:T(8,128)(2,1)S(1)}, bf16[768,128]{1,0:T(8,128)(2,1)S(1)}, u32[]{:S(2)}, u32[]{:S(2)}) collective-permute-start(bf16[768,128]{1,0:T(8,128)(2,1)S(1)} %add_convert_fusion.4.rest_3_), channel_id=1, source_target_pairs={{0,2},{1,3},{2,0},{3,1},{4,6},{5,7},{6,4},{7,5},{8,10},{9,11},{10,... | collective-permute-start | bytes 589832 | tf_op jit(solution)/shard_map/ppermute | solution.py:321
  79.7 56.9 %collective-permute-start.16 = (bf16[2,768,512]{2,1,0:T(8,128)(2,1)}, bf16[2,768,512]{2,1,0:T(8,128)(2,1)}, u32[]{:S(2)}, u32[]{:S(2)}) collective-permute-start(bf16[2,768,512]{2,1,0:T(8,128)(2,1)} %get-tuple-element.16), channel_id=1, source_target_pairs={{0,1},{1,0},{2,3},{3,2},{4,5},{5,4},{6,7},{7,6},{8,9},{9,8},{10,11... | collective-permute-start | bytes 4718600 | tf_op jit(solution)/shard_map/ppermute | solution.py:318
  94.1 50.5 %collective-permute-start = (bf16[2,768,512]{2,1,0:T(8,128)(2,1)}, bf16[2,768,512]{2,1,0:T(8,128)(2,1)S(1)}, u32[]{:S(2)}, u32[]{:S(2)}) collective-permute-start(bf16[2,768,512]{2,1,0:T(8,128)(2,1)} %get-tuple-element.14), channel_id=1, source_target_pairs={{0,1},{1,0},{2,3},{3,2},{4,5},{5,4},{6,7},{7,6},{8,9},{9,8},{10,11... | collective-permute-start | bytes 4718600 | tf_op jit(solution)/shard_map/ppermute | solution.py:318
  94.4 52.9 %collective-permute-start.7 = (bf16[3,2048,128]{2,1,0:T(8,128)(2,1)}, bf16[3,2048,128]{2,1,0:T(8,128)(2,1)S(1)}, u32[]{:S(2)}, u32[]{:S(2)}) collective-permute-start(bf16[3,2048,128]{2,1,0:T(8,128)(2,1)} %collective-permute-done.6.rest_5_), channel_id=1, source_target_pairs={{0,4},{4,8},{8,12},{1,5},{5,9},{9,13},{2,6},{6,10},{10,14},{3,7},{... | collective-permute-start | bytes 4718600 | tf_op jit(solution)/shard_map/ppermute | solution.py:331
  99.2 49.6 %collective-permute-start.4 = (bf16[3,2048,128]{2,1,0:T(8,128)(2,1)}, bf16[3,2048,128]{2,1,0:T(8,128)(2,1)S(1)}, u32[]{:S(2)}, u32[]{:S(2)}) collective-permute-start(bf16[3,2048,128]{2,1,0:T(8,128)(2,1)} %collective-permute-done.3.rest_2_), channel_id=1, source_target_pairs={{4,0},{8,4},{12,8},{5,1},{9,5},{13,9},{6,2},{10,6},{14,10},{7,3},{... | collective-permute-start | bytes 4718600 | tf_op jit(solution)/shard_map/ppermute | solution.py:328
  107.3 2.5 %collective-permute-start.22 = (bf16[768,128]{1,0:T(8,128)(2,1)S(1)}, bf16[768,128]{1,0:T(8,128)(2,1)S(1)}, u32[]{:S(2)}, u32[]{:S(2)}) collective-permute-start(bf16[768,128]{1,0:T(8,128)(2,1)S(1)} %rank_products.6), channel_id=1, source_target_pairs={{0,1},{1,0},{2,3},{3,2},{4,5},{5,4},{6,7},{7,6},{8,9},{9,8},{10,11... | collective-permute-start | bytes 589832 | tf_op jit(solution)/shard_map/ppermute | solution.py:318
  109.8 25.4 %collective-permute-start.14 = (bf16[3,2,64,256]{3,2,1,0:T(8,128)(2,1)S(1)}, bf16[3,2,64,256]{3,2,1,0:T(8,128)(2,1)S(1)}, u32[]{:S(2)}, u32[]{:S(2)}) collective-permute-start(bf16[3,2,64,256]{3,2,1,0:T(8,128)(2,1)S(1)} %copy-done.23), channel_id=1, source_target_pairs={{0,4},{4,8},{8,12},{1,5},{5,9},{9,13},{2,6},{6,10},{10,14},{3,7},{... | collective-permute-start | bytes 589832 | tf_op jit(solution)/shard_map/ppermute | solution.py:331
  135.2 8.8 %collective-permute-start.11 = (bf16[3,2,64,256]{3,2,1,0:T(8,128)(2,1)S(1)}, bf16[3,2,64,256]{3,2,1,0:T(8,128)(2,1)S(1)}, u32[]{:S(2)}, u32[]{:S(2)}) collective-permute-start(bf16[3,2,64,256]{3,2,1,0:T(8,128)(2,1)S(1)} %copy-done.26), channel_id=1, source_target_pairs={{4,0},{8,4},{12,8},{5,1},{9,5},{13,9},{6,2},{10,6},{14,10},{7,3},{... | collective-permute-start | bytes 589832 | tf_op jit(solution)/shard_map/ppermute | solution.py:328
  136.5 9.5 %collective-permute-start.23 = (bf16[768,128]{1,0:T(8,128)(2,1)S(1)}, bf16[768,128]{1,0:T(8,128)(2,1)S(1)}, u32[]{:S(2)}, u32[]{:S(2)}) collective-permute-start(bf16[768,128]{1,0:T(8,128)(2,1)S(1)} %add_convert_fusion.5.rest_3_), channel_id=1, source_target_pairs={{0,2},{1,3},{2,0},{3,1},{4,6},{5,7},{6,4},{7,5},{8,10},{9,11},{10,... | collective-permute-start | bytes 589832 | tf_op jit(solution)/shard_map/ppermute | solution.py:321
  144.0 20.7 %collective-permute-start.25 = (bf16[768,512]{1,0:T(8,128)(2,1)}, bf16[768,512]{1,0:T(8,128)(2,1)S(1)}, u32[]{:S(2)}, u32[]{:S(2)}) collective-permute-start(bf16[768,512]{1,0:T(8,128)(2,1)} %fusion.3), channel_id=1, source_target_pairs={{0,2},{1,3},{2,0},{3,1},{4,6},{5,7},{6,4},{7,5},{8,10},{9,11},{10,... | collective-permute-start | bytes 2359304 | tf_op jit(solution)/shard_map/ppermute | solution.py:321
  144.6 37.0 %collective-permute-start.21 = (bf16[768,512]{1,0:T(8,128)(2,1)}, bf16[768,512]{1,0:T(8,128)(2,1)S(1)}, u32[]{:S(2)}, u32[]{:S(2)}) collective-permute-start(bf16[768,512]{1,0:T(8,128)(2,1)} %fusion.2), channel_id=1, source_target_pairs={{0,2},{1,3},{2,0},{3,1},{4,6},{5,7},{6,4},{7,5},{8,10},{9,11},{10,... | collective-permute-start | bytes 2359304 | tf_op jit(solution)/shard_map/ppermute | solution.py:321
  146.8 51.7 %collective-permute-start.17 = (bf16[768,512]{1,0:T(8,128)(2,1)}, bf16[768,512]{1,0:T(8,128)(2,1)S(1)}, u32[]{:S(2)}, u32[]{:S(2)}) collective-permute-start(bf16[768,512]{1,0:T(8,128)(2,1)} %fusion.1), channel_id=1, source_target_pairs={{0,2},{1,3},{2,0},{3,1},{4,6},{5,7},{6,4},{7,5},{8,10},{9,11},{10,... | collective-permute-start | bytes 2359304 | tf_op jit(solution)/shard_map/ppermute | solution.py:321
  148.5 8.4 %collective-permute-start.18 = (bf16[768,128]{1,0:T(8,128)(2,1)S(1)}, bf16[768,128]{1,0:T(8,128)(2,1)S(1)}, u32[]{:S(2)}, u32[]{:S(2)}) collective-permute-start(bf16[768,128]{1,0:T(8,128)(2,1)S(1)} %rank_products.5), channel_id=1, source_target_pairs={{0,1},{1,0},{2,3},{3,2},{4,5},{5,4},{6,7},{7,6},{8,9},{9,8},{10,11... | collective-permute-start | bytes 589832 | tf_op jit(solution)/shard_map/ppermute | solution.py:318
  148.6 50.4 %copy-start.33 = (bf16[768,128]{1,0:T(8,128)(2,1)S(1)}, bf16[768,128]{1,0:T(8,128)(2,1)}, u32[]{:S(2)}) copy-start(bf16[768,128]{1,0:T(8,128)(2,1)} %copy-done.32) | copy-start | bytes 589828
  148.6 50.4 %copy-start.41 = (bf16[768,128]{1,0:T(8,128)(2,1)S(1)}, bf16[768,128]{1,0:T(8,128)(2,1)}, u32[]{:S(2)}) copy-start(bf16[768,128]{1,0:T(8,128)(2,1)} %copy-done.40) | copy-start | bytes 589828
  150.0 74.1 %collective-permute-start.1 = (bf16[768,512]{1,0:T(8,128)(2,1)S(1)}, bf16[768,512]{1,0:T(8,128)(2,1)S(1)}, u32[]{:S(2)}, u32[]{:S(2)}) collective-permute-start(bf16[768,512]{1,0:T(8,128)(2,1)S(1)} %fusion), channel_id=1, source_target_pairs={{0,2},{1,3},{2,0},{3,1},{4,6},{5,7},{6,4},{7,5},{8,10},{9,11},{10,... | collective-permute-start | bytes 2359304 | tf_op jit(solution)/shard_map/ppermute | solution.py:321
  152.9 46.1 %copy-start.10 = (bf16[2,768,512]{2,1,0:T(8,128)(2,1)S(1)}, bf16[2,768,512]{2,1,0:T(8,128)(2,1)}, u32[]{:S(2)}) copy-start(bf16[2,768,512]{2,1,0:T(8,128)(2,1)} %copy-done.8) | copy-start | bytes 4718596
  157.0 1.5 collective-permute-start.8
  158.5 60.8 %collective-permute-start.19 = (bf16[768,128]{1,0:T(8,128)(2,1)S(1)}, bf16[768,128]{1,0:T(8,128)(2,1)S(1)}, u32[]{:S(2)}, u32[]{:S(2)}) collective-permute-start(bf16[768,128]{1,0:T(8,128)(2,1)S(1)} %add_convert_fusion.6.rest_3_), channel_id=1, source_target_pairs={{0,2},{1,3},{2,0},{3,1},{4,6},{5,7},{6,4},{7,5},{8,10},{9,11},{10,... | collective-permute-start | bytes 589832 | tf_op jit(solution)/shard_map/ppermute | solution.py:321
  159.1 44.6 %copy-start.13 = (bf16[2,768,512]{2,1,0:T(8,128)(2,1)S(1)}, bf16[2,768,512]{2,1,0:T(8,128)(2,1)}, u32[]{:S(2)}) copy-start(bf16[2,768,512]{2,1,0:T(8,128)(2,1)} %copy-done.11) | copy-start | bytes 4718596
  164.7 59.3 %collective-permute-start.15 = (bf16[3,2,64,256]{3,2,1,0:T(8,128)(2,1)S(1)}, bf16[3,2,64,256]{3,2,1,0:T(8,128)(2,1)S(1)}, u32[]{:S(2)}, u32[]{:S(2)}) collective-permute-start(bf16[3,2,64,256]{3,2,1,0:T(8,128)(2,1)S(1)} %copy-done.37), channel_id=1, source_target_pairs={{0,4},{4,8},{8,12},{1,5},{5,9},{9,13},{2,6},{6,10},{10,14},{3,7},{... | collective-permute-start | bytes 589832 | tf_op jit(solution)/shard_map/ppermute | solution.py:331
  181.6 42.5 %collective-permute-start.12 = (bf16[3,2,64,256]{3,2,1,0:T(8,128)(2,1)S(1)}, bf16[3,2,64,256]{3,2,1,0:T(8,128)(2,1)S(1)}, u32[]{:S(2)}, u32[]{:S(2)}) collective-permute-start(bf16[3,2,64,256]{3,2,1,0:T(8,128)(2,1)S(1)} %copy-done.39), channel_id=1, source_target_pairs={{4,0},{8,4},{12,8},{5,1},{9,5},{13,9},{6,2},{10,6},{14,10},{7,3},{... | collective-permute-start | bytes 589832 | tf_op jit(solution)/shard_map/ppermute | solution.py:328
  198.4 25.7 %collective-permute-start.9 = (bf16[768,128]{1,0:T(8,128)(2,1)S(1)}, bf16[768,128]{1,0:T(8,128)(2,1)S(1)}, u32[]{:S(2)}, u32[]{:S(2)}) collective-permute-start(bf16[768,128]{1,0:T(8,128)(2,1)S(1)} %add_convert_fusion.7.rest_3_), channel_id=1, source_target_pairs={{0,2},{1,3},{2,0},{3,1},{4,6},{5,7},{6,4},{7,5},{8,10},{9,11},{10,... | collective-permute-start | bytes 589832 | tf_op jit(solution)/shard_map/ppermute | solution.py:321
  (45 other events, 599.9 us)

commit v2 on v1

v2 whole, which is shorter than its diff:
```python
import jax
import jax.numpy as jnp
from jax import lax
from jax.experimental import pallas as pl
from jax.experimental.pallas import tpu as pltpu
from jax.sharding import PartitionSpec as P

BF = jnp.bfloat16
F32 = jnp.float32
BASE_CHUNKS = (2, 2, 2, 2, 2, 2)
RANK_CHUNKS = 4
SMEM = pltpu.SMEM
ANY = pl.BlockSpec(memory_space=pl.ANY)


def cost(flops, moved):
    return pl.CostEstimate(
        flops=int(flops * 1), bytes_accessed=int(moved * 1), transcendentals=0
    )


ORDER, SOURCE, ROW, LENGTH = range(4)


def params(mib=60):
    return pltpu.CompilerParams(vmem_limit_bytes=mib * 1024 * 1024)


def plan_requests(table, adapters, lengths, here, n_z, stored):
    requests, known = adapters.shape[0], table.shape[0]
    shape = (requests, 128)

    def body(table_ref, adapter_ref, length_ref, here_ref, plan_ref):
        me = here_ref[0]
        request = lax.broadcasted_iota(jnp.int32, shape, 0)
        lane = lax.broadcasted_iota(jnp.int32, shape, 1)
        diagonal = request == lane

        def wide(ref, n):
            return jnp.pad(ref[...], ((0, 0), (0, 128 - n)))

        def down(a):
            return jnp.sum(jnp.where(diagonal, a, 0), axis=1, keepdims=True)

        def across(a):
            return jnp.sum(jnp.where(diagonal, a, 0), axis=0, keepdims=True)

        hit = (down(wide(adapter_ref, requests)) == lane) & (lane < known)
        slot = jnp.sum(jnp.where(hit, wide(table_ref, known), 0), 1, keepdims=True)
        owner = jnp.zeros_like(slot)
        for z in range(1, n_z):
            owner += jnp.where(slot >= z * stored, 1, 0)
        source = jnp.where(owner >= me, owner - me, n_z - 1 + me - owner)
        key = jnp.abs(owner - me) * 128 + request[:, :1]
        before = (across(key) < key) & (lane < requests)
        place = jnp.sum(jnp.where(before, 1, 0), axis=1, keepdims=True)
        at = place == lane

        def placed(a):
            return jnp.sum(jnp.where(at, a, 0), axis=0, keepdims=True)

        plan_ref[ORDER : ORDER + 1] = placed(request)
        plan_ref[SOURCE : SOURCE + 1] = placed(source)
        plan_ref[ROW : ROW + 1] = placed(slot - owner * stored)
        plan_ref[LENGTH : LENGTH + 1] = placed(down(wide(length_ref, requests)))

    vmem = pl.BlockSpec(memory_space=pltpu.VMEM)
    return pl.pallas_call(
        body,
        out_shape=jax.ShapeDtypeStruct((8, 128), jnp.int32),
        in_specs=[vmem, vmem, vmem, pl.BlockSpec(memory_space=SMEM)],
        out_specs=vmem,
        cost_estimate=cost(0, 1 << 20),
        name="plan_requests",
    )(table[None, :], adapters[None, :], lengths[None, :], here)


def split_weight(plan, slots, hidden, weight, count, prefill):
    features, _, columns = weight.shape
    n_t = slots.shape[0]
    n_x = n_t // 2
    width = columns // n_t
    rows, half = 256, 128
    steps = features // rows

    def body(plan_ref, slot_ref, *rest):
        x_refs, (w_ref, o_ref, send_ref, keep_ref, total) = rest[:count], rest[count:]
        step = pl.program_id(0)
        out_row = lax.broadcasted_iota(jnp.int32, (2 * half, 2 * half), 0)
        in_row = lax.broadcasted_iota(jnp.int32, (2 * half, 2 * half), 1)
        pick = in_row == 2 * (out_row % half) + out_row // half
        pick = pick.astype(F32).astype(BF)
        for b in range(rows // half):
            mixed = w_ref[b * half : (b + 1) * half].reshape(2 * half, columns)
            apart = jnp.dot(pick, mixed, preferred_element_type=F32).astype(BF)
            for t in range(n_t):
                for s in range(2):
                    o_ref[
                        slot_ref[t],
                        b * half : (b + 1) * half,
                        s * width : (s + 1) * width,
                    ] = apart[s * half : (s + 1) * half, t * width : (t + 1) * width]

        @pl.when(step == 0)
        def _():
            total[...] = jnp.zeros_like(total)

        for r in range(count):
            for j in range(n_t):
                total[j, r * prefill : (r + 1) * prefill] += jnp.dot(
                    x_refs[r][...], o_ref[j], preferred_element_type=F32
                )

        @pl.when(step == steps - 1)
        def _():
            for j in range(n_t):
                out = send_ref if j < n_x else keep_ref
                out[j % n_x] = total[j].astype(BF)

    out = jax.ShapeDtypeStruct((n_x, count * prefill, 2 * width), BF)
    block = pl.BlockSpec((n_x, count * prefill, 2 * width), lambda i, p, s: (0, 0, 0))
    return pl.pallas_call(
        body,
        out_shape=(jax.ShapeDtypeStruct((n_t, features, 2 * width), BF), out, out),
        grid_spec=pltpu.PrefetchScalarGridSpec(
            num_scalar_prefetch=2,
            grid=(steps,),
            in_specs=[
                pl.BlockSpec((prefill, rows), lambda i, p, s, r=r: (p[ORDER, r], i))
                for r in range(count)
            ]
            + [pl.BlockSpec((rows, 2, columns), lambda i, p, s: (i, 0, 0))],
            out_specs=(
                pl.BlockSpec((n_t, rows, 2 * width), lambda i, p, s: (0, i, 0)),
                block,
                block,
            ),
            scratch_shapes=[pltpu.VMEM((n_t, count * prefill, 2 * width), F32)],
        ),
        compiler_params=params(),
        cost_estimate=cost(2 * count * prefill * features * 2 * columns, 8 * features * columns),
        name="split_weight",
    )(plan, slots, *[hidden] * count, weight)


def base_products(plan, hidden, weight, first, count, prefill, after):
    n_t, features, width = weight.shape
    n_x = n_t // 2
    short = prefill // 2
    n_after = len(after)

    def body(plan_ref, x_ref, w_ref, *rest):
        send_ref, keep_ref = rest[n_after:]
        live = plan_ref[LENGTH, first + pl.program_id(0)]

        def products(rows):
            for j in range(n_t):
                out = send_ref if j < n_x else keep_ref
                out[j % n_x, :rows] = jnp.dot(
                    x_ref[:rows], w_ref[j], preferred_element_type=F32
                ).astype(BF)
                if rows < prefill:
                    out[j % n_x, rows:] = jnp.zeros((prefill - rows, width), BF)

        @pl.when(live > short)
        def _():
            products(prefill)

        @pl.when(live <= short)
        def _():
            products(short)

    out = jax.ShapeDtypeStruct((n_x, count * prefill, width), BF)
    block = pl.BlockSpec((n_x, prefill, width), lambda i, p: (0, i, 0))
    return pl.pallas_call(
        body,
        out_shape=(out, out),
        grid_spec=pltpu.PrefetchScalarGridSpec(
            num_scalar_prefetch=1,
            grid=(count,),
            in_specs=[
                pl.BlockSpec(
                    (prefill, features), lambda i, p: (p[ORDER, first + i], 0)
                ),
                pl.BlockSpec((n_t, features, width), lambda i, p: (0, 0, 0)),
            ]
            + [ANY] * n_after,
            out_specs=(block, block),
        ),
        compiler_params=params(),
        cost_estimate=cost(2 * count * prefill * features * width * n_t, 2 * n_t * features * width),
        name="base_products",
    )(plan, hidden, weight, *after)


def pair_sum(one, other, index, after):
    _, rows, width = one.shape
    block = rows // 2

    n_after = len(after)

    def body(a_ref, b_ref, *rest):
        rest[n_after][...] = (a_ref[0].astype(F32) + b_ref[0].astype(F32)).astype(BF)

    spec = pl.BlockSpec((1, block, width), lambda i: (index, i, 0))
    return pl.pallas_call(
        body,
        out_shape=jax.ShapeDtypeStruct((rows, width), BF),
        grid=(rows // block,),
        in_specs=[spec, spec] + [ANY] * n_after,
        out_specs=pl.BlockSpec((block, width), lambda i: (i, 0)),
        compiler_params=params(),
        cost_estimate=cost(rows * width, 6 * rows * width),
        name="pair_sum",
    )(one, other, *after)


def copy_after(a, after):
    def body(a_ref, *rest):
        rest[-1][...] = a_ref[...]

    vmem = pl.BlockSpec(memory_space=pltpu.VMEM)
    return pl.pallas_call(
        body,
        out_shape=jax.ShapeDtypeStruct(a.shape, a.dtype),
        in_specs=[vmem] + [ANY] * len(after),
        out_specs=vmem,
        compiler_params=params(),
        cost_estimate=cost(0, 4 * a.size),
        name="copy_after",
    )(a, *after)


def fetch(refs, source, row, target, sem):
    for k, ref in refs:

        @pl.when(source == k)
        def _():
            pltpu.make_async_copy(ref.at[row], target, sem).start()


def rank_products(plan, hidden, maps, first, count, prefill, after):
    sources = list(maps)
    _, features, ranks = maps[sources[0]].shape
    n_map, n_after = len(maps), len(after)

    def body(plan_ref, x_ref, *rest):
        refs = list(zip(sources, rest[:n_map]))
        o_ref, held, sems = rest[n_map + n_after :]
        step = pl.program_id(0)

        @pl.when(step == 0)
        def _():
            for i in range(count):
                fetch(
                    refs,
                    plan_ref[SOURCE, first + i],
                    plan_ref[ROW, first + i],
                    held.at[i],
                    sems.at[i],
                )

        pltpu.make_async_copy(rest[0].at[0], held.at[step], sems.at[step]).wait()
        o_ref[...] = jnp.dot(
            x_ref[...], held[step], preferred_element_type=F32
        ).astype(BF)

    return pl.pallas_call(
        body,
        out_shape=jax.ShapeDtypeStruct((count * prefill, ranks), BF),
        grid_spec=pltpu.PrefetchScalarGridSpec(
            num_scalar_prefetch=1,
            grid=(count,),
            in_specs=[
                pl.BlockSpec((prefill, features), lambda i, p: (p[ORDER, first + i], 0))
            ]
            + [ANY] * (n_map + n_after),
            out_specs=pl.BlockSpec((prefill, ranks), lambda i, p: (i, 0)),
            scratch_shapes=[
                pltpu.VMEM((count, features, ranks), BF),
                pltpu.SemaphoreType.DMA((count,)),
            ],
        ),
        compiler_params=params(),
        cost_estimate=cost(2 * count * prefill * features * ranks, 2 * count * features * (prefill + ranks)),
        name="rank_products",
    )(plan, hidden, *maps.values(), *after)


def finish(plan, bases, ranks, maps, before, first, count, prefill, shape):
    sources = list(maps)
    _, _, depth, columns = maps[sources[0]].shape
    half = prefill // 2
    n_map = len(maps)

    def body(plan_ref, *rest):
        base_refs, rank_refs = [], []
        for refs, pieces in ((base_refs, bases), (rank_refs, ranks)):
            for _, _, arrays in pieces:
                refs.append(rest[: len(arrays)])
                rest = rest[len(arrays) :]
        map_refs = list(zip(sources, rest[:n_map]))
        o_ref, held, sems = rest[-3:]
        step = pl.program_id(0)
        at = first + step

        @pl.when(step == 0)
        def _():
            for i in range(count):
                fetch(
                    map_refs,
                    plan_ref[SOURCE, first + i],
                    plan_ref[ROW, first + i],
                    held.at[i],
                    sems.at[i],
                )

        pltpu.make_async_copy(
            map_refs[0][1].at[0], held.at[step], sems.at[step]
        ).wait()
        live = plan_ref[LENGTH, at]
        up = held[step].reshape(2 * depth, columns)
        mix_row = lax.broadcasted_iota(jnp.int32, (2 * half, 2 * half), 0)
        mix_column = lax.broadcasted_iota(jnp.int32, (2 * half, 2 * half), 1)
        mix = mix_column == mix_row // 2 + half * (mix_row % 2)
        mix = mix.astype(F32).astype(BF)
        twice_row = lax.broadcasted_iota(jnp.int32, (2 * half, half), 0)
        twice_column = lax.broadcasted_iota(jnp.int32, (2 * half, half), 1)
        twice = (twice_column == twice_row // 2).astype(F32).astype(BF)
        lane = lax.broadcasted_iota(jnp.int32, (2 * half, 2 * depth), 1)
        side = lax.broadcasted_iota(jnp.int32, (2 * half, 2 * depth), 0) % 2
        own_side = lane // depth == side
        token = lax.broadcasted_iota(jnp.int32, (2 * half, columns), 0) // 2

        def rows_for(refs, b):
            rows = slice(b * half, (b + 1) * half)
            total = jnp.zeros((2 * half, columns), F32)
            for ref in refs:
                piece = ref[0, rows] if len(ref.shape) == 3 else ref[rows]
                piece = jnp.concatenate([piece[:, :columns], piece[:, columns:]], 0)
                total += jnp.dot(mix, piece, preferred_element_type=F32)
            rank = None
            for (start, _, _), pieces in zip(ranks, rank_refs):
                value = pieces[0][rows].astype(F32)
                for ref in pieces[1:]:
                    value += ref[rows].astype(F32)
                rank = value if rank is None else jnp.where(at >= start, value, rank)
            rank = jnp.dot(twice, rank.astype(BF), preferred_element_type=F32)
            rank = jnp.where(own_side, rank, 0.0).astype(BF)
            total += jnp.dot(rank, up, preferred_element_type=F32)
            total = jnp.where(token + b * half < live, total, 0.0)
            o_ref[rows] = total.astype(BF).reshape(half, 2, columns)

        for (start, n, _), refs in zip(bases, base_refs):

            @pl.when((at >= start) & (at < start + n))
            def _():
                rows_for(refs, 0)

                @pl.when(live > half)
                def _():
                    rows_for(refs, 1)

                @pl.when(live <= half)
                def _():
                    o_ref[half:] = jnp.zeros((half, 2, columns), BF)

    operands, specs = [plan], []
    for start, n, pieces in bases + ranks:

        def block(i, p, start=start, n=n):
            return jnp.clip(first + i - start, 0, n - 1)

        for a in pieces:
            operands.append(a)
            if a.ndim == 3:
                specs.append(
                    pl.BlockSpec(
                        (1, prefill, a.shape[2]),
                        lambda i, p, block=block: (0, block(i, p), 0),
                    )
                )
            else:
                specs.append(
                    pl.BlockSpec(
                        (prefill, a.shape[1]),
                        lambda i, p, block=block: (block(i, p), 0),
                    )
                )
    operands += maps.values()
    specs += [ANY] * n_map
    aliases = {}
    if before is not None:
        aliases = {len(operands): 0}
        operands.append(before)
        specs.append(ANY)
    return pl.pallas_call(
        body,
        out_shape=jax.ShapeDtypeStruct(shape, BF),
        grid_spec=pltpu.PrefetchScalarGridSpec(
            num_scalar_prefetch=1,
            grid=(count,),
            in_specs=specs,
            out_specs=pl.BlockSpec(
                (prefill, 2, columns), lambda i, p: (p[ORDER, first + i], 0, 0)
            ),
            scratch_shapes=[
                pltpu.VMEM((count, 2, depth, columns), BF),
                pltpu.SemaphoreType.DMA((count,)),
            ],
        ),
        input_output_aliases=aliases,
        compiler_params=params(),
        cost_estimate=cost(12 * count * prefill * prefill * 2 * columns, 20 * count * prefill * columns),
        name="finish",
    )(*operands)


def solution(mesh):
    n_z, n_t = mesh.shape["adapter"], mesh.shape["tensor"]
    n_x = n_t // 2

    def core_swap(a):
        return lax.ppermute(a, "tensor", [(t, t ^ 1) for t in range(n_t)])

    def chip_shift(a, k):
        return lax.ppermute(
            a,
            "tensor",
            [(2 * x + c, 2 * ((x + k) % n_x) + c) for x in range(n_x) for c in (0, 1)],
        )

    def leftward(a, hops=1):
        return lax.ppermute(a, "adapter", [(z, z - hops) for z in range(hops, n_z)])

    def rightward(a, hops=1):
        return lax.ppermute(a, "adapter", [(z - hops, z) for z in range(hops, n_z)])

    def per_device(hidden, weight, down, up, table, adapters, lengths):
        requests = adapters.shape[0]
        prefill = hidden.shape[0] // requests
        stored = down.shape[0]
        columns = up.shape[3]
        by_distance = n_z == RANK_CHUNKS
        z, t = lax.axis_index("adapter"), lax.axis_index("tensor")
        plan = plan_requests(
            table, adapters, lengths, jnp.reshape(z, (1,)), n_z, stored
        )

        downs = {0: down}
        for hops in range(1, n_z):
            left, right = downs[hops - 1], downs[0 if hops == 1 else n_z + hops - 2]
            downs[hops] = leftward(left)
            downs[n_z - 1 + hops] = rightward(right)

        def within(maps, hops):
            keys = range(hops + 1), range(n_z, n_z + hops)
            return {k: maps[k] for part in keys for k in part}

        dest = jnp.arange(n_t, dtype=jnp.int32)
        away = (dest // 2 - t // 2 + n_x) % n_x
        slots = jnp.where(dest % 2 == t % 2, n_x + away, away)

        bases, pairs = [], []
        waiting = []

        def send_on():
            first, count, keep, got = waiting.pop(0)
            pieces = [keep, got]
            for k in range(1, n_x):
                pairs.append(pair_sum(keep, got, k, waiting[0][2:3] if waiting else []))
                pieces.append(chip_shift(pairs[-1], k))
            bases.append((first, count, pieces))

        split, send, keep = split_weight(
            plan, slots, hidden, weight, BASE_CHUNKS[0], prefill
        )
        waiting.append((0, BASE_CHUNKS[0], keep, core_swap(send)))

        near = [downs[1], downs[n_z]]
        middle = [downs[2], downs[n_z + 1]]
        for chunk in range(1, len(BASE_CHUNKS)):
            first, count = sum(BASE_CHUNKS[:chunk]), BASE_CHUNKS[chunk]
            after = pairs[-1:]
            if chunk == 3:
                after = after + near
            if chunk >= 3:
                after = after + [bases[chunk - 3][2][-1]]
            send, keep = base_products(
                plan, hidden, split, first, count, prefill, after
            )
            waiting.append((first, count, keep, core_swap(send)))
            send_on()

        ups = {0: up}
        late_up = copy_after(up, middle)
        for hops in range(1, n_z):
            ups[hops] = leftward(late_up, hops)
            ups[n_z - 1 + hops] = rightward(late_up, hops)

        ranks = []

        def rank(chunk, after):
            count = requests // RANK_CHUNKS
            hops = chunk if by_distance else n_z - 1
            part = rank_products(
                plan, hidden, within(downs, hops), chunk * count, count, prefill, after
            )
            pair = (part.astype(F32) + core_swap(part).astype(F32)).astype(BF)
            pieces = [pair] + [chip_shift(pair, k) for k in range(1, n_x)]
            ranks.append((chunk * count, count, pieces))

        rank(0, [pairs[-1]])
        send_on()
        rank(1, [pairs[-1]])
        rank(2, [ranks[1][2][0]] + [b[2][-1] for b in bases[2:4]])
        shape = (requests * prefill, 2, columns)
        early = 3 * requests // RANK_CHUNKS
        out = finish(
            plan,
            bases,
            ranks[:3],
            within(ups, 2 if by_distance else n_z - 1),
            None,
            0,
            early,
            prefill,
            shape,
        )
        rank(3, [])
        return finish(
            plan,
            bases[-2:],
            ranks[3:],
            within(ups, n_z - 1),
            out,
            early,
            requests - early,
            prefill,
            shape,
        )

    return jax.shard_map(
        per_device,
        mesh=mesh,
        in_specs=(
            P(("group", "adapter"), "tensor"),
            P("tensor", None, None),
            P(("group", "adapter"), "tensor", None),
            P(("group", "adapter"), None, None, "tensor"),
            P("group"),
            P(("group", "adapter")),
            P(("group", "adapter")),
        ),
        out_specs=P(("group", "adapter"), None, "tensor"),
        check_vma=False,
    )
```

time: 229 us -> 208 us (0.908); the launches traced: 228 us -> 205 us
  waiting for transfers between devices: 77.4 us -> 18.4 us
  Pallas kernels: 74.9 us -> 121 us
  local copies, waits for them, and re-layouts: 24.8 us -> 6.5 us
  starting transfers between devices: 42.4 us -> 55.1 us
  other arithmetic: 7.5 us -> 2.43 us
    ppermute x8 -> x10, waiting for transfers between devices: 45 us -> 11.4 us  [chip_shift(): lax.ppermute(a, 'tensor', [(2 * x + c, 2 * ((x + k) % n_x) + c) for x in...]
    ppermute x12, waiting for transfers between devices: 31.3 us -> 5.13 us  [the longest x6 3.77 us: rightward(): return lax.ppermute(a, 'adapter', [(z - hops, z) for z in range(hops, n_z)])]
    pallas_call x2 -> x9, Pallas kernels: 7.72 us -> 30.6 us  [the longest x1 15.6 us: split_weight(): pl.pallas_call(body, out_shape=(jax.ShapeDtypeStruct((n_t, features, 2 *...]
    unnamed x98 -> x58, local copies, waits for them, and re-layouts: 24.8 us -> 6.5 us
    pallas_call x4, Pallas kernels: 12.1 us -> 23.5 us  [rank_products(): pl.pallas_call(body, out_shape=jax.ShapeDtypeStruct((count * prefill, ran...]
    ppermute x12, starting transfers between devices: 34.1 us -> 43.8 us  [the longest x6 35.5 us: rightward(): return lax.ppermute(a, 'adapter', [(z - hops, z) for z in range(hops, n_z)])]
    pallas_call x4 -> x5, Pallas kernels: 37.4 us -> 45.6 us  [base_products(): pl.pallas_call(body, out_shape=(out, out), grid_spec=pltpu.PrefetchScalar...]
    convert_element_type x8 -> x4, other arithmetic: 7.48 us -> 1.83 us  [rank(): pair = (part.astype(F32) + core_swap(part).astype(F32)).astype(BF)]
  transfers between devices with their start and end apart: 28 -> 32, of which waited for: 9 -> 5; matrix products, arithmetic and copies ran while one was open for 3% -> 1% of each run, Pallas kernels for 31% -> 56%
where the time goes in v2:
time: 208 us; the launch traced here: 205 us
  Pallas kernels  121 us (58%)
  starting transfers between devices  55.1 us (26%)
  waiting for transfers between devices  18.4 us (9%)
  local copies, waits for them, and re-layouts  6.5 us (3%)
  other arithmetic  2.43 us (1%)
    pallas_call x5, Pallas kernels, base_products(): pl.pallas_call(body, out_shape=(out, out), grid_spec=pltpu.PrefetchScalar...  45.6 us
    ppermute x6, starting transfers between devices, rightward(): return lax.ppermute(a, 'adapter', [(z - hops, z) for z in range(hops, n_z)])  35.5 us
    pallas_call x4, Pallas kernels, rank_products(): pl.pallas_call(body, out_shape=jax.ShapeDtypeStruct((count * prefill, ran...  23.5 us
    pallas_call x2, Pallas kernels, finish(): pl.pallas_call(body, out_shape=jax.ShapeDtypeStruct(shape, BF), grid_spec...  21.6 us
    pallas_call x1, Pallas kernels, split_weight(): pl.pallas_call(body, out_shape=(jax.ShapeDtypeStruct((n_t, features, 2 *...  15.6 us
    pallas_call x6, Pallas kernels, pair_sum(): pl.pallas_call(body, out_shape=jax.ShapeDtypeStruct((rows, width), BF), g...  11.7 us
    ppermute x10, waiting for transfers between devices, chip_shift(): lax.ppermute(a, 'tensor', [(2 * x + c, 2 * ((x + k) % n_x) + c) for x in...  11.4 us
    ppermute x10, starting transfers between devices, chip_shift(): lax.ppermute(a, 'tensor', [(2 * x + c, 2 * ((x + k) % n_x) + c) for x in...  9.84 us
  transfers between devices with their start and end apart: 32, of which 5 were waited for; matrix products, arithmetic and copies ran while one was open for 1% of the time, Pallas kernels for 56%

profile of v2, /device:TPU:0, one launch (start us, length us, event | category | flops | bytes accessed | tf_op | source)
XLA Modules:
  0.0 204.5 jit_solution(10211939354709304417)
XLA Ops:
  1.3 5.7 %collective-permute-start.4 = (bf16[3,2048,128]{2,1,0:T(8,128)(2,1)}, bf16[3,2048,128]{2,1,0:T(8,128)(2,1)S(1)}, u32[]{:S(2)}, u32[]{:S(2)}) collective-permute-start(bf16[3,2048,128]{2,1,0:T(8,128)(2,1)} %rest_0_.9), channel_id=1, source_target_pairs={{0,4},{4,8},{8,12},{1,5},{5,9},{9,13},{2,6},{6,10},{10,14},{3,7},{... | collective-permute-start | bytes 4718600 | tf_op jit(solution)/shard_map/ppermute | solution.py:437
  7.6 1.6 plan_requests.1.plan_ref
  9.1 15.6 %split_weight.1 = (bf16[4,2048,512]{2,1,0:T(8,128)(2,1)}, bf16[2,512,512]{2,1,0:T(8,128)(2,1)}, bf16[2,512,512]{2,1,0:T(8,128)(2,1)}) custom-call(s32[8,128]{1,0:T(8,128)} %plan_requests.1.plan_ref, s32[4]{0:T(128)} %compare_select_fusion.2.slot_ref, bf16[3072,2048]{1,0:T(8,128)(2,1)} %x_ref.17, bf16[3072,2048]{1,0:T(8,128)(2,1)} %x_ref.17, ...), custom_call_target="tpu_custom_call" | custom-call | flops 4294967296 | bytes 16777216 | tf_op jit(solution)/shard_map/split_weight/pallas_call | solution.py:122
  24.7 9.1 %base_products.5 = (bf16[2,512,512]{2,1,0:T(8,128)(2,1)}, bf16[2,512,512]{2,1,0:T(8,128)(2,1)}) custom-call(s32[8,128]{1,0:T(8,128)} %plan_requests.1.plan_ref, bf16[3072,2048]{1,0:T(8,128)(2,1)} %x_ref.17, bf16[4,2048,512]{2,1,0:T(8,128)(2,1)} %get-tuple-element.18.w_ref), custom_call_target="tpu_custom_call" | custom-call | flops 4294967296 | bytes 8388608 | tf_op jit(solution)/shard_map/base_products/pallas_call | solution.py:175
  34.4 2.0 pair_sum.6.rest_0_
  36.3 1.9 collective-permute-start.5
  38.3 10.2 %base_products.6 = (bf16[2,512,512]{2,1,0:T(8,128)(2,1)}, bf16[2,512,512]{2,1,0:T(8,128)(2,1)}) custom-call(s32[8,128]{1,0:T(8,128)} %plan_requests.1.plan_ref, bf16[3072,2048]{1,0:T(8,128)(2,1)} %x_ref.17, bf16[4,2048,512]{2,1,0:T(8,128)(2,1)} %get-tuple-element.18.w_ref, bf16[512,512]{1,0:T(8,128)(2,1)} %pair_sum.6.rest_0_), custom_call_target="tpu_custom_call" | custom-call | flops 4294967296 | bytes 8388608 | tf_op jit(solution)/shard_map/base_products/pallas_call | solution.py:175
  49.8 5.8 %collective-permute-start.15 = (bf16[3,2048,128]{2,1,0:T(8,128)(2,1)S(1)}, bf16[3,2048,128]{2,1,0:T(8,128)(2,1)}, u32[]{:S(2)}, u32[]{:S(2)}) collective-permute-start(bf16[3,2048,128]{2,1,0:T(8,128)(2,1)S(1)} %collective-permute-done.4.rest_2_.rest_4_.rest_3_), channel_id=1, source_target_pairs={{0,4},{4,8},{8,12},{1,5},{5,9},{9,13},{2,6},{6,10},{10,14},{3,7},{... | collective-permute-start | bytes 4718600 | tf_op jit(solution)/shard_map/ppermute | solution.py:437
  55.6 2.0 pair_sum.7.rest_0_
  58.4 8.1 %base_products.7 = (bf16[2,512,512]{2,1,0:T(8,128)(2,1)}, bf16[2,512,512]{2,1,0:T(8,128)(2,1)}) custom-call(s32[8,128]{1,0:T(8,128)} %plan_requests.1.plan_ref, bf16[3072,2048]{1,0:T(8,128)(2,1)} %x_ref.17, bf16[4,2048,512]{2,1,0:T(8,128)(2,1)} %get-tuple-element.18.w_ref, bf16[512,512]{1,0:T(8,128)(2,1)} %pair_sum.7.rest_0_, bf16[3,2048,128]{2,1,0:T(8,128)(2,1)} %copy-done, ...), custom_call_target="tpu_custom_call" | custom-call | flops 4294967296 | bytes 8388608 | tf_op jit(solution)/shard_map/base_products/pallas_call | solution.py:175
  66.6 1.9 pair_sum.8.rest_0_
  68.5 1.9 collective-permute-start.9
  70.4 11.1 %collective-permute-done.6.rest_1_.rest_5_ = bf16[512,512]{1,0:T(8,128)(2,1)} collective-permute-done((bf16[512,512]{1,0:T(8,128)(2,1)}, bf16[512,512]{1,0:T(8,128)(2,1)}, u32[]{:S(2)}, u32[]{:S(2)}) %collective-permute-start.6) | collective-permute-done | bytes 524320 | tf_op jit(solution)/shard_map/ppermute | solution.py:427
  81.5 9.2 %base_products.8 = (bf16[2,512,512]{2,1,0:T(8,128)(2,1)}, bf16[2,512,512]{2,1,0:T(8,128)(2,1)}) custom-call(s32[8,128]{1,0:T(8,128)} %plan_requests.1.plan_ref, bf16[3072,2048]{1,0:T(8,128)(2,1)} %x_ref.17, bf16[4,2048,512]{2,1,0:T(8,128)(2,1)} %get-tuple-element.18.w_ref, bf16[512,512]{1,0:T(8,128)(2,1)} %pair_sum.8.rest_0_, ...), custom_call_target="tpu_custom_call" | custom-call | flops 4294967296 | bytes 8388608 | tf_op jit(solution)/shard_map/base_products/pallas_call | solution.py:175
  90.7 2.0 pair_sum.9.rest_0_
  94.1 6.2 %collective-permute-start.16 = (bf16[3,2048,128]{2,1,0:T(8,128)(2,1)}, bf16[3,2048,128]{2,1,0:T(8,128)(2,1)}, u32[]{:S(2)}, u32[]{:S(2)}) collective-permute-start(bf16[3,2048,128]{2,1,0:T(8,128)(2,1)} %collective-permute-done.15.rest_5_.rest_1_.rest_4_), channel_id=1, source_target_pairs={{0,4},{4,8},{8,12},{1,5},{5,9},{9,13},{2,6},{6,10},{10,14},{3,7},{... | collective-permute-start | bytes 4718600 | tf_op jit(solution)/shard_map/ppermute | solution.py:437
  101.0 9.1 %base_products.9 = (bf16[2,512,512]{2,1,0:T(8,128)(2,1)}, bf16[2,512,512]{2,1,0:T(8,128)(2,1)}) custom-call(s32[8,128]{1,0:T(8,128)} %plan_requests.1.plan_ref, bf16[3072,2048]{1,0:T(8,128)(2,1)} %x_ref.17, bf16[4,2048,512]{2,1,0:T(8,128)(2,1)} %get-tuple-element.18.w_ref, bf16[512,512]{1,0:T(8,128)(2,1)} %pair_sum.9.rest_0_, bf16[512,512]{1,0:T(8,128)(2,1)} %copy-done.4), custom_call_target="tpu_custom_call" | custom-call | flops 4294967296 | bytes 8388608 | tf_op jit(solution)/shard_map/base_products/pallas_call | solution.py:175
  111.2 1.8 collective-permute-done.11.b_ref.rest_16_.rest_4_
  114.0 1.9 pair_sum.11.rest_3_
  116.0 5.9 %rank_products.6 = bf16[768,128]{1,0:T(8,128)(2,1)} custom-call(s32[8,128]{1,0:T(8,128)} %plan_requests.1.plan_ref, bf16[3072,2048]{1,0:T(8,128)(2,1)} %x_ref.17, bf16[3,2048,128]{2,1,0:T(8,128)(2,1)} %rest_0_.9, bf16[3,2048,128]{2,1,0:T(8,128)(2,1)} %copy-done, bf16[3,2048,128]{2,1,0:T(8,128)(2,1)} %copy-done.1, bf16[512,512]{1,0:T(8,128)(2,1)} %pair_sum.11.rest_3_), custom_call_target="tpu_custom_call" | custom-call | flops 402653184 | bytes 4718592 | tf_op jit(solution)/shard_map/rank_products/pallas_call | solution.py:268
  123.0 2.0 pair_sum.10.rest_1_
  125.6 5.8 %rank_products.5 = bf16[768,128]{1,0:T(8,128)(2,1)} custom-call(s32[8,128]{1,0:T(8,128)} %plan_requests.1.plan_ref, bf16[3072,2048]{1,0:T(8,128)(2,1)} %x_ref.17, bf16[3,2048,128]{2,1,0:T(8,128)(2,1)} %rest_0_.9, bf16[512,512]{1,0:T(8,128)(2,1)} %pair_sum.10.rest_1_), custom_call_target="tpu_custom_call" | custom-call | flops 402653184 | bytes 4718592 | tf_op jit(solution)/shard_map/rank_products/pallas_call | solution.py:268
  131.4 1.7 copy_after.1
  135.4 5.8 %rank_products.7 = bf16[768,128]{1,0:T(8,128)(2,1)} custom-call(s32[8,128]{1,0:T(8,128)} %plan_requests.1.plan_ref, bf16[3072,2048]{1,0:T(8,128)(2,1)} %x_ref.17, bf16[3,2048,128]{2,1,0:T(8,128)(2,1)} %rest_0_.9, bf16[3,2048,128]{2,1,0:T(8,128)(2,1)} %copy-done, bf16[3,2048,128]{2,1,0:T(8,128)(2,1)} %collective-permute-done.13.rest_2_.rest_0_, ...), custom_call_target="tpu_custom_call" | custom-call | flops 402653184 | bytes 4718592 | tf_op jit(solution)/shard_map/rank_products/pallas_call | solution.py:268
  142.6 1.5 collective-permute-start.12
  144.4 6.0 %rank_products.4 = bf16[768,128]{1,0:T(8,128)(2,1)} custom-call(s32[8,128]{1,0:T(8,128)} %plan_requests.1.plan_ref, bf16[3072,2048]{1,0:T(8,128)(2,1)} %x_ref.17, bf16[3,2048,128]{2,1,0:T(8,128)(2,1)} %rest_0_.9, bf16[3,2048,128]{2,1,0:T(8,128)(2,1)} %copy-done, bf16[3,2048,128]{2,1,0:T(8,128)(2,1)} %collective-permute-done.13.rest_2_.rest_0_, ...), custom_call_target="tpu_custom_call" | custom-call | flops 402653184 | bytes 4718592 | tf_op jit(solution)/shard_map/rank_products/pallas_call | solution.py:268
  150.4 4.4 %collective-permute-start.22 = (bf16[3,2,64,256]{3,2,1,0:T(8,128)(2,1)S(1)}, bf16[3,2,64,256]{3,2,1,0:T(8,128)(2,1)S(1)}, u32[]{:S(2)}, u32[]{:S(2)}) collective-permute-start(bf16[3,2,64,256]{3,2,1,0:T(8,128)(2,1)S(1)} %copy-done.25), channel_id=1, source_target_pairs={{0,4},{4,8},{8,12},{1,5},{5,9},{9,13},{2,6},{6,10},{10,14},{3,7},{... | collective-permute-start | bytes 589832 | tf_op jit(solution)/shard_map/ppermute | solution.py:437
  156.1 4.1 %collective-permute-start.23 = (bf16[3,2,64,256]{3,2,1,0:T(8,128)(2,1)S(1)}, bf16[3,2,64,256]{3,2,1,0:T(8,128)(2,1)S(1)}, u32[]{:S(2)}, u32[]{:S(2)}) collective-permute-start(bf16[3,2,64,256]{3,2,1,0:T(8,128)(2,1)S(1)} %copy-done.25), channel_id=1, source_target_pairs={{0,8},{4,12},{1,9},{5,13},{2,10},{6,14},{3,11},{7,15},{16,24},{20,... | collective-permute-start | bytes 589832 | tf_op jit(solution)/shard_map/ppermute | solution.py:437
  161.1 3.8 %collective-permute-done.23.rest_28_.rest_13_ = bf16[3,2,64,256]{3,2,1,0:T(8,128)(2,1)S(1)} collective-permute-done((bf16[3,2,64,256]{3,2,1,0:T(8,128)(2,1)S(1)}, bf16[3,2,64,256]{3,2,1,0:T(8,128)(2,1)S(1)}, u32[]{:S(2)}, u32[]{:S(2)}) %collective-permute-start.23) | collective-permute-done | bytes 196640 | tf_op jit(solution)/shard_map/ppermute | solution.py:437
  169.8 9.4 %collective-permute-start.24 = (bf16[3,2,64,256]{3,2,1,0:T(8,128)(2,1)S(1)}, bf16[3,2,64,256]{3,2,1,0:T(8,128)(2,1)S(1)}, u32[]{:S(2)}, u32[]{:S(2)}) collective-permute-start(bf16[3,2,64,256]{3,2,1,0:T(8,128)(2,1)S(1)} %copy-done.25), channel_id=1, source_target_pairs={{0,12},{1,13},{2,14},{3,15},{16,28},{17,29},{18,30},{19,31}} | collective-permute-start | bytes 589832 | tf_op jit(solution)/shard_map/ppermute | solution.py:437
  181.3 15.5 %finish.2.rest_15_ = bf16[3072,2,256]{2,1,0:T(2,128)(2,1)} custom-call(s32[8,128]{1,0:T(8,128)} %plan_requests.1.plan_ref, bf16[2,512,512]{2,1,0:T(8,128)(2,1)} %get-tuple-element.19.a_ref.rest_0_, bf16[2,512,512]{2,1,0:T(8,128)(2,1)} %collective-permute-done.b_ref.rest_1_, bf16[512,512]{1,0:T(8,128)(2,1)} %copy-done.10, ...), custom_call_target="tpu_custom_call" | custom-call | flops 3623878656 | bytes 11796480 | tf_op jit(solution)/shard_map/finish/pallas_call | solution.py:397
  198.3 6.1 %finish.3 = bf16[3072,2,256]{2,1,0:T(2,128)(2,1)} custom-call(s32[8,128]{1,0:T(8,128)} %plan_requests.1.plan_ref, bf16[2,512,512]{2,1,0:T(8,128)(2,1)} %get-tuple-element.26.rest_0_.a_ref.rest_12_, bf16[2,512,512]{2,1,0:T(8,128)(2,1)} %copy-done.2, bf16[512,512]{1,0:T(8,128)(2,1)} %copy-done.5, ...), custom_call_target="tpu_custom_call", output_to_operand_aliasing={{}: (16, {})} | custom-call | flops 1207959552 | bytes 3932160 | tf_op jit(solution)/shard_map/finish/pallas_call | solution.py:397
  (115 shorter events, 24.9 us)
Async XLA Ops:
  0.0 48.5 %collective-permute-start.3 = (bf16[3,2048,128]{2,1,0:T(8,128)(2,1)}, bf16[3,2048,128]{2,1,0:T(8,128)(2,1)S(1)}, u32[]{:S(2)}, u32[]{:S(2)}) collective-permute-start(bf16[3,2048,128]{2,1,0:T(8,128)(2,1)} %rest_0_.9), channel_id=1, source_target_pairs={{4,0},{8,4},{12,8},{5,1},{9,5},{13,9},{6,2},{10,6},{14,10},{7,3},{... | collective-permute-start | bytes 4718600 | tf_op jit(solution)/shard_map/ppermute | solution.py:434
  1.3 48.5 %collective-permute-start.4 = (bf16[3,2048,128]{2,1,0:T(8,128)(2,1)}, bf16[3,2048,128]{2,1,0:T(8,128)(2,1)S(1)}, u32[]{:S(2)}, u32[]{:S(2)}) collective-permute-start(bf16[3,2048,128]{2,1,0:T(8,128)(2,1)} %rest_0_.9), channel_id=1, source_target_pairs={{0,4},{4,8},{8,12},{1,5},{5,9},{9,13},{2,6},{6,10},{10,14},{3,7},{... | collective-permute-start | bytes 4718600 | tf_op jit(solution)/shard_map/ppermute | solution.py:437
  24.7 9.6 %collective-permute-start = (bf16[2,512,512]{2,1,0:T(8,128)(2,1)}, bf16[2,512,512]{2,1,0:T(8,128)(2,1)}, u32[]{:S(2)}, u32[]{:S(2)}) collective-permute-start(bf16[2,512,512]{2,1,0:T(8,128)(2,1)} %get-tuple-element.20), channel_id=1, source_target_pairs={{0,1},{1,0},{2,3},{3,2},{4,5},{5,4},{6,7},{7,6},{8,9},{9,8},{10,11... | collective-permute-start | bytes 3145736 | tf_op jit(solution)/shard_map/ppermute | solution.py:424
  33.9 21.7 %collective-permute-start.2 = (bf16[2,512,512]{2,1,0:T(8,128)(2,1)}, bf16[2,512,512]{2,1,0:T(8,128)(2,1)}, u32[]{:S(2)}, u32[]{:S(2)}) collective-permute-start(bf16[2,512,512]{2,1,0:T(8,128)(2,1)} %get-tuple-element.24), channel_id=1, source_target_pairs={{0,1},{1,0},{2,3},{3,2},{4,5},{5,4},{6,7},{7,6},{8,9},{9,8},{10,11... | collective-permute-start | bytes 3145736 | tf_op jit(solution)/shard_map/ppermute | solution.py:424
  36.3 21.2 %collective-permute-start.5 = (bf16[512,512]{1,0:T(8,128)(2,1)}, bf16[512,512]{1,0:T(8,128)(2,1)S(1)}, u32[]{:S(2)}, u32[]{:S(2)}) collective-permute-start(bf16[512,512]{1,0:T(8,128)(2,1)} %pair_sum.6.rest_0_), channel_id=1, source_target_pairs={{0,2},{1,3},{2,0},{3,1},{4,6},{5,7},{6,4},{7,5},{8,10},{9,11},{10,... | collective-permute-start | bytes 1572872 | tf_op jit(solution)/shard_map/ppermute | solution.py:427
  48.5 18.1 %collective-permute-start.1 = (bf16[2,512,512]{2,1,0:T(8,128)(2,1)}, bf16[2,512,512]{2,1,0:T(8,128)(2,1)}, u32[]{:S(2)}, u32[]{:S(2)}) collective-permute-start(bf16[2,512,512]{2,1,0:T(8,128)(2,1)} %get-tuple-element.23), channel_id=1, source_target_pairs={{0,1},{1,0},{2,3},{3,2},{4,5},{5,4},{6,7},{7,6},{8,9},{9,8},{10,11... | collective-permute-start | bytes 3145736 | tf_op jit(solution)/shard_map/ppermute | solution.py:424
  48.5 44.1 %collective-permute-start.13 = (bf16[3,2048,128]{2,1,0:T(8,128)(2,1)S(1)}, bf16[3,2048,128]{2,1,0:T(8,128)(2,1)}, u32[]{:S(2)}, u32[]{:S(2)}) collective-permute-start(bf16[3,2048,128]{2,1,0:T(8,128)(2,1)S(1)} %collective-permute-done.3.rest_1_), channel_id=1, source_target_pairs={{4,0},{8,4},{12,8},{5,1},{9,5},{13,9},{6,2},{10,6},{14,10},{7,3},{... | collective-permute-start | bytes 4718600 | tf_op jit(solution)/shard_map/ppermute | solution.py:434
  49.8 44.3 %collective-permute-start.15 = (bf16[3,2048,128]{2,1,0:T(8,128)(2,1)S(1)}, bf16[3,2048,128]{2,1,0:T(8,128)(2,1)}, u32[]{:S(2)}, u32[]{:S(2)}) collective-permute-start(bf16[3,2048,128]{2,1,0:T(8,128)(2,1)S(1)} %collective-permute-done.4.rest_2_.rest_4_.rest_3_), channel_id=1, source_target_pairs={{0,4},{4,8},{8,12},{1,5},{5,9},{9,13},{2,6},{6,10},{10,14},{3,7},{... | collective-permute-start | bytes 4718600 | tf_op jit(solution)/shard_map/ppermute | solution.py:437
  66.5 24.2 %collective-permute-start.8 = (bf16[2,512,512]{2,1,0:T(8,128)(2,1)}, bf16[2,512,512]{2,1,0:T(8,128)(2,1)}, u32[]{:S(2)}, u32[]{:S(2)}) collective-permute-start(bf16[2,512,512]{2,1,0:T(8,128)(2,1)} %get-tuple-element.28), channel_id=1, source_target_pairs={{0,1},{1,0},{2,3},{3,2},{4,5},{5,4},{6,7},{7,6},{8,9},{9,8},{10,11... | collective-permute-start | bytes 3145736 | tf_op jit(solution)/shard_map/ppermute | solution.py:424
  66.5 15.0 %collective-permute-start.6 = (bf16[512,512]{1,0:T(8,128)(2,1)}, bf16[512,512]{1,0:T(8,128)(2,1)}, u32[]{:S(2)}, u32[]{:S(2)}) collective-permute-start(bf16[512,512]{1,0:T(8,128)(2,1)} %pair_sum.7.rest_0_), channel_id=1, source_target_pairs={{0,2},{1,3},{2,0},{3,1},{4,6},{5,7},{6,4},{7,5},{8,10},{9,11},{10,... | collective-permute-start | bytes 1572872 | tf_op jit(solution)/shard_map/ppermute | solution.py:427
  68.5 31.7 %collective-permute-start.9 = (bf16[512,512]{1,0:T(8,128)(2,1)}, bf16[512,512]{1,0:T(8,128)(2,1)S(1)}, u32[]{:S(2)}, u32[]{:S(2)}) collective-permute-start(bf16[512,512]{1,0:T(8,128)(2,1)} %pair_sum.8.rest_0_), channel_id=1, source_target_pairs={{0,2},{1,3},{2,0},{3,1},{4,6},{5,7},{6,4},{7,5},{8,10},{9,11},{10,... | collective-permute-start | bytes 1572872 | tf_op jit(solution)/shard_map/ppermute | solution.py:427
  92.6 49.9 %collective-permute-start.14 = (bf16[3,2048,128]{2,1,0:T(8,128)(2,1)}, bf16[3,2048,128]{2,1,0:T(8,128)(2,1)}, u32[]{:S(2)}, u32[]{:S(2)}) collective-permute-start(bf16[3,2048,128]{2,1,0:T(8,128)(2,1)} %collective-permute-done.13.rest_2_.rest_0_), channel_id=1, source_target_pairs={{4,0},{8,4},{12,8},{5,1},{9,5},{13,9},{6,2},{10,6},{14,10},{7,3},{... | collective-permute-start | bytes 4718600 | tf_op jit(solution)/shard_map/ppermute | solution.py:434
  94.1 50.1 %collective-permute-start.16 = (bf16[3,2048,128]{2,1,0:T(8,128)(2,1)}, bf16[3,2048,128]{2,1,0:T(8,128)(2,1)}, u32[]{:S(2)}, u32[]{:S(2)}) collective-permute-start(bf16[3,2048,128]{2,1,0:T(8,128)(2,1)} %collective-permute-done.15.rest_5_.rest_1_.rest_4_), channel_id=1, source_target_pairs={{0,4},{4,8},{8,12},{1,5},{5,9},{9,13},{2,6},{6,10},{10,14},{3,7},{... | collective-permute-start | bytes 4718600 | tf_op jit(solution)/shard_map/ppermute | solution.py:437
  110.1 2.9 %collective-permute-start.11 = (bf16[2,512,512]{2,1,0:T(8,128)(2,1)}, bf16[2,512,512]{2,1,0:T(8,128)(2,1)S(1)}, u32[]{:S(2)}, u32[]{:S(2)}) collective-permute-start(bf16[2,512,512]{2,1,0:T(8,128)(2,1)} %get-tuple-element.30), channel_id=1, source_target_pairs={{0,1},{1,0},{2,3},{3,2},{4,5},{5,4},{6,7},{7,6},{8,9},{9,8},{10,11... | collective-permute-start | bytes 3145736 | tf_op jit(solution)/shard_map/ppermute | solution.py:424
  110.1 11.9 %collective-permute-start.7 = (bf16[2,512,512]{2,1,0:T(8,128)(2,1)}, bf16[2,512,512]{2,1,0:T(8,128)(2,1)S(1)}, u32[]{:S(2)}, u32[]{:S(2)}) collective-permute-start(bf16[2,512,512]{2,1,0:T(8,128)(2,1)} %get-tuple-element.27), channel_id=1, source_target_pairs={{0,1},{1,0},{2,3},{3,2},{4,5},{5,4},{6,7},{7,6},{8,9},{9,8},{10,11... | collective-permute-start | bytes 3145736 | tf_op jit(solution)/shard_map/ppermute | solution.py:424
  110.6 23.3 %collective-permute-start.25 = (bf16[512,512]{1,0:T(8,128)(2,1)S(1)}, bf16[512,512]{1,0:T(8,128)(2,1)S(1)}, u32[]{:S(2)}, u32[]{:S(2)}) collective-permute-start(bf16[512,512]{1,0:T(8,128)(2,1)S(1)} %copy-done.9), channel_id=1, source_target_pairs={{0,2},{1,3},{2,0},{3,1},{4,6},{5,7},{6,4},{7,5},{8,10},{9,11},{10,... | collective-permute-start | bytes 1572872 | tf_op jit(solution)/shard_map/ppermute | solution.py:427
  121.8 11.3 %collective-permute-start.28 = (bf16[768,128]{1,0:T(8,128)(2,1)}, bf16[768,128]{1,0:T(8,128)(2,1)S(1)}, u32[]{:S(2)}, u32[]{:S(2)}) collective-permute-start(bf16[768,128]{1,0:T(8,128)(2,1)} %rank_products.6), channel_id=1, source_target_pairs={{0,1},{1,0},{2,3},{3,2},{4,5},{5,4},{6,7},{7,6},{8,9},{9,8},{10,11... | collective-permute-start | bytes 589832 | tf_op jit(solution)/shard_map/ppermute | solution.py:424
  125.0 44.8 %collective-permute-start.10 = (bf16[512,512]{1,0:T(8,128)(2,1)}, bf16[512,512]{1,0:T(8,128)(2,1)S(1)}, u32[]{:S(2)}, u32[]{:S(2)}) collective-permute-start(bf16[512,512]{1,0:T(8,128)(2,1)} %pair_sum.10.rest_1_), channel_id=1, source_target_pairs={{0,2},{1,3},{2,0},{3,1},{4,6},{5,7},{6,4},{7,5},{8,10},{9,11},{10,... | collective-permute-start | bytes 1572872 | tf_op jit(solution)/shard_map/ppermute | solution.py:427
  133.1 8.1 %collective-permute-start.26 = (bf16[768,128]{1,0:T(8,128)(2,1)S(1)}, bf16[768,128]{1,0:T(8,128)(2,1)S(1)}, u32[]{:S(2)}, u32[]{:S(2)}) collective-permute-start(bf16[768,128]{1,0:T(8,128)(2,1)S(1)} %copy-done.15), channel_id=1, source_target_pairs={{0,1},{1,0},{2,3},{3,2},{4,5},{5,4},{6,7},{7,6},{8,9},{9,8},{10,11... | collective-permute-start | bytes 589832 | tf_op jit(solution)/shard_map/ppermute | solution.py:424
  133.9 16.4 %collective-permute-start.19 = (bf16[3,2,64,256]{3,2,1,0:T(8,128)(2,1)}, bf16[3,2,64,256]{3,2,1,0:T(8,128)(2,1)S(1)}, u32[]{:S(2)}, u32[]{:S(2)}) collective-permute-start(bf16[3,2,64,256]{3,2,1,0:T(8,128)(2,1)} %copy_after.1), channel_id=1, source_target_pairs={{4,0},{8,4},{12,8},{5,1},{9,5},{13,9},{6,2},{10,6},{14,10},{7,3},{... | collective-permute-start | bytes 589832 | tf_op jit(solution)/shard_map/ppermute | solution.py:434
  141.3 14.9 %collective-permute-start.20 = (bf16[3,2,64,256]{3,2,1,0:T(8,128)(2,1)S(1)}, bf16[3,2,64,256]{3,2,1,0:T(8,128)(2,1)S(1)}, u32[]{:S(2)}, u32[]{:S(2)}) collective-permute-start(bf16[3,2,64,256]{3,2,1,0:T(8,128)(2,1)S(1)} %copy-done.25), channel_id=1, source_target_pairs={{8,0},{12,4},{9,1},{13,5},{10,2},{14,6},{11,3},{15,7},{24,16},{28,... | collective-permute-start | bytes 589832 | tf_op jit(solution)/shard_map/ppermute | solution.py:434
  142.6 37.3 %collective-permute-start.12 = (bf16[512,512]{1,0:T(8,128)(2,1)S(1)}, bf16[512,512]{1,0:T(8,128)(2,1)S(1)}, u32[]{:S(2)}, u32[]{:S(2)}) collective-permute-start(bf16[512,512]{1,0:T(8,128)(2,1)S(1)} %copy-done.7), channel_id=1, source_target_pairs={{0,2},{1,3},{2,0},{3,1},{4,6},{5,7},{6,4},{7,5},{8,10},{9,11},{10,... | collective-permute-start | bytes 1572872 | tf_op jit(solution)/shard_map/ppermute | solution.py:427
  144.1 16.2 %collective-permute-start.30 = (bf16[768,128]{1,0:T(8,128)(2,1)}, bf16[768,128]{1,0:T(8,128)(2,1)S(1)}, u32[]{:S(2)}, u32[]{:S(2)}) collective-permute-start(bf16[768,128]{1,0:T(8,128)(2,1)} %rank_products.7), channel_id=1, source_target_pairs={{0,1},{1,0},{2,3},{3,2},{4,5},{5,4},{6,7},{7,6},{8,9},{9,8},{10,11... | collective-permute-start | bytes 589832 | tf_op jit(solution)/shard_map/ppermute | solution.py:424
  150.4 10.1 %collective-permute-start.22 = (bf16[3,2,64,256]{3,2,1,0:T(8,128)(2,1)S(1)}, bf16[3,2,64,256]{3,2,1,0:T(8,128)(2,1)S(1)}, u32[]{:S(2)}, u32[]{:S(2)}) collective-permute-start(bf16[3,2,64,256]{3,2,1,0:T(8,128)(2,1)S(1)} %copy-done.25), channel_id=1, source_target_pairs={{0,4},{4,8},{8,12},{1,5},{5,9},{9,13},{2,6},{6,10},{10,14},{3,7},{... | collective-permute-start | bytes 589832 | tf_op jit(solution)/shard_map/ppermute | solution.py:437
  156.1 8.7 %collective-permute-start.23 = (bf16[3,2,64,256]{3,2,1,0:T(8,128)(2,1)S(1)}, bf16[3,2,64,256]{3,2,1,0:T(8,128)(2,1)S(1)}, u32[]{:S(2)}, u32[]{:S(2)}) collective-permute-start(bf16[3,2,64,256]{3,2,1,0:T(8,128)(2,1)S(1)} %copy-done.25), channel_id=1, source_target_pairs={{0,8},{4,12},{1,9},{5,13},{2,10},{6,14},{3,11},{7,15},{16,24},{20,... | collective-permute-start | bytes 589832 | tf_op jit(solution)/shard_map/ppermute | solution.py:437
  160.3 5.1 %collective-permute-start.17 = (bf16[768,128]{1,0:T(8,128)(2,1)}, bf16[768,128]{1,0:T(8,128)(2,1)S(1)}, u32[]{:S(2)}, u32[]{:S(2)}) collective-permute-start(bf16[768,128]{1,0:T(8,128)(2,1)} %rank_products.4), channel_id=1, source_target_pairs={{0,1},{1,0},{2,3},{3,2},{4,5},{5,4},{6,7},{7,6},{8,9},{9,8},{10,11... | collective-permute-start | bytes 589832 | tf_op jit(solution)/shard_map/ppermute | solution.py:424
  160.5 7.8 %collective-permute-start.27 = (bf16[768,128]{1,0:T(8,128)(2,1)S(1)}, bf16[768,128]{1,0:T(8,128)(2,1)S(1)}, u32[]{:S(2)}, u32[]{:S(2)}) collective-permute-start(bf16[768,128]{1,0:T(8,128)(2,1)S(1)} %add_convert_fusion.2.rest_18_), channel_id=1, source_target_pairs={{0,2},{1,3},{2,0},{3,1},{4,6},{5,7},{6,4},{7,5},{8,10},{9,11},{10,... | collective-permute-start | bytes 589832 | tf_op jit(solution)/shard_map/ppermute | solution.py:427
  164.9 14.4 %collective-permute-start.29 = (bf16[768,128]{1,0:T(8,128)(2,1)S(1)}, bf16[768,128]{1,0:T(8,128)(2,1)S(1)}, u32[]{:S(2)}, u32[]{:S(2)}) collective-permute-start(bf16[768,128]{1,0:T(8,128)(2,1)S(1)} %copy-done.11), channel_id=1, source_target_pairs={{0,2},{1,3},{2,0},{3,1},{4,6},{5,7},{6,4},{7,5},{8,10},{9,11},{10,... | collective-permute-start | bytes 589832 | tf_op jit(solution)/shard_map/ppermute | solution.py:427
  165.4 14.4 %collective-permute-start.31 = (bf16[768,128]{1,0:T(8,128)(2,1)S(1)}, bf16[768,128]{1,0:T(8,128)(2,1)S(1)}, u32[]{:S(2)}, u32[]{:S(2)}) collective-permute-start(bf16[768,128]{1,0:T(8,128)(2,1)S(1)} %add_convert_fusion.rest_22_), channel_id=1, source_target_pairs={{0,2},{1,3},{2,0},{3,1},{4,6},{5,7},{6,4},{7,5},{8,10},{9,11},{10,... | collective-permute-start | bytes 589832 | tf_op jit(solution)/shard_map/ppermute | solution.py:427
  168.3 28.6 %collective-permute-start.21 = (bf16[3,2,64,256]{3,2,1,0:T(8,128)(2,1)S(1)}, bf16[3,2,64,256]{3,2,1,0:T(8,128)(2,1)S(1)}, u32[]{:S(2)}, u32[]{:S(2)}) collective-permute-start(bf16[3,2,64,256]{3,2,1,0:T(8,128)(2,1)S(1)} %copy-done.25), channel_id=1, source_target_pairs={{12,0},{13,1},{14,2},{15,3},{28,16},{29,17},{30,18},{31,19}} | collective-permute-start | bytes 589832 | tf_op jit(solution)/shard_map/ppermute | solution.py:434
  169.8 27.1 %collective-permute-start.24 = (bf16[3,2,64,256]{3,2,1,0:T(8,128)(2,1)S(1)}, bf16[3,2,64,256]{3,2,1,0:T(8,128)(2,1)S(1)}, u32[]{:S(2)}, u32[]{:S(2)}) collective-permute-start(bf16[3,2,64,256]{3,2,1,0:T(8,128)(2,1)S(1)} %copy-done.25), channel_id=1, source_target_pairs={{0,12},{1,13},{2,14},{3,15},{16,28},{17,29},{18,30},{19,31}} | collective-permute-start | bytes 589832 | tf_op jit(solution)/shard_map/ppermute | solution.py:437
  179.2 17.6 %collective-permute-start.18 = (bf16[768,128]{1,0:T(8,128)(2,1)S(1)}, bf16[768,128]{1,0:T(8,128)(2,1)S(1)}, u32[]{:S(2)}, u32[]{:S(2)}) collective-permute-start(bf16[768,128]{1,0:T(8,128)(2,1)S(1)} %add_convert_fusion.3.rest_6_), channel_id=1, source_target_pairs={{0,2},{1,3},{2,0},{3,1},{4,6},{5,7},{6,4},{7,5},{8,10},{9,11},{10,... | collective-permute-start | bytes 589832 | tf_op jit(solution)/shard_map/ppermute | solution.py:427
  (29 other events, 274.0 us)

commit v3 on v2

v3 whole, which is shorter than its diff:
```python
import jax
import jax.numpy as jnp
from jax import lax
from jax.experimental import pallas as pl
from jax.experimental.pallas import tpu as pltpu
from jax.sharding import PartitionSpec as P

BF = jnp.bfloat16
F32 = jnp.float32
BASE_CHUNKS = (3, 4, 5)
RANK_CHUNKS = 4
SMEM = pltpu.SMEM
ANY = pl.BlockSpec(memory_space=pl.ANY)


def cost(flops, moved):
    return pl.CostEstimate(
        flops=int(flops * 0.01), bytes_accessed=int(moved * 0.01), transcendentals=0
    )


ORDER, SOURCE, ROW, LENGTH = range(4)


def params(mib=60):
    return pltpu.CompilerParams(vmem_limit_bytes=mib * 1024 * 1024)


def plan_requests(table, adapters, lengths, here, n_z, stored):
    requests, known = adapters.shape[0], table.shape[0]
    shape = (requests, 128)

    def body(table_ref, adapter_ref, length_ref, here_ref, plan_ref):
        me = here_ref[0]
        request = lax.broadcasted_iota(jnp.int32, shape, 0)
        lane = lax.broadcasted_iota(jnp.int32, shape, 1)
        diagonal = request == lane

        def wide(ref, n):
            return jnp.pad(ref[...], ((0, 0), (0, 128 - n)))

        def down(a):
            return jnp.sum(jnp.where(diagonal, a, 0), axis=1, keepdims=True)

        def across(a):
            return jnp.sum(jnp.where(diagonal, a, 0), axis=0, keepdims=True)

        hit = (down(wide(adapter_ref, requests)) == lane) & (lane < known)
        slot = jnp.sum(jnp.where(hit, wide(table_ref, known), 0), 1, keepdims=True)
        owner = jnp.zeros_like(slot)
        for z in range(1, n_z):
            owner += jnp.where(slot >= z * stored, 1, 0)
        source = jnp.where(owner >= me, owner - me, n_z - 1 + me - owner)
        key = jnp.abs(owner - me) * 128 + request[:, :1]
        before = (across(key) < key) & (lane < requests)
        place = jnp.sum(jnp.where(before, 1, 0), axis=1, keepdims=True)
        at = place == lane

        def placed(a):
            return jnp.sum(jnp.where(at, a, 0), axis=0, keepdims=True)

        plan_ref[ORDER : ORDER + 1] = placed(request)
        plan_ref[SOURCE : SOURCE + 1] = placed(source)
        plan_ref[ROW : ROW + 1] = placed(slot - owner * stored)
        plan_ref[LENGTH : LENGTH + 1] = placed(down(wide(length_ref, requests)))

    vmem = pl.BlockSpec(memory_space=pltpu.VMEM)
    return pl.pallas_call(
        body,
        out_shape=jax.ShapeDtypeStruct((8, 128), jnp.int32),
        in_specs=[vmem, vmem, vmem, pl.BlockSpec(memory_space=SMEM)],
        out_specs=vmem,
        cost_estimate=cost(0, 1 << 20),
        name="plan_requests",
    )(table[None, :], adapters[None, :], lengths[None, :], here)


def split_weight(plan, slots, hidden, weight, count, prefill):
    features, _, columns = weight.shape
    n_t = slots.shape[0]
    n_x = n_t // 2
    width = columns // n_t
    rows, half = 512, 128
    steps = features // rows

    def body(plan_ref, slot_ref, *rest):
        x_refs, (w_ref, o_ref, *send_refs, keep_ref, total) = rest[:count], rest[count:]
        step = pl.program_id(0)
        out_row = lax.broadcasted_iota(jnp.int32, (2 * half, 2 * half), 0)
        in_row = lax.broadcasted_iota(jnp.int32, (2 * half, 2 * half), 1)
        pick = in_row == 2 * (out_row % half) + out_row // half
        pick = pick.astype(F32).astype(BF)
        for b in range(rows // half):
            mixed = w_ref[b * half : (b + 1) * half].reshape(2 * half, columns)
            apart = jnp.dot(pick, mixed, preferred_element_type=F32).astype(BF)
            for t in range(n_t):
                for s in range(2):
                    o_ref[
                        slot_ref[t],
                        b * half : (b + 1) * half,
                        s * width : (s + 1) * width,
                    ] = apart[s * half : (s + 1) * half, t * width : (t + 1) * width]

        @pl.when(step == 0)
        def _():
            total[...] = jnp.zeros_like(total)

        for r in range(count):
            for j in range(n_t):
                total[j, r * prefill : (r + 1) * prefill] += jnp.dot(
                    x_refs[r][...], o_ref[j], preferred_element_type=F32
                )

        @pl.when(step == steps - 1)
        def _():
            for j in range(n_x):
                send_refs[j][...] = total[j].astype(BF)
                keep_ref[j] = total[n_x + j].astype(BF)

    part = (count * prefill, 2 * width)
    split, *sends, keep = pl.pallas_call(
        body,
        out_shape=(
            jax.ShapeDtypeStruct((n_t, features, 2 * width), BF),
            *[jax.ShapeDtypeStruct(part, BF)] * n_x,
            jax.ShapeDtypeStruct((n_x, *part), BF),
        ),
        grid_spec=pltpu.PrefetchScalarGridSpec(
            num_scalar_prefetch=2,
            grid=(steps,),
            in_specs=[
                pl.BlockSpec((prefill, rows), lambda i, p, s, r=r: (p[ORDER, r], i))
                for r in range(count)
            ]
            + [pl.BlockSpec((rows, 2, columns), lambda i, p, s: (i, 0, 0))],
            out_specs=(
                pl.BlockSpec((n_t, rows, 2 * width), lambda i, p, s: (0, i, 0)),
                *[pl.BlockSpec(part, lambda i, p, s: (0, 0))] * n_x,
                pl.BlockSpec((n_x, *part), lambda i, p, s: (0, 0, 0)),
            ),
            scratch_shapes=[pltpu.VMEM((n_t, count * prefill, 2 * width), F32)],
        ),
        compiler_params=params(),
        cost_estimate=cost(2 * count * prefill * features * 2 * columns, 8 * features * columns),
        name="split_weight",
    )(plan, slots, *[hidden] * count, weight)
    return split, sends, keep


def base_products(plan, hidden, weight, first, count, prefill, after):
    n_t, features, width = weight.shape
    n_x = n_t // 2
    short = prefill // 2
    n_after = len(after)

    def body(plan_ref, x_ref, *rest):
        w_refs = rest[:n_t]
        *send_refs, keep_ref = rest[n_t + n_after :]
        live = plan_ref[LENGTH, first + pl.program_id(0)]

        def products(rows):
            for j in range(n_t):
                out = send_refs[j] if j < n_x else keep_ref.at[j - n_x]
                out[:rows] = jnp.dot(
                    x_ref[:rows], w_refs[j][0], preferred_element_type=F32
                ).astype(BF)
                if rows < prefill:
                    out[rows:] = jnp.zeros((prefill - rows, width), BF)

        @pl.when(live > short)
        def _():
            products(prefill)

        @pl.when(live <= short)
        def _():
            products(short)

    part = (count * prefill, width)
    *sends, keep = pl.pallas_call(
        body,
        out_shape=(
            *[jax.ShapeDtypeStruct(part, BF)] * n_x,
            jax.ShapeDtypeStruct((n_x, *part), BF),
        ),
        grid_spec=pltpu.PrefetchScalarGridSpec(
            num_scalar_prefetch=1,
            grid=(count,),
            in_specs=[
                pl.BlockSpec(
                    (prefill, features), lambda i, p: (p[ORDER, first + i], 0)
                ),
            ]
            + [
                pl.BlockSpec((1, features, width), lambda i, p, j=j: (j, 0, 0))
                for j in range(n_t)
            ]
            + [ANY] * n_after,
            out_specs=(
                *[pl.BlockSpec((prefill, width), lambda i, p: (i, 0))] * n_x,
                pl.BlockSpec((n_x, prefill, width), lambda i, p: (0, i, 0)),
            ),
        ),
        compiler_params=params(),
        cost_estimate=cost(2 * count * prefill * features * width * n_t, 2 * n_t * features * width),
        name="base_products",
    )(plan, hidden, *[weight] * n_t, *after)
    return sends, keep


def pair_sum(one, other, index):
    _, rows, width = one.shape
    block = rows // 2

    def body(a_ref, b_ref, o_ref):
        o_ref[...] = (a_ref[0].astype(F32) + b_ref[...].astype(F32)).astype(BF)

    spec = pl.BlockSpec((block, width), lambda i: (i, 0))
    return pl.pallas_call(
        body,
        out_shape=jax.ShapeDtypeStruct((rows, width), BF),
        grid=(rows // block,),
        in_specs=[pl.BlockSpec((1, block, width), lambda i: (index, i, 0)), spec],
        out_specs=spec,
        compiler_params=params(),
        cost_estimate=cost(rows * width, 6 * rows * width),
        name="pair_sum",
    )(one, other)


def copy_after(a, after):
    def body(a_ref, *rest):
        rest[-1][...] = a_ref[...]

    vmem = pl.BlockSpec(memory_space=pltpu.VMEM)
    return pl.pallas_call(
        body,
        out_shape=jax.ShapeDtypeStruct(a.shape, a.dtype),
        in_specs=[vmem] + [ANY] * len(after),
        out_specs=vmem,
        compiler_params=params(),
        cost_estimate=cost(0, 4 * a.size),
        name="copy_after",
    )(a, *after)


def fetch(refs, source, row, target, sem):
    for codes, ref in refs:
        hit = source == codes[0]
        for code in codes[1:]:
            hit |= source == code

        @pl.when(hit)
        def _():
            pltpu.make_async_copy(ref.at[row], target, sem).start()


def rank_products(plan, hidden, maps, first, count, prefill, after):
    sources = list(maps)
    _, features, ranks = maps[sources[0]].shape
    n_map, n_after = len(maps), len(after)

    def body(plan_ref, x_ref, *rest):
        refs = list(zip(sources, rest[:n_map]))
        o_ref, rows, held, sems = rest[n_map + n_after :]
        copies = []
        for i in range(count):
            fetch(
                refs,
                plan_ref[SOURCE, first + i],
                plan_ref[ROW, first + i],
                held.at[i],
                sems.at[0, i],
            )
            at = pl.multiple_of(plan_ref[ORDER, first + i] * prefill, prefill)
            copies.append(
                pltpu.make_async_copy(
                    x_ref.at[pl.ds(at, prefill)], rows.at[i], sems.at[1, i]
                )
            )
            copies[-1].start()
        for i in range(count):
            pltpu.make_async_copy(rest[0].at[0], held.at[i], sems.at[0, i]).wait()
            copies[i].wait()
            o_ref[i * prefill : (i + 1) * prefill] = jnp.dot(
                rows[i], held[i], preferred_element_type=F32
            ).astype(BF)

    return pl.pallas_call(
        body,
        out_shape=jax.ShapeDtypeStruct((count * prefill, ranks), BF),
        grid_spec=pltpu.PrefetchScalarGridSpec(
            num_scalar_prefetch=1,
            grid=(),
            in_specs=[ANY] * (1 + n_map + n_after),
            out_specs=pl.BlockSpec(memory_space=pltpu.VMEM),
            scratch_shapes=[
                pltpu.VMEM((count, prefill, features), BF),
                pltpu.VMEM((count, features, ranks), BF),
                pltpu.SemaphoreType.DMA((2, count)),
            ],
        ),
        compiler_params=params(),
        cost_estimate=cost(2 * count * prefill * features * ranks, 2 * count * features * (prefill + ranks)),
        name="rank_products",
    )(plan, hidden, *maps.values(), *after)


def finish(plan, bases, ranks, maps, before, first, count, prefill, shape):
    sources = list(maps)
    _, _, depth, columns = maps[sources[0]].shape
    half = prefill // 2
    n_map = len(maps)
    n_base = max(len(pieces) for _, _, pieces in bases)
    n_rank = max(len(pieces) for _, _, pieces in ranks)

    def body(plan_ref, *rest):
        base_refs, rank_refs = [], []
        for refs, pieces in ((base_refs, bases), (rank_refs, ranks)):
            for start, n, arrays in pieces:
                refs.append((start, n, rest[: len(arrays)]))
                rest = rest[len(arrays) :]
        map_refs = list(zip(sources, rest[:n_map]))
        o_ref, ups, base_rows, rank_rows, out_rows, sems, out_sems = rest[-7:]

        def start_pieces(refs, at, rows, sem):
            copies = []
            for start, n, arrays in refs:
                if start <= at < start + n:
                    block = pl.ds((at - start) * prefill, prefill)
                    for k, ref in enumerate(arrays):
                        source = ref.at[0, block] if len(ref.shape) == 3 else ref.at[block]
                        copies.append(pltpu.make_async_copy(source, rows.at[k], sem.at[k]))
                        copies[-1].start()
            return copies

        copies = []
        for i in range(count):
            at = first + i
            copies.append(
                start_pieces(base_refs, at, base_rows.at[i], sems.at[i])
                + start_pieces(
                    rank_refs, at, rank_rows.at[i], sems.at[i, pl.ds(n_base, n_rank)]
                )
            )
            fetch(
                map_refs,
                plan_ref[SOURCE, at],
                plan_ref[ROW, at],
                ups.at[i],
                sems.at[i, n_base + n_rank],
            )

        mix_row = lax.broadcasted_iota(jnp.int32, (2 * half, 2 * half), 0)
        mix_column = lax.broadcasted_iota(jnp.int32, (2 * half, 2 * half), 1)
        mix = mix_column == mix_row // 2 + half * (mix_row % 2)
        mix = mix.astype(F32).astype(BF)
        twice_row = lax.broadcasted_iota(jnp.int32, (2 * half, half), 0)
        twice_column = lax.broadcasted_iota(jnp.int32, (2 * half, half), 1)
        twice = (twice_column == twice_row // 2).astype(F32).astype(BF)
        lane = lax.broadcasted_iota(jnp.int32, (2 * half, 2 * depth), 1)
        side = lax.broadcasted_iota(jnp.int32, (2 * half, 2 * depth), 0) % 2
        own_side = lane // depth == side
        token = lax.broadcasted_iota(jnp.int32, (2 * half, columns), 0) // 2

        def rows_for(i, pieces, live, b):
            rows = slice(b * half, (b + 1) * half)
            total = jnp.zeros((2 * half, columns), F32)
            for k in range(pieces):
                piece = base_rows[i, k, rows]
                piece = jnp.concatenate([piece[:, :columns], piece[:, columns:]], 0)
                total += jnp.dot(mix, piece, preferred_element_type=F32)
            rank = rank_rows[i, 0, rows].astype(F32)
            for k in range(1, n_rank):
                rank += rank_rows[i, k, rows].astype(F32)
            rank = jnp.dot(twice, rank.astype(BF), preferred_element_type=F32)
            rank = jnp.where(own_side, rank, 0.0).astype(BF)
            up = ups[i].reshape(2 * depth, columns)
            total += jnp.dot(rank, up, preferred_element_type=F32)
            total = jnp.where(token + b * half < live, total, 0.0)
            out_rows[i, rows] = total.astype(BF).reshape(half, 2, columns)

        outs = []
        for i in range(count):
            for copy in copies[i]:
                copy.wait()
            pltpu.make_async_copy(
                map_refs[0][1].at[0], ups.at[i], sems.at[i, n_base + n_rank]
            ).wait()
            live = plan_ref[LENGTH, first + i]
            rows_for(i, n_base, live, 0)

            @pl.when(live > half)
            def _():
                rows_for(i, n_base, live, 1)

            @pl.when(live <= half)
            def _():
                out_rows[i, half:] = jnp.zeros((half, 2, columns), BF)

            row = pl.multiple_of(plan_ref[ORDER, first + i] * prefill, prefill)
            outs.append(
                pltpu.make_async_copy(
                    out_rows.at[i], o_ref.at[pl.ds(row, prefill)], out_sems.at[i]
                )
            )
            outs[-1].start()
        for copy in outs:
            copy.wait()

    operands = [plan]
    for _, _, pieces in bases + ranks:
        operands += pieces
    operands += maps.values()
    aliases = {}
    if before is not None:
        aliases = {len(operands): 0}
        operands.append(before)
    return pl.pallas_call(
        body,
        out_shape=jax.ShapeDtypeStruct(shape, BF),
        grid_spec=pltpu.PrefetchScalarGridSpec(
            num_scalar_prefetch=1,
            grid=(),
            in_specs=[ANY] * (len(operands) - 1),
            out_specs=ANY,
            scratch_shapes=[
                pltpu.VMEM((count, 2, depth, columns), BF),
                pltpu.VMEM((count, n_base, prefill, 2 * columns), BF),
                pltpu.VMEM((count, n_rank, prefill, 2 * depth), BF),
                pltpu.VMEM((count, prefill, 2, columns), BF),
                pltpu.SemaphoreType.DMA((count, n_base + n_rank + 1)),
                pltpu.SemaphoreType.DMA((count,)),
            ],
        ),
        input_output_aliases=aliases,
        compiler_params=params(),
        cost_estimate=cost(12 * count * prefill * prefill * 2 * columns, 20 * count * prefill * columns),
        name="finish",
    )(*operands)


def solution(mesh):
    n_z, n_t = mesh.shape["adapter"], mesh.shape["tensor"]
    n_x = n_t // 2

    def core_swap(a):
        return lax.ppermute(a, "tensor", [(t, t ^ 1) for t in range(n_t)])

    def chip_shift(a, k):
        return lax.ppermute(
            a,
            "tensor",
            [(2 * x + c, 2 * ((x + k) % n_x) + c) for x in range(n_x) for c in (0, 1)],
        )

    def leftward(a, hops=1):
        return lax.ppermute(a, "adapter", [(z, z - hops) for z in range(hops, n_z)])

    def rightward(a, hops=1):
        return lax.ppermute(a, "adapter", [(z - hops, z) for z in range(hops, n_z)])

    def per_device(hidden, weight, down, up, table, adapters, lengths):
        requests = adapters.shape[0]
        prefill = hidden.shape[0] // requests
        stored = down.shape[0]
        columns = up.shape[3]
        by_distance = n_z == RANK_CHUNKS
        z, t = lax.axis_index("adapter"), lax.axis_index("tensor")
        plan = plan_requests(
            table, adapters, lengths, jnp.reshape(z, (1,)), n_z, stored
        )

        downs = {0: down}
        for hops in range(1, n_z):
            left, right = downs[hops - 1], downs[0 if hops == 1 else n_z + hops - 2]
            downs[hops] = leftward(left)
            downs[n_z - 1 + hops] = rightward(right)

        def within(maps, hops):
            keys = range(hops + 1), range(n_z, n_z + hops)
            return {(k,): maps[k] for part in keys for k in part}

        dest = jnp.arange(n_t, dtype=jnp.int32)
        away = (dest // 2 - t // 2 + n_x) % n_x
        slots = jnp.where(dest % 2 == t % 2, n_x + away, away)

        bases, pairs = [], []

        def exchange(first, count, send, keep):
            beyond = [core_swap(send[k]) for k in range(1, n_x)]
            pieces = [keep, core_swap(send[0])]
            for k in range(1, n_x):
                pairs.append(pair_sum(keep, beyond[k - 1], k))
                pieces.append(chip_shift(pairs[-1], k))
            bases.append((first, count, pieces))

        split, send, keep = split_weight(
            plan, slots, hidden, weight, BASE_CHUNKS[0], prefill
        )
        exchange(0, BASE_CHUNKS[0], send, keep)

        near = [downs[1], downs[n_z]]
        middle = [downs[2], downs[n_z + 1]]
        for chunk in range(1, len(BASE_CHUNKS)):
            first, count = sum(BASE_CHUNKS[:chunk]), BASE_CHUNKS[chunk]
            after = pairs[-1:]
            if chunk == 2:
                after = after + near + [bases[0][2][-1]]
            send, keep = base_products(
                plan, hidden, split, first, count, prefill, after
            )
            exchange(first, count, send, keep)

        ups = {(0,): up}
        late_up = copy_after(up, middle)
        for hops in range(1, n_z):
            ups[hops, 2 * n_z - 1 - hops] = lax.ppermute(
                late_up, "adapter", [(z, (z - hops) % n_z) for z in range(n_z)]
            )

        ranks = []
        count = requests // RANK_CHUNKS

        def rank(chunk, after):
            hops = chunk if by_distance else n_z - 1
            part = rank_products(
                plan, hidden, within(downs, hops), chunk * count, count, prefill, after
            )
            pair = (part.astype(F32) + core_swap(part).astype(F32)).astype(BF)
            pieces = [pair] + [chip_shift(pair, k) for k in range(1, n_x)]
            ranks.append((chunk * count, count, pieces))
            return part

        shape = (requests * prefill, 2, columns)

        def write(out, first, last):
            held = [
                b
                for b in bases
                if b[0] < last * count and b[0] + b[1] > first * count
            ]
            return finish(
                plan,
                held,
                ranks[first:last],
                ups,
                out,
                first * count,
                (last - first) * count,
                prefill,
                shape,
            )

        part = rank(0, pairs[-1:])
        part = rank(1, [part])
        part = rank(2, [part, bases[1][2][-1]])
        out = write(None, 0, 2)
        out = write(out, 2, 3)
        rank(3, [])
        return write(out, 3, 4)

    return jax.shard_map(
        per_device,
        mesh=mesh,
        in_specs=(
            P(("group", "adapter"), "tensor"),
            P("tensor", None, None),
            P(("group", "adapter"), "tensor", None),
            P(("group", "adapter"), None, None, "tensor"),
            P("group"),
            P(("group", "adapter")),
            P(("group", "adapter")),
        ),
        out_specs=P(("group", "adapter"), None, "tensor"),
        check_vma=False,
    )
```

time: 208 us -> 189 us (0.909); the launches traced: 205 us -> 188 us
  Pallas kernels: 121 us -> 91.7 us
  waiting for transfers between devices: 18.4 us -> 47.6 us
  starting transfers between devices: 55.1 us -> 38 us
  other arithmetic: 2.43 us -> 7.35 us
  local copies, waits for them, and re-layouts: 6.5 us -> 2.81 us
    ppermute x6 -> x3, starting transfers between devices: 35.5 us -> 15.1 us  [rightward(): return lax.ppermute(a, 'adapter', [(z - hops, z) for z in range(hops, n_z)])]
    ppermute x10 -> x7, waiting for transfers between devices: 11.4 us -> 29.9 us  [chip_shift(): lax.ppermute(a, 'tensor', [(2 * x + c, 2 * ((x + k) % n_x) + c) for x in...]
    pallas_call x5 -> x2, Pallas kernels: 45.6 us -> 29.7 us  [base_products(): pl.pallas_call(body, out_shape=(*[jax.ShapeDtypeStruct(part, BF)] * n_x,...]
    ppermute x0 -> x3, waiting for transfers between devices: none -> 12.2 us  [per_device(): lax.ppermute(late_up, 'adapter', [(z, (z - hops) % n_z) for z in range(n_...]
    ppermute x0 -> x3, starting transfers between devices: none -> 9.5 us  [per_device(): lax.ppermute(late_up, 'adapter', [(z, (z - hops) % n_z) for z in range(n_...]
    pallas_call x4, Pallas kernels: 23.5 us -> 17.2 us  [rank_products(): pl.pallas_call(body, out_shape=jax.ShapeDtypeStruct((count * prefill, ran...]
    convert_element_type x4, other arithmetic: 1.83 us -> 6.83 us  [rank(): pair = (part.astype(F32) + core_swap(part).astype(F32)).astype(BF)]
    pallas_call x6 -> x3, Pallas kernels: 11.7 us -> 7.26 us  [pair_sum(): pl.pallas_call(body, out_shape=jax.ShapeDtypeStruct((rows, width), BF), g...]
  transfers between devices with their start and end apart: 32 -> 26, of which waited for: 5 -> 8; matrix products, arithmetic and copies ran while one was open for 1% -> 4% of each run, Pallas kernels for 56% -> 46%
where the time goes in v3:
time: 189 us; the launch traced here: 188 us
  Pallas kernels  91.7 us (49%)
  waiting for transfers between devices  47.6 us (25%)
  starting transfers between devices  38 us (20%)
  other arithmetic  7.35 us (4%)
  local copies, waits for them, and re-layouts  2.81 us (1%)
    ppermute x7, waiting for transfers between devices, chip_shift(): lax.ppermute(a, 'tensor', [(2 * x + c, 2 * ((x + k) % n_x) + c) for x in...  29.9 us
    pallas_call x2, Pallas kernels, base_products(): pl.pallas_call(body, out_shape=(*[jax.ShapeDtypeStruct(part, BF)] * n_x,...  29.7 us
    pallas_call x3, Pallas kernels, finish(): pl.pallas_call(body, out_shape=jax.ShapeDtypeStruct(shape, BF), grid_spec...  18.2 us
    pallas_call x4, Pallas kernels, rank_products(): pl.pallas_call(body, out_shape=jax.ShapeDtypeStruct((count * prefill, ran...  17.2 us
    pallas_call x1, Pallas kernels, split_weight(): pl.pallas_call(body, out_shape=(jax.ShapeDtypeStruct((n_t, features, 2 *...  16.1 us
    ppermute x3, starting transfers between devices, rightward(): return lax.ppermute(a, 'adapter', [(z - hops, z) for z in range(hops, n_z)])  15.1 us
    ppermute x3, waiting for transfers between devices, per_device(): lax.ppermute(late_up, 'adapter', [(z, (z - hops) % n_z) for z in range(n_...  12.2 us
    ppermute x3, starting transfers between devices, per_device(): lax.ppermute(late_up, 'adapter', [(z, (z - hops) % n_z) for z in range(n_...  9.5 us
  transfers between devices with their start and end apart: 26, of which 8 were waited for; matrix products, arithmetic and copies ran while one was open for 4% of the time, Pallas kernels for 46%

profile of v3, /device:TPU:0, one launch (start us, length us, event | category | flops | bytes accessed | tf_op | source)
XLA Modules:
  0.0 187.9 jit_solution(10774180884131097304)
XLA Ops:
  0.0 5.0 %collective-permute-start.3 = (bf16[3,2048,128]{2,1,0:T(8,128)(2,1)}, bf16[3,2048,128]{2,1,0:T(8,128)(2,1)S(1)}, u32[]{:S(2)}, u32[]{:S(2)}) collective-permute-start(bf16[3,2048,128]{2,1,0:T(8,128)(2,1)} %rest_0_.9), channel_id=1, source_target_pairs={{0,4},{4,8},{8,12},{1,5},{5,9},{9,13},{2,6},{6,10},{10,14},{3,7},{... | collective-permute-start | bytes 4718600 | tf_op jit(solution)/shard_map/ppermute | solution.py:460
  6.3 1.6 plan_requests.1.plan_ref
  8.4 16.1 %split_weight.1 = (bf16[4,2048,512]{2,1,0:T(8,128)(2,1)}, bf16[768,512]{1,0:T(8,128)(2,1)}, bf16[768,512]{1,0:T(8,128)(2,1)}, bf16[2,768,512]{2,1,0:T(8,128)(2,1)}) custom-call(s32[8,128]{1,0:T(8,128)} %plan_requests.1.plan_ref, s32[4]{0:T(128)} %compare_select_fusion.2.slot_ref, bf16[3072,2048]{1,0:T(8,128)(2,1)} %x_ref.11, bf16[3072,2048]{1,0:T(8,128)(2,1)} %x_ref.11, ...), custom_call_target="tpu_custom_call" | custom-call | flops 64424508 | bytes 167772 | tf_op jit(solution)/shard_map/split_weight/pallas_call | solution.py:121
  24.6 2.6 %collective-permute-done.b_ref = bf16[768,512]{1,0:T(8,128)(2,1)} collective-permute-done((bf16[768,512]{1,0:T(8,128)(2,1)}, bf16[768,512]{1,0:T(8,128)(2,1)}, u32[]{:S(2)}, u32[]{:S(2)}) %collective-permute-start) | collective-permute-done | bytes 786464 | tf_op jit(solution)/shard_map/ppermute | solution.py:447
  27.2 2.2 %pair_sum.3.rest_4_ = bf16[768,512]{1,0:T(8,128)(2,1)} custom-call(bf16[2,768,512]{2,1,0:T(8,128)(2,1)} %get-tuple-element.16.a_ref.rest_0_, bf16[768,512]{1,0:T(8,128)(2,1)} %collective-permute-done.b_ref), custom_call_target="tpu_custom_call" | custom-call | flops 3932 | bytes 23592 | tf_op jit(solution)/shard_map/pair_sum/pallas_call | solution.py:218
  29.4 13.2 %base_products.2 = (bf16[1024,512]{1,0:T(8,128)(2,1)}, bf16[1024,512]{1,0:T(8,128)(2,1)}, bf16[2,1024,512]{2,1,0:T(8,128)(2,1)}) custom-call(s32[8,128]{1,0:T(8,128)} %plan_requests.1.plan_ref, bf16[3072,2048]{1,0:T(8,128)(2,1)} %x_ref.11, bf16[4,2048,512]{2,1,0:T(8,128)(2,1)} %get-tuple-element.15.rest_0_.rest_1_.rest_2_.rest_3_, ...), custom_call_target="tpu_custom_call" | custom-call | flops 85899344 | bytes 83886 | tf_op jit(solution)/shard_map/base_products/pallas_call | solution.py:179
  42.7 5.7 %collective-permute-start.10 = (bf16[3,2048,128]{2,1,0:T(8,128)(2,1)S(1)}, bf16[3,2048,128]{2,1,0:T(8,128)(2,1)}, u32[]{:S(2)}, u32[]{:S(2)}) collective-permute-start(bf16[3,2048,128]{2,1,0:T(8,128)(2,1)S(1)} %collective-permute-done.3.rest_6_.rest_4_.rest_2_.rest_3_), channel_id=1, source_target_pairs={{0,4},{4,8},{8,12},{1,5},{5,9},{9,13},{2,6},{6,10},{10,14},{3,7},{... | collective-permute-start | bytes 4718600 | tf_op jit(solution)/shard_map/ppermute | solution.py:460
  49.7 1.6 collective-permute-start.4
  51.2 2.4 %pair_sum.4.rest_4_ = bf16[1024,512]{1,0:T(8,128)(2,1)} custom-call(bf16[2,1024,512]{2,1,0:T(8,128)(2,1)} %get-tuple-element.18.a_ref.rest_3_.rest_0_, bf16[1024,512]{1,0:T(8,128)(2,1)} %collective-permute-done.1.b_ref), custom_call_target="tpu_custom_call" | custom-call | flops 5242 | bytes 31457 | tf_op jit(solution)/shard_map/pair_sum/pallas_call | solution.py:218
  53.7 15.9 %collective-permute-done.4.rest_7_.rest_2_ = bf16[768,512]{1,0:T(8,128)(2,1)} collective-permute-done((bf16[768,512]{1,0:T(8,128)(2,1)}, bf16[768,512]{1,0:T(8,128)(2,1)}, u32[]{:S(2)}, u32[]{:S(2)}) %collective-permute-start.4) | collective-permute-done | bytes 786464 | tf_op jit(solution)/shard_map/ppermute | solution.py:450
  69.6 16.5 %base_products.3 = (bf16[1280,512]{1,0:T(8,128)(2,1)}, bf16[1280,512]{1,0:T(8,128)(2,1)}, bf16[2,1280,512]{2,1,0:T(8,128)(2,1)}) custom-call(s32[8,128]{1,0:T(8,128)} %plan_requests.1.plan_ref, bf16[3072,2048]{1,0:T(8,128)(2,1)} %x_ref.11, bf16[4,2048,512]{2,1,0:T(8,128)(2,1)} %get-tuple-element.15.rest_0_.rest_1_.rest_2_.rest_3_, ...), custom_call_target="tpu_custom_call" | custom-call | flops 107374184 | bytes 83886 | tf_op jit(solution)/shard_map/base_products/pallas_call | solution.py:179
  87.6 4.4 %collective-permute-start.11 = (bf16[3,2048,128]{2,1,0:T(8,128)(2,1)}, bf16[3,2048,128]{2,1,0:T(8,128)(2,1)}, u32[]{:S(2)}, u32[]{:S(2)}) collective-permute-start(bf16[3,2048,128]{2,1,0:T(8,128)(2,1)} %collective-permute-done.10.rest_5_.rest_1_.rest_4_), channel_id=1, source_target_pairs={{0,4},{4,8},{8,12},{1,5},{5,9},{9,13},{2,6},{6,10},{10,14},{3,7},{... | collective-permute-start | bytes 4718600 | tf_op jit(solution)/shard_map/ppermute | solution.py:460
  94.1 2.7 %pair_sum.5.rest_1_ = bf16[1280,512]{1,0:T(8,128)(2,1)} custom-call(bf16[2,1280,512]{2,1,0:T(8,128)(2,1)} %get-tuple-element.20.a_ref.rest_3_.rest_0_, bf16[1280,512]{1,0:T(8,128)(2,1)} %collective-permute-done.6.b_ref), custom_call_target="tpu_custom_call" | custom-call | flops 6553 | bytes 39321 | tf_op jit(solution)/shard_map/pair_sum/pallas_call | solution.py:218
  96.8 4.2 %rank_products.5.rest_3_ = bf16[768,128]{1,0:T(8,128)(2,1)} custom-call(s32[8,128]{1,0:T(8,128)} %plan_requests.1.plan_ref, bf16[3072,2048]{1,0:T(8,128)(2,1)} %x_ref.11, bf16[3,2048,128]{2,1,0:T(8,128)(2,1)} %rest_0_.9, bf16[1280,512]{1,0:T(8,128)(2,1)} %pair_sum.5.rest_1_), custom_call_target="tpu_custom_call" | custom-call | flops 4026531 | bytes 47185 | tf_op jit(solution)/shard_map/rank_products/pallas_call | solution.py:288
  101.1 4.3 %rank_products.6.rest_5_ = bf16[768,128]{1,0:T(8,128)(2,1)} custom-call(s32[8,128]{1,0:T(8,128)} %plan_requests.1.plan_ref, bf16[3072,2048]{1,0:T(8,128)(2,1)} %x_ref.11, bf16[3,2048,128]{2,1,0:T(8,128)(2,1)} %rest_0_.9, bf16[3,2048,128]{2,1,0:T(8,128)(2,1)} %copy-done.1, bf16[3,2048,128]{2,1,0:T(8,128)(2,1)} %copy-done, bf16[768,128]{1,0:T(8,128)(2,1)} %rank_products.5.rest_3_), custom_call_target="tpu_custom_call" | custom-call | flops 4026531 | bytes 47185 | tf_op jit(solution)/shard_map/rank_products/pallas_call | solution.py:288
  105.6 6.4 %collective-permute-done.18.rest_6_.rest_5_.rest_2_ = bf16[1024,512]{1,0:T(8,128)(2,1)} collective-permute-done((bf16[1024,512]{1,0:T(8,128)(2,1)}, bf16[1024,512]{1,0:T(8,128)(2,1)}, u32[]{:S(2)}, u32[]{:S(2)}) %collective-permute-start.18) | collective-permute-done | bytes 1048608 | tf_op jit(solution)/shard_map/ppermute | solution.py:450
  115.1 1.6 copy_after.1
  116.7 4.2 %rank_products.7 = bf16[768,128]{1,0:T(8,128)(2,1)} custom-call(s32[8,128]{1,0:T(8,128)} %plan_requests.1.plan_ref, bf16[3072,2048]{1,0:T(8,128)(2,1)} %x_ref.11, bf16[3,2048,128]{2,1,0:T(8,128)(2,1)} %rest_0_.9, bf16[3,2048,128]{2,1,0:T(8,128)(2,1)} %copy-done.1, bf16[3,2048,128]{2,1,0:T(8,128)(2,1)} %collective-permute-done.8.rest_2_.rest_0_, ...), custom_call_target="tpu_custom_call" | custom-call | flops 4026531 | bytes 47185 | tf_op jit(solution)/shard_map/rank_products/pallas_call | solution.py:288
  121.0 1.7 add_convert_fusion.rest_8_
  122.7 2.5 %collective-permute-done.11.rest_6_ = bf16[3,2048,128]{2,1,0:T(8,128)(2,1)} collective-permute-done((bf16[3,2048,128]{2,1,0:T(8,128)(2,1)}, bf16[3,2048,128]{2,1,0:T(8,128)(2,1)}, u32[]{:S(2)}, u32[]{:S(2)}) %collective-permute-start.11) | collective-permute-done | bytes 1572896 | tf_op jit(solution)/shard_map/ppermute | solution.py:460
  125.2 6.3 %collective-permute-start.14 = (bf16[3,2,64,256]{3,2,1,0:T(8,128)(2,1)}, bf16[3,2,64,256]{3,2,1,0:T(8,128)(2,1)}, u32[]{:S(2)}, u32[]{:S(2)}) collective-permute-start(bf16[3,2,64,256]{3,2,1,0:T(8,128)(2,1)} %copy_after.1), channel_id=1, source_target_pairs={{0,12},{4,0},{8,4},{12,8},{1,13},{5,1},{9,5},{13,9},{2,14},{6,2},{... | collective-permute-start | bytes 589832 | tf_op jit(solution)/shard_map/ppermute | solution.py:517
  131.6 1.7 add_convert_fusion.1.rest_6_
  133.2 4.4 %rank_products.4 = bf16[768,128]{1,0:T(8,128)(2,1)} custom-call(s32[8,128]{1,0:T(8,128)} %plan_requests.1.plan_ref, bf16[3072,2048]{1,0:T(8,128)(2,1)} %x_ref.11, bf16[3,2048,128]{2,1,0:T(8,128)(2,1)} %rest_0_.9, bf16[3,2048,128]{2,1,0:T(8,128)(2,1)} %copy-done.1, bf16[3,2048,128]{2,1,0:T(8,128)(2,1)} %collective-permute-done.8.rest_2_.rest_0_, ...), custom_call_target="tpu_custom_call" | custom-call | flops 4026531 | bytes 47185 | tf_op jit(solution)/shard_map/rank_products/pallas_call | solution.py:288
  137.7 3.2 %collective-permute-start.15 = (bf16[3,2,64,256]{3,2,1,0:T(8,128)(2,1)}, bf16[3,2,64,256]{3,2,1,0:T(8,128)(2,1)S(1)}, u32[]{:S(2)}, u32[]{:S(2)}) collective-permute-start(bf16[3,2,64,256]{3,2,1,0:T(8,128)(2,1)} %copy_after.1), channel_id=1, source_target_pairs={{0,8},{4,12},{8,0},{12,4},{1,9},{5,13},{9,1},{13,5},{2,10},{6,14},... | collective-permute-start | bytes 589832 | tf_op jit(solution)/shard_map/ppermute | solution.py:517
  141.2 1.8 add_convert_fusion.2.rest_6_
  142.9 12.1 %collective-permute-done.15.rest_12_.rest_10_.rest_7_ = bf16[3,2,64,256]{3,2,1,0:T(8,128)(2,1)S(1)} collective-permute-done((bf16[3,2,64,256]{3,2,1,0:T(8,128)(2,1)}, bf16[3,2,64,256]{3,2,1,0:T(8,128)(2,1)S(1)}, u32[]{:S(2)}, u32[]{:S(2)}) %collective-permute-start.15) | collective-permute-done | bytes 196640 | tf_op jit(solution)/shard_map/ppermute | solution.py:517
  157.7 1.7 add_convert_fusion.3.rest_3_
  159.3 3.9 %collective-permute-done.25.rest_9_ = bf16[768,128]{1,0:T(8,128)(2,1)} collective-permute-done((bf16[768,128]{1,0:T(8,128)(2,1)}, bf16[768,128]{1,0:T(8,128)(2,1)}, u32[]{:S(2)}, u32[]{:S(2)}) %collective-permute-start.25) | collective-permute-done | bytes 196640 | tf_op jit(solution)/shard_map/ppermute | solution.py:450
  163.7 3.7 %collective-permute-done.23.rest_7_ = bf16[768,128]{1,0:T(8,128)(2,1)} collective-permute-done((bf16[768,128]{1,0:T(8,128)(2,1)}, bf16[768,128]{1,0:T(8,128)(2,1)}, u32[]{:S(2)}, u32[]{:S(2)}) %collective-permute-start.23) | collective-permute-done | bytes 196640 | tf_op jit(solution)/shard_map/ppermute | solution.py:450
  167.4 7.4 %finish.3.rest_12_ = bf16[3072,2,256]{2,1,0:T(2,128)(2,1)} custom-call(s32[8,128]{1,0:T(8,128)} %plan_requests.1.plan_ref, bf16[2,768,512]{2,1,0:T(8,128)(2,1)} %get-tuple-element.16.a_ref.rest_0_, bf16[768,512]{1,0:T(8,128)(2,1)} %copy-done.7, bf16[768,512]{1,0:T(8,128)(2,1)} %collective-permute-done.4.rest_7_.rest_2_, ...), custom_call_target="tpu_custom_call" | custom-call | flops 24159192 | bytes 78643 | tf_op jit(solution)/shard_map/finish/pallas_call | solution.py:418
  177.0 5.0 %finish.4.rest_9_ = bf16[3072,2,256]{2,1,0:T(2,128)(2,1)} custom-call(s32[8,128]{1,0:T(8,128)} %plan_requests.1.plan_ref, bf16[2,1024,512]{2,1,0:T(8,128)(2,1)} %get-tuple-element.18.a_ref.rest_3_.rest_0_, bf16[1024,512]{1,0:T(8,128)(2,1)} %collective-permute-done.17.rest_4_.rest_1_, ...), custom_call_target="tpu_custom_call", output_to_operand_aliasing={{}: (13, {})} | custom-call | flops 12079595 | bytes 39321 | tf_op jit(solution)/shard_map/finish/pallas_call | solution.py:418
  182.0 5.8 %finish.5 = bf16[3072,2,256]{2,1,0:T(2,128)(2,1)} custom-call(s32[8,128]{1,0:T(8,128)} %plan_requests.1.plan_ref, bf16[2,1280,512]{2,1,0:T(8,128)(2,1)} %get-tuple-element.20.a_ref.rest_3_.rest_0_, bf16[1280,512]{1,0:T(8,128)(2,1)} %copy-done.3, bf16[1280,512]{1,0:T(8,128)(2,1)} %copy-done.4, ...), custom_call_target="tpu_custom_call", output_to_operand_aliasing={{}: (10, {})} | custom-call | flops 12079595 | bytes 39321 | tf_op jit(solution)/shard_map/finish/pallas_call | solution.py:418
  (58 shorter events, 15.6 us)
Async XLA Ops:
  0.0 42.7 %collective-permute-start.3 = (bf16[3,2048,128]{2,1,0:T(8,128)(2,1)}, bf16[3,2048,128]{2,1,0:T(8,128)(2,1)S(1)}, u32[]{:S(2)}, u32[]{:S(2)}) collective-permute-start(bf16[3,2048,128]{2,1,0:T(8,128)(2,1)} %rest_0_.9), channel_id=1, source_target_pairs={{0,4},{4,8},{8,12},{1,5},{5,9},{9,13},{2,6},{6,10},{10,14},{3,7},{... | collective-permute-start | bytes 4718600 | tf_op jit(solution)/shard_map/ppermute | solution.py:460
  5.0 43.4 %collective-permute-start.2 = (bf16[3,2048,128]{2,1,0:T(8,128)(2,1)}, bf16[3,2048,128]{2,1,0:T(8,128)(2,1)S(1)}, u32[]{:S(2)}, u32[]{:S(2)}) collective-permute-start(bf16[3,2048,128]{2,1,0:T(8,128)(2,1)} %rest_0_.9), channel_id=1, source_target_pairs={{4,0},{8,4},{12,8},{5,1},{9,5},{13,9},{6,2},{10,6},{14,10},{7,3},{... | collective-permute-start | bytes 4718600 | tf_op jit(solution)/shard_map/ppermute | solution.py:457
  24.6 2.6 %collective-permute-start = (bf16[768,512]{1,0:T(8,128)(2,1)}, bf16[768,512]{1,0:T(8,128)(2,1)}, u32[]{:S(2)}, u32[]{:S(2)}) collective-permute-start(bf16[768,512]{1,0:T(8,128)(2,1)} %get-tuple-element.17), channel_id=1, source_target_pairs={{0,1},{1,0},{2,3},{3,2},{4,5},{5,4},{6,7},{7,6},{8,9},{9,8},{10,11... | collective-permute-start | bytes 2359304 | tf_op jit(solution)/shard_map/ppermute | solution.py:447
  42.5 8.7 %collective-permute-start.1 = (bf16[1024,512]{1,0:T(8,128)(2,1)}, bf16[1024,512]{1,0:T(8,128)(2,1)}, u32[]{:S(2)}, u32[]{:S(2)}) collective-permute-start(bf16[1024,512]{1,0:T(8,128)(2,1)} %get-tuple-element.19), channel_id=1, source_target_pairs={{0,1},{1,0},{2,3},{3,2},{4,5},{5,4},{6,7},{7,6},{8,9},{9,8},{10,11... | collective-permute-start | bytes 3145736 | tf_op jit(solution)/shard_map/ppermute | solution.py:447
  42.7 11.0 %copy-start = (bf16[3,2048,128]{2,1,0:T(8,128)(2,1)}, bf16[3,2048,128]{2,1,0:T(8,128)(2,1)S(1)}, u32[]{:S(2)}) copy-start(bf16[3,2048,128]{2,1,0:T(8,128)(2,1)S(1)} %collective-permute-done.3.rest_6_.rest_4_.rest_2_.rest_3_) | copy-start | bytes 4718596
  42.7 45.0 %collective-permute-start.10 = (bf16[3,2048,128]{2,1,0:T(8,128)(2,1)S(1)}, bf16[3,2048,128]{2,1,0:T(8,128)(2,1)}, u32[]{:S(2)}, u32[]{:S(2)}) collective-permute-start(bf16[3,2048,128]{2,1,0:T(8,128)(2,1)S(1)} %collective-permute-done.3.rest_6_.rest_4_.rest_2_.rest_3_), channel_id=1, source_target_pairs={{0,4},{4,8},{8,12},{1,5},{5,9},{9,13},{2,6},{6,10},{10,14},{3,7},{... | collective-permute-start | bytes 4718600 | tf_op jit(solution)/shard_map/ppermute | solution.py:460
  48.4 5.3 %copy-start.1 = (bf16[3,2048,128]{2,1,0:T(8,128)(2,1)}, bf16[3,2048,128]{2,1,0:T(8,128)(2,1)S(1)}, u32[]{:S(2)}) copy-start(bf16[3,2048,128]{2,1,0:T(8,128)(2,1)S(1)} %collective-permute-done.2.rest_5_.rest_1_) | copy-start | bytes 4718596
  48.4 43.7 %collective-permute-start.8 = (bf16[3,2048,128]{2,1,0:T(8,128)(2,1)S(1)}, bf16[3,2048,128]{2,1,0:T(8,128)(2,1)}, u32[]{:S(2)}, u32[]{:S(2)}) collective-permute-start(bf16[3,2048,128]{2,1,0:T(8,128)(2,1)S(1)} %collective-permute-done.2.rest_5_.rest_1_), channel_id=1, source_target_pairs={{4,0},{8,4},{12,8},{5,1},{9,5},{13,9},{6,2},{10,6},{14,10},{7,3},{... | collective-permute-start | bytes 4718600 | tf_op jit(solution)/shard_map/ppermute | solution.py:457
  49.7 19.9 %collective-permute-start.4 = (bf16[768,512]{1,0:T(8,128)(2,1)}, bf16[768,512]{1,0:T(8,128)(2,1)}, u32[]{:S(2)}, u32[]{:S(2)}) collective-permute-start(bf16[768,512]{1,0:T(8,128)(2,1)} %pair_sum.3.rest_4_), channel_id=1, source_target_pairs={{0,2},{1,3},{2,0},{3,1},{4,6},{5,7},{6,4},{7,5},{8,10},{9,11},{10,... | collective-permute-start | bytes 2359304 | tf_op jit(solution)/shard_map/ppermute | solution.py:450
  86.1 7.5 %collective-permute-start.6 = (bf16[1280,512]{1,0:T(8,128)(2,1)}, bf16[1280,512]{1,0:T(8,128)(2,1)}, u32[]{:S(2)}, u32[]{:S(2)}) collective-permute-start(bf16[1280,512]{1,0:T(8,128)(2,1)} %get-tuple-element.22), channel_id=1, source_target_pairs={{0,1},{1,0},{2,3},{3,2},{4,5},{5,4},{6,7},{7,6},{8,9},{9,8},{10,11... | collective-permute-start | bytes 3932168 | tf_op jit(solution)/shard_map/ppermute | solution.py:447
  86.1 25.9 %collective-permute-start.18 = (bf16[1024,512]{1,0:T(8,128)(2,1)}, bf16[1024,512]{1,0:T(8,128)(2,1)}, u32[]{:S(2)}, u32[]{:S(2)}) collective-permute-start(bf16[1024,512]{1,0:T(8,128)(2,1)} %pair_sum.4.rest_4_), channel_id=1, source_target_pairs={{0,2},{1,3},{2,0},{3,1},{4,6},{5,7},{6,4},{7,5},{8,10},{9,11},{10,... | collective-permute-start | bytes 3145736 | tf_op jit(solution)/shard_map/ppermute | solution.py:450
  87.6 37.6 %collective-permute-start.11 = (bf16[3,2048,128]{2,1,0:T(8,128)(2,1)}, bf16[3,2048,128]{2,1,0:T(8,128)(2,1)}, u32[]{:S(2)}, u32[]{:S(2)}) collective-permute-start(bf16[3,2048,128]{2,1,0:T(8,128)(2,1)} %collective-permute-done.10.rest_5_.rest_1_.rest_4_), channel_id=1, source_target_pairs={{0,4},{4,8},{8,12},{1,5},{5,9},{9,13},{2,6},{6,10},{10,14},{3,7},{... | collective-permute-start | bytes 4718600 | tf_op jit(solution)/shard_map/ppermute | solution.py:460
  92.1 39.5 %collective-permute-start.9 = (bf16[3,2048,128]{2,1,0:T(8,128)(2,1)}, bf16[3,2048,128]{2,1,0:T(8,128)(2,1)}, u32[]{:S(2)}, u32[]{:S(2)}) collective-permute-start(bf16[3,2048,128]{2,1,0:T(8,128)(2,1)} %collective-permute-done.8.rest_2_.rest_0_), channel_id=1, source_target_pairs={{4,0},{8,4},{12,8},{5,1},{9,5},{13,9},{6,2},{10,6},{14,10},{7,3},{... | collective-permute-start | bytes 4718600 | tf_op jit(solution)/shard_map/ppermute | solution.py:457
  93.5 11.9 %collective-permute-start.21 = (bf16[768,512]{1,0:T(8,128)(2,1)}, bf16[768,512]{1,0:T(8,128)(2,1)S(1)}, u32[]{:S(2)}, u32[]{:S(2)}) collective-permute-start(bf16[768,512]{1,0:T(8,128)(2,1)} %get-tuple-element.24), channel_id=1, source_target_pairs={{0,1},{1,0},{2,3},{3,2},{4,5},{5,4},{6,7},{7,6},{8,9},{9,8},{10,11... | collective-permute-start | bytes 2359304 | tf_op jit(solution)/shard_map/ppermute | solution.py:447
  93.6 44.0 %collective-permute-start.17 = (bf16[1024,512]{1,0:T(8,128)(2,1)}, bf16[1024,512]{1,0:T(8,128)(2,1)}, u32[]{:S(2)}, u32[]{:S(2)}) collective-permute-start(bf16[1024,512]{1,0:T(8,128)(2,1)} %get-tuple-element.23), channel_id=1, source_target_pairs={{0,1},{1,0},{2,3},{3,2},{4,5},{5,4},{6,7},{7,6},{8,9},{9,8},{10,11... | collective-permute-start | bytes 3145736 | tf_op jit(solution)/shard_map/ppermute | solution.py:447
  101.0 11.0 %copy-start.5 = (bf16[768,128]{1,0:T(8,128)(2,1)S(1)}, bf16[768,128]{1,0:T(8,128)(2,1)}, u32[]{:S(2)}) copy-start(bf16[768,128]{1,0:T(8,128)(2,1)} %rank_products.5.rest_3_) | copy-start | bytes 589828
  101.0 12.6 %copy-start.2 = (bf16[1280,512]{1,0:T(8,128)(2,1)S(1)}, bf16[1280,512]{1,0:T(8,128)(2,1)}, u32[]{:S(2)}) copy-start(bf16[1280,512]{1,0:T(8,128)(2,1)} %pair_sum.5.rest_1_) | copy-start | bytes 3932164
  105.4 6.6 %copy-start.7 = (bf16[768,512]{1,0:T(8,128)(2,1)}, bf16[768,512]{1,0:T(8,128)(2,1)S(1)}, u32[]{:S(2)}) copy-start(bf16[768,512]{1,0:T(8,128)(2,1)S(1)} %collective-permute-done.21.rest_1_) | copy-start | bytes 2359300
  105.4 6.6 %collective-permute-start.24 = (bf16[768,128]{1,0:T(8,128)(2,1)}, bf16[768,128]{1,0:T(8,128)(2,1)S(1)}, u32[]{:S(2)}, u32[]{:S(2)}) collective-permute-start(bf16[768,128]{1,0:T(8,128)(2,1)} %rank_products.6.rest_5_), channel_id=1, source_target_pairs={{0,1},{1,0},{2,3},{3,2},{4,5},{5,4},{6,7},{7,6},{8,9},{9,8},{10,11... | collective-permute-start | bytes 589832 | tf_op jit(solution)/shard_map/ppermute | solution.py:447
  112.0 1.6 collective-permute-start.22
  112.7 62.1 %collective-permute-start.5 = (bf16[1280,512]{1,0:T(8,128)(2,1)}, bf16[1280,512]{1,0:T(8,128)(2,1)S(1)}, u32[]{:S(2)}, u32[]{:S(2)}) collective-permute-start(bf16[1280,512]{1,0:T(8,128)(2,1)} %get-tuple-element.21), channel_id=1, source_target_pairs={{0,1},{1,0},{2,3},{3,2},{4,5},{5,4},{6,7},{7,6},{8,9},{9,8},{10,11... | collective-permute-start | bytes 3932168 | tf_op jit(solution)/shard_map/ppermute | solution.py:447
  113.6 61.3 %collective-permute-start.7 = (bf16[1280,512]{1,0:T(8,128)(2,1)S(1)}, bf16[1280,512]{1,0:T(8,128)(2,1)S(1)}, u32[]{:S(2)}, u32[]{:S(2)}) collective-permute-start(bf16[1280,512]{1,0:T(8,128)(2,1)S(1)} %copy-done.2), channel_id=1, source_target_pairs={{0,2},{1,3},{2,0},{3,1},{4,6},{5,7},{6,4},{7,5},{8,10},{9,11},{10,... | collective-permute-start | bytes 3932168 | tf_op jit(solution)/shard_map/ppermute | solution.py:450
  125.2 15.6 %collective-permute-start.14 = (bf16[3,2,64,256]{3,2,1,0:T(8,128)(2,1)}, bf16[3,2,64,256]{3,2,1,0:T(8,128)(2,1)}, u32[]{:S(2)}, u32[]{:S(2)}) collective-permute-start(bf16[3,2,64,256]{3,2,1,0:T(8,128)(2,1)} %copy_after.1), channel_id=1, source_target_pairs={{0,12},{4,0},{8,4},{12,8},{1,13},{5,1},{9,5},{13,9},{2,14},{6,2},{... | collective-permute-start | bytes 589832 | tf_op jit(solution)/shard_map/ppermute | solution.py:517
  131.6 9.3 %collective-permute-start.19 = (bf16[768,128]{1,0:T(8,128)(2,1)}, bf16[768,128]{1,0:T(8,128)(2,1)}, u32[]{:S(2)}, u32[]{:S(2)}) collective-permute-start(bf16[768,128]{1,0:T(8,128)(2,1)} %rank_products.7), channel_id=1, source_target_pairs={{0,1},{1,0},{2,3},{3,2},{4,5},{5,4},{6,7},{7,6},{8,9},{9,8},{10,11... | collective-permute-start | bytes 589832 | tf_op jit(solution)/shard_map/ppermute | solution.py:447
  137.7 17.4 %collective-permute-start.15 = (bf16[3,2,64,256]{3,2,1,0:T(8,128)(2,1)}, bf16[3,2,64,256]{3,2,1,0:T(8,128)(2,1)S(1)}, u32[]{:S(2)}, u32[]{:S(2)}) collective-permute-start(bf16[3,2,64,256]{3,2,1,0:T(8,128)(2,1)} %copy_after.1), channel_id=1, source_target_pairs={{0,8},{4,12},{8,0},{12,4},{1,9},{5,13},{9,1},{13,5},{2,10},{6,14},... | collective-permute-start | bytes 589832 | tf_op jit(solution)/shard_map/ppermute | solution.py:517
  140.9 14.7 %collective-permute-start.16 = (bf16[3,2,64,256]{3,2,1,0:T(8,128)(2,1)}, bf16[3,2,64,256]{3,2,1,0:T(8,128)(2,1)}, u32[]{:S(2)}, u32[]{:S(2)}) collective-permute-start(bf16[3,2,64,256]{3,2,1,0:T(8,128)(2,1)} %copy_after.1), channel_id=1, source_target_pairs={{0,4},{4,8},{8,12},{12,0},{1,5},{5,9},{9,13},{13,1},{2,6},{6,10},{... | collective-permute-start | bytes 589832 | tf_op jit(solution)/shard_map/ppermute | solution.py:517
  140.9 16.2 %collective-permute-start.12 = (bf16[768,128]{1,0:T(8,128)(2,1)}, bf16[768,128]{1,0:T(8,128)(2,1)S(1)}, u32[]{:S(2)}, u32[]{:S(2)}) collective-permute-start(bf16[768,128]{1,0:T(8,128)(2,1)} %rank_products.4), channel_id=1, source_target_pairs={{0,1},{1,0},{2,3},{3,2},{4,5},{5,4},{6,7},{7,6},{8,9},{9,8},{10,11... | collective-permute-start | bytes 589832 | tf_op jit(solution)/shard_map/ppermute | solution.py:447
  155.1 12.3 %copy-start.6 = (bf16[3,2,64,256]{3,2,1,0:T(8,128)(2,1)}, bf16[3,2,64,256]{3,2,1,0:T(8,128)(2,1)S(1)}, u32[]{:S(2)}) copy-start(bf16[3,2,64,256]{3,2,1,0:T(8,128)(2,1)S(1)} %collective-permute-done.15.rest_12_.rest_10_.rest_7_) | copy-start | bytes 589828
  155.1 8.1 %collective-permute-start.25 = (bf16[768,128]{1,0:T(8,128)(2,1)}, bf16[768,128]{1,0:T(8,128)(2,1)}, u32[]{:S(2)}, u32[]{:S(2)}) collective-permute-start(bf16[768,128]{1,0:T(8,128)(2,1)} %add_convert_fusion.rest_8_), channel_id=1, source_target_pairs={{0,2},{1,3},{2,0},{3,1},{4,6},{5,7},{6,4},{7,5},{8,10},{9,11},{10,... | collective-permute-start | bytes 589832 | tf_op jit(solution)/shard_map/ppermute | solution.py:450
  155.6 11.8 %collective-permute-start.23 = (bf16[768,128]{1,0:T(8,128)(2,1)}, bf16[768,128]{1,0:T(8,128)(2,1)}, u32[]{:S(2)}, u32[]{:S(2)}) collective-permute-start(bf16[768,128]{1,0:T(8,128)(2,1)} %add_convert_fusion.1.rest_6_), channel_id=1, source_target_pairs={{0,2},{1,3},{2,0},{3,1},{4,6},{5,7},{6,4},{7,5},{8,10},{9,11},{10,... | collective-permute-start | bytes 589832 | tf_op jit(solution)/shard_map/ppermute | solution.py:450
  157.1 17.7 %collective-permute-start.20 = (bf16[768,128]{1,0:T(8,128)(2,1)}, bf16[768,128]{1,0:T(8,128)(2,1)}, u32[]{:S(2)}, u32[]{:S(2)}) collective-permute-start(bf16[768,128]{1,0:T(8,128)(2,1)} %add_convert_fusion.2.rest_6_), channel_id=1, source_target_pairs={{0,2},{1,3},{2,0},{3,1},{4,6},{5,7},{6,4},{7,5},{8,10},{9,11},{10,... | collective-permute-start | bytes 589832 | tf_op jit(solution)/shard_map/ppermute | solution.py:450
  163.2 18.8 %collective-permute-start.13 = (bf16[768,128]{1,0:T(8,128)(2,1)}, bf16[768,128]{1,0:T(8,128)(2,1)}, u32[]{:S(2)}, u32[]{:S(2)}) collective-permute-start(bf16[768,128]{1,0:T(8,128)(2,1)} %add_convert_fusion.3.rest_3_), channel_id=1, source_target_pairs={{0,2},{1,3},{2,0},{3,1},{4,6},{5,7},{6,4},{7,5},{8,10},{9,11},{10,... | collective-permute-start | bytes 589832 | tf_op jit(solution)/shard_map/ppermute | solution.py:450
  (3 other events, 2.8 us)

commit v4 on v3

--- a/solution.py
+++ b/solution.py
@@ -7,7 +7,7 @@
 
 BF = jnp.bfloat16
 F32 = jnp.float32
-BASE_CHUNKS = (3, 4, 5)
+BASE_CHUNKS = (3, 5, 4)
 RANK_CHUNKS = 4
 SMEM = pltpu.SMEM
 ANY = pl.BlockSpec(memory_space=pl.ANY)
@@ -24,6 +24,51 @@
 
 def params(mib=60):
     return pltpu.CompilerParams(vmem_limit_bytes=mib * 1024 * 1024)
+
+
+def pack_maps(down, up):
+    stored, features, lanes = down.shape
+    _, sides, depth, columns = up.shape
+    tiles = columns // lanes
+    part = sides * depth
+
+    def body(down_ref, up_ref, o_ref, held, sems):
+        copies = []
+        for a in range(stored):
+            copies.append(
+                pltpu.make_async_copy(
+                    down_ref.at[a], o_ref.at[a, pl.ds(0, features)], sems.at[0, a]
+                )
+            )
+            copies[-1].start()
+        for a in range(stored):
+            flat = up_ref[a].reshape(part, columns)
+            for j in range(tiles):
+                held[a, j * part : (j + 1) * part] = flat[:, j * lanes : (j + 1) * lanes]
+            copies.append(
+                pltpu.make_async_copy(
+                    held.at[a],
+                    o_ref.at[a, pl.ds(features, tiles * part)],
+                    sems.at[1, a],
+                )
+            )
+            copies[-1].start()
+        for copy in copies:
+            copy.wait()
+
+    return pl.pallas_call(
+        body,
+        out_shape=jax.ShapeDtypeStruct((stored, features + tiles * part, lanes), BF),
+        in_specs=[pl.BlockSpec(memory_space=pltpu.VMEM)] * 2,
+        out_specs=ANY,
+        scratch_shapes=[
+            pltpu.VMEM((stored, tiles * part, lanes), BF),
+            pltpu.SemaphoreType.DMA((2, stored)),
+        ],
+        compiler_params=params(),
+        cost_estimate=cost(0, 4 * down.size),
+        name="pack_maps",
+    )(down, up)
 
 
 def plan_requests(table, adapters, lengths, here, n_z, stored):
@@ -113,16 +158,22 @@
 
         @pl.when(step == steps - 1)
         def _():
+            send_refs[0][...] = total[0].astype(BF)
+            for j in range(1, n_x):
+                send_refs[2 * j - 1][...] = total[j, :cut].astype(BF)
+                send_refs[2 * j][...] = total[j, cut:].astype(BF)
             for j in range(n_x):
-                send_refs[j][...] = total[j].astype(BF)
                 keep_ref[j] = total[n_x + j].astype(BF)
 
     part = (count * prefill, 2 * width)
+    cut = (count // 2) * prefill
+    upper, lower = (cut, 2 * width), (count * prefill - cut, 2 * width)
+    outs = [part] + [upper, lower] * (n_x - 1)
     split, *sends, keep = pl.pallas_call(
         body,
         out_shape=(
             jax.ShapeDtypeStruct((n_t, features, 2 * width), BF),
-            *[jax.ShapeDtypeStruct(part, BF)] * n_x,
+            *[jax.ShapeDtypeStruct(out, BF) for out in outs],
             jax.ShapeDtypeStruct((n_x, *part), BF),
         ),
         grid_spec=pltpu.PrefetchScalarGridSpec(
@@ -135,7 +186,7 @@
             + [pl.BlockSpec((rows, 2, columns), lambda i, p, s: (i, 0, 0))],
             out_specs=(
                 pl.BlockSpec((n_t, rows, 2 * width), lambda i, p, s: (0, i, 0)),
-                *[pl.BlockSpec(part, lambda i, p, s: (0, 0))] * n_x,
+                *[pl.BlockSpec(out, lambda i, p, s: (0, 0)) for out in outs],
                 pl.BlockSpec((n_x, *part), lambda i, p, s: (0, 0, 0)),
             ),
             scratch_shapes=[pltpu.VMEM((n_t, count * prefill, 2 * width), F32)],
@@ -159,13 +210,26 @@
         live = plan_ref[LENGTH, first + pl.program_id(0)]
 
         def products(rows):
+            dead = jnp.zeros((prefill - rows, width), BF)
             for j in range(n_t):
-                out = send_refs[j] if j < n_x else keep_ref.at[j - n_x]
-                out[:rows] = jnp.dot(
+                out = jnp.dot(
                     x_ref[:rows], w_refs[j][0], preferred_element_type=F32
                 ).astype(BF)
                 if rows < prefill:
-                    out[rows:] = jnp.zeros((prefill - rows, width), BF)
+                    out = jnp.concatenate([out, dead], 0)
+                if j == 0:
+                    send_refs[0][...] = out
+                elif j >= n_x:
+                    keep_ref[j - n_x] = out
+                else:
+
+                    @pl.when(pl.program_id(0) < cut)
+                    def _():
+                        send_refs[2 * j - 1][...] = out
+
+                    @pl.when(pl.program_id(0) >= cut)
+                    def _():
+                        send_refs[2 * j][...] = out
 
         @pl.when(live > short)
         def _():
@@ -175,12 +239,18 @@
         def _():
             products(short)
 
-    part = (count * prefill, width)
+    cut = count // 2
+    parts = [count] + [cut, count - cut] * (n_x - 1)
+    block = (prefill, width)
+    places = [lambda i, p: (i, 0)] + [
+        lambda i, p: (jnp.minimum(i, cut - 1), 0),
+        lambda i, p: (jnp.maximum(i - cut, 0), 0),
+    ] * (n_x - 1)
     *sends, keep = pl.pallas_call(
         body,
         out_shape=(
-            *[jax.ShapeDtypeStruct(part, BF)] * n_x,
-            jax.ShapeDtypeStruct((n_x, *part), BF),
+            *[jax.ShapeDtypeStruct((n * prefill, width), BF) for n in parts],
+            jax.ShapeDtypeStruct((n_x, count * prefill, width), BF),
         ),
         grid_spec=pltpu.PrefetchScalarGridSpec(
             num_scalar_prefetch=1,
@@ -196,7 +266,7 @@
             ]
             + [ANY] * n_after,
             out_specs=(
-                *[pl.BlockSpec((prefill, width), lambda i, p: (i, 0))] * n_x,
+                *[pl.BlockSpec(block, place) for place in places],
                 pl.BlockSpec((n_x, prefill, width), lambda i, p: (0, i, 0)),
             ),
         ),
@@ -207,43 +277,70 @@
     return sends, keep
 
 
-def pair_sum(one, other, index):
+def pair_sum(one, others, index, after):
     _, rows, width = one.shape
-    block = rows // 2
-
-    def body(a_ref, b_ref, o_ref):
-        o_ref[...] = (a_ref[0].astype(F32) + b_ref[...].astype(F32)).astype(BF)
-
-    spec = pl.BlockSpec((block, width), lambda i: (i, 0))
+    cut = others[0].shape[0]
+
+    def body(a_ref, *rest):
+        b_refs = rest[:2]
+        o_ref, mine, theirs, total, sems, out_sems = rest[2 + len(after) :]
+        copies, outs = [], []
+        spans = [pl.ds(0, cut), pl.ds(cut, rows - cut)]
+        for k, span in enumerate(spans):
+            copies.append(
+                (
+                    pltpu.make_async_copy(
+                        a_ref.at[index, span], mine.at[span], sems.at[0, k]
+                    ),
+                    pltpu.make_async_copy(b_refs[k], theirs.at[span], sems.at[1, k]),
+                )
+            )
+            for copy in copies[-1]:
+                copy.start()
+        for k, span in enumerate(spans):
+            for copy in copies[k]:
+                copy.wait()
+            value = mine[span].astype(F32) + theirs[span].astype(F32)
+            total[span] = value.astype(BF)
+            outs.append(
+                pltpu.make_async_copy(total.at[span], o_ref.at[span], out_sems.at[k])
+            )
+            outs[-1].start()
+        for copy in outs:
+            copy.wait()
+
     return pl.pallas_call(
         body,
         out_shape=jax.ShapeDtypeStruct((rows, width), BF),
-        grid=(rows // block,),
-        in_specs=[pl.BlockSpec((1, block, width), lambda i: (index, i, 0)), spec],
-        out_specs=spec,
+        in_specs=[ANY] * (3 + len(after)),
+        out_specs=ANY,
+        scratch_shapes=[pltpu.VMEM((rows, width), BF)] * 3
+        + [pltpu.SemaphoreType.DMA((2, 2)), pltpu.SemaphoreType.DMA((2,))],
         compiler_params=params(),
         cost_estimate=cost(rows * width, 6 * rows * width),
         name="pair_sum",
-    )(one, other)
-
-
-def copy_after(a, after):
-    def body(a_ref, *rest):
-        rest[-1][...] = a_ref[...]
-
-    vmem = pl.BlockSpec(memory_space=pltpu.VMEM)
+    )(one, *others, *after)
+
+
+def hold(arrays, after):
+    n = len(arrays)
+
+    def body(*refs):
+        pass
+
     return pl.pallas_call(
         body,
-        out_shape=jax.ShapeDtypeStruct(a.shape, a.dtype),
-        in_specs=[vmem] + [ANY] * len(after),
-        out_specs=vmem,
+        out_shape=[jax.ShapeDtypeStruct(a.shape, a.dtype) for a in arrays],
+        in_specs=[ANY] * (n + len(after)),
+        out_specs=[ANY] * n,
+        input_output_aliases={i: i for i in range(n)},
         compiler_params=params(),
-        cost_estimate=cost(0, 4 * a.size),
-        name="copy_after",
-    )(a, *after)
-
-
-def fetch(refs, source, row, target, sem):
+        cost_estimate=cost(0, 1 << 20),
+        name="hold",
+    )(*arrays, *after)
+
+
+def fetch(refs, source, row, part, target, sem):
     for codes, ref in refs:
         hit = source == codes[0]
         for code in codes[1:]:
@@ -251,13 +348,15 @@
 
         @pl.when(hit)
         def _():
-            pltpu.make_async_copy(ref.at[row], target, sem).start()
+            pltpu.make_async_copy(ref.at[row, part], target, sem).start()
 
 
 def rank_products(plan, hidden, maps, first, count, prefill, after):
     sources = list(maps)
-    _, features, ranks = maps[sources[0]].shape
+    features, ranks = hidden.shape[1], maps[sources[0]].shape[2]
     n_map, n_after = len(maps), len(after)
+    short = prefill // 2
+    down = pl.ds(0, features)
 
     def body(plan_ref, x_ref, *rest):
         refs = list(zip(sources, rest[:n_map]))
@@ -268,6 +367,7 @@
                 refs,
                 plan_ref[SOURCE, first + i],
                 plan_ref[ROW, first + i],
+                down,
                 held.at[i],
                 sems.at[0, i],
             )
@@ -279,11 +379,25 @@
             )
             copies[-1].start()
         for i in range(count):
-            pltpu.make_async_copy(rest[0].at[0], held.at[i], sems.at[0, i]).wait()
+            pltpu.make_async_copy(
+                rest[0].at[0, down], held.at[i], sems.at[0, i]
+            ).wait()
             copies[i].wait()
-            o_ref[i * prefill : (i + 1) * prefill] = jnp.dot(
-                rows[i], held[i], preferred_element_type=F32
-            ).astype(BF)
+            live = plan_ref[LENGTH, first + i]
+            above, below = i * prefill, i * prefill + short
+
+            @pl.when(live > short)
+            def _():
+                o_ref[above : above + prefill] = jnp.dot(
+                    rows[i], held[i], preferred_element_type=F32
+                ).astype(BF)
+
+            @pl.when(live <= short)
+            def _():
+                o_ref[above:below] = jnp.dot(
+                    rows[i, :short], held[i], preferred_element_type=F32
+                ).astype(BF)
+                o_ref[below : below + short] = jnp.zeros((short, ranks), BF)
 
     return pl.pallas_call(
         body,
@@ -307,7 +421,11 @@
 
 def finish(plan, bases, ranks, maps, before, first, count, prefill, shape):
     sources = list(maps)
-    _, _, depth, columns = maps[sources[0]].shape
+    columns, depth = shape[2], ranks[0][2][0].shape[1] // 2
+    _, packed, lanes = maps[sources[0]].shape
+    tiles = columns // lanes
+    extra = tiles * 2 * depth
+    up_part = pl.ds(packed - extra, extra)
     half = prefill // 2
     n_map = len(maps)
     n_base = max(len(pieces) for _, _, pieces in bases)
@@ -346,6 +464,7 @@
                 map_refs,
                 plan_ref[SOURCE, at],
                 plan_ref[ROW, at],
+                up_part,
                 ups.at[i],
                 sems.at[i, n_base + n_rank],
             )
@@ -374,7 +493,9 @@
                 rank += rank_rows[i, k, rows].astype(F32)
             rank = jnp.dot(twice, rank.astype(BF), preferred_element_type=F32)
             rank = jnp.where(own_side, rank, 0.0).astype(BF)
-            up = ups[i].reshape(2 * depth, columns)
+            up = jnp.concatenate(
+                [ups[i, j * 2 * depth : (j + 1) * 2 * depth] for j in range(tiles)], 1
+            )
             total += jnp.dot(rank, up, preferred_element_type=F32)
             total = jnp.where(token + b * half < live, total, 0.0)
             out_rows[i, rows] = total.astype(BF).reshape(half, 2, columns)
@@ -384,7 +505,7 @@
             for copy in copies[i]:
                 copy.wait()
             pltpu.make_async_copy(
-                map_refs[0][1].at[0], ups.at[i], sems.at[i, n_base + n_rank]
+                map_refs[0][1].at[0, up_part], ups.at[i], sems.at[i, n_base + n_rank]
             ).wait()
             live = plan_ref[LENGTH, first + i]
             rows_for(i, n_base, live, 0)
@@ -424,7 +545,7 @@
             in_specs=[ANY] * (len(operands) - 1),
             out_specs=ANY,
             scratch_shapes=[
-                pltpu.VMEM((count, 2, depth, columns), BF),
+                pltpu.VMEM((count, extra, lanes), BF),
                 pltpu.VMEM((count, n_base, prefill, 2 * columns), BF),
                 pltpu.VMEM((count, n_rank, prefill, 2 * depth), BF),
                 pltpu.VMEM((count, prefill, 2, columns), BF),
@@ -470,11 +591,17 @@
             table, adapters, lengths, jnp.reshape(z, (1,)), n_z, stored
         )
 
-        downs = {0: down}
-        for hops in range(1, n_z):
+        downs = {0: pack_maps(down, up)}
+
+        def relay(hops, after):
             left, right = downs[hops - 1], downs[0 if hops == 1 else n_z + hops - 2]
+            if after:
+                left, right = hold([left, right], after)
+                downs[hops - 1], downs[n_z + hops - 2] = left, right
             downs[hops] = leftward(left)
             downs[n_z - 1 + hops] = rightward(right)
+
+        relay(1, [])
 
         def within(maps, hops):
             keys = range(hops + 1), range(n_z, n_z + hops)
@@ -486,36 +613,18 @@
 
         bases, pairs = [], []
 
-        def exchange(first, count, send, keep):
-            beyond = [core_swap(send[k]) for k in range(1, n_x)]
-            pieces = [keep, core_swap(send[0])]
+        def send_on(first, count, sends, keep, after):
+            got = [core_swap(part) for part in sends[1:]] + [core_swap(sends[0])]
+            pieces = [keep, got.pop()]
             for k in range(1, n_x):
-                pairs.append(pair_sum(keep, beyond[k - 1], k))
+                pairs.append(pair_sum(keep, got[2 * k - 2 : 2 * k], k, after))
                 pieces.append(chip_shift(pairs[-1], k))
             bases.append((first, count, pieces))
 
-        split, send, keep = split_weight(
-            plan, slots, hidden, weight, BASE_CHUNKS[0], prefill
-        )
-        exchange(0, BASE_CHUNKS[0], send, keep)
-
-        near = [downs[1], downs[n_z]]
-        middle = [downs[2], downs[n_z + 1]]
-        for chunk in range(1, len(BASE_CHUNKS)):
+        def base(chunk):
             first, count = sum(BASE_CHUNKS[:chunk]), BASE_CHUNKS[chunk]
-            after = pairs[-1:]
-            if chunk == 2:
-                after = after + near + [bases[0][2][-1]]
-            send, keep = base_products(
-                plan, hidden, split, first, count, prefill, after
-            )
-            exchange(first, count, send, keep)
-
-        ups = {(0,): up}
-        late_up = copy_after(up, middle)
-        for hops in range(1, n_z):
-            ups[hops, 2 * n_z - 1 - hops] = lax.ppermute(
-                late_up, "adapter", [(z, (z - hops) % n_z) for z in range(n_z)]
+            return (first, count) + base_products(
+                plan, hidden, split, first, count, prefill, pairs[-1:]
             )
 
         ranks = []
@@ -543,7 +652,7 @@
                 plan,
                 held,
                 ranks[first:last],
-                ups,
+                within(downs, last - 1 if by_distance else n_z - 1),
                 out,
                 first * count,
                 (last - first) * count,
@@ -551,12 +660,28 @@
                 shape,
             )
 
-        part = rank(0, pairs[-1:])
-        part = rank(1, [part])
-        part = rank(2, [part, bases[1][2][-1]])
+        split, sends, keep = split_weight(
+            plan, slots, hidden, weight, BASE_CHUNKS[0], prefill
+        )
+        send_on(0, BASE_CHUNKS[0], sends, keep, [])
+        second = base(1)
+        if n_z > 2:
+            relay(2, [second[3], bases[0][2][-1]])
+        send_on(*second, [bases[0][2][-1]])
+        third = base(2)
+        part = rank(0, [third[3]]) if by_distance else third[3]
+        part = rank(1, [part]) if by_distance else part
+        for hops in range(3, n_z):
+            relay(hops, [part])
+        send_on(*third, [part, bases[1][2][-1]])
+        if by_distance:
+            part = rank(2, [pairs[-1], ranks[0][2][-1]])
+        else:
+            for chunk in range(3):
+                part = rank(chunk, [pairs[-1]])
         out = write(None, 0, 2)
         out = write(out, 2, 3)
-        rank(3, [])
+        rank(3, [out])
         return write(out, 3, 4)
 
     return jax.shard_map(

time: 189 us -> 186 us (0.984)
  starting transfers between devices: 38 us -> 30.3 us
  Pallas kernels: 91.7 us -> 98.7 us
  other arithmetic: 7.35 us -> 2.57 us
  local copies, waits for them, and re-layouts: 2.81 us -> 7.22 us
    ppermute x3 -> x0, waiting for transfers between devices: 12.2 us -> none  [per_device(): lax.ppermute(late_up, 'adapter', [(z, (z - hops) % n_z) for z in range(n_...]
    ppermute x3 -> x0, starting transfers between devices: 9.5 us -> none  [per_device(): lax.ppermute(late_up, 'adapter', [(z, (z - hops) % n_z) for z in range(n_...]
    ppermute x3, waiting for transfers between devices: 0.03 us -> 7.01 us  [leftward(): return lax.ppermute(a, 'adapter', [(z, z - hops) for z in range(hops, n_z)])]
    ppermute x10 -> x13, waiting for transfers between devices: 3.02 us -> 8.74 us  [core_swap(): return lax.ppermute(a, 'tensor', [(t, t ^ 1) for t in range(n_t)])]
    pallas_call x6 -> x8, Pallas kernels: 38.6 us -> 43.7 us  [the longest x2 33.4 us: base_products(): pl.pallas_call(body, out_shape=(*[jax.ShapeDtypeStruct((n * prefill, widt...]
    convert_element_type x4, other arithmetic: 6.83 us -> 2.08 us  [rank(): pair = (part.astype(F32) + core_swap(part).astype(F32)).astype(BF)]
    unnamed x18 -> x36, local copies, waits for them, and re-layouts: 2.81 us -> 7.22 us
  transfers between devices with their start and end apart: 26 -> 26, of which waited for: 8 -> 10; matrix products, arithmetic and copies ran while one was open for 4% -> 1% of each run, Pallas kernels for 46% -> 47%
where the time goes in v4:
time: 186 us; the launch traced here: 185 us
  Pallas kernels  98.7 us (53%)
  waiting for transfers between devices  45.9 us (25%)
  starting transfers between devices  30.3 us (16%)
  local copies, waits for them, and re-layouts  7.22 us (4%)
  other arithmetic  2.57 us (1%)
    pallas_call x2, Pallas kernels, base_products(): pl.pallas_call(body, out_shape=(*[jax.ShapeDtypeStruct((n * prefill, widt...  33.4 us
    ppermute x7, waiting for transfers between devices, chip_shift(): lax.ppermute(a, 'tensor', [(2 * x + c, 2 * ((x + k) % n_x) + c) for x in...  28.9 us
    pallas_call x3, Pallas kernels, finish(): pl.pallas_call(body, out_shape=jax.ShapeDtypeStruct(shape, BF), grid_spec...  19.8 us
    pallas_call x4, Pallas kernels, rank_products(): pl.pallas_call(body, out_shape=jax.ShapeDtypeStruct((count * prefill, ran...  17.4 us
    pallas_call x1, Pallas kernels, split_weight(): pl.pallas_call(body, out_shape=(jax.ShapeDtypeStruct((n_t, features, 2 *...  16.1 us
    ppermute x3, starting transfers between devices, rightward(): return lax.ppermute(a, 'adapter', [(z - hops, z) for z in range(hops, n_z)])  15.3 us
    ppermute x13, waiting for transfers between devices, core_swap(): return lax.ppermute(a, 'tensor', [(t, t ^ 1) for t in range(n_t)])  8.74 us
    ppermute x7, starting transfers between devices, chip_shift(): lax.ppermute(a, 'tensor', [(2 * x + c, 2 * ((x + k) % n_x) + c) for x in...  8.48 us
  transfers between devices with their start and end apart: 26, of which 10 were waited for; matrix products, arithmetic and copies ran while one was open for 1% of the time, Pallas kernels for 47%

profile of v4, /device:TPU:0, one launch (start us, length us, event | category | flops | bytes accessed | tf_op | source)
XLA Modules:
  0.0 185.3 jit_solution(16337348670558313283)
XLA Ops:
  0.0 2.7 %pack_maps.1.rest_0_.rest_10_.rest_8_.rest_5_ = bf16[3,2304,128]{2,1,0:T(8,128)(2,1)} custom-call(bf16[3,2048,128]{2,1,0:T(8,128)(2,1)} %down_ref.1, bf16[3,2,64,256]{3,2,1,0:T(8,128)(2,1)} %up_ref.1), custom_call_target="tpu_custom_call" | custom-call | bytes 31457 | tf_op jit(solution)/shard_map/pack_maps/pallas_call | solution.py:59
  2.7 1.3 collective-permute-start.8
  4.0 5.7 %collective-permute-start.9 = (bf16[3,2304,128]{2,1,0:T(8,128)(2,1)}, bf16[3,2304,128]{2,1,0:T(8,128)(2,1)S(1)}, u32[]{:S(2)}, u32[]{:S(2)}) collective-permute-start(bf16[3,2304,128]{2,1,0:T(8,128)(2,1)} %pack_maps.1.rest_0_.rest_10_.rest_8_.rest_5_), channel_id=1, source_target_pairs={{0,4},{4,8},{8,12},{1,5},{5,9},{9,13},{2,6},{6,10},{10,14},{3,7},{... | collective-permute-start | bytes 5308424 | tf_op jit(solution)/shard_map/ppermute | solution.py:581
  9.7 1.6 plan_requests.1.plan_ref
  11.7 16.1 %split_weight.1 = (bf16[4,2048,512]{2,1,0:T(8,128)(2,1)}, bf16[768,512]{1,0:T(8,128)(2,1)}, bf16[256,512]{1,0:T(8,128)(2,1)}, bf16[512,512]{1,0:T(8,128)(2,1)}, bf16[2,768,512]{2,1,0:T(8,128)(2,1)}) custom-call(s32[8,128]{1,0:T(8,128)} %plan_requests.1.plan_ref, s32[4]{0:T(128)} %compare_select_fusion.2.slot_ref, bf16[3072,2048]{1,0:T(8,128)(2,1)} %x_ref.11, ...), custom_call_target="tpu_custom_call" | custom-call | flops 64424508 | bytes 167772 | tf_op jit(solution)/shard_map/split_weight/pallas_call | solution.py:172
  28.4 2.0 %collective-permute-done.rest_0_ = bf16[256,512]{1,0:T(8,128)(2,1)S(1)} collective-permute-done((bf16[256,512]{1,0:T(8,128)(2,1)}, bf16[256,512]{1,0:T(8,128)(2,1)S(1)}, u32[]{:S(2)}, u32[]{:S(2)}) %collective-permute-start) | collective-permute-done | bytes 262176 | tf_op jit(solution)/shard_map/ppermute | solution.py:568
  31.9 2.4 %pair_sum.3.rest_4_ = bf16[768,512]{1,0:T(8,128)(2,1)} custom-call(bf16[2,768,512]{2,1,0:T(8,128)(2,1)} %get-tuple-element.23.a_ref.rest_0_, bf16[256,512]{1,0:T(8,128)(2,1)} %copy-done.15, bf16[512,512]{1,0:T(8,128)(2,1)} %copy-done.14), custom_call_target="tpu_custom_call" | custom-call | flops 3932 | bytes 23592 | tf_op jit(solution)/shard_map/pair_sum/pallas_call | solution.py:312
  34.2 2.0 %collective-permute-start.4 = (bf16[768,512]{1,0:T(8,128)(2,1)}, bf16[768,512]{1,0:T(8,128)(2,1)}, u32[]{:S(2)}, u32[]{:S(2)}) collective-permute-start(bf16[768,512]{1,0:T(8,128)(2,1)} %pair_sum.3.rest_4_), channel_id=1, source_target_pairs={{0,2},{1,3},{2,0},{3,1},{4,6},{5,7},{6,4},{7,5},{8,10},{9,11},{10,... | collective-permute-start | bytes 2359304 | tf_op jit(solution)/shard_map/ppermute | solution.py:571
  36.2 18.5 %base_products.2 = (bf16[1280,512]{1,0:T(8,128)(2,1)}, bf16[512,512]{1,0:T(8,128)(2,1)}, bf16[768,512]{1,0:T(8,128)(2,1)}, bf16[2,1280,512]{2,1,0:T(8,128)(2,1)}) custom-call(s32[8,128]{1,0:T(8,128)} %plan_requests.1.plan_ref, bf16[3072,2048]{1,0:T(8,128)(2,1)} %x_ref.11, bf16[4,2048,512]{2,1,0:T(8,128)(2,1)} %get-tuple-element.22.rest_0_.rest_1_.rest_2_.rest_3_, ...), custom_call_target="tpu_custom_call" | custom-call | flops 107374184 | bytes 83886 | tf_op jit(solution)/shard_map/base_products/pallas_call | solution.py:249
  56.5 1.3 collective-permute-start.12
  57.8 4.7 %collective-permute-start.13 = (bf16[3,2304,128]{2,1,0:T(8,128)(2,1)}, bf16[3,2304,128]{2,1,0:T(8,128)(2,1)S(1)}, u32[]{:S(2)}, u32[]{:S(2)}) collective-permute-start(bf16[3,2304,128]{2,1,0:T(8,128)(2,1)} %get-tuple-element.34.rest_2_.rest_3_.rest_12_.rest_11_.rest_4_.rest_9_), channel_id=1, source_target_pairs={{0,4},{4,8},{8,12},{1,5},{5,9},{9,13},{2,6},{6,10},{10,14},{3,7},{... | collective-permute-start | bytes 5308424 | tf_op jit(solution)/shard_map/ppermute | solution.py:581
  63.1 2.7 %collective-permute-done.2.rest_0_ = bf16[512,512]{1,0:T(8,128)(2,1)S(1)} collective-permute-done((bf16[512,512]{1,0:T(8,128)(2,1)}, bf16[512,512]{1,0:T(8,128)(2,1)S(1)}, u32[]{:S(2)}, u32[]{:S(2)}) %collective-permute-start.2) | collective-permute-done | bytes 524320 | tf_op jit(solution)/shard_map/ppermute | solution.py:568
  66.6 2.8 %pair_sum.4.rest_4_ = bf16[1280,512]{1,0:T(8,128)(2,1)} custom-call(bf16[2,1280,512]{2,1,0:T(8,128)(2,1)} %get-tuple-element.26.a_ref.refs_2_.rest_3_.rest_0_, bf16[512,512]{1,0:T(8,128)(2,1)} %copy-done.13, bf16[768,512]{1,0:T(8,128)(2,1)} %collective-permute-done.3.rest_1_, bf16[768,512]{1,0:T(8,128)(2,1)} %collective-permute-done.4.rest_2_.refs_3_), custom_call_target="tpu_custom_call" | custom-call | flops 6553 | bytes 39321 | tf_op jit(solution)/shard_map/pair_sum/pallas_call | solution.py:312
  69.4 1.4 collective-permute-start.10
  70.9 14.9 %base_products.3 = (bf16[1024,512]{1,0:T(8,128)(2,1)}, bf16[512,512]{1,0:T(8,128)(2,1)}, bf16[512,512]{1,0:T(8,128)(2,1)}, bf16[2,1024,512]{2,1,0:T(8,128)(2,1)}) custom-call(s32[8,128]{1,0:T(8,128)} %plan_requests.1.plan_ref, bf16[3072,2048]{1,0:T(8,128)(2,1)} %x_ref.11, bf16[4,2048,512]{2,1,0:T(8,128)(2,1)} %get-tuple-element.22.rest_0_.rest_1_.rest_2_.rest_3_, ...), custom_call_target="tpu_custom_call" | custom-call | flops 85899344 | bytes 83886 | tf_op jit(solution)/shard_map/base_products/pallas_call | solution.py:249
  85.8 4.3 %rank_products.4.rest_3_ = bf16[768,128]{1,0:T(8,128)(2,1)} custom-call(s32[8,128]{1,0:T(8,128)} %plan_requests.1.plan_ref, bf16[3072,2048]{1,0:T(8,128)(2,1)} %x_ref.11, bf16[3,2304,128]{2,1,0:T(8,128)(2,1)} %pack_maps.1.rest_0_.rest_10_.rest_8_.rest_5_, bf16[2,1024,512]{2,1,0:T(8,128)(2,1)} %get-tuple-element.29.rest_1_.a_ref.rest_3_.rest_0_), custom_call_target="tpu_custom_call" | custom-call | flops 4026531 | bytes 47185 | tf_op jit(solution)/shard_map/rank_products/pallas_call | solution.py:402
  92.0 7.0 %collective-permute-done.12.refs_0_ = bf16[3,2304,128]{2,1,0:T(8,128)(2,1)S(1)} collective-permute-done((bf16[3,2304,128]{2,1,0:T(8,128)(2,1)}, bf16[3,2304,128]{2,1,0:T(8,128)(2,1)S(1)}, u32[]{:S(2)}, u32[]{:S(2)}) %collective-permute-start.12) | collective-permute-done | bytes 1769504 | tf_op jit(solution)/shard_map/ppermute | solution.py:578
  99.0 1.3 collective-permute-done.13.refs_1_
  100.3 4.3 %rank_products.5.rest_2_.refs_2_ = bf16[768,128]{1,0:T(8,128)(2,1)} custom-call(s32[8,128]{1,0:T(8,128)} %plan_requests.1.plan_ref, bf16[3072,2048]{1,0:T(8,128)(2,1)} %x_ref.11, bf16[3,2304,128]{2,1,0:T(8,128)(2,1)} %pack_maps.1.rest_0_.rest_10_.rest_8_.rest_5_, bf16[3,2304,128]{2,1,0:T(8,128)(2,1)} %get-tuple-element.33.rest_1_.rest_11_.rest_9_.rest_6_, ...), custom_call_target="tpu_custom_call" | custom-call | flops 4026531 | bytes 47185 | tf_op jit(solution)/shard_map/rank_products/pallas_call | solution.py:402
  104.6 1.4 collective-permute-start.14
  106.1 5.0 %collective-permute-start.15 = (bf16[3,2304,128]{2,1,0:T(8,128)(2,1)}, bf16[3,2304,128]{2,1,0:T(8,128)(2,1)S(1)}, u32[]{:S(2)}, u32[]{:S(2)}) collective-permute-start(bf16[3,2304,128]{2,1,0:T(8,128)(2,1)} %get-tuple-element.36.rest_4_.rest_12_.rest_5_.rest_10_), channel_id=1, source_target_pairs={{0,4},{4,8},{8,12},{1,5},{5,9},{9,13},{2,6},{6,10},{10,14},{3,7},{... | collective-permute-start | bytes 5308424 | tf_op jit(solution)/shard_map/ppermute | solution.py:581
  112.1 2.5 %pair_sum.5.rest_5_ = bf16[1024,512]{1,0:T(8,128)(2,1)} custom-call(bf16[2,1024,512]{2,1,0:T(8,128)(2,1)} %get-tuple-element.29.rest_1_.a_ref.rest_3_.rest_0_, bf16[512,512]{1,0:T(8,128)(2,1)} %collective-permute-done.6.rest_0_, bf16[512,512]{1,0:T(8,128)(2,1)} %collective-permute-done.7.rest_1_, bf16[768,128]{1,0:T(8,128)(2,1)} %rank_products.5.rest_2_.refs_2_, ...), custom_call_target="tpu_custom_call" | custom-call | flops 5242 | bytes 31457 | tf_op jit(solution)/shard_map/pair_sum/pallas_call | solution.py:312
  114.7 3.6 %collective-permute-done.18.rest_6_.rest_7_ = bf16[768,128]{1,0:T(8,128)(2,1)S(1)} collective-permute-done((bf16[768,128]{1,0:T(8,128)(2,1)S(1)}, bf16[768,128]{1,0:T(8,128)(2,1)S(1)}, u32[]{:S(2)}, u32[]{:S(2)}) %collective-permute-start.18) | collective-permute-done | bytes 196640 | tf_op jit(solution)/shard_map/ppermute | solution.py:571
  119.1 4.4 %rank_products.6 = bf16[768,128]{1,0:T(8,128)(2,1)} custom-call(s32[8,128]{1,0:T(8,128)} %plan_requests.1.plan_ref, bf16[3072,2048]{1,0:T(8,128)(2,1)} %x_ref.11, bf16[3,2304,128]{2,1,0:T(8,128)(2,1)} %pack_maps.1.rest_0_.rest_10_.rest_8_.rest_5_, bf16[3,2304,128]{2,1,0:T(8,128)(2,1)} %get-tuple-element.33.rest_1_.rest_11_.rest_9_.rest_6_, ...), custom_call_target="tpu_custom_call" | custom-call | flops 4026531 | bytes 47185 | tf_op jit(solution)/shard_map/rank_products/pallas_call | solution.py:402
  127.6 19.6 %collective-permute-done.23.rest_9_ = bf16[768,128]{1,0:T(8,128)(2,1)S(1)} collective-permute-done((bf16[768,128]{1,0:T(8,128)(2,1)S(1)}, bf16[768,128]{1,0:T(8,128)(2,1)S(1)}, u32[]{:S(2)}, u32[]{:S(2)}) %collective-permute-start.23) | collective-permute-done | bytes 196640 | tf_op jit(solution)/shard_map/ppermute | solution.py:571
  148.0 8.5 %finish.3.rest_13_ = bf16[3072,2,256]{2,1,0:T(2,128)(2,1)} custom-call(s32[8,128]{1,0:T(8,128)} %plan_requests.1.plan_ref, bf16[2,768,512]{2,1,0:T(8,128)(2,1)} %get-tuple-element.23.a_ref.rest_0_, bf16[768,512]{1,0:T(8,128)(2,1)} %collective-permute-done.21.rest_1_, bf16[768,512]{1,0:T(8,128)(2,1)} %collective-permute-done.4.rest_2_.refs_3_, ...), custom_call_target="tpu_custom_call" | custom-call | flops 24159192 | bytes 78643 | tf_op jit(solution)/shard_map/finish/pallas_call | solution.py:539
  156.6 6.0 %finish.4.rest_7_.rest_12_ = bf16[3072,2,256]{2,1,0:T(2,128)(2,1)} custom-call(s32[8,128]{1,0:T(8,128)} %plan_requests.1.plan_ref, bf16[2,1280,512]{2,1,0:T(8,128)(2,1)} %get-tuple-element.26.a_ref.refs_2_.rest_3_.rest_0_, bf16[1280,512]{1,0:T(8,128)(2,1)} %collective-permute-done.16.rest_4_.rest_1_, ...), custom_call_target="tpu_custom_call", output_to_operand_aliasing={{}: (14, {})} | custom-call | flops 12079595 | bytes 39321 | tf_op jit(solution)/shard_map/finish/pallas_call | solution.py:539
  165.0 4.3 %rank_products.7 = bf16[768,128]{1,0:T(8,128)(2,1)} custom-call(s32[8,128]{1,0:T(8,128)} %plan_requests.1.plan_ref, bf16[3072,2048]{1,0:T(8,128)(2,1)} %x_ref.11, bf16[3,2304,128]{2,1,0:T(8,128)(2,1)} %pack_maps.1.rest_0_.rest_10_.rest_8_.rest_5_, bf16[3,2304,128]{2,1,0:T(8,128)(2,1)} %get-tuple-element.33.rest_1_.rest_11_.rest_9_.rest_6_, ...), custom_call_target="tpu_custom_call" | custom-call | flops 4026531 | bytes 47185 | tf_op jit(solution)/shard_map/rank_products/pallas_call | solution.py:402
  169.4 1.6 collective-permute-done.24
  172.0 1.3 collective-permute-start.25
  173.3 5.7 %collective-permute-done.25.rest_4_ = bf16[768,128]{1,0:T(8,128)(2,1)S(1)} collective-permute-done((bf16[768,128]{1,0:T(8,128)(2,1)S(1)}, bf16[768,128]{1,0:T(8,128)(2,1)S(1)}, u32[]{:S(2)}, u32[]{:S(2)}) %collective-permute-start.25) | collective-permute-done | bytes 196640 | tf_op jit(solution)/shard_map/ppermute | solution.py:571
  179.7 5.4 %finish.5 = bf16[3072,2,256]{2,1,0:T(2,128)(2,1)} custom-call(s32[8,128]{1,0:T(8,128)} %plan_requests.1.plan_ref, bf16[2,1024,512]{2,1,0:T(8,128)(2,1)} %get-tuple-element.29.rest_1_.a_ref.rest_3_.rest_0_, bf16[1024,512]{1,0:T(8,128)(2,1)} %collective-permute-done.5.rest_4_.rest_1_, ...), custom_call_target="tpu_custom_call", output_to_operand_aliasing={{}: (13, {})} | custom-call | flops 12079595 | bytes 39321 | tf_op jit(solution)/shard_map/finish/pallas_call | solution.py:539
  (78 shorter events, 18.5 us)
Async XLA Ops:
  2.7 52.1 %collective-permute-start.8 = (bf16[3,2304,128]{2,1,0:T(8,128)(2,1)}, bf16[3,2304,128]{2,1,0:T(8,128)(2,1)S(1)}, u32[]{:S(2)}, u32[]{:S(2)}) collective-permute-start(bf16[3,2304,128]{2,1,0:T(8,128)(2,1)} %pack_maps.1.rest_0_.rest_10_.rest_8_.rest_5_), channel_id=1, source_target_pairs={{4,0},{8,4},{12,8},{5,1},{9,5},{13,9},{6,2},{10,6},{14,10},{7,3},{... | collective-permute-start | bytes 5308424 | tf_op jit(solution)/shard_map/ppermute | solution.py:578
  4.0 50.8 %collective-permute-start.9 = (bf16[3,2304,128]{2,1,0:T(8,128)(2,1)}, bf16[3,2304,128]{2,1,0:T(8,128)(2,1)S(1)}, u32[]{:S(2)}, u32[]{:S(2)}) collective-permute-start(bf16[3,2304,128]{2,1,0:T(8,128)(2,1)} %pack_maps.1.rest_0_.rest_10_.rest_8_.rest_5_), channel_id=1, source_target_pairs={{0,4},{4,8},{8,12},{1,5},{5,9},{9,13},{2,6},{6,10},{10,14},{3,7},{... | collective-permute-start | bytes 5308424 | tf_op jit(solution)/shard_map/ppermute | solution.py:581
  27.9 2.5 %collective-permute-start.1 = (bf16[512,512]{1,0:T(8,128)(2,1)}, bf16[512,512]{1,0:T(8,128)(2,1)S(1)}, u32[]{:S(2)}, u32[]{:S(2)}) collective-permute-start(bf16[512,512]{1,0:T(8,128)(2,1)} %get-tuple-element.25), channel_id=1, source_target_pairs={{0,1},{1,0},{2,3},{3,2},{4,5},{5,4},{6,7},{7,6},{8,9},{9,8},{10,11... | collective-permute-start | bytes 1572872 | tf_op jit(solution)/shard_map/ppermute | solution.py:568
  27.9 2.5 %collective-permute-start = (bf16[256,512]{1,0:T(8,128)(2,1)}, bf16[256,512]{1,0:T(8,128)(2,1)S(1)}, u32[]{:S(2)}, u32[]{:S(2)}) collective-permute-start(bf16[256,512]{1,0:T(8,128)(2,1)} %get-tuple-element.24), channel_id=1, source_target_pairs={{0,1},{1,0},{2,3},{3,2},{4,5},{5,4},{6,7},{7,6},{8,9},{9,8},{10,11... | collective-permute-start | bytes 786440 | tf_op jit(solution)/shard_map/ppermute | solution.py:568
  34.2 20.5 %collective-permute-start.4 = (bf16[768,512]{1,0:T(8,128)(2,1)}, bf16[768,512]{1,0:T(8,128)(2,1)}, u32[]{:S(2)}, u32[]{:S(2)}) collective-permute-start(bf16[768,512]{1,0:T(8,128)(2,1)} %pair_sum.3.rest_4_), channel_id=1, source_target_pairs={{0,2},{1,3},{2,0},{3,1},{4,6},{5,7},{6,4},{7,5},{8,10},{9,11},{10,... | collective-permute-start | bytes 2359304 | tf_op jit(solution)/shard_map/ppermute | solution.py:571
  56.5 42.5 %collective-permute-start.12 = (bf16[3,2304,128]{2,1,0:T(8,128)(2,1)}, bf16[3,2304,128]{2,1,0:T(8,128)(2,1)S(1)}, u32[]{:S(2)}, u32[]{:S(2)}) collective-permute-start(bf16[3,2304,128]{2,1,0:T(8,128)(2,1)} %get-tuple-element.33.rest_1_.rest_11_.rest_9_.rest_6_), channel_id=1, source_target_pairs={{4,0},{8,4},{12,8},{5,1},{9,5},{13,9},{6,2},{10,6},{14,10},{7,3},{... | collective-permute-start | bytes 5308424 | tf_op jit(solution)/shard_map/ppermute | solution.py:578
  57.8 42.5 %collective-permute-start.13 = (bf16[3,2304,128]{2,1,0:T(8,128)(2,1)}, bf16[3,2304,128]{2,1,0:T(8,128)(2,1)S(1)}, u32[]{:S(2)}, u32[]{:S(2)}) collective-permute-start(bf16[3,2304,128]{2,1,0:T(8,128)(2,1)} %get-tuple-element.34.rest_2_.rest_3_.rest_12_.rest_11_.rest_4_.rest_9_), channel_id=1, source_target_pairs={{0,4},{4,8},{8,12},{1,5},{5,9},{9,13},{2,6},{6,10},{10,14},{3,7},{... | collective-permute-start | bytes 5308424 | tf_op jit(solution)/shard_map/ppermute | solution.py:581
  62.5 3.3 %collective-permute-start.3 = (bf16[768,512]{1,0:T(8,128)(2,1)}, bf16[768,512]{1,0:T(8,128)(2,1)}, u32[]{:S(2)}, u32[]{:S(2)}) collective-permute-start(bf16[768,512]{1,0:T(8,128)(2,1)} %get-tuple-element.28), channel_id=1, source_target_pairs={{0,1},{1,0},{2,3},{3,2},{4,5},{5,4},{6,7},{7,6},{8,9},{9,8},{10,11... | collective-permute-start | bytes 2359304 | tf_op jit(solution)/shard_map/ppermute | solution.py:568
  62.6 3.2 %collective-permute-start.2 = (bf16[512,512]{1,0:T(8,128)(2,1)}, bf16[512,512]{1,0:T(8,128)(2,1)S(1)}, u32[]{:S(2)}, u32[]{:S(2)}) collective-permute-start(bf16[512,512]{1,0:T(8,128)(2,1)} %get-tuple-element.27), channel_id=1, source_target_pairs={{0,1},{1,0},{2,3},{3,2},{4,5},{5,4},{6,7},{7,6},{8,9},{9,8},{10,11... | collective-permute-start | bytes 1572872 | tf_op jit(solution)/shard_map/ppermute | solution.py:568
  69.4 41.7 %collective-permute-start.10 = (bf16[1280,512]{1,0:T(8,128)(2,1)}, bf16[1280,512]{1,0:T(8,128)(2,1)}, u32[]{:S(2)}, u32[]{:S(2)}) collective-permute-start(bf16[1280,512]{1,0:T(8,128)(2,1)} %pair_sum.4.rest_4_), channel_id=1, source_target_pairs={{0,2},{1,3},{2,0},{3,1},{4,6},{5,7},{6,4},{7,5},{8,10},{9,11},{10,... | collective-permute-start | bytes 3932168 | tf_op jit(solution)/shard_map/ppermute | solution.py:571
  90.1 1.7 collective-permute-start.17
  90.2 14.4 %collective-permute-start.6 = (bf16[512,512]{1,0:T(8,128)(2,1)}, bf16[512,512]{1,0:T(8,128)(2,1)}, u32[]{:S(2)}, u32[]{:S(2)}) collective-permute-start(bf16[512,512]{1,0:T(8,128)(2,1)} %get-tuple-element.31), channel_id=1, source_target_pairs={{0,1},{1,0},{2,3},{3,2},{4,5},{5,4},{6,7},{7,6},{8,9},{9,8},{10,11... | collective-permute-start | bytes 1572872 | tf_op jit(solution)/shard_map/ppermute | solution.py:568
  91.8 14.2 %collective-permute-start.7 = (bf16[512,512]{1,0:T(8,128)(2,1)}, bf16[512,512]{1,0:T(8,128)(2,1)}, u32[]{:S(2)}, u32[]{:S(2)}) collective-permute-start(bf16[512,512]{1,0:T(8,128)(2,1)} %get-tuple-element.32), channel_id=1, source_target_pairs={{0,1},{1,0},{2,3},{3,2},{4,5},{5,4},{6,7},{7,6},{8,9},{9,8},{10,11... | collective-permute-start | bytes 1572872 | tf_op jit(solution)/shard_map/ppermute | solution.py:568
  99.0 5.6 %copy-start.2 = (bf16[3,2304,128]{2,1,0:T(8,128)(2,1)}, bf16[3,2304,128]{2,1,0:T(8,128)(2,1)S(1)}, u32[]{:S(2)}) copy-start(bf16[3,2304,128]{2,1,0:T(8,128)(2,1)S(1)} %collective-permute-done.12.refs_0_) | copy-start | bytes 5308420
  99.0 20.1 %collective-permute-start.16 = (bf16[1280,512]{1,0:T(8,128)(2,1)}, bf16[1280,512]{1,0:T(8,128)(2,1)}, u32[]{:S(2)}, u32[]{:S(2)}) collective-permute-start(bf16[1280,512]{1,0:T(8,128)(2,1)} %get-tuple-element.37), channel_id=1, source_target_pairs={{0,1},{1,0},{2,3},{3,2},{4,5},{5,4},{6,7},{7,6},{8,9},{9,8},{10,11... | collective-permute-start | bytes 3932168 | tf_op jit(solution)/shard_map/ppermute | solution.py:568
  100.3 14.3 %collective-permute-start.21 = (bf16[768,512]{1,0:T(8,128)(2,1)}, bf16[768,512]{1,0:T(8,128)(2,1)}, u32[]{:S(2)}, u32[]{:S(2)}) collective-permute-start(bf16[768,512]{1,0:T(8,128)(2,1)} %get-tuple-element.38), channel_id=1, source_target_pairs={{0,1},{1,0},{2,3},{3,2},{4,5},{5,4},{6,7},{7,6},{8,9},{9,8},{10,11... | collective-permute-start | bytes 2359304 | tf_op jit(solution)/shard_map/ppermute | solution.py:568
  104.6 6.5 %copy-start.7 = (bf16[768,128]{1,0:T(8,128)(2,1)S(1)}, bf16[768,128]{1,0:T(8,128)(2,1)}, u32[]{:S(2)}) copy-start(bf16[768,128]{1,0:T(8,128)(2,1)} %rank_products.4.rest_3_) | copy-start | bytes 589828
  104.6 57.9 %collective-permute-start.14 = (bf16[3,2304,128]{2,1,0:T(8,128)(2,1)}, bf16[3,2304,128]{2,1,0:T(8,128)(2,1)S(1)}, u32[]{:S(2)}, u32[]{:S(2)}) collective-permute-start(bf16[3,2304,128]{2,1,0:T(8,128)(2,1)} %get-tuple-element.35.rest_2_.rest_10_.rest_7_), channel_id=1, source_target_pairs={{4,0},{8,4},{12,8},{5,1},{9,5},{13,9},{6,2},{10,6},{14,10},{7,3},{... | collective-permute-start | bytes 5308424 | tf_op jit(solution)/shard_map/ppermute | solution.py:578
  106.1 56.5 %collective-permute-start.15 = (bf16[3,2304,128]{2,1,0:T(8,128)(2,1)}, bf16[3,2304,128]{2,1,0:T(8,128)(2,1)S(1)}, u32[]{:S(2)}, u32[]{:S(2)}) collective-permute-start(bf16[3,2304,128]{2,1,0:T(8,128)(2,1)} %get-tuple-element.36.rest_4_.rest_12_.rest_5_.rest_10_), channel_id=1, source_target_pairs={{0,4},{4,8},{8,12},{1,5},{5,9},{9,13},{2,6},{6,10},{10,14},{3,7},{... | collective-permute-start | bytes 5308424 | tf_op jit(solution)/shard_map/ppermute | solution.py:581
  111.2 8.0 %copy-start.6 = (bf16[768,128]{1,0:T(8,128)(2,1)S(1)}, bf16[768,128]{1,0:T(8,128)(2,1)}, u32[]{:S(2)}) copy-start(bf16[768,128]{1,0:T(8,128)(2,1)} %rank_products.5.rest_2_.refs_2_) | copy-start | bytes 589828
  111.2 7.1 %collective-permute-start.18 = (bf16[768,128]{1,0:T(8,128)(2,1)S(1)}, bf16[768,128]{1,0:T(8,128)(2,1)S(1)}, u32[]{:S(2)}, u32[]{:S(2)}) collective-permute-start(bf16[768,128]{1,0:T(8,128)(2,1)S(1)} %add_convert_fusion.3.rest_6_), channel_id=1, source_target_pairs={{0,2},{1,3},{2,0},{3,1},{4,6},{5,7},{6,4},{7,5},{8,10},{9,11},{10,... | collective-permute-start | bytes 589832 | tf_op jit(solution)/shard_map/ppermute | solution.py:571
  114.6 41.9 %collective-permute-start.5 = (bf16[1024,512]{1,0:T(8,128)(2,1)}, bf16[1024,512]{1,0:T(8,128)(2,1)}, u32[]{:S(2)}, u32[]{:S(2)}) collective-permute-start(bf16[1024,512]{1,0:T(8,128)(2,1)} %get-tuple-element.30), channel_id=1, source_target_pairs={{0,1},{1,0},{2,3},{3,2},{4,5},{5,4},{6,7},{7,6},{8,9},{9,8},{10,11... | collective-permute-start | bytes 3145736 | tf_op jit(solution)/shard_map/ppermute | solution.py:568
  118.3 38.2 %collective-permute-start.11 = (bf16[1024,512]{1,0:T(8,128)(2,1)}, bf16[1024,512]{1,0:T(8,128)(2,1)}, u32[]{:S(2)}, u32[]{:S(2)}) collective-permute-start(bf16[1024,512]{1,0:T(8,128)(2,1)} %pair_sum.5.rest_5_), channel_id=1, source_target_pairs={{0,2},{1,3},{2,0},{3,1},{4,6},{5,7},{6,4},{7,5},{8,10},{9,11},{10,... | collective-permute-start | bytes 3145736 | tf_op jit(solution)/shard_map/ppermute | solution.py:571
  119.1 4.4 %collective-permute-start.22 = (bf16[768,128]{1,0:T(8,128)(2,1)S(1)}, bf16[768,128]{1,0:T(8,128)(2,1)S(1)}, u32[]{:S(2)}, u32[]{:S(2)}) collective-permute-start(bf16[768,128]{1,0:T(8,128)(2,1)S(1)} %copy-done.6), channel_id=1, source_target_pairs={{0,1},{1,0},{2,3},{3,2},{4,5},{5,4},{6,7},{7,6},{8,9},{9,8},{10,11... | collective-permute-start | bytes 589832 | tf_op jit(solution)/shard_map/ppermute | solution.py:568
  123.6 1.8 collective-permute-start.19
  124.2 23.8 %copy-start.10 = (bf16[768,128]{1,0:T(8,128)(2,1)}, bf16[768,128]{1,0:T(8,128)(2,1)S(1)}, u32[]{:S(2)}) copy-start(bf16[768,128]{1,0:T(8,128)(2,1)S(1)} %add_convert_fusion.1.rest_8_) | copy-start | bytes 589828
  125.4 21.8 %collective-permute-start.23 = (bf16[768,128]{1,0:T(8,128)(2,1)S(1)}, bf16[768,128]{1,0:T(8,128)(2,1)S(1)}, u32[]{:S(2)}, u32[]{:S(2)}) collective-permute-start(bf16[768,128]{1,0:T(8,128)(2,1)S(1)} %add_convert_fusion.1.rest_8_), channel_id=1, source_target_pairs={{0,2},{1,3},{2,0},{3,1},{4,6},{5,7},{6,4},{7,5},{8,10},{9,11},{10,... | collective-permute-start | bytes 589832 | tf_op jit(solution)/shard_map/ppermute | solution.py:571
  127.6 28.9 %copy-start.12 = (bf16[768,128]{1,0:T(8,128)(2,1)}, bf16[768,128]{1,0:T(8,128)(2,1)S(1)}, u32[]{:S(2)}) copy-start(bf16[768,128]{1,0:T(8,128)(2,1)S(1)} %add_convert_fusion.2.rest_6_) | copy-start | bytes 589828
  147.2 9.4 %collective-permute-start.20 = (bf16[768,128]{1,0:T(8,128)(2,1)S(1)}, bf16[768,128]{1,0:T(8,128)(2,1)}, u32[]{:S(2)}, u32[]{:S(2)}) collective-permute-start(bf16[768,128]{1,0:T(8,128)(2,1)S(1)} %add_convert_fusion.2.rest_6_), channel_id=1, source_target_pairs={{0,2},{1,3},{2,0},{3,1},{4,6},{5,7},{6,4},{7,5},{8,10},{9,11},{10,... | collective-permute-start | bytes 589832 | tf_op jit(solution)/shard_map/ppermute | solution.py:571
  169.3 1.7 collective-permute-start.24
  172.0 7.0 %copy-start.11 = (bf16[768,128]{1,0:T(8,128)(2,1)}, bf16[768,128]{1,0:T(8,128)(2,1)S(1)}, u32[]{:S(2)}) copy-start(bf16[768,128]{1,0:T(8,128)(2,1)S(1)} %add_convert_fusion.rest_3_) | copy-start | bytes 589828
  172.0 7.0 %collective-permute-start.25 = (bf16[768,128]{1,0:T(8,128)(2,1)S(1)}, bf16[768,128]{1,0:T(8,128)(2,1)S(1)}, u32[]{:S(2)}, u32[]{:S(2)}) collective-permute-start(bf16[768,128]{1,0:T(8,128)(2,1)S(1)} %add_convert_fusion.rest_3_), channel_id=1, source_target_pairs={{0,2},{1,3},{2,0},{3,1},{4,6},{5,7},{6,4},{7,5},{8,10},{9,11},{10,... | collective-permute-start | bytes 589832 | tf_op jit(solution)/shard_map/ppermute | solution.py:571
  (12 other events, 17.9 us)

commit v5 on v4

--- a/solution.py
+++ b/solution.py
@@ -7,9 +7,16 @@
 
 BF = jnp.bfloat16
 F32 = jnp.float32
-BASE_CHUNKS = (3, 5, 4)
+BASE_CHUNKS = (3, 3, 3, 3)
 RANK_CHUNKS = 4
 SMEM = pltpu.SMEM
+PIECE = 2
+
+
+def pieces_of(count):
+    return [(at, min(PIECE, count - at)) for at in range(0, count, PIECE)]
+
+
 ANY = pl.BlockSpec(memory_space=pl.ANY)
 
 
@@ -65,7 +72,7 @@
             pltpu.VMEM((stored, tiles * part, lanes), BF),
             pltpu.SemaphoreType.DMA((2, stored)),
         ],
-        compiler_params=params(),
+        compiler_params=params(60),
         cost_estimate=cost(0, 4 * down.size),
         name="pack_maps",
     )(down, up)
@@ -131,6 +138,7 @@
     def body(plan_ref, slot_ref, *rest):
         x_refs, (w_ref, o_ref, *send_refs, keep_ref, total) = rest[:count], rest[count:]
         step = pl.program_id(0)
+        above = pl.multiple_of(step * rows, rows)
         out_row = lax.broadcasted_iota(jnp.int32, (2 * half, 2 * half), 0)
         in_row = lax.broadcasted_iota(jnp.int32, (2 * half, 2 * half), 1)
         pick = in_row == 2 * (out_row % half) + out_row // half
@@ -142,7 +150,7 @@
                 for s in range(2):
                     o_ref[
                         slot_ref[t],
-                        b * half : (b + 1) * half,
+                        pl.ds(above + b * half, half),
                         s * width : (s + 1) * width,
                     ] = apart[s * half : (s + 1) * half, t * width : (t + 1) * width]
 
@@ -153,22 +161,25 @@
         for r in range(count):
             for j in range(n_t):
                 total[j, r * prefill : (r + 1) * prefill] += jnp.dot(
-                    x_refs[r][...], o_ref[j], preferred_element_type=F32
+                    x_refs[r][...], o_ref[j, pl.ds(above, rows)], preferred_element_type=F32
                 )
 
         @pl.when(step == steps - 1)
         def _():
             send_refs[0][...] = total[0].astype(BF)
+            k = 1
             for j in range(1, n_x):
-                send_refs[2 * j - 1][...] = total[j, :cut].astype(BF)
-                send_refs[2 * j][...] = total[j, cut:].astype(BF)
+                for at, n in pieces_of(count):
+                    rows_of = slice(at * prefill, (at + n) * prefill)
+                    send_refs[k][...] = total[j, rows_of].astype(BF)
+                    k += 1
             for j in range(n_x):
                 keep_ref[j] = total[n_x + j].astype(BF)
 
     part = (count * prefill, 2 * width)
-    cut = (count // 2) * prefill
-    upper, lower = (cut, 2 * width), (count * prefill - cut, 2 * width)
-    outs = [part] + [upper, lower] * (n_x - 1)
+    outs = [part] + [
+        (n * prefill, 2 * width) for _, n in pieces_of(count)
+    ] * (n_x - 1)
     split, *sends, keep = pl.pallas_call(
         body,
         out_shape=(
@@ -185,13 +196,13 @@
             ]
             + [pl.BlockSpec((rows, 2, columns), lambda i, p, s: (i, 0, 0))],
             out_specs=(
-                pl.BlockSpec((n_t, rows, 2 * width), lambda i, p, s: (0, i, 0)),
+                pl.BlockSpec(memory_space=pltpu.VMEM),
                 *[pl.BlockSpec(out, lambda i, p, s: (0, 0)) for out in outs],
                 pl.BlockSpec((n_x, *part), lambda i, p, s: (0, 0, 0)),
             ),
             scratch_shapes=[pltpu.VMEM((n_t, count * prefill, 2 * width), F32)],
         ),
-        compiler_params=params(),
+        compiler_params=params(36),
         cost_estimate=cost(2 * count * prefill * features * 2 * columns, 8 * features * columns),
         name="split_weight",
     )(plan, slots, *[hidden] * count, weight)
@@ -205,15 +216,15 @@
     n_after = len(after)
 
     def body(plan_ref, x_ref, *rest):
-        w_refs = rest[:n_t]
-        *send_refs, keep_ref = rest[n_t + n_after :]
+        w_ref = rest[0]
+        *send_refs, keep_ref = rest[1 + n_after :]
         live = plan_ref[LENGTH, first + pl.program_id(0)]
 
         def products(rows):
             dead = jnp.zeros((prefill - rows, width), BF)
             for j in range(n_t):
                 out = jnp.dot(
-                    x_ref[:rows], w_refs[j][0], preferred_element_type=F32
+                    x_ref[:rows], w_ref[j], preferred_element_type=F32
                 ).astype(BF)
                 if rows < prefill:
                     out = jnp.concatenate([out, dead], 0)
@@ -223,13 +234,13 @@
                     keep_ref[j - n_x] = out
                 else:
 
-                    @pl.when(pl.program_id(0) < cut)
-                    def _():
-                        send_refs[2 * j - 1][...] = out
-
-                    @pl.when(pl.program_id(0) >= cut)
-                    def _():
-                        send_refs[2 * j][...] = out
+                    spans = pieces_of(count)
+                    for k, (at, n) in enumerate(spans, 1 + (j - 1) * len(spans)):
+                        inside = (pl.program_id(0) >= at) & (pl.program_id(0) < at + n)
+
+                        @pl.when(inside)
+                        def _():
+                            send_refs[k][...] = out
 
         @pl.when(live > short)
         def _():
@@ -239,13 +250,12 @@
         def _():
             products(short)
 
-    cut = count // 2
-    parts = [count] + [cut, count - cut] * (n_x - 1)
+    spans = [(0, count)] + pieces_of(count) * (n_x - 1)
+    parts = [n for _, n in spans]
     block = (prefill, width)
-    places = [lambda i, p: (i, 0)] + [
-        lambda i, p: (jnp.minimum(i, cut - 1), 0),
-        lambda i, p: (jnp.maximum(i - cut, 0), 0),
-    ] * (n_x - 1)
+    places = [
+        lambda i, p, at=at, n=n: (jnp.clip(i - at, 0, n - 1), 0) for at, n in spans
+    ]
     *sends, keep = pl.pallas_call(
         body,
         out_shape=(
@@ -260,32 +270,32 @@
                     (prefill, features), lambda i, p: (p[ORDER, first + i], 0)
                 ),
             ]
-            + [
-                pl.BlockSpec((1, features, width), lambda i, p, j=j: (j, 0, 0))
-                for j in range(n_t)
-            ]
+            + [pl.BlockSpec(memory_space=pltpu.VMEM)]
             + [ANY] * n_after,
             out_specs=(
                 *[pl.BlockSpec(block, place) for place in places],
                 pl.BlockSpec((n_x, prefill, width), lambda i, p: (0, i, 0)),
             ),
         ),
-        compiler_params=params(),
+        compiler_params=params(24),
         cost_estimate=cost(2 * count * prefill * features * width * n_t, 2 * n_t * features * width),
         name="base_products",
-    )(plan, hidden, *[weight] * n_t, *after)
+    )(plan, hidden, weight, *after)
     return sends, keep
 
 
 def pair_sum(one, others, index, after):
     _, rows, width = one.shape
-    cut = others[0].shape[0]
+    n_piece = len(others)
 
     def body(a_ref, *rest):
-        b_refs = rest[:2]
-        o_ref, mine, theirs, total, sems, out_sems = rest[2 + len(after) :]
+        b_refs = rest[:n_piece]
+        o_ref, mine, theirs, total, sems, out_sems = rest[n_piece + len(after) :]
         copies, outs = [], []
-        spans = [pl.ds(0, cut), pl.ds(cut, rows - cut)]
+        spans, at = [], 0
+        for b_ref in b_refs:
+            spans.append(pl.ds(at, b_ref.shape[0]))
+            at += b_ref.shape[0]
         for k, span in enumerate(spans):
             copies.append(
                 (
@@ -312,11 +322,11 @@
     return pl.pallas_call(
         body,
         out_shape=jax.ShapeDtypeStruct((rows, width), BF),
-        in_specs=[ANY] * (3 + len(after)),
+        in_specs=[ANY] * (1 + n_piece + len(after)),
         out_specs=ANY,
         scratch_shapes=[pltpu.VMEM((rows, width), BF)] * 3
-        + [pltpu.SemaphoreType.DMA((2, 2)), pltpu.SemaphoreType.DMA((2,))],
-        compiler_params=params(),
+        + [pltpu.SemaphoreType.DMA((2, n_piece)), pltpu.SemaphoreType.DMA((n_piece,))],
+        compiler_params=params(16),
         cost_estimate=cost(rows * width, 6 * rows * width),
         name="pair_sum",
     )(one, *others, *after)
@@ -334,7 +344,7 @@
         in_specs=[ANY] * (n + len(after)),
         out_specs=[ANY] * n,
         input_output_aliases={i: i for i in range(n)},
-        compiler_params=params(),
+        compiler_params=params(16),
         cost_estimate=cost(0, 1 << 20),
         name="hold",
     )(*arrays, *after)
@@ -413,7 +423,7 @@
                 pltpu.SemaphoreType.DMA((2, count)),
             ],
         ),
-        compiler_params=params(),
+        compiler_params=params(60),
         cost_estimate=cost(2 * count * prefill * features * ranks, 2 * count * features * (prefill + ranks)),
         name="rank_products",
     )(plan, hidden, *maps.values(), *after)
@@ -473,32 +483,34 @@
         mix_column = lax.broadcasted_iota(jnp.int32, (2 * half, 2 * half), 1)
         mix = mix_column == mix_row // 2 + half * (mix_row % 2)
         mix = mix.astype(F32).astype(BF)
-        twice_row = lax.broadcasted_iota(jnp.int32, (2 * half, half), 0)
-        twice_column = lax.broadcasted_iota(jnp.int32, (2 * half, half), 1)
-        twice = (twice_column == twice_row // 2).astype(F32).astype(BF)
-        lane = lax.broadcasted_iota(jnp.int32, (2 * half, 2 * depth), 1)
-        side = lax.broadcasted_iota(jnp.int32, (2 * half, 2 * depth), 0) % 2
-        own_side = lane // depth == side
-        token = lax.broadcasted_iota(jnp.int32, (2 * half, columns), 0) // 2
-
-        def rows_for(i, pieces, live, b):
+        token = lax.broadcasted_iota(jnp.int32, (half, 2 * columns), 0)
+
+        def rows_for(i, live, b):
             rows = slice(b * half, (b + 1) * half)
-            total = jnp.zeros((2 * half, columns), F32)
-            for k in range(pieces):
-                piece = base_rows[i, k, rows]
-                piece = jnp.concatenate([piece[:, :columns], piece[:, columns:]], 0)
-                total += jnp.dot(mix, piece, preferred_element_type=F32)
             rank = rank_rows[i, 0, rows].astype(F32)
             for k in range(1, n_rank):
                 rank += rank_rows[i, k, rows].astype(F32)
-            rank = jnp.dot(twice, rank.astype(BF), preferred_element_type=F32)
-            rank = jnp.where(own_side, rank, 0.0).astype(BF)
+            rank = rank.astype(BF)
             up = jnp.concatenate(
                 [ups[i, j * 2 * depth : (j + 1) * 2 * depth] for j in range(tiles)], 1
             )
-            total += jnp.dot(rank, up, preferred_element_type=F32)
-            total = jnp.where(token + b * half < live, total, 0.0)
-            out_rows[i, rows] = total.astype(BF).reshape(half, 2, columns)
+            total = jnp.concatenate(
+                [
+                    jnp.dot(
+                        rank[:, s * depth : (s + 1) * depth],
+                        up[s * depth : (s + 1) * depth],
+                        preferred_element_type=F32,
+                    )
+                    for s in range(2)
+                ],
+                1,
+            )
+            for k in range(n_base):
+                total += base_rows[i, k, rows].astype(F32)
+            total = jnp.where(token + b * half < live, total, 0.0).astype(BF)
+            total = jnp.concatenate([total[:, :columns], total[:, columns:]], 0)
+            total = jnp.dot(mix, total, preferred_element_type=F32).astype(BF)
+            out_rows[i, rows] = total.reshape(half, 2, columns)
 
         outs = []
         for i in range(count):
@@ -508,11 +520,11 @@
                 map_refs[0][1].at[0, up_part], ups.at[i], sems.at[i, n_base + n_rank]
             ).wait()
             live = plan_ref[LENGTH, first + i]
-            rows_for(i, n_base, live, 0)
+            rows_for(i, live, 0)
 
             @pl.when(live > half)
             def _():
-                rows_for(i, n_base, live, 1)
+                rows_for(i, live, 1)
 
             @pl.when(live <= half)
             def _():
@@ -554,7 +566,7 @@
             ],
         ),
         input_output_aliases=aliases,
-        compiler_params=params(),
+        compiler_params=params(60),
         cost_estimate=cost(12 * count * prefill * prefill * 2 * columns, 20 * count * prefill * columns),
         name="finish",
     )(*operands)
@@ -616,8 +628,9 @@
         def send_on(first, count, sends, keep, after):
             got = [core_swap(part) for part in sends[1:]] + [core_swap(sends[0])]
             pieces = [keep, got.pop()]
+            n_piece = len(pieces_of(count))
             for k in range(1, n_x):
-                pairs.append(pair_sum(keep, got[2 * k - 2 : 2 * k], k, after))
+                pairs.append(pair_sum(keep, got[(k - 1) * n_piece : k * n_piece], k, after))
                 pieces.append(chip_shift(pairs[-1], k))
             bases.append((first, count, pieces))
 
@@ -666,19 +679,22 @@
         send_on(0, BASE_CHUNKS[0], sends, keep, [])
         second = base(1)
         if n_z > 2:
-            relay(2, [second[3], bases[0][2][-1]])
+            relay(2, [second[3]])
         send_on(*second, [bases[0][2][-1]])
         third = base(2)
-        part = rank(0, [third[3]]) if by_distance else third[3]
-        part = rank(1, [part]) if by_distance else part
+        part = third[3]
+        if by_distance:
+            part = rank(0, [third[3], bases[1][2][-1]])
+        send_on(*third, [part, bases[1][2][-1]])
+        fourth = base(3)
         for hops in range(3, n_z):
-            relay(hops, [part])
-        send_on(*third, [part, bases[1][2][-1]])
+            relay(hops, [fourth[3]])
+        part = fourth[3]
         if by_distance:
-            part = rank(2, [pairs[-1], ranks[0][2][-1]])
-        else:
-            for chunk in range(3):
-                part = rank(chunk, [pairs[-1]])
+            part = rank(1, [fourth[3], bases[2][2][-1]])
+        send_on(*fourth, [part, bases[2][2][-1]])
+        for chunk in range(len(ranks), 3):
+            part = rank(chunk, [pairs[-1]])
         out = write(None, 0, 2)
         out = write(out, 2, 3)
         rank(3, [out])

time: 186 us -> 177 us (0.952)
  Pallas kernels: 98.7 us -> 77.9 us
  local copies, waits for them, and re-layouts: 7.22 us -> 25.7 us
  waiting for transfers between devices: 45.9 us -> 31.4 us
  starting transfers between devices: 30.3 us -> 34.6 us
  other arithmetic: 2.57 us -> 4.61 us
    unnamed x36 -> x78, local copies, waits for them, and re-layouts: 7.22 us -> 25.7 us
    pallas_call x2 -> x3, Pallas kernels: 33.4 us -> 22.4 us  [base_products(): pl.pallas_call(body, out_shape=(*[jax.ShapeDtypeStruct((n * prefill, widt...]
    ppermute x7 -> x8, waiting for transfers between devices: 28.9 us -> 22.2 us  [chip_shift(): lax.ppermute(a, 'tensor', [(2 * x + c, 2 * ((x + k) % n_x) + c) for x in...]
    ppermute x3, waiting for transfers between devices: 7.01 us -> 1.54 us  [leftward(): return lax.ppermute(a, 'adapter', [(z, z - hops) for z in range(hops, n_z)])]
    pallas_call x3 -> x4, Pallas kernels: 7.69 us -> 2.6 us  [pair_sum(): pl.pallas_call(body, out_shape=jax.ShapeDtypeStruct((rows, width), BF), i...]
    pallas_call x3, Pallas kernels: 19.8 us -> 16.4 us  [finish(): pl.pallas_call(body, out_shape=jax.ShapeDtypeStruct(shape, BF), grid_spec...]
    convert_element_type x4, other arithmetic: 2.08 us -> 4.6 us  [rank(): pair = (part.astype(F32) + core_swap(part).astype(F32)).astype(BF)]
    ppermute x13 -> x16, waiting for transfers between devices: 8.74 us -> 6.38 us  [core_swap(): return lax.ppermute(a, 'tensor', [(t, t ^ 1) for t in range(n_t)])]
  transfers between devices with their start and end apart: 26 -> 30, of which waited for: 10 -> 11; matrix products, arithmetic and copies ran while one was open for 1% -> 3% of each run, Pallas kernels for 47% -> 40%
where the time goes in v5:
time: 177 us; the launch traced here: 175 us
  Pallas kernels  77.9 us (44%)
  starting transfers between devices  34.6 us (20%)
  waiting for transfers between devices  31.4 us (18%)
  local copies, waits for them, and re-layouts  25.7 us (15%)
  other arithmetic  4.61 us (3%)
    unnamed x78, local copies, waits for them, and re-layouts  25.7 us
    pallas_call x3, Pallas kernels, base_products(): pl.pallas_call(body, out_shape=(*[jax.ShapeDtypeStruct((n * prefill, widt...  22.4 us
    ppermute x8, waiting for transfers between devices, chip_shift(): lax.ppermute(a, 'tensor', [(2 * x + c, 2 * ((x + k) % n_x) + c) for x in...  22.2 us
    ppermute x3, starting transfers between devices, rightward(): return lax.ppermute(a, 'adapter', [(z - hops, z) for z in range(hops, n_z)])  17.6 us
    pallas_call x4, Pallas kernels, rank_products(): pl.pallas_call(body, out_shape=jax.ShapeDtypeStruct((count * prefill, ran...  17.1 us
    pallas_call x3, Pallas kernels, finish(): pl.pallas_call(body, out_shape=jax.ShapeDtypeStruct(shape, BF), grid_spec...  16.4 us
    pallas_call x1, Pallas kernels, split_weight(): pl.pallas_call(body, out_shape=(jax.ShapeDtypeStruct((n_t, features, 2 *...  15.1 us
    ppermute x8, starting transfers between devices, chip_shift(): lax.ppermute(a, 'tensor', [(2 * x + c, 2 * ((x + k) % n_x) + c) for x in...  9.69 us
  transfers between devices with their start and end apart: 30, of which 11 were waited for; matrix products, arithmetic and copies ran while one was open for 3% of the time, Pallas kernels for 40%

profile of v5, /device:TPU:0, one launch (start us, length us, event | category | flops | bytes accessed | tf_op | source)
XLA Modules:
  0.0 174.8 jit_solution(9284153853323523179)
XLA Ops:
  0.0 2.7 %pack_maps.1.rest_0_.rest_10_.rest_5_ = bf16[3,2304,128]{2,1,0:T(8,128)(2,1)} custom-call(bf16[3,2048,128]{2,1,0:T(8,128)(2,1)} %down_ref.1, bf16[3,2,64,256]{3,2,1,0:T(8,128)(2,1)} %up_ref.1), custom_call_target="tpu_custom_call" | custom-call | bytes 31457 | tf_op jit(solution)/shard_map/pack_maps/pallas_call | solution.py:66
  4.0 5.7 %collective-permute-start.12 = (bf16[3,2304,128]{2,1,0:T(8,128)(2,1)}, bf16[3,2304,128]{2,1,0:T(8,128)(2,1)S(1)}, u32[]{:S(2)}, u32[]{:S(2)}) collective-permute-start(bf16[3,2304,128]{2,1,0:T(8,128)(2,1)} %pack_maps.1.rest_0_.rest_10_.rest_5_), channel_id=1, source_target_pairs={{0,4},{4,8},{8,12},{1,5},{5,9},{9,13},{2,6},{6,10},{10,14},{3,7},{... | collective-permute-start | bytes 5308424 | tf_op jit(solution)/shard_map/ppermute | solution.py:593
  9.7 1.6 plan_requests.1.plan_ref
  12.1 15.1 %split_weight.1 = (bf16[4,2048,512]{2,1,0:T(8,128)(2,1)S(1)}, bf16[768,512]{1,0:T(8,128)(2,1)}, bf16[512,512]{1,0:T(8,128)(2,1)S(1)}, bf16[256,512]{1,0:T(8,128)(2,1)S(1)}, bf16[2,768,512]{2,1,0:T(8,128)(2,1)S(1)}) custom-call(s32[8,128]{1,0:T(8,128)S(1)} %copy-done.20, s32[4]{0:T(128)S(1)} %compare_select_fusion.2.slot_ref, bf16[3072,2048]{1,0:T(8,128)(2,1)} %x_ref.13, ...), custom_call_target="tpu_custom_call" | custom-call | flops 64424508 | bytes 167772 | tf_op jit(solution)/shard_map/split_weight/pallas_call | solution.py:183
  27.2 3.3 %copy-done.3 = bf16[4,2048,512]{2,1,0:T(8,128)(2,1)} copy-done((bf16[4,2048,512]{2,1,0:T(8,128)(2,1)}, bf16[4,2048,512]{2,1,0:T(8,128)(2,1)S(1)}, u32[]{:S(2)}) %copy-start.3) | copy-done | bytes 8388632
  31.0 1.8 %collective-permute-done.1.rest_1_ = bf16[256,512]{1,0:T(8,128)(2,1)S(1)} collective-permute-done((bf16[256,512]{1,0:T(8,128)(2,1)S(1)}, bf16[256,512]{1,0:T(8,128)(2,1)S(1)}, u32[]{:S(2)}, u32[]{:S(2)}) %collective-permute-start.1) | collective-permute-done | bytes 262176 | tf_op jit(solution)/shard_map/ppermute | solution.py:580
  33.2 2.0 %collective-permute-start.4 = (bf16[768,512]{1,0:T(8,128)(2,1)S(1)}, bf16[768,512]{1,0:T(8,128)(2,1)S(1)}, u32[]{:S(2)}, u32[]{:S(2)}) collective-permute-start(bf16[768,512]{1,0:T(8,128)(2,1)S(1)} %pair_sum.4.rest_1_), channel_id=1, source_target_pairs={{0,2},{1,3},{2,0},{3,1},{4,6},{5,7},{6,4},{7,5},{8,10},{9,11},{10,... | collective-permute-start | bytes 2359304 | tf_op jit(solution)/shard_map/ppermute | solution.py:583
  35.2 3.4 %copy-done.4 = bf16[4,2048,512]{2,1,0:T(8,128)(2,1)S(1)} copy-done((bf16[4,2048,512]{2,1,0:T(8,128)(2,1)S(1)}, bf16[4,2048,512]{2,1,0:T(8,128)(2,1)}, u32[]{:S(2)}) %copy-start.4) | copy-done | bytes 8388632
  38.6 6.2 %base_products.3 = (bf16[768,512]{1,0:T(8,128)(2,1)S(1)}, bf16[512,512]{1,0:T(8,128)(2,1)S(1)}, bf16[256,512]{1,0:T(8,128)(2,1)S(1)}, bf16[2,768,512]{2,1,0:T(8,128)(2,1)S(1)}) custom-call(s32[8,128]{1,0:T(8,128)S(1)} %copy-done.20, bf16[3072,2048]{1,0:T(8,128)(2,1)S(1)} %bitcast.5, bf16[4,2048,512]{2,1,0:T(8,128)(2,1)S(1)} %copy-done.4, ...), custom_call_target="tpu_custom_call" | custom-call | flops 64424508 | bytes 83886 | tf_op jit(solution)/shard_map/base_products/pallas_call | solution.py:259
  49.0 6.2 %collective-permute-start.16 = (bf16[3,2304,128]{2,1,0:T(8,128)(2,1)S(1)}, bf16[3,2304,128]{2,1,0:T(8,128)(2,1)}, u32[]{:S(2)}, u32[]{:S(2)}) collective-permute-start(bf16[3,2304,128]{2,1,0:T(8,128)(2,1)S(1)} %get-tuple-element.41.rest_2_.rest_3_.rest_12_.rest_8_.rest_4_.rest_9_), channel_id=1, source_target_pairs={{0,4},{4,8},{8,12},{1,5},{5,9},{9,13},{2,6},{6,10},{10,14},{3,7},{... | collective-permute-start | bytes 5308424 | tf_op jit(solution)/shard_map/ppermute | solution.py:593
  55.7 1.8 %collective-permute-done.3.rest_1_ = bf16[256,512]{1,0:T(8,128)(2,1)S(1)} collective-permute-done((bf16[256,512]{1,0:T(8,128)(2,1)S(1)}, bf16[256,512]{1,0:T(8,128)(2,1)S(1)}, u32[]{:S(2)}, u32[]{:S(2)}) %collective-permute-start.3) | collective-permute-done | bytes 262176 | tf_op jit(solution)/shard_map/ppermute | solution.py:580
  58.8 1.6 collective-permute-start.7
  60.4 8.2 %base_products.4 = (bf16[768,512]{1,0:T(8,128)(2,1)}, bf16[512,512]{1,0:T(8,128)(2,1)}, bf16[256,512]{1,0:T(8,128)(2,1)}, bf16[2,768,512]{2,1,0:T(8,128)(2,1)S(1)}) custom-call(s32[8,128]{1,0:T(8,128)S(1)} %copy-done.20, bf16[3072,2048]{1,0:T(8,128)(2,1)S(1)} %bitcast.5, bf16[4,2048,512]{2,1,0:T(8,128)(2,1)S(1)} %copy-done.4, ...), custom_call_target="tpu_custom_call" | custom-call | flops 64424508 | bytes 83886 | tf_op jit(solution)/shard_map/base_products/pallas_call | solution.py:259
  70.3 8.1 %collective-permute-done.7.rest_2_.rest_3_.rest_5_ = bf16[768,512]{1,0:T(8,128)(2,1)} collective-permute-done((bf16[768,512]{1,0:T(8,128)(2,1)S(1)}, bf16[768,512]{1,0:T(8,128)(2,1)}, u32[]{:S(2)}, u32[]{:S(2)}) %collective-permute-start.7) | collective-permute-done | bytes 786464 | tf_op jit(solution)/shard_map/ppermute | solution.py:583
  78.5 4.2 %rank_products.4.rest_2_ = bf16[768,128]{1,0:T(8,128)(2,1)} custom-call(s32[8,128]{1,0:T(8,128)} %plan_requests.1.plan_ref, bf16[3072,2048]{1,0:T(8,128)(2,1)} %x_ref.13, bf16[3,2304,128]{2,1,0:T(8,128)(2,1)} %pack_maps.1.rest_0_.rest_10_.rest_5_, bf16[2,768,512]{2,1,0:T(8,128)(2,1)} %copy-done.8, bf16[768,512]{1,0:T(8,128)(2,1)} %collective-permute-done.7.rest_2_.rest_3_.rest_5_), custom_call_target="tpu_custom_call" | custom-call | flops 4026531 | bytes 47185 | tf_op jit(solution)/shard_map/rank_products/pallas_call | solution.py:412
  86.4 1.7 collective-permute-start.13
  88.1 4.6 %copy-done = bf16[3072,2048]{1,0:T(8,128)(2,1)S(1)} copy-done((bf16[3072,2048]{1,0:T(8,128)(2,1)S(1)}, bf16[3072,2048]{1,0:T(8,128)(2,1)}, u32[]{:S(2)}) %copy-start) | copy-done | bytes 12582936
  92.7 3.4 %copy-done.5 = bf16[4,2048,512]{2,1,0:T(8,128)(2,1)S(1)} copy-done((bf16[4,2048,512]{2,1,0:T(8,128)(2,1)S(1)}, bf16[4,2048,512]{2,1,0:T(8,128)(2,1)}, u32[]{:S(2)}) %copy-start.5) | copy-done | bytes 8388632
  96.1 8.0 %base_products.5 = (bf16[768,512]{1,0:T(8,128)(2,1)S(1)}, bf16[512,512]{1,0:T(8,128)(2,1)}, bf16[256,512]{1,0:T(8,128)(2,1)S(1)}, bf16[2,768,512]{2,1,0:T(8,128)(2,1)S(1)}) custom-call(s32[8,128]{1,0:T(8,128)S(1)} %copy-done.21, bf16[3072,2048]{1,0:T(8,128)(2,1)S(1)} %copy-done, bf16[4,2048,512]{2,1,0:T(8,128)(2,1)S(1)} %copy-done.5, ...), custom_call_target="tpu_custom_call" | custom-call | flops 64424508 | bytes 83886 | tf_op jit(solution)/shard_map/base_products/pallas_call | solution.py:259
  106.9 5.8 %collective-permute-start.18 = (bf16[3,2304,128]{2,1,0:T(8,128)(2,1)}, bf16[3,2304,128]{2,1,0:T(8,128)(2,1)}, u32[]{:S(2)}, u32[]{:S(2)}) collective-permute-start(bf16[3,2304,128]{2,1,0:T(8,128)(2,1)} %get-tuple-element.43.rest_4_.rest_9_.rest_5_.rest_10_), channel_id=1, source_target_pairs={{0,4},{4,8},{8,12},{1,5},{5,9},{9,13},{2,6},{6,10},{10,14},{3,7},{... | collective-permute-start | bytes 5308424 | tf_op jit(solution)/shard_map/ppermute | solution.py:593
  115.9 4.2 %rank_products.5.rest_2_ = bf16[768,128]{1,0:T(8,128)(2,1)} custom-call(s32[8,128]{1,0:T(8,128)} %plan_requests.1.plan_ref, bf16[3072,2048]{1,0:T(8,128)(2,1)} %x_ref.13, bf16[3,2304,128]{2,1,0:T(8,128)(2,1)} %pack_maps.1.rest_0_.rest_10_.rest_5_, bf16[3,2304,128]{2,1,0:T(8,128)(2,1)} %copy-done.1, bf16[3,2304,128]{2,1,0:T(8,128)(2,1)} %copy-done.2, ...), custom_call_target="tpu_custom_call" | custom-call | flops 4026531 | bytes 47185 | tf_op jit(solution)/shard_map/rank_products/pallas_call | solution.py:412
  120.5 1.7 add_convert_fusion.2.rest_6_
  124.3 4.3 %rank_products.6 = bf16[768,128]{1,0:T(8,128)(2,1)} custom-call(s32[8,128]{1,0:T(8,128)} %plan_requests.1.plan_ref, bf16[3072,2048]{1,0:T(8,128)(2,1)} %x_ref.13, bf16[3,2304,128]{2,1,0:T(8,128)(2,1)} %pack_maps.1.rest_0_.rest_10_.rest_5_, bf16[3,2304,128]{2,1,0:T(8,128)(2,1)} %copy-done.1, bf16[3,2304,128]{2,1,0:T(8,128)(2,1)} %get-tuple-element.42.rest_2_.rest_7_, ...), custom_call_target="tpu_custom_call" | custom-call | flops 4026531 | bytes 47185 | tf_op jit(solution)/shard_map/rank_products/pallas_call | solution.py:412
  130.5 1.6 collective-permute-start.27
  133.6 4.3 %collective-permute-done.25.rest_7_ = bf16[768,128]{1,0:T(8,128)(2,1)S(1)} collective-permute-done((bf16[768,128]{1,0:T(8,128)(2,1)S(1)}, bf16[768,128]{1,0:T(8,128)(2,1)S(1)}, u32[]{:S(2)}, u32[]{:S(2)}) %collective-permute-start.25) | collective-permute-done | bytes 196640 | tf_op jit(solution)/shard_map/ppermute | solution.py:583
  137.8 4.2 %collective-permute-done.27.rest_9_ = bf16[768,128]{1,0:T(8,128)(2,1)S(1)} collective-permute-done((bf16[768,128]{1,0:T(8,128)(2,1)S(1)}, bf16[768,128]{1,0:T(8,128)(2,1)S(1)}, u32[]{:S(2)}, u32[]{:S(2)}) %collective-permute-start.27) | collective-permute-done | bytes 196640 | tf_op jit(solution)/shard_map/ppermute | solution.py:583
  142.7 6.5 %finish.3.rest_10_ = bf16[3072,2,256]{2,1,0:T(2,128)(2,1)} custom-call(s32[8,128]{1,0:T(8,128)} %plan_requests.1.plan_ref, bf16[2,768,512]{2,1,0:T(8,128)(2,1)} %copy-done.13, bf16[768,512]{1,0:T(8,128)(2,1)} %collective-permute-done.22.rest_1_, bf16[768,512]{1,0:T(8,128)(2,1)} %copy-done.14, bf16[2,768,512]{2,1,0:T(8,128)(2,1)} %copy-done.10, ...), custom_call_target="tpu_custom_call" | custom-call | flops 24159192 | bytes 78643 | tf_op jit(solution)/shard_map/finish/pallas_call | solution.py:551
  150.0 4.9 %finish.4.rest_7_.rest_12_ = bf16[3072,2,256]{2,1,0:T(2,128)(2,1)} custom-call(s32[8,128]{1,0:T(8,128)} %plan_requests.1.plan_ref, bf16[2,768,512]{2,1,0:T(8,128)(2,1)} %copy-done.8, bf16[768,512]{1,0:T(8,128)(2,1)} %collective-permute-done.19.rest_1_, bf16[768,512]{1,0:T(8,128)(2,1)} %copy-done.11, ...), custom_call_target="tpu_custom_call", output_to_operand_aliasing={{}: (11, {})} | custom-call | flops 12079595 | bytes 39321 | tf_op jit(solution)/shard_map/finish/pallas_call | solution.py:551
  154.9 4.4 %rank_products.7 = bf16[768,128]{1,0:T(8,128)(2,1)} custom-call(s32[8,128]{1,0:T(8,128)} %plan_requests.1.plan_ref, bf16[3072,2048]{1,0:T(8,128)(2,1)} %x_ref.13, bf16[3,2304,128]{2,1,0:T(8,128)(2,1)} %pack_maps.1.rest_0_.rest_10_.rest_5_, bf16[3,2304,128]{2,1,0:T(8,128)(2,1)} %copy-done.1, bf16[3,2304,128]{2,1,0:T(8,128)(2,1)} %get-tuple-element.42.rest_2_.rest_7_, ...), custom_call_target="tpu_custom_call" | custom-call | flops 4026531 | bytes 47185 | tf_op jit(solution)/shard_map/rank_products/pallas_call | solution.py:412
  159.4 1.6 collective-permute-done.28
  163.5 5.6 %collective-permute-done.29.rest_4_ = bf16[768,128]{1,0:T(8,128)(2,1)S(1)} collective-permute-done((bf16[768,128]{1,0:T(8,128)(2,1)S(1)}, bf16[768,128]{1,0:T(8,128)(2,1)S(1)}, u32[]{:S(2)}, u32[]{:S(2)}) %collective-permute-start.29) | collective-permute-done | bytes 196640 | tf_op jit(solution)/shard_map/ppermute | solution.py:583
  169.7 4.9 %finish.5 = bf16[3072,2,256]{2,1,0:T(2,128)(2,1)} custom-call(s32[8,128]{1,0:T(8,128)} %plan_requests.1.plan_ref, bf16[2,768,512]{2,1,0:T(8,128)(2,1)} %copy-done.6, bf16[768,512]{1,0:T(8,128)(2,1)} %copy-done.30, bf16[768,512]{1,0:T(8,128)(2,1)} %copy-done.31, bf16[768,128]{1,0:T(8,128)(2,1)} %copy-done.29, ...), custom_call_target="tpu_custom_call", output_to_operand_aliasing={{}: (13, {})} | custom-call | flops 12079595 | bytes 39321 | tf_op jit(solution)/shard_map/finish/pallas_call | solution.py:551
  (131 shorter events, 30.6 us)
Async XLA Ops:
  2.7 43.7 %collective-permute-start.11 = (bf16[3,2304,128]{2,1,0:T(8,128)(2,1)}, bf16[3,2304,128]{2,1,0:T(8,128)(2,1)S(1)}, u32[]{:S(2)}, u32[]{:S(2)}) collective-permute-start(bf16[3,2304,128]{2,1,0:T(8,128)(2,1)} %pack_maps.1.rest_0_.rest_10_.rest_5_), channel_id=1, source_target_pairs={{4,0},{8,4},{12,8},{5,1},{9,5},{13,9},{6,2},{10,6},{14,10},{7,3},{... | collective-permute-start | bytes 5308424 | tf_op jit(solution)/shard_map/ppermute | solution.py:590
  4.0 43.7 %collective-permute-start.12 = (bf16[3,2304,128]{2,1,0:T(8,128)(2,1)}, bf16[3,2304,128]{2,1,0:T(8,128)(2,1)S(1)}, u32[]{:S(2)}, u32[]{:S(2)}) collective-permute-start(bf16[3,2304,128]{2,1,0:T(8,128)(2,1)} %pack_maps.1.rest_0_.rest_10_.rest_5_), channel_id=1, source_target_pairs={{0,4},{4,8},{8,12},{1,5},{5,9},{9,13},{2,6},{6,10},{10,14},{3,7},{... | collective-permute-start | bytes 5308424 | tf_op jit(solution)/shard_map/ppermute | solution.py:593
  11.2 24.0 %slice-start = ((s8[12582912]{0:T(1024)(128)(4,1)}), s8[4194304]{0:T(1024)(128)(4,1)S(1)}, s32[]{:S(2)}) async-start(s8[12582912]{0:T(1024)(128)(4,1)} %bitcast.4), calls=%async_computation | async-start | bytes 8388608
  12.1 23.2 %slice-start.2 = ((s8[12582912]{0:T(1024)(128)(4,1)}), s8[4194304]{0:T(1024)(128)(4,1)S(1)}, s32[]{:S(2)}) async-start(s8[12582912]{0:T(1024)(128)(4,1)} %bitcast.4), calls=%async_computation.2 | async-start | bytes 8388608
  30.5 2.3 %collective-permute-start = (bf16[512,512]{1,0:T(8,128)(2,1)S(1)}, bf16[512,512]{1,0:T(8,128)(2,1)S(1)}, u32[]{:S(2)}, u32[]{:S(2)}) collective-permute-start(bf16[512,512]{1,0:T(8,128)(2,1)S(1)} %get-tuple-element.28), channel_id=1, source_target_pairs={{0,1},{1,0},{2,3},{3,2},{4,5},{5,4},{6,7},{7,6},{8,9},{9,8},{10,11... | collective-permute-start | bytes 1572872 | tf_op jit(solution)/shard_map/ppermute | solution.py:580
  30.5 2.3 %collective-permute-start.1 = (bf16[256,512]{1,0:T(8,128)(2,1)S(1)}, bf16[256,512]{1,0:T(8,128)(2,1)S(1)}, u32[]{:S(2)}, u32[]{:S(2)}) collective-permute-start(bf16[256,512]{1,0:T(8,128)(2,1)S(1)} %get-tuple-element.29), channel_id=1, source_target_pairs={{0,1},{1,0},{2,3},{3,2},{4,5},{5,4},{6,7},{7,6},{8,9},{9,8},{10,11... | collective-permute-start | bytes 786440 | tf_op jit(solution)/shard_map/ppermute | solution.py:580
  33.2 24.2 %collective-permute-start.4 = (bf16[768,512]{1,0:T(8,128)(2,1)S(1)}, bf16[768,512]{1,0:T(8,128)(2,1)S(1)}, u32[]{:S(2)}, u32[]{:S(2)}) collective-permute-start(bf16[768,512]{1,0:T(8,128)(2,1)S(1)} %pair_sum.4.rest_1_), channel_id=1, source_target_pairs={{0,2},{1,3},{2,0},{3,1},{4,6},{5,7},{6,4},{7,5},{8,10},{9,11},{10,... | collective-permute-start | bytes 2359304 | tf_op jit(solution)/shard_map/ppermute | solution.py:583
  47.7 56.4 %collective-permute-start.15 = (bf16[3,2304,128]{2,1,0:T(8,128)(2,1)S(1)}, bf16[3,2304,128]{2,1,0:T(8,128)(2,1)}, u32[]{:S(2)}, u32[]{:S(2)}) collective-permute-start(bf16[3,2304,128]{2,1,0:T(8,128)(2,1)S(1)} %get-tuple-element.40.rest_1_.rest_11_.rest_6_), channel_id=1, source_target_pairs={{4,0},{8,4},{12,8},{5,1},{9,5},{13,9},{6,2},{10,6},{14,10},{7,3},{... | collective-permute-start | bytes 5308424 | tf_op jit(solution)/shard_map/ppermute | solution.py:590
  49.0 55.1 %collective-permute-start.16 = (bf16[3,2304,128]{2,1,0:T(8,128)(2,1)S(1)}, bf16[3,2304,128]{2,1,0:T(8,128)(2,1)}, u32[]{:S(2)}, u32[]{:S(2)}) collective-permute-start(bf16[3,2304,128]{2,1,0:T(8,128)(2,1)S(1)} %get-tuple-element.41.rest_2_.rest_3_.rest_12_.rest_8_.rest_4_.rest_9_), channel_id=1, source_target_pairs={{0,4},{4,8},{8,12},{1,5},{5,9},{9,13},{2,6},{6,10},{10,14},{3,7},{... | collective-permute-start | bytes 5308424 | tf_op jit(solution)/shard_map/ppermute | solution.py:593
  55.1 2.3 %collective-permute-start.2 = (bf16[512,512]{1,0:T(8,128)(2,1)S(1)}, bf16[512,512]{1,0:T(8,128)(2,1)S(1)}, u32[]{:S(2)}, u32[]{:S(2)}) collective-permute-start(bf16[512,512]{1,0:T(8,128)(2,1)S(1)} %get-tuple-element.31), channel_id=1, source_target_pairs={{0,1},{1,0},{2,3},{3,2},{4,5},{5,4},{6,7},{7,6},{8,9},{9,8},{10,11... | collective-permute-start | bytes 1572872 | tf_op jit(solution)/shard_map/ppermute | solution.py:580
  55.2 2.3 %collective-permute-start.3 = (bf16[256,512]{1,0:T(8,128)(2,1)S(1)}, bf16[256,512]{1,0:T(8,128)(2,1)S(1)}, u32[]{:S(2)}, u32[]{:S(2)}) collective-permute-start(bf16[256,512]{1,0:T(8,128)(2,1)S(1)} %get-tuple-element.32), channel_id=1, source_target_pairs={{0,1},{1,0},{2,3},{3,2},{4,5},{5,4},{6,7},{7,6},{8,9},{9,8},{10,11... | collective-permute-start | bytes 786440 | tf_op jit(solution)/shard_map/ppermute | solution.py:580
  58.8 19.7 %collective-permute-start.7 = (bf16[768,512]{1,0:T(8,128)(2,1)S(1)}, bf16[768,512]{1,0:T(8,128)(2,1)}, u32[]{:S(2)}, u32[]{:S(2)}) collective-permute-start(bf16[768,512]{1,0:T(8,128)(2,1)S(1)} %pair_sum.5.rest_1_), channel_id=1, source_target_pairs={{0,2},{1,3},{2,0},{3,1},{4,6},{5,7},{6,4},{7,5},{8,10},{9,11},{10,... | collective-permute-start | bytes 2359304 | tf_op jit(solution)/shard_map/ppermute | solution.py:583
  69.8 12.9 %collective-permute-start.5 = (bf16[512,512]{1,0:T(8,128)(2,1)}, bf16[512,512]{1,0:T(8,128)(2,1)}, u32[]{:S(2)}, u32[]{:S(2)}) collective-permute-start(bf16[512,512]{1,0:T(8,128)(2,1)} %get-tuple-element.34), channel_id=1, source_target_pairs={{0,1},{1,0},{2,3},{3,2},{4,5},{5,4},{6,7},{7,6},{8,9},{9,8},{10,11... | collective-permute-start | bytes 1572872 | tf_op jit(solution)/shard_map/ppermute | solution.py:580
  69.8 42.9 %collective-permute-start.22 = (bf16[768,512]{1,0:T(8,128)(2,1)}, bf16[768,512]{1,0:T(8,128)(2,1)}, u32[]{:S(2)}, u32[]{:S(2)}) collective-permute-start(bf16[768,512]{1,0:T(8,128)(2,1)} %get-tuple-element.45), channel_id=1, source_target_pairs={{0,1},{1,0},{2,3},{3,2},{4,5},{5,4},{6,7},{7,6},{8,9},{9,8},{10,11... | collective-permute-start | bytes 2359304 | tf_op jit(solution)/shard_map/ppermute | solution.py:580
  78.5 4.2 %collective-permute-start.6 = (bf16[256,512]{1,0:T(8,128)(2,1)}, bf16[256,512]{1,0:T(8,128)(2,1)S(1)}, u32[]{:S(2)}, u32[]{:S(2)}) collective-permute-start(bf16[256,512]{1,0:T(8,128)(2,1)} %get-tuple-element.35), channel_id=1, source_target_pairs={{0,1},{1,0},{2,3},{3,2},{4,5},{5,4},{6,7},{7,6},{8,9},{9,8},{10,11... | collective-permute-start | bytes 786440 | tf_op jit(solution)/shard_map/ppermute | solution.py:580
  86.4 28.3 %collective-permute-start.13 = (bf16[768,512]{1,0:T(8,128)(2,1)S(1)}, bf16[768,512]{1,0:T(8,128)(2,1)S(1)}, u32[]{:S(2)}, u32[]{:S(2)}) collective-permute-start(bf16[768,512]{1,0:T(8,128)(2,1)S(1)} %pair_sum.6.rest_1_), channel_id=1, source_target_pairs={{0,2},{1,3},{2,0},{3,1},{4,6},{5,7},{6,4},{7,5},{8,10},{9,11},{10,... | collective-permute-start | bytes 2359304 | tf_op jit(solution)/shard_map/ppermute | solution.py:583
  105.6 49.3 %collective-permute-start.17 = (bf16[3,2304,128]{2,1,0:T(8,128)(2,1)}, bf16[3,2304,128]{2,1,0:T(8,128)(2,1)}, u32[]{:S(2)}, u32[]{:S(2)}) collective-permute-start(bf16[3,2304,128]{2,1,0:T(8,128)(2,1)} %get-tuple-element.42.rest_2_.rest_7_), channel_id=1, source_target_pairs={{4,0},{8,4},{12,8},{5,1},{9,5},{13,9},{6,2},{10,6},{14,10},{7,3},{... | collective-permute-start | bytes 5308424 | tf_op jit(solution)/shard_map/ppermute | solution.py:590
  106.9 48.1 %collective-permute-start.18 = (bf16[3,2304,128]{2,1,0:T(8,128)(2,1)}, bf16[3,2304,128]{2,1,0:T(8,128)(2,1)}, u32[]{:S(2)}, u32[]{:S(2)}) collective-permute-start(bf16[3,2304,128]{2,1,0:T(8,128)(2,1)} %get-tuple-element.43.rest_4_.rest_9_.rest_5_.rest_10_), channel_id=1, source_target_pairs={{0,4},{4,8},{8,12},{1,5},{5,9},{9,13},{2,6},{6,10},{10,14},{3,7},{... | collective-permute-start | bytes 5308424 | tf_op jit(solution)/shard_map/ppermute | solution.py:593
  112.7 1.6 collective-permute-start.24
  112.7 1.8 %collective-permute-start.10 = (bf16[256,512]{1,0:T(8,128)(2,1)S(1)}, bf16[256,512]{1,0:T(8,128)(2,1)S(1)}, u32[]{:S(2)}, u32[]{:S(2)}) collective-permute-start(bf16[256,512]{1,0:T(8,128)(2,1)S(1)} %get-tuple-element.39), channel_id=1, source_target_pairs={{0,1},{1,0},{2,3},{3,2},{4,5},{5,4},{6,7},{7,6},{8,9},{9,8},{10,11... | collective-permute-start | bytes 786440 | tf_op jit(solution)/shard_map/ppermute | solution.py:580
  114.2 5.9 %collective-permute-start.9 = (bf16[512,512]{1,0:T(8,128)(2,1)}, bf16[512,512]{1,0:T(8,128)(2,1)S(1)}, u32[]{:S(2)}, u32[]{:S(2)}) collective-permute-start(bf16[512,512]{1,0:T(8,128)(2,1)} %get-tuple-element.38), channel_id=1, source_target_pairs={{0,1},{1,0},{2,3},{3,2},{4,5},{5,4},{6,7},{7,6},{8,9},{9,8},{10,11... | collective-permute-start | bytes 1572872 | tf_op jit(solution)/shard_map/ppermute | solution.py:580
  114.5 15.5 %collective-permute-start.23 = (bf16[768,512]{1,0:T(8,128)(2,1)S(1)}, bf16[768,512]{1,0:T(8,128)(2,1)}, u32[]{:S(2)}, u32[]{:S(2)}) collective-permute-start(bf16[768,512]{1,0:T(8,128)(2,1)S(1)} %copy-done.23), channel_id=1, source_target_pairs={{0,1},{1,0},{2,3},{3,2},{4,5},{5,4},{6,7},{7,6},{8,9},{9,8},{10,11... | collective-permute-start | bytes 2359304 | tf_op jit(solution)/shard_map/ppermute | solution.py:580
  115.6 17.5 %collective-permute-start.19 = (bf16[768,512]{1,0:T(8,128)(2,1)}, bf16[768,512]{1,0:T(8,128)(2,1)}, u32[]{:S(2)}, u32[]{:S(2)}) collective-permute-start(bf16[768,512]{1,0:T(8,128)(2,1)} %get-tuple-element.44), channel_id=1, source_target_pairs={{0,1},{1,0},{2,3},{3,2},{4,5},{5,4},{6,7},{7,6},{8,9},{9,8},{10,11... | collective-permute-start | bytes 2359304 | tf_op jit(solution)/shard_map/ppermute | solution.py:580
  120.1 8.6 %collective-permute-start.26 = (bf16[768,128]{1,0:T(8,128)(2,1)}, bf16[768,128]{1,0:T(8,128)(2,1)}, u32[]{:S(2)}, u32[]{:S(2)}) collective-permute-start(bf16[768,128]{1,0:T(8,128)(2,1)} %rank_products.5.rest_2_), channel_id=1, source_target_pairs={{0,1},{1,0},{2,3},{3,2},{4,5},{5,4},{6,7},{7,6},{8,9},{9,8},{10,11... | collective-permute-start | bytes 589832 | tf_op jit(solution)/shard_map/ppermute | solution.py:580
  128.7 1.8 %collective-permute-start.20 = (bf16[768,128]{1,0:T(8,128)(2,1)}, bf16[768,128]{1,0:T(8,128)(2,1)S(1)}, u32[]{:S(2)}, u32[]{:S(2)}) collective-permute-start(bf16[768,128]{1,0:T(8,128)(2,1)} %rank_products.6), channel_id=1, source_target_pairs={{0,1},{1,0},{2,3},{3,2},{4,5},{5,4},{6,7},{7,6},{8,9},{9,8},{10,11... | collective-permute-start | bytes 589832 | tf_op jit(solution)/shard_map/ppermute | solution.py:580
  130.0 7.8 %collective-permute-start.25 = (bf16[768,128]{1,0:T(8,128)(2,1)S(1)}, bf16[768,128]{1,0:T(8,128)(2,1)S(1)}, u32[]{:S(2)}, u32[]{:S(2)}) collective-permute-start(bf16[768,128]{1,0:T(8,128)(2,1)S(1)} %copy-done.26), channel_id=1, source_target_pairs={{0,2},{1,3},{2,0},{3,1},{4,6},{5,7},{6,4},{7,5},{8,10},{9,11},{10,... | collective-permute-start | bytes 589832 | tf_op jit(solution)/shard_map/ppermute | solution.py:583
  130.5 11.6 %collective-permute-start.27 = (bf16[768,128]{1,0:T(8,128)(2,1)S(1)}, bf16[768,128]{1,0:T(8,128)(2,1)S(1)}, u32[]{:S(2)}, u32[]{:S(2)}) collective-permute-start(bf16[768,128]{1,0:T(8,128)(2,1)S(1)} %add_convert_fusion.1.rest_8_), channel_id=1, source_target_pairs={{0,2},{1,3},{2,0},{3,1},{4,6},{5,7},{6,4},{7,5},{8,10},{9,11},{10,... | collective-permute-start | bytes 589832 | tf_op jit(solution)/shard_map/ppermute | solution.py:583
  133.1 16.2 %collective-permute-start.21 = (bf16[768,128]{1,0:T(8,128)(2,1)S(1)}, bf16[768,128]{1,0:T(8,128)(2,1)S(1)}, u32[]{:S(2)}, u32[]{:S(2)}) collective-permute-start(bf16[768,128]{1,0:T(8,128)(2,1)S(1)} %add_convert_fusion.3.rest_3_), channel_id=1, source_target_pairs={{0,2},{1,3},{2,0},{3,1},{4,6},{5,7},{6,4},{7,5},{8,10},{9,11},{10,... | collective-permute-start | bytes 589832 | tf_op jit(solution)/shard_map/ppermute | solution.py:583
  137.8 25.6 %collective-permute-start.8 = (bf16[768,512]{1,0:T(8,128)(2,1)S(1)}, bf16[768,512]{1,0:T(8,128)(2,1)S(1)}, u32[]{:S(2)}, u32[]{:S(2)}) collective-permute-start(bf16[768,512]{1,0:T(8,128)(2,1)S(1)} %copy-done.25), channel_id=1, source_target_pairs={{0,1},{1,0},{2,3},{3,2},{4,5},{5,4},{6,7},{7,6},{8,9},{9,8},{10,11... | collective-permute-start | bytes 2359304 | tf_op jit(solution)/shard_map/ppermute | solution.py:580
  142.0 21.4 %collective-permute-start.14 = (bf16[768,512]{1,0:T(8,128)(2,1)}, bf16[768,512]{1,0:T(8,128)(2,1)S(1)}, u32[]{:S(2)}, u32[]{:S(2)}) collective-permute-start(bf16[768,512]{1,0:T(8,128)(2,1)} %copy-done.15), channel_id=1, source_target_pairs={{0,2},{1,3},{2,0},{3,1},{4,6},{5,7},{6,4},{7,5},{8,10},{9,11},{10,... | collective-permute-start | bytes 2359304 | tf_op jit(solution)/shard_map/ppermute | solution.py:583
  159.3 1.7 collective-permute-start.28
  162.0 7.0 %collective-permute-start.29 = (bf16[768,128]{1,0:T(8,128)(2,1)S(1)}, bf16[768,128]{1,0:T(8,128)(2,1)S(1)}, u32[]{:S(2)}, u32[]{:S(2)}) collective-permute-start(bf16[768,128]{1,0:T(8,128)(2,1)S(1)} %add_convert_fusion.rest_3_), channel_id=1, source_target_pairs={{0,2},{1,3},{2,0},{3,1},{4,6},{5,7},{6,4},{7,5},{8,10},{9,11},{10,... | collective-permute-start | bytes 589832 | tf_op jit(solution)/shard_map/ppermute | solution.py:583
  (37 other events, 207.7 us)

commit v6 on v5

--- a/solution.py
+++ b/solution.py
@@ -72,7 +72,7 @@
             pltpu.VMEM((stored, tiles * part, lanes), BF),
             pltpu.SemaphoreType.DMA((2, stored)),
         ],
-        compiler_params=params(60),
+        compiler_params=params(24),
         cost_estimate=cost(0, 4 * down.size),
         name="pack_maps",
     )(down, up)
@@ -202,7 +202,7 @@
             ),
             scratch_shapes=[pltpu.VMEM((n_t, count * prefill, 2 * width), F32)],
         ),
-        compiler_params=params(36),
+        compiler_params=params(46),
         cost_estimate=cost(2 * count * prefill * features * 2 * columns, 8 * features * columns),
         name="split_weight",
     )(plan, slots, *[hidden] * count, weight)
@@ -277,7 +277,7 @@
                 pl.BlockSpec((n_x, prefill, width), lambda i, p: (0, i, 0)),
             ),
         ),
-        compiler_params=params(24),
+        compiler_params=params(46),
         cost_estimate=cost(2 * count * prefill * features * width * n_t, 2 * n_t * features * width),
         name="base_products",
     )(plan, hidden, weight, *after)
@@ -326,7 +326,7 @@
         out_specs=ANY,
         scratch_shapes=[pltpu.VMEM((rows, width), BF)] * 3
         + [pltpu.SemaphoreType.DMA((2, n_piece)), pltpu.SemaphoreType.DMA((n_piece,))],
-        compiler_params=params(16),
+        compiler_params=params(12),
         cost_estimate=cost(rows * width, 6 * rows * width),
         name="pair_sum",
     )(one, *others, *after)
@@ -344,7 +344,7 @@
         in_specs=[ANY] * (n + len(after)),
         out_specs=[ANY] * n,
         input_output_aliases={i: i for i in range(n)},
-        compiler_params=params(16),
+        compiler_params=params(8),
         cost_estimate=cost(0, 1 << 20),
         name="hold",
     )(*arrays, *after)
@@ -423,7 +423,7 @@
                 pltpu.SemaphoreType.DMA((2, count)),
             ],
         ),
-        compiler_params=params(60),
+        compiler_params=params(16),
         cost_estimate=cost(2 * count * prefill * features * ranks, 2 * count * features * (prefill + ranks)),
         name="rank_products",
     )(plan, hidden, *maps.values(), *after)
@@ -479,9 +479,11 @@
                 sems.at[i, n_base + n_rank],
             )
 
+        group = half // tiles
         mix_row = lax.broadcasted_iota(jnp.int32, (2 * half, 2 * half), 0)
         mix_column = lax.broadcasted_iota(jnp.int32, (2 * half, 2 * half), 1)
-        mix = mix_column == mix_row // 2 + half * (mix_row % 2)
+        mix_token, mix_tile = mix_row // (2 * tiles), mix_row // 2 % tiles
+        mix = mix_column == (mix_row % 2 * tiles + mix_tile) * group + mix_token
         mix = mix.astype(F32).astype(BF)
         token = lax.broadcasted_iota(jnp.int32, (half, 2 * columns), 0)
 
@@ -508,9 +510,24 @@
             for k in range(n_base):
                 total += base_rows[i, k, rows].astype(F32)
             total = jnp.where(token + b * half < live, total, 0.0).astype(BF)
-            total = jnp.concatenate([total[:, :columns], total[:, columns:]], 0)
-            total = jnp.dot(mix, total, preferred_element_type=F32).astype(BF)
-            out_rows[i, rows] = total.reshape(half, 2, columns)
+            parts = [
+                jnp.concatenate(
+                    [
+                        total[g * group : (g + 1) * group, k * lanes : (k + 1) * lanes]
+                        for k in range(2 * tiles)
+                    ],
+                    0,
+                )
+                for g in range(tiles)
+            ]
+            mixed = jnp.dot(
+                mix, jnp.concatenate(parts, 1), preferred_element_type=F32
+            ).astype(BF)
+            for g in range(tiles):
+                at = b * half * tiles + g * half
+                out_rows[i, at : at + half] = mixed[
+                    :, g * lanes : (g + 1) * lanes
+                ].reshape(half, 2, lanes)
 
         outs = []
         for i in range(count):
@@ -528,12 +545,13 @@
 
             @pl.when(live <= half)
             def _():
-                out_rows[i, half:] = jnp.zeros((half, 2, columns), BF)
-
-            row = pl.multiple_of(plan_ref[ORDER, first + i] * prefill, prefill)
+                out_rows[i, half * tiles :] = jnp.zeros((half * tiles, 2, lanes), BF)
+
+            block = prefill * tiles
+            row = pl.multiple_of(plan_ref[ORDER, first + i] * block, block)
             outs.append(
                 pltpu.make_async_copy(
-                    out_rows.at[i], o_ref.at[pl.ds(row, prefill)], out_sems.at[i]
+                    out_rows.at[i], o_ref.at[pl.ds(row, block)], out_sems.at[i]
                 )
             )
             outs[-1].start()
@@ -550,7 +568,7 @@
         operands.append(before)
     return pl.pallas_call(
         body,
-        out_shape=jax.ShapeDtypeStruct(shape, BF),
+        out_shape=jax.ShapeDtypeStruct((shape[0] * tiles, 2, lanes), BF),
         grid_spec=pltpu.PrefetchScalarGridSpec(
             num_scalar_prefetch=1,
             grid=(),
@@ -560,7 +578,7 @@
                 pltpu.VMEM((count, extra, lanes), BF),
                 pltpu.VMEM((count, n_base, prefill, 2 * columns), BF),
                 pltpu.VMEM((count, n_rank, prefill, 2 * depth), BF),
-                pltpu.VMEM((count, prefill, 2, columns), BF),
+                pltpu.VMEM((count, prefill * tiles, 2, lanes), BF),
                 pltpu.SemaphoreType.DMA((count, n_base + n_rank + 1)),
                 pltpu.SemaphoreType.DMA((count,)),
             ],
@@ -698,7 +716,10 @@
         out = write(None, 0, 2)
         out = write(out, 2, 3)
         rank(3, [out])
-        return write(out, 3, 4)
+        out = write(out, 3, 4)
+        tiles = out.shape[0] // shape[0]
+        out = out.reshape(shape[0], tiles, 2, columns // tiles)
+        return out.transpose(0, 2, 1, 3).reshape(shape)
 
     return jax.shard_map(
         per_device,

time: 177 us -> 166 us (0.938)
  local copies, waits for them, and re-layouts: 25.7 us -> 11.2 us
  Pallas kernels: 77.9 us -> 84.7 us
  other arithmetic: 4.61 us -> 0.23 us
    unnamed x78 -> x70, local copies, waits for them, and re-layouts: 25.7 us -> 11.2 us
    pallas_call x3, Pallas kernels: 22.4 us -> 33.7 us  [base_products(): pl.pallas_call(body, out_shape=(*[jax.ShapeDtypeStruct((n * prefill, widt...]
    pallas_call x4, Pallas kernels: 17.1 us -> 10.6 us  [rank_products(): pl.pallas_call(body, out_shape=jax.ShapeDtypeStruct((count * prefill, ran...]
    convert_element_type x4, other arithmetic: 4.6 us -> 0.22 us  [rank(): pair = (part.astype(F32) + core_swap(part).astype(F32)).astype(BF)]
    pallas_call x1, Pallas kernels: 2.66 us -> 0.45 us  [pack_maps(): pl.pallas_call(body, out_shape=jax.ShapeDtypeStruct((stored, features + t...]
    ppermute x3, waiting for transfers between devices: 1.54 us -> 3.56 us  [leftward(): return lax.ppermute(a, 'adapter', [(z, z - hops) for z in range(hops, n_z)])]
    ppermute x8, waiting for transfers between devices: 22.2 us -> 20.2 us  [chip_shift(): lax.ppermute(a, 'tensor', [(2 * x + c, 2 * ((x + k) % n_x) + c) for x in...]
    pallas_call x1, Pallas kernels: 15.1 us -> 17 us  [split_weight(): pl.pallas_call(body, out_shape=(jax.ShapeDtypeStruct((n_t, features, 2 *...]
  transfers between devices with their start and end apart: 30 -> 30, of which waited for: 11 -> 14; matrix products, arithmetic and copies ran while one was open for 3% -> 0% of each run, Pallas kernels for 40% -> 48%
where the time goes in v6:
time: 166 us; the launch traced here: 165 us
  Pallas kernels  84.7 us (51%)
  starting transfers between devices  35.8 us (22%)
  waiting for transfers between devices  32.1 us (19%)
  local copies, waits for them, and re-layouts  11.2 us (7%)
    pallas_call x3, Pallas kernels, base_products(): pl.pallas_call(body, out_shape=(*[jax.ShapeDtypeStruct((n * prefill, widt...  33.7 us
    ppermute x8, waiting for transfers between devices, chip_shift(): lax.ppermute(a, 'tensor', [(2 * x + c, 2 * ((x + k) % n_x) + c) for x in...  20.2 us
    ppermute x3, starting transfers between devices, rightward(): return lax.ppermute(a, 'adapter', [(z - hops, z) for z in range(hops, n_z)])  19.1 us
    pallas_call x3, Pallas kernels, finish(): pl.pallas_call(body, out_shape=jax.ShapeDtypeStruct((shape[0] * tiles, 2,...  17.5 us
    pallas_call x1, Pallas kernels, split_weight(): pl.pallas_call(body, out_shape=(jax.ShapeDtypeStruct((n_t, features, 2 *...  17 us
    unnamed x70, local copies, waits for them, and re-layouts  11.2 us
    pallas_call x4, Pallas kernels, rank_products(): pl.pallas_call(body, out_shape=jax.ShapeDtypeStruct((count * prefill, ran...  10.6 us
    ppermute x8, starting transfers between devices, chip_shift(): lax.ppermute(a, 'tensor', [(2 * x + c, 2 * ((x + k) % n_x) + c) for x in...  9.56 us
  transfers between devices with their start and end apart: 30, of which 14 were waited for; matrix products, arithmetic and copies ran while one was open for 0% of the time, Pallas kernels for 48%

profile of v6, /device:TPU:0, one launch (start us, length us, event | category | flops | bytes accessed | tf_op | source)
XLA Modules:
  0.0 164.8 jit_solution(2862746433875066601)
XLA Ops:
  0.0 1.4 copy-done.9
  2.8 1.3 collective-permute-start.11
  4.1 6.8 %collective-permute-start.12 = (bf16[3,2304,128]{2,1,0:T(8,128)(2,1)S(1)}, bf16[3,2304,128]{2,1,0:T(8,128)(2,1)}, u32[]{:S(2)}, u32[]{:S(2)}) collective-permute-start(bf16[3,2304,128]{2,1,0:T(8,128)(2,1)S(1)} %pack_maps.1.rest_0_.rest_10_.rest_5_), channel_id=1, source_target_pairs={{0,4},{4,8},{8,12},{1,5},{5,9},{9,13},{2,6},{6,10},{10,14},{3,7},{... | collective-permute-start | bytes 5308424 | tf_op jit(solution)/shard_map/ppermute | solution.py:611
  10.9 1.6 plan_requests.1.plan_ref
  13.1 17.0 %split_weight.1 = (bf16[4,2048,512]{2,1,0:T(8,128)(2,1)}, bf16[768,512]{1,0:T(8,128)(2,1)S(1)}, bf16[512,512]{1,0:T(8,128)(2,1)S(1)}, bf16[256,512]{1,0:T(8,128)(2,1)S(1)}, bf16[2,768,512]{2,1,0:T(8,128)(2,1)S(1)}) custom-call(s32[8,128]{1,0:T(8,128)S(1)} %copy-done.10, s32[4]{0:T(128)S(1)} %compare_select_fusion.2.slot_ref, bf16[3072,2048]{1,0:T(8,128)(2,1)} %x_ref.13, ...), custom_call_target="tpu_custom_call" | custom-call | flops 64424508 | bytes 167772 | tf_op jit(solution)/shard_map/split_weight/pallas_call | solution.py:183
  31.0 1.5 collective-permute-done.1.rest_1_
  33.0 2.0 %collective-permute-start.4 = (bf16[768,512]{1,0:T(8,128)(2,1)S(1)}, bf16[768,512]{1,0:T(8,128)(2,1)S(1)}, u32[]{:S(2)}, u32[]{:S(2)}) collective-permute-start(bf16[768,512]{1,0:T(8,128)(2,1)S(1)} %pair_sum.4.rest_1_), channel_id=1, source_target_pairs={{0,2},{1,3},{2,0},{3,1},{4,6},{5,7},{6,4},{7,5},{8,10},{9,11},{10,... | collective-permute-start | bytes 2359304 | tf_op jit(solution)/shard_map/ppermute | solution.py:601
  34.9 8.9 %base_products.3 = (bf16[768,512]{1,0:T(8,128)(2,1)S(1)}, bf16[512,512]{1,0:T(8,128)(2,1)S(1)}, bf16[256,512]{1,0:T(8,128)(2,1)S(1)}, bf16[2,768,512]{2,1,0:T(8,128)(2,1)S(1)}) custom-call(s32[8,128]{1,0:T(8,128)S(1)} %copy-done.10, bf16[3072,2048]{1,0:T(8,128)(2,1)} %x_ref.13, bf16[4,2048,512]{2,1,0:T(8,128)(2,1)} %get-tuple-element.26.rest_0_, ...), custom_call_target="tpu_custom_call" | custom-call | flops 64424508 | bytes 83886 | tf_op jit(solution)/shard_map/base_products/pallas_call | solution.py:259
  43.9 2.6 %collective-permute-done.11.refs_0_ = bf16[3,2304,128]{2,1,0:T(8,128)(2,1)} collective-permute-done((bf16[3,2304,128]{2,1,0:T(8,128)(2,1)S(1)}, bf16[3,2304,128]{2,1,0:T(8,128)(2,1)}, u32[]{:S(2)}, u32[]{:S(2)}) %collective-permute-start.11) | collective-permute-done | bytes 1769504 | tf_op jit(solution)/shard_map/ppermute | solution.py:608
  47.5 1.3 collective-permute-start.15
  48.8 6.3 %collective-permute-start.16 = (bf16[3,2304,128]{2,1,0:T(8,128)(2,1)}, bf16[3,2304,128]{2,1,0:T(8,128)(2,1)}, u32[]{:S(2)}, u32[]{:S(2)}) collective-permute-start(bf16[3,2304,128]{2,1,0:T(8,128)(2,1)} %get-tuple-element.41.rest_2_.rest_3_.rest_12_.rest_8_.rest_4_.rest_9_), channel_id=1, source_target_pairs={{0,4},{4,8},{8,12},{1,5},{5,9},{9,13},{2,6},{6,10},{10,14},{3,7},{... | collective-permute-start | bytes 5308424 | tf_op jit(solution)/shard_map/ppermute | solution.py:611
  55.7 1.8 %collective-permute-done.3.rest_1_ = bf16[256,512]{1,0:T(8,128)(2,1)S(1)} collective-permute-done((bf16[256,512]{1,0:T(8,128)(2,1)S(1)}, bf16[256,512]{1,0:T(8,128)(2,1)S(1)}, u32[]{:S(2)}, u32[]{:S(2)}) %collective-permute-start.3) | collective-permute-done | bytes 262176 | tf_op jit(solution)/shard_map/ppermute | solution.py:598
  58.7 1.7 %collective-permute-start.7 = (bf16[768,512]{1,0:T(8,128)(2,1)}, bf16[768,512]{1,0:T(8,128)(2,1)}, u32[]{:S(2)}, u32[]{:S(2)}) collective-permute-start(bf16[768,512]{1,0:T(8,128)(2,1)} %pair_sum.5.rest_1_), channel_id=1, source_target_pairs={{0,2},{1,3},{2,0},{3,1},{4,6},{5,7},{6,4},{7,5},{8,10},{9,11},{10,... | collective-permute-start | bytes 2359304 | tf_op jit(solution)/shard_map/ppermute | solution.py:601
  60.4 12.7 %base_products.4 = (bf16[768,512]{1,0:T(8,128)(2,1)S(1)}, bf16[512,512]{1,0:T(8,128)(2,1)S(1)}, bf16[256,512]{1,0:T(8,128)(2,1)S(1)}, bf16[2,768,512]{2,1,0:T(8,128)(2,1)S(1)}) custom-call(s32[8,128]{1,0:T(8,128)S(1)} %copy-done.10, bf16[3072,2048]{1,0:T(8,128)(2,1)} %x_ref.13, bf16[4,2048,512]{2,1,0:T(8,128)(2,1)} %get-tuple-element.26.rest_0_, ...), custom_call_target="tpu_custom_call" | custom-call | flops 64424508 | bytes 83886 | tf_op jit(solution)/shard_map/base_products/pallas_call | solution.py:259
  73.7 4.9 %collective-permute-done.7.rest_2_.rest_3_.rest_5_ = bf16[768,512]{1,0:T(8,128)(2,1)} collective-permute-done((bf16[768,512]{1,0:T(8,128)(2,1)}, bf16[768,512]{1,0:T(8,128)(2,1)}, u32[]{:S(2)}, u32[]{:S(2)}) %collective-permute-start.7) | collective-permute-done | bytes 786464 | tf_op jit(solution)/shard_map/ppermute | solution.py:601
  78.7 2.2 %rank_products.4.rest_2_ = bf16[768,128]{1,0:T(8,128)(2,1)S(1)} custom-call(s32[8,128]{1,0:T(8,128)S(1)} %copy-done.10, bf16[3072,2048]{1,0:T(8,128)(2,1)S(1)} %bitcast.10, bf16[3,2304,128]{2,1,0:T(8,128)(2,1)S(1)} %pack_maps.1.rest_0_.rest_10_.rest_5_, bf16[2,768,512]{2,1,0:T(8,128)(2,1)S(1)} %get-tuple-element.33.rest_1_.a_ref.rest_0_, ...), custom_call_target="tpu_custom_call" | custom-call | flops 4026531 | bytes 47185 | tf_op jit(solution)/shard_map/rank_products/pallas_call | solution.py:412
  82.1 1.7 %collective-permute-start.13 = (bf16[768,512]{1,0:T(8,128)(2,1)}, bf16[768,512]{1,0:T(8,128)(2,1)}, u32[]{:S(2)}, u32[]{:S(2)}) collective-permute-start(bf16[768,512]{1,0:T(8,128)(2,1)} %pair_sum.6.rest_1_), channel_id=1, source_target_pairs={{0,2},{1,3},{2,0},{3,1},{4,6},{5,7},{6,4},{7,5},{8,10},{9,11},{10,... | collective-permute-start | bytes 2359304 | tf_op jit(solution)/shard_map/ppermute | solution.py:601
  83.8 12.1 %base_products.5 = (bf16[768,512]{1,0:T(8,128)(2,1)}, bf16[512,512]{1,0:T(8,128)(2,1)S(1)}, bf16[256,512]{1,0:T(8,128)(2,1)S(1)}, bf16[2,768,512]{2,1,0:T(8,128)(2,1)S(1)}) custom-call(s32[8,128]{1,0:T(8,128)S(1)} %copy-done.10, bf16[3072,2048]{1,0:T(8,128)(2,1)} %x_ref.13, bf16[4,2048,512]{2,1,0:T(8,128)(2,1)} %get-tuple-element.26.rest_0_, ...), custom_call_target="tpu_custom_call" | custom-call | flops 64424508 | bytes 83886 | tf_op jit(solution)/shard_map/base_products/pallas_call | solution.py:259
  95.9 1.6 collective-permute-start.17
  97.5 6.0 %collective-permute-start.18 = (bf16[3,2304,128]{2,1,0:T(8,128)(2,1)}, bf16[3,2304,128]{2,1,0:T(8,128)(2,1)}, u32[]{:S(2)}, u32[]{:S(2)}) collective-permute-start(bf16[3,2304,128]{2,1,0:T(8,128)(2,1)} %get-tuple-element.43.rest_4_.rest_9_.rest_5_.rest_10_), channel_id=1, source_target_pairs={{0,4},{4,8},{8,12},{1,5},{5,9},{9,13},{2,6},{6,10},{10,14},{3,7},{... | collective-permute-start | bytes 5308424 | tf_op jit(solution)/shard_map/ppermute | solution.py:611
  105.8 2.6 %rank_products.5.rest_2_ = bf16[768,128]{1,0:T(8,128)(2,1)S(1)} custom-call(s32[8,128]{1,0:T(8,128)S(1)} %copy-done.10, bf16[3072,2048]{1,0:T(8,128)(2,1)S(1)} %bitcast.12, bf16[3,2304,128]{2,1,0:T(8,128)(2,1)S(1)} %pack_maps.1.rest_0_.rest_10_.rest_5_, bf16[3,2304,128]{2,1,0:T(8,128)(2,1)} %get-tuple-element.40.rest_1_.rest_11_.rest_6_, ...), custom_call_target="tpu_custom_call" | custom-call | flops 4026531 | bytes 47185 | tf_op jit(solution)/shard_map/rank_products/pallas_call | solution.py:412
  110.0 3.0 %rank_products.6 = bf16[768,128]{1,0:T(8,128)(2,1)S(1)} custom-call(s32[8,128]{1,0:T(8,128)S(1)} %copy-done.10, bf16[3072,2048]{1,0:T(8,128)(2,1)S(1)} %bitcast.12, bf16[3,2304,128]{2,1,0:T(8,128)(2,1)S(1)} %pack_maps.1.rest_0_.rest_10_.rest_5_, bf16[3,2304,128]{2,1,0:T(8,128)(2,1)} %get-tuple-element.40.rest_1_.rest_11_.rest_6_, ...), custom_call_target="tpu_custom_call" | custom-call | flops 4026531 | bytes 47185 | tf_op jit(solution)/shard_map/rank_products/pallas_call | solution.py:412
  116.7 4.5 %collective-permute-done.25.rest_7_ = bf16[768,128]{1,0:T(8,128)(2,1)S(1)} collective-permute-done((bf16[768,128]{1,0:T(8,128)(2,1)S(1)}, bf16[768,128]{1,0:T(8,128)(2,1)S(1)}, u32[]{:S(2)}, u32[]{:S(2)}) %collective-permute-start.25) | collective-permute-done | bytes 196640 | tf_op jit(solution)/shard_map/ppermute | solution.py:601
  121.2 4.2 %collective-permute-done.27.rest_9_ = bf16[768,128]{1,0:T(8,128)(2,1)S(1)} collective-permute-done((bf16[768,128]{1,0:T(8,128)(2,1)S(1)}, bf16[768,128]{1,0:T(8,128)(2,1)S(1)}, u32[]{:S(2)}, u32[]{:S(2)}) %collective-permute-start.27) | collective-permute-done | bytes 196640 | tf_op jit(solution)/shard_map/ppermute | solution.py:601
  126.3 7.1 %finish.3.rest_10_ = bf16[6144,2,128]{2,1,0:T(2,128)(2,1)} custom-call(s32[8,128]{1,0:T(8,128)} %plan_requests.1.plan_ref, bf16[2,768,512]{2,1,0:T(8,128)(2,1)} %copy-done.7, bf16[768,512]{1,0:T(8,128)(2,1)} %collective-permute-done.22.rest_1_, bf16[768,512]{1,0:T(8,128)(2,1)} %copy-done.8, bf16[2,768,512]{2,1,0:T(8,128)(2,1)} %copy-done.6, ...), custom_call_target="tpu_custom_call" | custom-call | flops 24159192 | bytes 78643 | tf_op jit(solution)/shard_map/finish/pallas_call | solution.py:569
  133.4 5.5 %finish.4.rest_7_.rest_12_ = bf16[6144,2,128]{2,1,0:T(2,128)(2,1)} custom-call(s32[8,128]{1,0:T(8,128)} %plan_requests.1.plan_ref, bf16[2,768,512]{2,1,0:T(8,128)(2,1)} %copy-done.5, bf16[768,512]{1,0:T(8,128)(2,1)} %copy-done.22, bf16[768,512]{1,0:T(8,128)(2,1)} %collective-permute-done.13.rest_4_.rest_3_.rest_2_, ...), custom_call_target="tpu_custom_call", output_to_operand_aliasing={{}: (11, {})} | custom-call | flops 12079595 | bytes 39321 | tf_op jit(solution)/shard_map/finish/pallas_call | solution.py:569
  141.1 4.6 %copy-done = bf16[3072,2048]{1,0:T(8,128)(2,1)S(1)} copy-done((bf16[3072,2048]{1,0:T(8,128)(2,1)S(1)}, bf16[3072,2048]{1,0:T(8,128)(2,1)}, u32[]{:S(2)}) %copy-start) | copy-done | bytes 12582936
  145.7 1.9 %copy-done.3 = bf16[6144,2,128]{2,1,0:T(2,128)(2,1)S(1)} copy-done((bf16[6144,2,128]{2,1,0:T(2,128)(2,1)S(1)}, bf16[6144,2,128]{2,1,0:T(2,128)(2,1)}, u32[]{:S(2)}) %copy-start.3) | copy-done | bytes 3145752
  147.6 2.9 %rank_products.7 = bf16[768,128]{1,0:T(8,128)(2,1)S(1)} custom-call(s32[8,128]{1,0:T(8,128)S(1)} %copy-done.11, bf16[3072,2048]{1,0:T(8,128)(2,1)S(1)} %copy-done, bf16[3,2304,128]{2,1,0:T(8,128)(2,1)S(1)} %copy-done.2, bf16[3,2304,128]{2,1,0:T(8,128)(2,1)} %get-tuple-element.40.rest_1_.rest_11_.rest_6_, ...), custom_call_target="tpu_custom_call" | custom-call | flops 4026531 | bytes 47185 | tf_op jit(solution)/shard_map/rank_products/pallas_call | solution.py:412
  150.5 1.4 collective-permute-done.28
  152.5 6.5 %collective-permute-done.29.rest_4_ = bf16[768,128]{1,0:T(8,128)(2,1)S(1)} collective-permute-done((bf16[768,128]{1,0:T(8,128)(2,1)S(1)}, bf16[768,128]{1,0:T(8,128)(2,1)S(1)}, u32[]{:S(2)}, u32[]{:S(2)}) %collective-permute-start.29) | collective-permute-done | bytes 196640 | tf_op jit(solution)/shard_map/ppermute | solution.py:601
  159.7 5.0 %finish.5 = bf16[6144,2,128]{2,1,0:T(2,128)(2,1)} custom-call(s32[8,128]{1,0:T(8,128)} %plan_requests.1.plan_ref, bf16[2,768,512]{2,1,0:T(8,128)(2,1)} %copy-done.4, bf16[768,512]{1,0:T(8,128)(2,1)} %copy-done.24, bf16[768,512]{1,0:T(8,128)(2,1)} %copy-done.25, bf16[768,128]{1,0:T(8,128)(2,1)} %copy-done.21, ...), custom_call_target="tpu_custom_call", output_to_operand_aliasing={{}: (13, {})} | custom-call | flops 12079595 | bytes 39321 | tf_op jit(solution)/shard_map/finish/pallas_call | solution.py:569
  (124 shorter events, 19.8 us)
Async XLA Ops:
  2.8 107.2 %copy-start.1 = (bf16[3,2304,128]{2,1,0:T(8,128)(2,1)}, bf16[3,2304,128]{2,1,0:T(8,128)(2,1)S(1)}, u32[]{:S(2)}) copy-start(bf16[3,2304,128]{2,1,0:T(8,128)(2,1)S(1)} %pack_maps.1.rest_0_.rest_10_.rest_5_) | copy-start | bytes 5308420
  2.8 43.6 %collective-permute-start.11 = (bf16[3,2304,128]{2,1,0:T(8,128)(2,1)S(1)}, bf16[3,2304,128]{2,1,0:T(8,128)(2,1)}, u32[]{:S(2)}, u32[]{:S(2)}) collective-permute-start(bf16[3,2304,128]{2,1,0:T(8,128)(2,1)S(1)} %pack_maps.1.rest_0_.rest_10_.rest_5_), channel_id=1, source_target_pairs={{4,0},{8,4},{12,8},{5,1},{9,5},{13,9},{6,2},{10,6},{14,10},{7,3},{... | collective-permute-start | bytes 5308424 | tf_op jit(solution)/shard_map/ppermute | solution.py:608
  4.1 43.4 %collective-permute-start.12 = (bf16[3,2304,128]{2,1,0:T(8,128)(2,1)S(1)}, bf16[3,2304,128]{2,1,0:T(8,128)(2,1)}, u32[]{:S(2)}, u32[]{:S(2)}) collective-permute-start(bf16[3,2304,128]{2,1,0:T(8,128)(2,1)S(1)} %pack_maps.1.rest_0_.rest_10_.rest_5_), channel_id=1, source_target_pairs={{0,4},{4,8},{8,12},{1,5},{5,9},{9,13},{2,6},{6,10},{10,14},{3,7},{... | collective-permute-start | bytes 5308424 | tf_op jit(solution)/shard_map/ppermute | solution.py:611
  30.1 2.4 %collective-permute-start = (bf16[512,512]{1,0:T(8,128)(2,1)S(1)}, bf16[512,512]{1,0:T(8,128)(2,1)S(1)}, u32[]{:S(2)}, u32[]{:S(2)}) collective-permute-start(bf16[512,512]{1,0:T(8,128)(2,1)S(1)} %get-tuple-element.28), channel_id=1, source_target_pairs={{0,1},{1,0},{2,3},{3,2},{4,5},{5,4},{6,7},{7,6},{8,9},{9,8},{10,11... | collective-permute-start | bytes 1572872 | tf_op jit(solution)/shard_map/ppermute | solution.py:598
  31.0 1.5 collective-permute-start.1
  33.0 24.5 %collective-permute-start.4 = (bf16[768,512]{1,0:T(8,128)(2,1)S(1)}, bf16[768,512]{1,0:T(8,128)(2,1)S(1)}, u32[]{:S(2)}, u32[]{:S(2)}) collective-permute-start(bf16[768,512]{1,0:T(8,128)(2,1)S(1)} %pair_sum.4.rest_1_), channel_id=1, source_target_pairs={{0,2},{1,3},{2,0},{3,1},{4,6},{5,7},{6,4},{7,5},{8,10},{9,11},{10,... | collective-permute-start | bytes 2359304 | tf_op jit(solution)/shard_map/ppermute | solution.py:601
  47.5 48.4 %collective-permute-start.15 = (bf16[3,2304,128]{2,1,0:T(8,128)(2,1)}, bf16[3,2304,128]{2,1,0:T(8,128)(2,1)}, u32[]{:S(2)}, u32[]{:S(2)}) collective-permute-start(bf16[3,2304,128]{2,1,0:T(8,128)(2,1)} %get-tuple-element.40.rest_1_.rest_11_.rest_6_), channel_id=1, source_target_pairs={{4,0},{8,4},{12,8},{5,1},{9,5},{13,9},{6,2},{10,6},{14,10},{7,3},{... | collective-permute-start | bytes 5308424 | tf_op jit(solution)/shard_map/ppermute | solution.py:608
  48.8 47.1 %collective-permute-start.16 = (bf16[3,2304,128]{2,1,0:T(8,128)(2,1)}, bf16[3,2304,128]{2,1,0:T(8,128)(2,1)}, u32[]{:S(2)}, u32[]{:S(2)}) collective-permute-start(bf16[3,2304,128]{2,1,0:T(8,128)(2,1)} %get-tuple-element.41.rest_2_.rest_3_.rest_12_.rest_8_.rest_4_.rest_9_), channel_id=1, source_target_pairs={{0,4},{4,8},{8,12},{1,5},{5,9},{9,13},{2,6},{6,10},{10,14},{3,7},{... | collective-permute-start | bytes 5308424 | tf_op jit(solution)/shard_map/ppermute | solution.py:611
  55.2 2.3 %collective-permute-start.2 = (bf16[512,512]{1,0:T(8,128)(2,1)S(1)}, bf16[512,512]{1,0:T(8,128)(2,1)S(1)}, u32[]{:S(2)}, u32[]{:S(2)}) collective-permute-start(bf16[512,512]{1,0:T(8,128)(2,1)S(1)} %get-tuple-element.31), channel_id=1, source_target_pairs={{0,1},{1,0},{2,3},{3,2},{4,5},{5,4},{6,7},{7,6},{8,9},{9,8},{10,11... | collective-permute-start | bytes 1572872 | tf_op jit(solution)/shard_map/ppermute | solution.py:598
  55.2 2.3 %collective-permute-start.3 = (bf16[256,512]{1,0:T(8,128)(2,1)S(1)}, bf16[256,512]{1,0:T(8,128)(2,1)S(1)}, u32[]{:S(2)}, u32[]{:S(2)}) collective-permute-start(bf16[256,512]{1,0:T(8,128)(2,1)S(1)} %get-tuple-element.32), channel_id=1, source_target_pairs={{0,1},{1,0},{2,3},{3,2},{4,5},{5,4},{6,7},{7,6},{8,9},{9,8},{10,11... | collective-permute-start | bytes 786440 | tf_op jit(solution)/shard_map/ppermute | solution.py:598
  58.7 19.9 %collective-permute-start.7 = (bf16[768,512]{1,0:T(8,128)(2,1)}, bf16[768,512]{1,0:T(8,128)(2,1)}, u32[]{:S(2)}, u32[]{:S(2)}) collective-permute-start(bf16[768,512]{1,0:T(8,128)(2,1)} %pair_sum.5.rest_1_), channel_id=1, source_target_pairs={{0,2},{1,3},{2,0},{3,1},{4,6},{5,7},{6,4},{7,5},{8,10},{9,11},{10,... | collective-permute-start | bytes 2359304 | tf_op jit(solution)/shard_map/ppermute | solution.py:601
  73.1 7.8 %collective-permute-start.5 = (bf16[512,512]{1,0:T(8,128)(2,1)S(1)}, bf16[512,512]{1,0:T(8,128)(2,1)S(1)}, u32[]{:S(2)}, u32[]{:S(2)}) collective-permute-start(bf16[512,512]{1,0:T(8,128)(2,1)S(1)} %get-tuple-element.34), channel_id=1, source_target_pairs={{0,1},{1,0},{2,3},{3,2},{4,5},{5,4},{6,7},{7,6},{8,9},{9,8},{10,11... | collective-permute-start | bytes 1572872 | tf_op jit(solution)/shard_map/ppermute | solution.py:598
  73.2 30.5 %collective-permute-start.22 = (bf16[768,512]{1,0:T(8,128)(2,1)}, bf16[768,512]{1,0:T(8,128)(2,1)}, u32[]{:S(2)}, u32[]{:S(2)}) collective-permute-start(bf16[768,512]{1,0:T(8,128)(2,1)} %copy-done.15), channel_id=1, source_target_pairs={{0,1},{1,0},{2,3},{3,2},{4,5},{5,4},{6,7},{7,6},{8,9},{9,8},{10,11... | collective-permute-start | bytes 2359304 | tf_op jit(solution)/shard_map/ppermute | solution.py:598
  78.6 2.3 %collective-permute-start.6 = (bf16[256,512]{1,0:T(8,128)(2,1)S(1)}, bf16[256,512]{1,0:T(8,128)(2,1)S(1)}, u32[]{:S(2)}, u32[]{:S(2)}) collective-permute-start(bf16[256,512]{1,0:T(8,128)(2,1)S(1)} %get-tuple-element.35), channel_id=1, source_target_pairs={{0,1},{1,0},{2,3},{3,2},{4,5},{5,4},{6,7},{7,6},{8,9},{9,8},{10,11... | collective-permute-start | bytes 786440 | tf_op jit(solution)/shard_map/ppermute | solution.py:598
  80.9 24.9 %slice-start.3 = ((s8[12582912]{0:T(1024)(128)(4,1)}), s8[4194304]{0:T(1024)(128)(4,1)S(1)}, s32[]{:S(2)}) async-start(s8[12582912]{0:T(1024)(128)(4,1)} %bitcast.11), calls=%async_computation.3 | async-start | bytes 8388608
  82.1 23.4 %collective-permute-start.13 = (bf16[768,512]{1,0:T(8,128)(2,1)}, bf16[768,512]{1,0:T(8,128)(2,1)}, u32[]{:S(2)}, u32[]{:S(2)}) collective-permute-start(bf16[768,512]{1,0:T(8,128)(2,1)} %pair_sum.6.rest_1_), channel_id=1, source_target_pairs={{0,2},{1,3},{2,0},{3,1},{4,6},{5,7},{6,4},{7,5},{8,10},{9,11},{10,... | collective-permute-start | bytes 2359304 | tf_op jit(solution)/shard_map/ppermute | solution.py:601
  95.9 44.0 %collective-permute-start.17 = (bf16[3,2304,128]{2,1,0:T(8,128)(2,1)}, bf16[3,2304,128]{2,1,0:T(8,128)(2,1)}, u32[]{:S(2)}, u32[]{:S(2)}) collective-permute-start(bf16[3,2304,128]{2,1,0:T(8,128)(2,1)} %get-tuple-element.42.rest_2_.rest_7_), channel_id=1, source_target_pairs={{4,0},{8,4},{12,8},{5,1},{9,5},{13,9},{6,2},{10,6},{14,10},{7,3},{... | collective-permute-start | bytes 5308424 | tf_op jit(solution)/shard_map/ppermute | solution.py:608
  97.5 43.6 %collective-permute-start.18 = (bf16[3,2304,128]{2,1,0:T(8,128)(2,1)}, bf16[3,2304,128]{2,1,0:T(8,128)(2,1)}, u32[]{:S(2)}, u32[]{:S(2)}) collective-permute-start(bf16[3,2304,128]{2,1,0:T(8,128)(2,1)} %get-tuple-element.43.rest_4_.rest_9_.rest_5_.rest_10_), channel_id=1, source_target_pairs={{0,4},{4,8},{8,12},{1,5},{5,9},{9,13},{2,6},{6,10},{10,14},{3,7},{... | collective-permute-start | bytes 5308424 | tf_op jit(solution)/shard_map/ppermute | solution.py:611
  103.5 1.4 collective-permute-start.24
  103.7 1.6 collective-permute-start.10
  104.9 3.5 %collective-permute-start.9 = (bf16[512,512]{1,0:T(8,128)(2,1)S(1)}, bf16[512,512]{1,0:T(8,128)(2,1)S(1)}, u32[]{:S(2)}, u32[]{:S(2)}) collective-permute-start(bf16[512,512]{1,0:T(8,128)(2,1)S(1)} %get-tuple-element.38), channel_id=1, source_target_pairs={{0,1},{1,0},{2,3},{3,2},{4,5},{5,4},{6,7},{7,6},{8,9},{9,8},{10,11... | collective-permute-start | bytes 1572872 | tf_op jit(solution)/shard_map/ppermute | solution.py:598
  105.3 8.1 %collective-permute-start.23 = (bf16[768,512]{1,0:T(8,128)(2,1)S(1)}, bf16[768,512]{1,0:T(8,128)(2,1)S(1)}, u32[]{:S(2)}, u32[]{:S(2)}) collective-permute-start(bf16[768,512]{1,0:T(8,128)(2,1)S(1)} %copy-done.14), channel_id=1, source_target_pairs={{0,1},{1,0},{2,3},{3,2},{4,5},{5,4},{6,7},{7,6},{8,9},{9,8},{10,11... | collective-permute-start | bytes 2359304 | tf_op jit(solution)/shard_map/ppermute | solution.py:598
  105.5 10.1 %collective-permute-start.19 = (bf16[768,512]{1,0:T(8,128)(2,1)S(1)}, bf16[768,512]{1,0:T(8,128)(2,1)S(1)}, u32[]{:S(2)}, u32[]{:S(2)}) collective-permute-start(bf16[768,512]{1,0:T(8,128)(2,1)S(1)} %copy-done.17), channel_id=1, source_target_pairs={{0,1},{1,0},{2,3},{3,2},{4,5},{5,4},{6,7},{7,6},{8,9},{9,8},{10,11... | collective-permute-start | bytes 2359304 | tf_op jit(solution)/shard_map/ppermute | solution.py:598
  108.4 4.6 %collective-permute-start.26 = (bf16[768,128]{1,0:T(8,128)(2,1)S(1)}, bf16[768,128]{1,0:T(8,128)(2,1)S(1)}, u32[]{:S(2)}, u32[]{:S(2)}) collective-permute-start(bf16[768,128]{1,0:T(8,128)(2,1)S(1)} %rank_products.5.rest_2_), channel_id=1, source_target_pairs={{0,1},{1,0},{2,3},{3,2},{4,5},{5,4},{6,7},{7,6},{8,9},{9,8},{10,11... | collective-permute-start | bytes 589832 | tf_op jit(solution)/shard_map/ppermute | solution.py:598
  113.0 1.5 collective-permute-start.20
  113.4 7.8 %collective-permute-start.25 = (bf16[768,128]{1,0:T(8,128)(2,1)S(1)}, bf16[768,128]{1,0:T(8,128)(2,1)S(1)}, u32[]{:S(2)}, u32[]{:S(2)}) collective-permute-start(bf16[768,128]{1,0:T(8,128)(2,1)S(1)} %add_convert_fusion.2.rest_6_), channel_id=1, source_target_pairs={{0,2},{1,3},{2,0},{3,1},{4,6},{5,7},{6,4},{7,5},{8,10},{9,11},{10,... | collective-permute-start | bytes 589832 | tf_op jit(solution)/shard_map/ppermute | solution.py:601
  114.5 10.9 %collective-permute-start.27 = (bf16[768,128]{1,0:T(8,128)(2,1)S(1)}, bf16[768,128]{1,0:T(8,128)(2,1)S(1)}, u32[]{:S(2)}, u32[]{:S(2)}) collective-permute-start(bf16[768,128]{1,0:T(8,128)(2,1)S(1)} %add_convert_fusion.1.rest_8_), channel_id=1, source_target_pairs={{0,2},{1,3},{2,0},{3,1},{4,6},{5,7},{6,4},{7,5},{8,10},{9,11},{10,... | collective-permute-start | bytes 589832 | tf_op jit(solution)/shard_map/ppermute | solution.py:601
  115.6 17.8 %collective-permute-start.21 = (bf16[768,128]{1,0:T(8,128)(2,1)S(1)}, bf16[768,128]{1,0:T(8,128)(2,1)}, u32[]{:S(2)}, u32[]{:S(2)}) collective-permute-start(bf16[768,128]{1,0:T(8,128)(2,1)S(1)} %add_convert_fusion.3.rest_3_), channel_id=1, source_target_pairs={{0,2},{1,3},{2,0},{3,1},{4,6},{5,7},{6,4},{7,5},{8,10},{9,11},{10,... | collective-permute-start | bytes 589832 | tf_op jit(solution)/shard_map/ppermute | solution.py:601
  121.2 31.2 %collective-permute-start.8 = (bf16[768,512]{1,0:T(8,128)(2,1)}, bf16[768,512]{1,0:T(8,128)(2,1)S(1)}, u32[]{:S(2)}, u32[]{:S(2)}) collective-permute-start(bf16[768,512]{1,0:T(8,128)(2,1)} %get-tuple-element.37), channel_id=1, source_target_pairs={{0,1},{1,0},{2,3},{3,2},{4,5},{5,4},{6,7},{7,6},{8,9},{9,8},{10,11... | collective-permute-start | bytes 2359304 | tf_op jit(solution)/shard_map/ppermute | solution.py:598
  125.5 27.0 %collective-permute-start.14 = (bf16[768,512]{1,0:T(8,128)(2,1)}, bf16[768,512]{1,0:T(8,128)(2,1)S(1)}, u32[]{:S(2)}, u32[]{:S(2)}) collective-permute-start(bf16[768,512]{1,0:T(8,128)(2,1)} %pair_sum.7.rest_5_), channel_id=1, source_target_pairs={{0,2},{1,3},{2,0},{3,1},{4,6},{5,7},{6,4},{7,5},{8,10},{9,11},{10,... | collective-permute-start | bytes 2359304 | tf_op jit(solution)/shard_map/ppermute | solution.py:601
  150.4 1.5 collective-permute-start.28
  152.0 7.0 %collective-permute-start.29 = (bf16[768,128]{1,0:T(8,128)(2,1)S(1)}, bf16[768,128]{1,0:T(8,128)(2,1)S(1)}, u32[]{:S(2)}, u32[]{:S(2)}) collective-permute-start(bf16[768,128]{1,0:T(8,128)(2,1)S(1)} %add_convert_fusion.rest_3_), channel_id=1, source_target_pairs={{0,2},{1,3},{2,0},{3,1},{4,6},{5,7},{6,4},{7,5},{8,10},{9,11},{10,... | collective-permute-start | bytes 589832 | tf_op jit(solution)/shard_map/ppermute | solution.py:601
  (33 other events, 288.9 us)

commit v7 on v6

--- a/solution.py
+++ b/solution.py
@@ -7,7 +7,7 @@
 
 BF = jnp.bfloat16
 F32 = jnp.float32
-BASE_CHUNKS = (3, 3, 3, 3)
+BASE_CHUNKS = (3, 3, 4, 2)
 RANK_CHUNKS = 4
 SMEM = pltpu.SMEM
 PIECE = 2
@@ -18,6 +18,7 @@
 
 
 ANY = pl.BlockSpec(memory_space=pl.ANY)
+HBM = pl.BlockSpec(memory_space=pltpu.HBM)
 
 
 def cost(flops, moved):
@@ -67,7 +68,7 @@
         body,
         out_shape=jax.ShapeDtypeStruct((stored, features + tiles * part, lanes), BF),
         in_specs=[pl.BlockSpec(memory_space=pltpu.VMEM)] * 2,
-        out_specs=ANY,
+        out_specs=HBM,
         scratch_shapes=[
             pltpu.VMEM((stored, tiles * part, lanes), BF),
             pltpu.SemaphoreType.DMA((2, stored)),
@@ -341,8 +342,8 @@
     return pl.pallas_call(
         body,
         out_shape=[jax.ShapeDtypeStruct(a.shape, a.dtype) for a in arrays],
-        in_specs=[ANY] * (n + len(after)),
-        out_specs=[ANY] * n,
+        in_specs=[HBM] * (n + len(after)),
+        out_specs=[HBM] * n,
         input_output_aliases={i: i for i in range(n)},
         compiler_params=params(8),
         cost_estimate=cost(0, 1 << 20),
@@ -415,7 +416,7 @@
         grid_spec=pltpu.PrefetchScalarGridSpec(
             num_scalar_prefetch=1,
             grid=(),
-            in_specs=[ANY] * (1 + n_map + n_after),
+            in_specs=[HBM] * (1 + n_map + n_after),
             out_specs=pl.BlockSpec(memory_space=pltpu.VMEM),
             scratch_shapes=[
                 pltpu.VMEM((count, prefill, features), BF),
@@ -448,7 +449,8 @@
                 refs.append((start, n, rest[: len(arrays)]))
                 rest = rest[len(arrays) :]
         map_refs = list(zip(sources, rest[:n_map]))
-        o_ref, ups, base_rows, rank_rows, out_rows, sems, out_sems = rest[-7:]
+        o_ref, token_ref, ups, base_rows, rank_rows, out_rows, sems, out_sems = rest[-8:]
+        token_ref[...] = jnp.zeros_like(token_ref)
 
         def start_pieces(refs, at, rows, sem):
             copies = []
@@ -568,12 +570,15 @@
         operands.append(before)
     return pl.pallas_call(
         body,
-        out_shape=jax.ShapeDtypeStruct((shape[0] * tiles, 2, lanes), BF),
+        out_shape=(
+            jax.ShapeDtypeStruct((shape[0] * tiles, 2, lanes), BF),
+            jax.ShapeDtypeStruct((8, 128), F32),
+        ),
         grid_spec=pltpu.PrefetchScalarGridSpec(
             num_scalar_prefetch=1,
             grid=(),
-            in_specs=[ANY] * (len(operands) - 1),
-            out_specs=ANY,
+            in_specs=[HBM] * (len(operands) - 1),
+            out_specs=(HBM, pl.BlockSpec(memory_space=pltpu.VMEM)),
             scratch_shapes=[
                 pltpu.VMEM((count, extra, lanes), BF),
                 pltpu.VMEM((count, n_base, prefill, 2 * columns), BF),
@@ -584,7 +589,7 @@
             ],
         ),
         input_output_aliases=aliases,
-        compiler_params=params(60),
+        compiler_params=params(24),
         cost_estimate=cost(12 * count * prefill * prefill * 2 * columns, 20 * count * prefill * columns),
         name="finish",
     )(*operands)
@@ -713,10 +718,10 @@
         send_on(*fourth, [part, bases[2][2][-1]])
         for chunk in range(len(ranks), 3):
             part = rank(chunk, [pairs[-1]])
-        out = write(None, 0, 2)
-        out = write(out, 2, 3)
-        rank(3, [out])
-        out = write(out, 3, 4)
+        out, _ = write(None, 0, 2)
+        out, written = write(out, 2, 3)
+        rank(3, [written])
+        out, _ = write(out, 3, 4)
         tiles = out.shape[0] // shape[0]
         out = out.reshape(shape[0], tiles, 2, columns // tiles)
         return out.transpose(0, 2, 1, 3).reshape(shape)

time: 166 us -> 171 us (1.030)
  waiting for transfers between devices: 32.1 us -> 36.7 us
  starting transfers between devices: 35.8 us -> 38.1 us
  local copies, waits for them, and re-layouts: 11.2 us -> 9.14 us
    ppermute x8, waiting for transfers between devices: 20.2 us -> 30.6 us  [chip_shift(): lax.ppermute(a, 'tensor', [(2 * x + c, 2 * ((x + k) % n_x) + c) for x in...]
    ppermute x3, waiting for transfers between devices: 3.56 us -> 0.01 us  [leftward(): return lax.ppermute(a, 'adapter', [(z, z - hops) for z in range(hops, n_z)])]
    ppermute x8, starting transfers between devices: 9.56 us -> 12.7 us  [chip_shift(): lax.ppermute(a, 'tensor', [(2 * x + c, 2 * ((x + k) % n_x) + c) for x in...]
    unnamed x70 -> x60, local copies, waits for them, and re-layouts: 11.2 us -> 9.14 us
    ppermute x16 -> x15, waiting for transfers between devices: 6.11 us -> 5.26 us  [core_swap(): return lax.ppermute(a, 'tensor', [(t, t ^ 1) for t in range(n_t)])]
    ppermute x16 -> x15, starting transfers between devices: 3.03 us -> 3.45 us  [core_swap(): return lax.ppermute(a, 'tensor', [(t, t ^ 1) for t in range(n_t)])]
  transfers between devices with their start and end apart: 30 -> 29, of which waited for: 14 -> 10; matrix products, arithmetic and copies ran while one was open for 0% -> 0% of each run, Pallas kernels for 48% -> 46%
where the time goes in v7:
time: 171 us
  Pallas kernels  85.9 us (50%)
  starting transfers between devices  38.1 us (22%)
  waiting for transfers between devices  36.7 us (21%)
  local copies, waits for them, and re-layouts  9.14 us (5%)
    pallas_call x3, Pallas kernels, base_products(): pl.pallas_call(body, out_shape=(*[jax.ShapeDtypeStruct((n * prefill, widt...  34 us
    ppermute x8, waiting for transfers between devices, chip_shift(): lax.ppermute(a, 'tensor', [(2 * x + c, 2 * ((x + k) % n_x) + c) for x in...  30.6 us
    pallas_call x3, Pallas kernels, finish(): pl.pallas_call(body, out_shape=(jax.ShapeDtypeStruct((shape[0] * tiles, 2...  19.2 us
    ppermute x3, starting transfers between devices, rightward(): return lax.ppermute(a, 'adapter', [(z - hops, z) for z in range(hops, n_z)])  17.8 us
    pallas_call x1, Pallas kernels, split_weight(): pl.pallas_call(body, out_shape=(jax.ShapeDtypeStruct((n_t, features, 2 *...  16.9 us
    ppermute x8, starting transfers between devices, chip_shift(): lax.ppermute(a, 'tensor', [(2 * x + c, 2 * ((x + k) % n_x) + c) for x in...  12.7 us
    pallas_call x4, Pallas kernels, rank_products(): pl.pallas_call(body, out_shape=jax.ShapeDtypeStruct((count * prefill, ran...  10.7 us
    unnamed x60, local copies, waits for them, and re-layouts  9.14 us
  transfers between devices with their start and end apart: 29, of which 10 were waited for; matrix products, arithmetic and copies ran while one was open for 0% of the time, Pallas kernels for 46%

profile of v7, /device:TPU:0, one launch (start us, length us, event | category | flops | bytes accessed | tf_op | source)
XLA Modules:
  0.0 170.9 jit_solution(16434740258335323663)
XLA Ops:
  4.1 6.8 %collective-permute-start.13 = (bf16[3,2304,128]{2,1,0:T(8,128)(2,1)S(1)}, bf16[3,2304,128]{2,1,0:T(8,128)(2,1)}, u32[]{:S(2)}, u32[]{:S(2)}) collective-permute-start(bf16[3,2304,128]{2,1,0:T(8,128)(2,1)S(1)} %pack_maps.1.rest_0_.rest_10_.rest_5_.rest_8_), channel_id=1, source_target_pairs={{0,4},{4,8},{8,12},{1,5},{5,9},{9,13},{2,6},{6,10},{10,14},{3,7},{... | collective-permute-start | bytes 5308424 | tf_op jit(solution)/shard_map/ppermute | solution.py:616
  10.9 1.6 plan_requests.1.plan_ref
  13.1 16.9 %split_weight.1 = (bf16[4,2048,512]{2,1,0:T(8,128)(2,1)}, bf16[768,512]{1,0:T(8,128)(2,1)S(1)}, bf16[512,512]{1,0:T(8,128)(2,1)S(1)}, bf16[256,512]{1,0:T(8,128)(2,1)S(1)}, bf16[2,768,512]{2,1,0:T(8,128)(2,1)S(1)}) custom-call(s32[8,128]{1,0:T(8,128)S(1)} %copy-done.15, s32[4]{0:T(128)S(1)} %compare_select_fusion.2.slot_ref, bf16[3072,2048]{1,0:T(8,128)(2,1)} %x_ref.13, ...), custom_call_target="tpu_custom_call" | custom-call | flops 64424508 | bytes 167772 | tf_op jit(solution)/shard_map/split_weight/pallas_call | solution.py:184
  31.4 1.8 %collective-permute-done.1.rest_1_ = bf16[256,512]{1,0:T(8,128)(2,1)S(1)} collective-permute-done((bf16[256,512]{1,0:T(8,128)(2,1)S(1)}, bf16[256,512]{1,0:T(8,128)(2,1)S(1)}, u32[]{:S(2)}, u32[]{:S(2)}) %collective-permute-start.1) | collective-permute-done | bytes 262176 | tf_op jit(solution)/shard_map/ppermute | solution.py:603
  33.6 2.0 %collective-permute-start.4 = (bf16[768,512]{1,0:T(8,128)(2,1)S(1)}, bf16[768,512]{1,0:T(8,128)(2,1)S(1)}, u32[]{:S(2)}, u32[]{:S(2)}) collective-permute-start(bf16[768,512]{1,0:T(8,128)(2,1)S(1)} %pair_sum.4.rest_1_), channel_id=1, source_target_pairs={{0,2},{1,3},{2,0},{3,1},{4,6},{5,7},{6,4},{7,5},{8,10},{9,11},{10,... | collective-permute-start | bytes 2359304 | tf_op jit(solution)/shard_map/ppermute | solution.py:606
  35.6 11.0 %base_products.3 = (bf16[768,512]{1,0:T(8,128)(2,1)S(1)}, bf16[512,512]{1,0:T(8,128)(2,1)S(1)}, bf16[256,512]{1,0:T(8,128)(2,1)S(1)}, bf16[2,768,512]{2,1,0:T(8,128)(2,1)S(1)}) custom-call(s32[8,128]{1,0:T(8,128)S(1)} %copy-done.15, bf16[3072,2048]{1,0:T(8,128)(2,1)} %x_ref.13, bf16[4,2048,512]{2,1,0:T(8,128)(2,1)} %get-tuple-element.29.rest_0_, ...), custom_call_target="tpu_custom_call" | custom-call | flops 64424508 | bytes 83886 | tf_op jit(solution)/shard_map/base_products/pallas_call | solution.py:260
  48.8 6.4 %collective-permute-start.16 = (bf16[3,2304,128]{2,1,0:T(8,128)(2,1)}, bf16[3,2304,128]{2,1,0:T(8,128)(2,1)}, u32[]{:S(2)}, u32[]{:S(2)}) collective-permute-start(bf16[3,2304,128]{2,1,0:T(8,128)(2,1)} %get-tuple-element.44.rest_2_.rest_3_.rest_12_.rest_8_.rest_4_), channel_id=1, source_target_pairs={{0,4},{4,8},{8,12},{1,5},{5,9},{9,13},{2,6},{6,10},{10,14},{3,7},{... | collective-permute-start | bytes 5308424 | tf_op jit(solution)/shard_map/ppermute | solution.py:616
  55.7 1.8 %collective-permute-done.3.rest_1_ = bf16[256,512]{1,0:T(8,128)(2,1)S(1)} collective-permute-done((bf16[256,512]{1,0:T(8,128)(2,1)S(1)}, bf16[256,512]{1,0:T(8,128)(2,1)S(1)}, u32[]{:S(2)}, u32[]{:S(2)}) %collective-permute-start.3) | collective-permute-done | bytes 262176 | tf_op jit(solution)/shard_map/ppermute | solution.py:603
  58.7 1.7 %collective-permute-start.8 = (bf16[768,512]{1,0:T(8,128)(2,1)}, bf16[768,512]{1,0:T(8,128)(2,1)S(1)}, u32[]{:S(2)}, u32[]{:S(2)}) collective-permute-start(bf16[768,512]{1,0:T(8,128)(2,1)} %pair_sum.5.rest_1_), channel_id=1, source_target_pairs={{0,2},{1,3},{2,0},{3,1},{4,6},{5,7},{6,4},{7,5},{8,10},{9,11},{10,... | collective-permute-start | bytes 2359304 | tf_op jit(solution)/shard_map/ppermute | solution.py:606
  60.4 14.3 %base_products.4 = (bf16[1024,512]{1,0:T(8,128)(2,1)S(1)}, bf16[512,512]{1,0:T(8,128)(2,1)S(1)}, bf16[512,512]{1,0:T(8,128)(2,1)S(1)}, bf16[2,1024,512]{2,1,0:T(8,128)(2,1)S(1)}) custom-call(s32[8,128]{1,0:T(8,128)S(1)} %copy-done.15, bf16[3072,2048]{1,0:T(8,128)(2,1)} %x_ref.13, bf16[4,2048,512]{2,1,0:T(8,128)(2,1)} %get-tuple-element.29.rest_0_, ...), custom_call_target="tpu_custom_call" | custom-call | flops 85899344 | bytes 83886 | tf_op jit(solution)/shard_map/base_products/pallas_call | solution.py:260
  78.6 1.7 %copy-done.1 = bf16[3,2304,128]{2,1,0:T(8,128)(2,1)S(1)} copy-done((bf16[3,2304,128]{2,1,0:T(8,128)(2,1)S(1)}, bf16[3,2304,128]{2,1,0:T(8,128)(2,1)}, u32[]{:S(2)}) %copy-start.1) | copy-done | bytes 1769496
  80.3 2.5 %rank_products.4.rest_2_ = bf16[768,128]{1,0:T(8,128)(2,1)S(1)} custom-call(s32[8,128]{1,0:T(8,128)S(1)} %copy-done.15, bf16[3072,2048]{1,0:T(8,128)(2,1)S(1)} %bitcast.10, bf16[3,2304,128]{2,1,0:T(8,128)(2,1)S(1)} %copy-done.1, bf16[2,1024,512]{2,1,0:T(8,128)(2,1)S(1)} %get-tuple-element.36.rest_1_.a_ref.rest_0_, ...), custom_call_target="tpu_custom_call" | custom-call | flops 4026531 | bytes 47185 | tf_op jit(solution)/shard_map/rank_products/pallas_call | solution.py:413
  82.9 1.6 copy-done.4
  85.8 1.7 %collective-permute-start.9 = (bf16[1024,512]{1,0:T(8,128)(2,1)}, bf16[1024,512]{1,0:T(8,128)(2,1)S(1)}, u32[]{:S(2)}, u32[]{:S(2)}) collective-permute-start(bf16[1024,512]{1,0:T(8,128)(2,1)} %pair_sum.6.rest_1_), channel_id=1, source_target_pairs={{0,2},{1,3},{2,0},{3,1},{4,6},{5,7},{6,4},{7,5},{8,10},{9,11},{10,... | collective-permute-start | bytes 3145736 | tf_op jit(solution)/shard_map/ppermute | solution.py:606
  87.5 8.8 %base_products.5 = (bf16[512,512]{1,0:T(8,128)(2,1)S(1)}, bf16[512,512]{1,0:T(8,128)(2,1)S(1)}, bf16[2,512,512]{2,1,0:T(8,128)(2,1)S(1)}) custom-call(s32[8,128]{1,0:T(8,128)S(1)} %copy-done.15, bf16[3072,2048]{1,0:T(8,128)(2,1)} %x_ref.13, bf16[4,2048,512]{2,1,0:T(8,128)(2,1)} %get-tuple-element.29.rest_0_, bf16[1024,512]{1,0:T(8,128)(2,1)} %pair_sum.6.rest_1_), custom_call_target="tpu_custom_call" | custom-call | flops 42949672 | bytes 83886 | tf_op jit(solution)/shard_map/base_products/pallas_call | solution.py:260
  96.3 1.6 collective-permute-start.17
  97.9 4.7 %collective-permute-start.18 = (bf16[3,2304,128]{2,1,0:T(8,128)(2,1)}, bf16[3,2304,128]{2,1,0:T(8,128)(2,1)S(1)}, u32[]{:S(2)}, u32[]{:S(2)}) collective-permute-start(bf16[3,2304,128]{2,1,0:T(8,128)(2,1)} %get-tuple-element.46.rest_4_.rest_9_.rest_5_.rest_13_), channel_id=1, source_target_pairs={{0,4},{4,8},{8,12},{1,5},{5,9},{9,13},{2,6},{6,10},{10,14},{3,7},{... | collective-permute-start | bytes 5308424 | tf_op jit(solution)/shard_map/ppermute | solution.py:616
  103.2 1.7 collective-permute-done.23
  105.0 6.4 %collective-permute-done.9.rest_4_.rest_2_ = bf16[1024,512]{1,0:T(8,128)(2,1)S(1)} collective-permute-done((bf16[1024,512]{1,0:T(8,128)(2,1)}, bf16[1024,512]{1,0:T(8,128)(2,1)S(1)}, u32[]{:S(2)}, u32[]{:S(2)}) %collective-permute-start.9) | collective-permute-done | bytes 1048608 | tf_op jit(solution)/shard_map/ppermute | solution.py:606
  111.4 2.9 %rank_products.5.rest_1_ = bf16[768,128]{1,0:T(8,128)(2,1)S(1)} custom-call(s32[8,128]{1,0:T(8,128)S(1)} %copy-done.16, bf16[3072,2048]{1,0:T(8,128)(2,1)S(1)} %bitcast.12, bf16[3,2304,128]{2,1,0:T(8,128)(2,1)S(1)} %copy-done.2, bf16[3,2304,128]{2,1,0:T(8,128)(2,1)} %get-tuple-element.43.rest_1_.rest_11_.rest_6_.rest_9_, ...), custom_call_target="tpu_custom_call" | custom-call | flops 4026531 | bytes 47185 | tf_op jit(solution)/shard_map/rank_products/pallas_call | solution.py:413
  115.2 3.2 %rank_products.6 = bf16[768,128]{1,0:T(8,128)(2,1)S(1)} custom-call(s32[8,128]{1,0:T(8,128)S(1)} %copy-done.16, bf16[3072,2048]{1,0:T(8,128)(2,1)S(1)} %bitcast.12, bf16[3,2304,128]{2,1,0:T(8,128)(2,1)S(1)} %copy-done.2, bf16[3,2304,128]{2,1,0:T(8,128)(2,1)} %get-tuple-element.43.rest_1_.rest_11_.rest_6_.rest_9_, ...), custom_call_target="tpu_custom_call" | custom-call | flops 4026531 | bytes 47185 | tf_op jit(solution)/shard_map/rank_products/pallas_call | solution.py:413
  118.5 1.7 %collective-permute-start.24 = (bf16[768,128]{1,0:T(8,128)(2,1)S(1)}, bf16[768,128]{1,0:T(8,128)(2,1)S(1)}, u32[]{:S(2)}, u32[]{:S(2)}) collective-permute-start(bf16[768,128]{1,0:T(8,128)(2,1)S(1)} %add_convert_fusion.2.rest_6_), channel_id=1, source_target_pairs={{0,2},{1,3},{2,0},{3,1},{4,6},{5,7},{6,4},{7,5},{8,10},{9,11},{10,... | collective-permute-start | bytes 589832 | tf_op jit(solution)/shard_map/ppermute | solution.py:606
  121.6 4.7 %collective-permute-done.24.rest_7_ = bf16[768,128]{1,0:T(8,128)(2,1)S(1)} collective-permute-done((bf16[768,128]{1,0:T(8,128)(2,1)S(1)}, bf16[768,128]{1,0:T(8,128)(2,1)S(1)}, u32[]{:S(2)}, u32[]{:S(2)}) %collective-permute-start.24) | collective-permute-done | bytes 196640 | tf_op jit(solution)/shard_map/ppermute | solution.py:606
  126.3 1.6 collective-permute-start.20
  128.0 2.6 %collective-permute-done.26.rest_9_ = bf16[768,128]{1,0:T(8,128)(2,1)S(1)} collective-permute-done((bf16[768,128]{1,0:T(8,128)(2,1)S(1)}, bf16[768,128]{1,0:T(8,128)(2,1)S(1)}, u32[]{:S(2)}, u32[]{:S(2)}) %collective-permute-start.26) | collective-permute-done | bytes 196640 | tf_op jit(solution)/shard_map/ppermute | solution.py:606
  130.6 9.0 %finish.3 = (bf16[6144,2,128]{2,1,0:T(2,128)(2,1)}, f32[8,128]{1,0:T(8,128)}) custom-call(s32[8,128]{1,0:T(8,128)S(1)} %copy-done.16, bf16[2,768,512]{2,1,0:T(8,128)(2,1)S(1)} %copy-done.11, bf16[768,512]{1,0:T(8,128)(2,1)} %collective-permute-done.21.rest_1_, bf16[768,512]{1,0:T(8,128)(2,1)S(1)} %copy-done.13, bf16[2,768,512]{2,1,0:T(8,128)(2,1)S(1)} %copy-done.7, ...), custom_call_target="tpu_custom_call" | custom-call | flops 24159192 | bytes 78643 | tf_op jit(solution)/shard_map/finish/pallas_call | solution.py:571
  139.6 4.8 %finish.4 = (bf16[6144,2,128]{2,1,0:T(2,128)(2,1)}, f32[8,128]{1,0:T(8,128)S(1)}) custom-call(s32[8,128]{1,0:T(8,128)S(1)} %copy-done.16, bf16[2,1024,512]{2,1,0:T(8,128)(2,1)S(1)} %copy-done.5, bf16[1024,512]{1,0:T(8,128)(2,1)S(1)} %collective-permute-done.5.rest_1_, ...), custom_call_target="tpu_custom_call", output_to_operand_aliasing={{0}: (11, {})} | custom-call | flops 12079595 | bytes 39321 | tf_op jit(solution)/shard_map/finish/pallas_call | solution.py:571
  144.4 2.2 %rank_products.7 = bf16[768,128]{1,0:T(8,128)(2,1)S(1)} custom-call(s32[8,128]{1,0:T(8,128)S(1)} %copy-done.16, bf16[3072,2048]{1,0:T(8,128)(2,1)S(1)} %bitcast.12, bf16[3,2304,128]{2,1,0:T(8,128)(2,1)S(1)} %copy-done.2, bf16[3,2304,128]{2,1,0:T(8,128)(2,1)} %get-tuple-element.43.rest_1_.rest_11_.rest_6_.rest_9_, ...), custom_call_target="tpu_custom_call" | custom-call | flops 4026531 | bytes 47185 | tf_op jit(solution)/shard_map/rank_products/pallas_call | solution.py:413
  147.2 1.6 collective-permute-start.14
  149.9 12.1 %collective-permute-done.14.rest_5_ = bf16[512,512]{1,0:T(8,128)(2,1)S(1)} collective-permute-done((bf16[512,512]{1,0:T(8,128)(2,1)S(1)}, bf16[512,512]{1,0:T(8,128)(2,1)S(1)}, u32[]{:S(2)}, u32[]{:S(2)}) %collective-permute-start.14) | collective-permute-done | bytes 524320 | tf_op jit(solution)/shard_map/ppermute | solution.py:606
  162.0 3.3 %collective-permute-done.28.rest_7_ = bf16[768,128]{1,0:T(8,128)(2,1)S(1)} collective-permute-done((bf16[768,128]{1,0:T(8,128)(2,1)S(1)}, bf16[768,128]{1,0:T(8,128)(2,1)S(1)}, u32[]{:S(2)}, u32[]{:S(2)}) %collective-permute-start.28) | collective-permute-done | bytes 196640 | tf_op jit(solution)/shard_map/ppermute | solution.py:606
  165.3 5.4 %finish.5 = (bf16[6144,2,128]{2,1,0:T(2,128)(2,1)}, f32[8,128]{1,0:T(8,128)}) custom-call(s32[8,128]{1,0:T(8,128)S(1)} %copy-done.16, bf16[2,1024,512]{2,1,0:T(8,128)(2,1)S(1)} %copy-done.5, bf16[1024,512]{1,0:T(8,128)(2,1)S(1)} %collective-permute-done.5.rest_1_, ...), custom_call_target="tpu_custom_call", output_to_operand_aliasing={{0}: (16, {})} | custom-call | flops 12079595 | bytes 39321 | tf_op jit(solution)/shard_map/finish/pallas_call | solution.py:571
  (112 shorter events, 20.4 us)
Async XLA Ops:
  2.8 27.2 %copy-start = (bf16[3,2304,128]{2,1,0:T(8,128)(2,1)}, bf16[3,2304,128]{2,1,0:T(8,128)(2,1)S(1)}, u32[]{:S(2)}) copy-start(bf16[3,2304,128]{2,1,0:T(8,128)(2,1)S(1)} %pack_maps.1.rest_0_.rest_10_.rest_5_.rest_8_) | copy-start | bytes 5308420
  2.8 43.8 %collective-permute-start.12 = (bf16[3,2304,128]{2,1,0:T(8,128)(2,1)S(1)}, bf16[3,2304,128]{2,1,0:T(8,128)(2,1)}, u32[]{:S(2)}, u32[]{:S(2)}) collective-permute-start(bf16[3,2304,128]{2,1,0:T(8,128)(2,1)S(1)} %pack_maps.1.rest_0_.rest_10_.rest_5_.rest_8_), channel_id=1, source_target_pairs={{4,0},{8,4},{12,8},{5,1},{9,5},{13,9},{6,2},{10,6},{14,10},{7,3},{... | collective-permute-start | bytes 5308424 | tf_op jit(solution)/shard_map/ppermute | solution.py:613
  4.1 43.4 %collective-permute-start.13 = (bf16[3,2304,128]{2,1,0:T(8,128)(2,1)S(1)}, bf16[3,2304,128]{2,1,0:T(8,128)(2,1)}, u32[]{:S(2)}, u32[]{:S(2)}) collective-permute-start(bf16[3,2304,128]{2,1,0:T(8,128)(2,1)S(1)} %pack_maps.1.rest_0_.rest_10_.rest_5_.rest_8_), channel_id=1, source_target_pairs={{0,4},{4,8},{8,12},{1,5},{5,9},{9,13},{2,6},{6,10},{10,14},{3,7},{... | collective-permute-start | bytes 5308424 | tf_op jit(solution)/shard_map/ppermute | solution.py:616
  30.9 2.3 %collective-permute-start = (bf16[512,512]{1,0:T(8,128)(2,1)S(1)}, bf16[512,512]{1,0:T(8,128)(2,1)S(1)}, u32[]{:S(2)}, u32[]{:S(2)}) collective-permute-start(bf16[512,512]{1,0:T(8,128)(2,1)S(1)} %get-tuple-element.31), channel_id=1, source_target_pairs={{0,1},{1,0},{2,3},{3,2},{4,5},{5,4},{6,7},{7,6},{8,9},{9,8},{10,11... | collective-permute-start | bytes 1572872 | tf_op jit(solution)/shard_map/ppermute | solution.py:603
  30.9 2.3 %collective-permute-start.1 = (bf16[256,512]{1,0:T(8,128)(2,1)S(1)}, bf16[256,512]{1,0:T(8,128)(2,1)S(1)}, u32[]{:S(2)}, u32[]{:S(2)}) collective-permute-start(bf16[256,512]{1,0:T(8,128)(2,1)S(1)} %get-tuple-element.32), channel_id=1, source_target_pairs={{0,1},{1,0},{2,3},{3,2},{4,5},{5,4},{6,7},{7,6},{8,9},{9,8},{10,11... | collective-permute-start | bytes 786440 | tf_op jit(solution)/shard_map/ppermute | solution.py:603
  33.6 23.9 %collective-permute-start.4 = (bf16[768,512]{1,0:T(8,128)(2,1)S(1)}, bf16[768,512]{1,0:T(8,128)(2,1)S(1)}, u32[]{:S(2)}, u32[]{:S(2)}) collective-permute-start(bf16[768,512]{1,0:T(8,128)(2,1)S(1)} %pair_sum.4.rest_1_), channel_id=1, source_target_pairs={{0,2},{1,3},{2,0},{3,1},{4,6},{5,7},{6,4},{7,5},{8,10},{9,11},{10,... | collective-permute-start | bytes 2359304 | tf_op jit(solution)/shard_map/ppermute | solution.py:606
  47.5 48.8 %collective-permute-start.15 = (bf16[3,2304,128]{2,1,0:T(8,128)(2,1)}, bf16[3,2304,128]{2,1,0:T(8,128)(2,1)}, u32[]{:S(2)}, u32[]{:S(2)}) collective-permute-start(bf16[3,2304,128]{2,1,0:T(8,128)(2,1)} %get-tuple-element.43.rest_1_.rest_11_.rest_6_.rest_9_), channel_id=1, source_target_pairs={{4,0},{8,4},{12,8},{5,1},{9,5},{13,9},{6,2},{10,6},{14,10},{7,3},{... | collective-permute-start | bytes 5308424 | tf_op jit(solution)/shard_map/ppermute | solution.py:613
  48.8 47.5 %collective-permute-start.16 = (bf16[3,2304,128]{2,1,0:T(8,128)(2,1)}, bf16[3,2304,128]{2,1,0:T(8,128)(2,1)}, u32[]{:S(2)}, u32[]{:S(2)}) collective-permute-start(bf16[3,2304,128]{2,1,0:T(8,128)(2,1)} %get-tuple-element.44.rest_2_.rest_3_.rest_12_.rest_8_.rest_4_), channel_id=1, source_target_pairs={{0,4},{4,8},{8,12},{1,5},{5,9},{9,13},{2,6},{6,10},{10,14},{3,7},{... | collective-permute-start | bytes 5308424 | tf_op jit(solution)/shard_map/ppermute | solution.py:616
  55.2 2.3 %collective-permute-start.2 = (bf16[512,512]{1,0:T(8,128)(2,1)S(1)}, bf16[512,512]{1,0:T(8,128)(2,1)S(1)}, u32[]{:S(2)}, u32[]{:S(2)}) collective-permute-start(bf16[512,512]{1,0:T(8,128)(2,1)S(1)} %get-tuple-element.34), channel_id=1, source_target_pairs={{0,1},{1,0},{2,3},{3,2},{4,5},{5,4},{6,7},{7,6},{8,9},{9,8},{10,11... | collective-permute-start | bytes 1572872 | tf_op jit(solution)/shard_map/ppermute | solution.py:603
  55.2 2.3 %collective-permute-start.3 = (bf16[256,512]{1,0:T(8,128)(2,1)S(1)}, bf16[256,512]{1,0:T(8,128)(2,1)S(1)}, u32[]{:S(2)}, u32[]{:S(2)}) collective-permute-start(bf16[256,512]{1,0:T(8,128)(2,1)S(1)} %get-tuple-element.35), channel_id=1, source_target_pairs={{0,1},{1,0},{2,3},{3,2},{4,5},{5,4},{6,7},{7,6},{8,9},{9,8},{10,11... | collective-permute-start | bytes 786440 | tf_op jit(solution)/shard_map/ppermute | solution.py:603
  58.7 19.9 %collective-permute-start.8 = (bf16[768,512]{1,0:T(8,128)(2,1)}, bf16[768,512]{1,0:T(8,128)(2,1)S(1)}, u32[]{:S(2)}, u32[]{:S(2)}) collective-permute-start(bf16[768,512]{1,0:T(8,128)(2,1)} %pair_sum.5.rest_1_), channel_id=1, source_target_pairs={{0,2},{1,3},{2,0},{3,1},{4,6},{5,7},{6,4},{7,5},{8,10},{9,11},{10,... | collective-permute-start | bytes 2359304 | tf_op jit(solution)/shard_map/ppermute | solution.py:606
  76.5 6.3 %collective-permute-start.6 = (bf16[512,512]{1,0:T(8,128)(2,1)}, bf16[512,512]{1,0:T(8,128)(2,1)S(1)}, u32[]{:S(2)}, u32[]{:S(2)}) collective-permute-start(bf16[512,512]{1,0:T(8,128)(2,1)} %copy-done.23), channel_id=1, source_target_pairs={{0,1},{1,0},{2,3},{3,2},{4,5},{5,4},{6,7},{7,6},{8,9},{9,8},{10,11... | collective-permute-start | bytes 1572872 | tf_op jit(solution)/shard_map/ppermute | solution.py:603
  76.5 6.3 %collective-permute-start.7 = (bf16[512,512]{1,0:T(8,128)(2,1)S(1)}, bf16[512,512]{1,0:T(8,128)(2,1)S(1)}, u32[]{:S(2)}, u32[]{:S(2)}) collective-permute-start(bf16[512,512]{1,0:T(8,128)(2,1)S(1)} %get-tuple-element.39), channel_id=1, source_target_pairs={{0,1},{1,0},{2,3},{3,2},{4,5},{5,4},{6,7},{7,6},{8,9},{9,8},{10,11... | collective-permute-start | bytes 1572872 | tf_op jit(solution)/shard_map/ppermute | solution.py:603
  78.6 24.1 %collective-permute-start.21 = (bf16[768,512]{1,0:T(8,128)(2,1)}, bf16[768,512]{1,0:T(8,128)(2,1)}, u32[]{:S(2)}, u32[]{:S(2)}) collective-permute-start(bf16[768,512]{1,0:T(8,128)(2,1)} %copy-done.22), channel_id=1, source_target_pairs={{0,1},{1,0},{2,3},{3,2},{4,5},{5,4},{6,7},{7,6},{8,9},{9,8},{10,11... | collective-permute-start | bytes 2359304 | tf_op jit(solution)/shard_map/ppermute | solution.py:603
  84.5 26.9 %slice-start.3 = ((s8[12582912]{0:T(1024)(128)(4,1)}), s8[4194304]{0:T(1024)(128)(4,1)S(1)}, s32[]{:S(2)}) async-start(s8[12582912]{0:T(1024)(128)(4,1)} %bitcast.11), calls=%async_computation.3 | async-start | bytes 8388608
  85.8 25.6 %slice-start.4 = ((s8[12582912]{0:T(1024)(128)(4,1)}), s8[4194304]{0:T(1024)(128)(4,1)S(1)}, s32[]{:S(2)}) async-start(s8[12582912]{0:T(1024)(128)(4,1)} %bitcast.11), calls=%async_computation.4 | async-start | bytes 8388608
  85.8 25.6 %collective-permute-start.9 = (bf16[1024,512]{1,0:T(8,128)(2,1)}, bf16[1024,512]{1,0:T(8,128)(2,1)S(1)}, u32[]{:S(2)}, u32[]{:S(2)}) collective-permute-start(bf16[1024,512]{1,0:T(8,128)(2,1)} %pair_sum.6.rest_1_), channel_id=1, source_target_pairs={{0,2},{1,3},{2,0},{3,1},{4,6},{5,7},{6,4},{7,5},{8,10},{9,11},{10,... | collective-permute-start | bytes 3145736 | tf_op jit(solution)/shard_map/ppermute | solution.py:606
  96.3 48.1 %collective-permute-start.17 = (bf16[3,2304,128]{2,1,0:T(8,128)(2,1)}, bf16[3,2304,128]{2,1,0:T(8,128)(2,1)S(1)}, u32[]{:S(2)}, u32[]{:S(2)}) collective-permute-start(bf16[3,2304,128]{2,1,0:T(8,128)(2,1)} %get-tuple-element.45.rest_2_.rest_7_.rest_10_), channel_id=1, source_target_pairs={{4,0},{8,4},{12,8},{5,1},{9,5},{13,9},{6,2},{10,6},{14,10},{7,3},{... | collective-permute-start | bytes 5308424 | tf_op jit(solution)/shard_map/ppermute | solution.py:613
  97.9 46.5 %collective-permute-start.18 = (bf16[3,2304,128]{2,1,0:T(8,128)(2,1)}, bf16[3,2304,128]{2,1,0:T(8,128)(2,1)S(1)}, u32[]{:S(2)}, u32[]{:S(2)}) collective-permute-start(bf16[3,2304,128]{2,1,0:T(8,128)(2,1)} %get-tuple-element.46.rest_4_.rest_9_.rest_5_.rest_13_), channel_id=1, source_target_pairs={{0,4},{4,8},{8,12},{1,5},{5,9},{9,13},{2,6},{6,10},{10,14},{3,7},{... | collective-permute-start | bytes 5308424 | tf_op jit(solution)/shard_map/ppermute | solution.py:616
  102.6 11.7 %collective-permute-start.11 = (bf16[512,512]{1,0:T(8,128)(2,1)S(1)}, bf16[512,512]{1,0:T(8,128)(2,1)S(1)}, u32[]{:S(2)}, u32[]{:S(2)}) collective-permute-start(bf16[512,512]{1,0:T(8,128)(2,1)S(1)} %get-tuple-element.42), channel_id=1, source_target_pairs={{0,1},{1,0},{2,3},{3,2},{4,5},{5,4},{6,7},{7,6},{8,9},{9,8},{10,11... | collective-permute-start | bytes 1572872 | tf_op jit(solution)/shard_map/ppermute | solution.py:603
  102.7 2.2 %collective-permute-start.23 = (bf16[768,128]{1,0:T(8,128)(2,1)S(1)}, bf16[768,128]{1,0:T(8,128)(2,1)S(1)}, u32[]{:S(2)}, u32[]{:S(2)}) collective-permute-start(bf16[768,128]{1,0:T(8,128)(2,1)S(1)} %rank_products.4.rest_2_), channel_id=1, source_target_pairs={{0,1},{1,0},{2,3},{3,2},{4,5},{5,4},{6,7},{7,6},{8,9},{9,8},{10,11... | collective-permute-start | bytes 589832 | tf_op jit(solution)/shard_map/ppermute | solution.py:603
  104.8 13.7 %collective-permute-start.22 = (bf16[768,512]{1,0:T(8,128)(2,1)S(1)}, bf16[768,512]{1,0:T(8,128)(2,1)S(1)}, u32[]{:S(2)}, u32[]{:S(2)}) collective-permute-start(bf16[768,512]{1,0:T(8,128)(2,1)S(1)} %copy-done.21), channel_id=1, source_target_pairs={{0,1},{1,0},{2,3},{3,2},{4,5},{5,4},{6,7},{7,6},{8,9},{9,8},{10,11... | collective-permute-start | bytes 2359304 | tf_op jit(solution)/shard_map/ppermute | solution.py:603
  111.3 28.2 %collective-permute-start.5 = (bf16[1024,512]{1,0:T(8,128)(2,1)S(1)}, bf16[1024,512]{1,0:T(8,128)(2,1)S(1)}, u32[]{:S(2)}, u32[]{:S(2)}) collective-permute-start(bf16[1024,512]{1,0:T(8,128)(2,1)S(1)} %copy-done.19), channel_id=1, source_target_pairs={{0,1},{1,0},{2,3},{3,2},{4,5},{5,4},{6,7},{7,6},{8,9},{9,8},{10,11... | collective-permute-start | bytes 3145736 | tf_op jit(solution)/shard_map/ppermute | solution.py:603
  114.3 4.1 %collective-permute-start.25 = (bf16[768,128]{1,0:T(8,128)(2,1)S(1)}, bf16[768,128]{1,0:T(8,128)(2,1)S(1)}, u32[]{:S(2)}, u32[]{:S(2)}) collective-permute-start(bf16[768,128]{1,0:T(8,128)(2,1)S(1)} %rank_products.5.rest_1_), channel_id=1, source_target_pairs={{0,1},{1,0},{2,3},{3,2},{4,5},{5,4},{6,7},{7,6},{8,9},{9,8},{10,11... | collective-permute-start | bytes 589832 | tf_op jit(solution)/shard_map/ppermute | solution.py:603
  118.4 1.9 %collective-permute-start.19 = (bf16[768,128]{1,0:T(8,128)(2,1)S(1)}, bf16[768,128]{1,0:T(8,128)(2,1)S(1)}, u32[]{:S(2)}, u32[]{:S(2)}) collective-permute-start(bf16[768,128]{1,0:T(8,128)(2,1)S(1)} %rank_products.6), channel_id=1, source_target_pairs={{0,1},{1,0},{2,3},{3,2},{4,5},{5,4},{6,7},{7,6},{8,9},{9,8},{10,11... | collective-permute-start | bytes 589832 | tf_op jit(solution)/shard_map/ppermute | solution.py:603
  118.5 7.8 %collective-permute-start.24 = (bf16[768,128]{1,0:T(8,128)(2,1)S(1)}, bf16[768,128]{1,0:T(8,128)(2,1)S(1)}, u32[]{:S(2)}, u32[]{:S(2)}) collective-permute-start(bf16[768,128]{1,0:T(8,128)(2,1)S(1)} %add_convert_fusion.2.rest_6_), channel_id=1, source_target_pairs={{0,2},{1,3},{2,0},{3,1},{4,6},{5,7},{6,4},{7,5},{8,10},{9,11},{10,... | collective-permute-start | bytes 589832 | tf_op jit(solution)/shard_map/ppermute | solution.py:606
  120.3 10.3 %collective-permute-start.26 = (bf16[768,128]{1,0:T(8,128)(2,1)S(1)}, bf16[768,128]{1,0:T(8,128)(2,1)S(1)}, u32[]{:S(2)}, u32[]{:S(2)}) collective-permute-start(bf16[768,128]{1,0:T(8,128)(2,1)S(1)} %add_convert_fusion.1.rest_8_), channel_id=1, source_target_pairs={{0,2},{1,3},{2,0},{3,1},{4,6},{5,7},{6,4},{7,5},{8,10},{9,11},{10,... | collective-permute-start | bytes 589832 | tf_op jit(solution)/shard_map/ppermute | solution.py:606
  126.3 13.3 %collective-permute-start.20 = (bf16[768,128]{1,0:T(8,128)(2,1)S(1)}, bf16[768,128]{1,0:T(8,128)(2,1)S(1)}, u32[]{:S(2)}, u32[]{:S(2)}) collective-permute-start(bf16[768,128]{1,0:T(8,128)(2,1)S(1)} %add_convert_fusion.3.rest_3_), channel_id=1, source_target_pairs={{0,2},{1,3},{2,0},{3,1},{4,6},{5,7},{6,4},{7,5},{8,10},{9,11},{10,... | collective-permute-start | bytes 589832 | tf_op jit(solution)/shard_map/ppermute | solution.py:606
  146.6 2.2 %collective-permute-start.27 = (bf16[768,128]{1,0:T(8,128)(2,1)S(1)}, bf16[768,128]{1,0:T(8,128)(2,1)S(1)}, u32[]{:S(2)}, u32[]{:S(2)}) collective-permute-start(bf16[768,128]{1,0:T(8,128)(2,1)S(1)} %rank_products.7), channel_id=1, source_target_pairs={{0,1},{1,0},{2,3},{3,2},{4,5},{5,4},{6,7},{7,6},{8,9},{9,8},{10,11... | collective-permute-start | bytes 589832 | tf_op jit(solution)/shard_map/ppermute | solution.py:603
  146.7 3.2 %collective-permute-start.10 = (bf16[512,512]{1,0:T(8,128)(2,1)S(1)}, bf16[512,512]{1,0:T(8,128)(2,1)S(1)}, u32[]{:S(2)}, u32[]{:S(2)}) collective-permute-start(bf16[512,512]{1,0:T(8,128)(2,1)S(1)} %get-tuple-element.41), channel_id=1, source_target_pairs={{0,1},{1,0},{2,3},{3,2},{4,5},{5,4},{6,7},{7,6},{8,9},{9,8},{10,11... | collective-permute-start | bytes 1572872 | tf_op jit(solution)/shard_map/ppermute | solution.py:603
  147.2 14.8 %collective-permute-start.14 = (bf16[512,512]{1,0:T(8,128)(2,1)S(1)}, bf16[512,512]{1,0:T(8,128)(2,1)S(1)}, u32[]{:S(2)}, u32[]{:S(2)}) collective-permute-start(bf16[512,512]{1,0:T(8,128)(2,1)S(1)} %pair_sum.7.rest_5_), channel_id=1, source_target_pairs={{0,2},{1,3},{2,0},{3,1},{4,6},{5,7},{6,4},{7,5},{8,10},{9,11},{10,... | collective-permute-start | bytes 1572872 | tf_op jit(solution)/shard_map/ppermute | solution.py:606
  148.9 16.4 %collective-permute-start.28 = (bf16[768,128]{1,0:T(8,128)(2,1)S(1)}, bf16[768,128]{1,0:T(8,128)(2,1)S(1)}, u32[]{:S(2)}, u32[]{:S(2)}) collective-permute-start(bf16[768,128]{1,0:T(8,128)(2,1)S(1)} %add_convert_fusion.rest_6_), channel_id=1, source_target_pairs={{0,2},{1,3},{2,0},{3,1},{4,6},{5,7},{6,4},{7,5},{8,10},{9,11},{10,... | collective-permute-start | bytes 589832 | tf_op jit(solution)/shard_map/ppermute | solution.py:606
  (27 other events, 257.0 us)

commit v8 on v7

--- a/solution.py
+++ b/solution.py
@@ -714,13 +714,14 @@
             relay(hops, [fourth[3]])
         part = fourth[3]
         if by_distance:
-            part = rank(1, [fourth[3], bases[2][2][-1]])
+            part = rank(1, [part])
+            part = rank(2, [part, bases[2][2][-1]])
         send_on(*fourth, [part, bases[2][2][-1]])
         for chunk in range(len(ranks), 3):
             part = rank(chunk, [pairs[-1]])
         out, _ = write(None, 0, 2)
         out, written = write(out, 2, 3)
-        rank(3, [written])
+        rank(3, [written, bases[3][2][-1]])
         out, _ = write(out, 3, 4)
         tiles = out.shape[0] // shape[0]
         out = out.reshape(shape[0], tiles, 2, columns // tiles)

time: 171 us -> 167 us (0.977)
  starting transfers between devices: 38.1 us -> 34 us
  waiting for transfers between devices: 36.7 us -> 34.7 us
    ppermute x8, waiting for transfers between devices: 30.6 us -> 26.8 us  [chip_shift(): lax.ppermute(a, 'tensor', [(2 * x + c, 2 * ((x + k) % n_x) + c) for x in...]
    ppermute x8, starting transfers between devices: 12.7 us -> 9.31 us  [chip_shift(): lax.ppermute(a, 'tensor', [(2 * x + c, 2 * ((x + k) % n_x) + c) for x in...]
    ppermute x15, waiting for transfers between devices: 5.26 us -> 7.89 us  [core_swap(): return lax.ppermute(a, 'tensor', [(t, t ^ 1) for t in range(n_t)])]
    unnamed x60 -> x58, local copies, waits for them, and re-layouts: 9.14 us -> 10.1 us
  transfers between devices with their start and end apart: 29 -> 29, of which waited for: 10 -> 10; matrix products, arithmetic and copies ran while one was open for 0% -> 0% of each run, Pallas kernels for 46% -> 47%
where the time goes in v8:
time: 167 us; the launch traced here: 165 us
  Pallas kernels  85.6 us (51%)
  waiting for transfers between devices  34.7 us (21%)
  starting transfers between devices  34 us (20%)
  local copies, waits for them, and re-layouts  10.1 us (6%)
    pallas_call x3, Pallas kernels, base_products(): pl.pallas_call(body, out_shape=(*[jax.ShapeDtypeStruct((n * prefill, widt...  34.5 us
    ppermute x8, waiting for transfers between devices, chip_shift(): lax.ppermute(a, 'tensor', [(2 * x + c, 2 * ((x + k) % n_x) + c) for x in...  26.8 us
    pallas_call x3, Pallas kernels, finish(): pl.pallas_call(body, out_shape=(jax.ShapeDtypeStruct((shape[0] * tiles, 2...  18.8 us
    ppermute x3, starting transfers between devices, rightward(): return lax.ppermute(a, 'adapter', [(z - hops, z) for z in range(hops, n_z)])  17.2 us
    pallas_call x1, Pallas kernels, split_weight(): pl.pallas_call(body, out_shape=(jax.ShapeDtypeStruct((n_t, features, 2 *...  16.9 us
    pallas_call x4, Pallas kernels, rank_products(): pl.pallas_call(body, out_shape=jax.ShapeDtypeStruct((count * prefill, ran...  10.2 us
    unnamed x58, local copies, waits for them, and re-layouts  10.1 us
    ppermute x8, starting transfers between devices, chip_shift(): lax.ppermute(a, 'tensor', [(2 * x + c, 2 * ((x + k) % n_x) + c) for x in...  9.31 us
  transfers between devices with their start and end apart: 29, of which 10 were waited for; matrix products, arithmetic and copies ran while one was open for 0% of the time, Pallas kernels for 47%

profile of v8, /device:TPU:0, one launch (start us, length us, event | category | flops | bytes accessed | tf_op | source)
XLA Modules:
  0.0 165.4 jit_solution(13035193453910170264)
XLA Ops:
  0.0 1.4 copy-done.14
  2.8 1.3 collective-permute-start.12
  4.1 6.8 %collective-permute-start.13 = (bf16[3,2304,128]{2,1,0:T(8,128)(2,1)S(1)}, bf16[3,2304,128]{2,1,0:T(8,128)(2,1)}, u32[]{:S(2)}, u32[]{:S(2)}) collective-permute-start(bf16[3,2304,128]{2,1,0:T(8,128)(2,1)S(1)} %pack_maps.1.rest_0_.rest_10_.rest_5_.rest_8_), channel_id=1, source_target_pairs={{0,4},{4,8},{8,12},{1,5},{5,9},{9,13},{2,6},{6,10},{10,14},{3,7},{... | collective-permute-start | bytes 5308424 | tf_op jit(solution)/shard_map/ppermute | solution.py:616
  10.9 1.6 plan_requests.1.plan_ref
  13.1 16.9 %split_weight.1 = (bf16[4,2048,512]{2,1,0:T(8,128)(2,1)}, bf16[768,512]{1,0:T(8,128)(2,1)S(1)}, bf16[512,512]{1,0:T(8,128)(2,1)S(1)}, bf16[256,512]{1,0:T(8,128)(2,1)S(1)}, bf16[2,768,512]{2,1,0:T(8,128)(2,1)S(1)}) custom-call(s32[8,128]{1,0:T(8,128)S(1)} %copy-done.15, s32[4]{0:T(128)S(1)} %compare_select_fusion.2.slot_ref, bf16[3072,2048]{1,0:T(8,128)(2,1)} %x_ref.13, ...), custom_call_target="tpu_custom_call" | custom-call | flops 64424508 | bytes 167772 | tf_op jit(solution)/shard_map/split_weight/pallas_call | solution.py:184
  31.4 1.8 %collective-permute-done.1.rest_1_ = bf16[256,512]{1,0:T(8,128)(2,1)S(1)} collective-permute-done((bf16[256,512]{1,0:T(8,128)(2,1)S(1)}, bf16[256,512]{1,0:T(8,128)(2,1)S(1)}, u32[]{:S(2)}, u32[]{:S(2)}) %collective-permute-start.1) | collective-permute-done | bytes 262176 | tf_op jit(solution)/shard_map/ppermute | solution.py:603
  33.6 2.0 %collective-permute-start.4 = (bf16[768,512]{1,0:T(8,128)(2,1)S(1)}, bf16[768,512]{1,0:T(8,128)(2,1)S(1)}, u32[]{:S(2)}, u32[]{:S(2)}) collective-permute-start(bf16[768,512]{1,0:T(8,128)(2,1)S(1)} %pair_sum.4.rest_1_), channel_id=1, source_target_pairs={{0,2},{1,3},{2,0},{3,1},{4,6},{5,7},{6,4},{7,5},{8,10},{9,11},{10,... | collective-permute-start | bytes 2359304 | tf_op jit(solution)/shard_map/ppermute | solution.py:606
  35.6 12.1 %base_products.3 = (bf16[768,512]{1,0:T(8,128)(2,1)S(1)}, bf16[512,512]{1,0:T(8,128)(2,1)S(1)}, bf16[256,512]{1,0:T(8,128)(2,1)S(1)}, bf16[2,768,512]{2,1,0:T(8,128)(2,1)S(1)}) custom-call(s32[8,128]{1,0:T(8,128)S(1)} %copy-done.15, bf16[3072,2048]{1,0:T(8,128)(2,1)} %x_ref.13, bf16[4,2048,512]{2,1,0:T(8,128)(2,1)} %get-tuple-element.29.rest_0_, ...), custom_call_target="tpu_custom_call" | custom-call | flops 64424508 | bytes 83886 | tf_op jit(solution)/shard_map/base_products/pallas_call | solution.py:260
  48.7 1.3 collective-permute-start.14
  50.0 5.8 %collective-permute-start.15 = (bf16[3,2304,128]{2,1,0:T(8,128)(2,1)}, bf16[3,2304,128]{2,1,0:T(8,128)(2,1)}, u32[]{:S(2)}, u32[]{:S(2)}) collective-permute-start(bf16[3,2304,128]{2,1,0:T(8,128)(2,1)} %get-tuple-element.44.rest_2_.rest_3_.rest_12_.rest_8_.rest_4_), channel_id=1, source_target_pairs={{0,4},{4,8},{8,12},{1,5},{5,9},{9,13},{2,6},{6,10},{10,14},{3,7},{... | collective-permute-start | bytes 5308424 | tf_op jit(solution)/shard_map/ppermute | solution.py:616
  56.3 1.8 %collective-permute-done.3.rest_1_ = bf16[256,512]{1,0:T(8,128)(2,1)S(1)} collective-permute-done((bf16[256,512]{1,0:T(8,128)(2,1)S(1)}, bf16[256,512]{1,0:T(8,128)(2,1)S(1)}, u32[]{:S(2)}, u32[]{:S(2)}) %collective-permute-start.3) | collective-permute-done | bytes 262176 | tf_op jit(solution)/shard_map/ppermute | solution.py:603
  58.1 1.2 pair_sum.5.rest_1_
  60.4 13.3 %base_products.4 = (bf16[1024,512]{1,0:T(8,128)(2,1)S(1)}, bf16[512,512]{1,0:T(8,128)(2,1)S(1)}, bf16[512,512]{1,0:T(8,128)(2,1)S(1)}, bf16[2,1024,512]{2,1,0:T(8,128)(2,1)S(1)}) custom-call(s32[8,128]{1,0:T(8,128)S(1)} %copy-done.15, bf16[3072,2048]{1,0:T(8,128)(2,1)} %x_ref.13, bf16[4,2048,512]{2,1,0:T(8,128)(2,1)} %get-tuple-element.29.rest_0_, ...), custom_call_target="tpu_custom_call" | custom-call | flops 85899344 | bytes 83886 | tf_op jit(solution)/shard_map/base_products/pallas_call | solution.py:260
  76.0 2.3 %collective-permute-done.6.rest_0_ = bf16[512,512]{1,0:T(8,128)(2,1)S(1)} collective-permute-done((bf16[512,512]{1,0:T(8,128)(2,1)}, bf16[512,512]{1,0:T(8,128)(2,1)S(1)}, u32[]{:S(2)}, u32[]{:S(2)}) %collective-permute-start.6) | collective-permute-done | bytes 524320 | tf_op jit(solution)/shard_map/ppermute | solution.py:603
  79.2 1.7 %copy-done.1 = bf16[3,2304,128]{2,1,0:T(8,128)(2,1)S(1)} copy-done((bf16[3,2304,128]{2,1,0:T(8,128)(2,1)S(1)}, bf16[3,2304,128]{2,1,0:T(8,128)(2,1)}, u32[]{:S(2)}) %copy-start.1) | copy-done | bytes 1769496
  80.9 2.3 %rank_products.4.rest_2_ = bf16[768,128]{1,0:T(8,128)(2,1)S(1)} custom-call(s32[8,128]{1,0:T(8,128)S(1)} %copy-done.15, bf16[3072,2048]{1,0:T(8,128)(2,1)S(1)} %bitcast.10, bf16[3,2304,128]{2,1,0:T(8,128)(2,1)S(1)} %copy-done.1, bf16[2,1024,512]{2,1,0:T(8,128)(2,1)S(1)} %get-tuple-element.36.rest_1_.a_ref.rest_0_, ...), custom_call_target="tpu_custom_call" | custom-call | flops 4026531 | bytes 47185 | tf_op jit(solution)/shard_map/rank_products/pallas_call | solution.py:413
  83.3 1.6 copy-done.4
  84.9 1.3 pair_sum.6.rest_1_
  87.3 9.1 %base_products.5 = (bf16[512,512]{1,0:T(8,128)(2,1)S(1)}, bf16[512,512]{1,0:T(8,128)(2,1)S(1)}, bf16[2,512,512]{2,1,0:T(8,128)(2,1)S(1)}) custom-call(s32[8,128]{1,0:T(8,128)S(1)} %copy-done.15, bf16[3072,2048]{1,0:T(8,128)(2,1)} %x_ref.13, bf16[4,2048,512]{2,1,0:T(8,128)(2,1)} %get-tuple-element.29.rest_0_, bf16[1024,512]{1,0:T(8,128)(2,1)} %pair_sum.6.rest_1_), custom_call_target="tpu_custom_call" | custom-call | flops 42949672 | bytes 83886 | tf_op jit(solution)/shard_map/base_products/pallas_call | solution.py:260
  96.5 1.4 collective-permute-start.17
  98.0 4.7 %collective-permute-start.18 = (bf16[3,2304,128]{2,1,0:T(8,128)(2,1)}, bf16[3,2304,128]{2,1,0:T(8,128)(2,1)S(1)}, u32[]{:S(2)}, u32[]{:S(2)}) collective-permute-start(bf16[3,2304,128]{2,1,0:T(8,128)(2,1)} %get-tuple-element.46.rest_4_.rest_9_.rest_5_.rest_13_), channel_id=1, source_target_pairs={{0,4},{4,8},{8,12},{1,5},{5,9},{9,13},{2,6},{6,10},{10,14},{3,7},{... | collective-permute-start | bytes 5308424 | tf_op jit(solution)/shard_map/ppermute | solution.py:616
  102.8 3.0 %rank_products.5.rest_5_ = bf16[768,128]{1,0:T(8,128)(2,1)S(1)} custom-call(s32[8,128]{1,0:T(8,128)S(1)} %copy-done.16, bf16[3072,2048]{1,0:T(8,128)(2,1)S(1)} %bitcast.12, bf16[3,2304,128]{2,1,0:T(8,128)(2,1)S(1)} %copy-done.2, bf16[3,2304,128]{2,1,0:T(8,128)(2,1)} %get-tuple-element.43.rest_1_.rest_11_.rest_6_.rest_9_, ...), custom_call_target="tpu_custom_call" | custom-call | flops 4026531 | bytes 47185 | tf_op jit(solution)/shard_map/rank_products/pallas_call | solution.py:413
  108.0 3.8 %collective-permute-done.9.rest_6_.rest_2_ = bf16[1024,512]{1,0:T(8,128)(2,1)S(1)} collective-permute-done((bf16[1024,512]{1,0:T(8,128)(2,1)}, bf16[1024,512]{1,0:T(8,128)(2,1)S(1)}, u32[]{:S(2)}, u32[]{:S(2)}) %collective-permute-start.9) | collective-permute-done | bytes 1048608 | tf_op jit(solution)/shard_map/ppermute | solution.py:606
  112.8 2.7 %rank_products.6.rest_1_ = bf16[768,128]{1,0:T(8,128)(2,1)S(1)} custom-call(s32[8,128]{1,0:T(8,128)S(1)} %copy-done.16, bf16[3072,2048]{1,0:T(8,128)(2,1)S(1)} %bitcast.12, bf16[3,2304,128]{2,1,0:T(8,128)(2,1)S(1)} %copy-done.2, bf16[3,2304,128]{2,1,0:T(8,128)(2,1)} %get-tuple-element.43.rest_1_.rest_11_.rest_6_.rest_9_, ...), custom_call_target="tpu_custom_call" | custom-call | flops 4026531 | bytes 47185 | tf_op jit(solution)/shard_map/rank_products/pallas_call | solution.py:413
  115.9 2.1 %collective-permute-done.26.rest_9_ = bf16[768,128]{1,0:T(8,128)(2,1)S(1)} collective-permute-done((bf16[768,128]{1,0:T(8,128)(2,1)S(1)}, bf16[768,128]{1,0:T(8,128)(2,1)S(1)}, u32[]{:S(2)}, u32[]{:S(2)}) %collective-permute-start.26) | collective-permute-done | bytes 196640 | tf_op jit(solution)/shard_map/ppermute | solution.py:606
  119.1 1.1 collective-permute-start.24
  120.2 14.3 %collective-permute-done.24.rest_7_ = bf16[768,128]{1,0:T(8,128)(2,1)S(1)} collective-permute-done((bf16[768,128]{1,0:T(8,128)(2,1)S(1)}, bf16[768,128]{1,0:T(8,128)(2,1)S(1)}, u32[]{:S(2)}, u32[]{:S(2)}) %collective-permute-start.24) | collective-permute-done | bytes 196640 | tf_op jit(solution)/shard_map/ppermute | solution.py:606
  135.5 9.0 %finish.3 = (bf16[6144,2,128]{2,1,0:T(2,128)(2,1)}, f32[8,128]{1,0:T(8,128)}) custom-call(s32[8,128]{1,0:T(8,128)S(1)} %copy-done.16, bf16[2,768,512]{2,1,0:T(8,128)(2,1)S(1)} %copy-done.11, bf16[768,512]{1,0:T(8,128)(2,1)} %collective-permute-done.21.rest_1_, bf16[768,512]{1,0:T(8,128)(2,1)S(1)} %copy-done.13, bf16[2,768,512]{2,1,0:T(8,128)(2,1)S(1)} %copy-done.7, ...), custom_call_target="tpu_custom_call" | custom-call | flops 24159192 | bytes 78643 | tf_op jit(solution)/shard_map/finish/pallas_call | solution.py:571
  144.5 4.5 %finish.4 = (bf16[6144,2,128]{2,1,0:T(2,128)(2,1)}, f32[8,128]{1,0:T(8,128)S(1)}) custom-call(s32[8,128]{1,0:T(8,128)S(1)} %copy-done.16, bf16[2,1024,512]{2,1,0:T(8,128)(2,1)S(1)} %copy-done.5, bf16[1024,512]{1,0:T(8,128)(2,1)S(1)} %collective-permute-done.5.rest_1_, ...), custom_call_target="tpu_custom_call", output_to_operand_aliasing={{0}: (11, {})} | custom-call | flops 12079595 | bytes 39321 | tf_op jit(solution)/shard_map/finish/pallas_call | solution.py:571
  149.0 2.2 %rank_products.7 = bf16[768,128]{1,0:T(8,128)(2,1)S(1)} custom-call(s32[8,128]{1,0:T(8,128)S(1)} %copy-done.16, bf16[3072,2048]{1,0:T(8,128)(2,1)S(1)} %bitcast.12, bf16[3,2304,128]{2,1,0:T(8,128)(2,1)S(1)} %copy-done.2, bf16[3,2304,128]{2,1,0:T(8,128)(2,1)} %get-tuple-element.43.rest_1_.rest_11_.rest_6_.rest_9_, ...), custom_call_target="tpu_custom_call" | custom-call | flops 4026531 | bytes 47185 | tf_op jit(solution)/shard_map/rank_products/pallas_call | solution.py:413
  153.9 5.9 %collective-permute-done.28.rest_7_ = bf16[768,128]{1,0:T(8,128)(2,1)S(1)} collective-permute-done((bf16[768,128]{1,0:T(8,128)(2,1)S(1)}, bf16[768,128]{1,0:T(8,128)(2,1)S(1)}, u32[]{:S(2)}, u32[]{:S(2)}) %collective-permute-start.28) | collective-permute-done | bytes 196640 | tf_op jit(solution)/shard_map/ppermute | solution.py:606
  159.8 5.4 %finish.5 = (bf16[6144,2,128]{2,1,0:T(2,128)(2,1)}, f32[8,128]{1,0:T(8,128)}) custom-call(s32[8,128]{1,0:T(8,128)S(1)} %copy-done.16, bf16[2,1024,512]{2,1,0:T(8,128)(2,1)S(1)} %copy-done.5, bf16[1024,512]{1,0:T(8,128)(2,1)S(1)} %collective-permute-done.5.rest_1_, ...), custom_call_target="tpu_custom_call", output_to_operand_aliasing={{0}: (16, {})} | custom-call | flops 12079595 | bytes 39321 | tf_op jit(solution)/shard_map/finish/pallas_call | solution.py:571
  (110 shorter events, 19.2 us)
Async XLA Ops:
  2.8 27.3 %copy-start = (bf16[3,2304,128]{2,1,0:T(8,128)(2,1)}, bf16[3,2304,128]{2,1,0:T(8,128)(2,1)S(1)}, u32[]{:S(2)}) copy-start(bf16[3,2304,128]{2,1,0:T(8,128)(2,1)S(1)} %pack_maps.1.rest_0_.rest_10_.rest_5_.rest_8_) | copy-start | bytes 5308420
  2.8 45.9 %collective-permute-start.12 = (bf16[3,2304,128]{2,1,0:T(8,128)(2,1)S(1)}, bf16[3,2304,128]{2,1,0:T(8,128)(2,1)}, u32[]{:S(2)}, u32[]{:S(2)}) collective-permute-start(bf16[3,2304,128]{2,1,0:T(8,128)(2,1)S(1)} %pack_maps.1.rest_0_.rest_10_.rest_5_.rest_8_), channel_id=1, source_target_pairs={{4,0},{8,4},{12,8},{5,1},{9,5},{13,9},{6,2},{10,6},{14,10},{7,3},{... | collective-permute-start | bytes 5308424 | tf_op jit(solution)/shard_map/ppermute | solution.py:613
  4.1 44.6 %collective-permute-start.13 = (bf16[3,2304,128]{2,1,0:T(8,128)(2,1)S(1)}, bf16[3,2304,128]{2,1,0:T(8,128)(2,1)}, u32[]{:S(2)}, u32[]{:S(2)}) collective-permute-start(bf16[3,2304,128]{2,1,0:T(8,128)(2,1)S(1)} %pack_maps.1.rest_0_.rest_10_.rest_5_.rest_8_), channel_id=1, source_target_pairs={{0,4},{4,8},{8,12},{1,5},{5,9},{9,13},{2,6},{6,10},{10,14},{3,7},{... | collective-permute-start | bytes 5308424 | tf_op jit(solution)/shard_map/ppermute | solution.py:616
  30.9 2.3 %collective-permute-start = (bf16[512,512]{1,0:T(8,128)(2,1)S(1)}, bf16[512,512]{1,0:T(8,128)(2,1)S(1)}, u32[]{:S(2)}, u32[]{:S(2)}) collective-permute-start(bf16[512,512]{1,0:T(8,128)(2,1)S(1)} %get-tuple-element.31), channel_id=1, source_target_pairs={{0,1},{1,0},{2,3},{3,2},{4,5},{5,4},{6,7},{7,6},{8,9},{9,8},{10,11... | collective-permute-start | bytes 1572872 | tf_op jit(solution)/shard_map/ppermute | solution.py:603
  30.9 2.3 %collective-permute-start.1 = (bf16[256,512]{1,0:T(8,128)(2,1)S(1)}, bf16[256,512]{1,0:T(8,128)(2,1)S(1)}, u32[]{:S(2)}, u32[]{:S(2)}) collective-permute-start(bf16[256,512]{1,0:T(8,128)(2,1)S(1)} %get-tuple-element.32), channel_id=1, source_target_pairs={{0,1},{1,0},{2,3},{3,2},{4,5},{5,4},{6,7},{7,6},{8,9},{9,8},{10,11... | collective-permute-start | bytes 786440 | tf_op jit(solution)/shard_map/ppermute | solution.py:603
  33.6 24.4 %collective-permute-start.4 = (bf16[768,512]{1,0:T(8,128)(2,1)S(1)}, bf16[768,512]{1,0:T(8,128)(2,1)S(1)}, u32[]{:S(2)}, u32[]{:S(2)}) collective-permute-start(bf16[768,512]{1,0:T(8,128)(2,1)S(1)} %pair_sum.4.rest_1_), channel_id=1, source_target_pairs={{0,2},{1,3},{2,0},{3,1},{4,6},{5,7},{6,4},{7,5},{8,10},{9,11},{10,... | collective-permute-start | bytes 2359304 | tf_op jit(solution)/shard_map/ppermute | solution.py:606
  48.7 47.8 %collective-permute-start.14 = (bf16[3,2304,128]{2,1,0:T(8,128)(2,1)}, bf16[3,2304,128]{2,1,0:T(8,128)(2,1)}, u32[]{:S(2)}, u32[]{:S(2)}) collective-permute-start(bf16[3,2304,128]{2,1,0:T(8,128)(2,1)} %get-tuple-element.43.rest_1_.rest_11_.rest_6_.rest_9_), channel_id=1, source_target_pairs={{4,0},{8,4},{12,8},{5,1},{9,5},{13,9},{6,2},{10,6},{14,10},{7,3},{... | collective-permute-start | bytes 5308424 | tf_op jit(solution)/shard_map/ppermute | solution.py:613
  50.0 46.5 %collective-permute-start.15 = (bf16[3,2304,128]{2,1,0:T(8,128)(2,1)}, bf16[3,2304,128]{2,1,0:T(8,128)(2,1)}, u32[]{:S(2)}, u32[]{:S(2)}) collective-permute-start(bf16[3,2304,128]{2,1,0:T(8,128)(2,1)} %get-tuple-element.44.rest_2_.rest_3_.rest_12_.rest_8_.rest_4_), channel_id=1, source_target_pairs={{0,4},{4,8},{8,12},{1,5},{5,9},{9,13},{2,6},{6,10},{10,14},{3,7},{... | collective-permute-start | bytes 5308424 | tf_op jit(solution)/shard_map/ppermute | solution.py:616
  55.8 2.3 %collective-permute-start.2 = (bf16[512,512]{1,0:T(8,128)(2,1)S(1)}, bf16[512,512]{1,0:T(8,128)(2,1)S(1)}, u32[]{:S(2)}, u32[]{:S(2)}) collective-permute-start(bf16[512,512]{1,0:T(8,128)(2,1)S(1)} %get-tuple-element.34), channel_id=1, source_target_pairs={{0,1},{1,0},{2,3},{3,2},{4,5},{5,4},{6,7},{7,6},{8,9},{9,8},{10,11... | collective-permute-start | bytes 1572872 | tf_op jit(solution)/shard_map/ppermute | solution.py:603
  55.8 2.3 %collective-permute-start.3 = (bf16[256,512]{1,0:T(8,128)(2,1)S(1)}, bf16[256,512]{1,0:T(8,128)(2,1)S(1)}, u32[]{:S(2)}, u32[]{:S(2)}) collective-permute-start(bf16[256,512]{1,0:T(8,128)(2,1)S(1)} %get-tuple-element.35), channel_id=1, source_target_pairs={{0,1},{1,0},{2,3},{3,2},{4,5},{5,4},{6,7},{7,6},{8,9},{9,8},{10,11... | collective-permute-start | bytes 786440 | tf_op jit(solution)/shard_map/ppermute | solution.py:603
  59.3 19.8 %collective-permute-start.8 = (bf16[768,512]{1,0:T(8,128)(2,1)}, bf16[768,512]{1,0:T(8,128)(2,1)S(1)}, u32[]{:S(2)}, u32[]{:S(2)}) collective-permute-start(bf16[768,512]{1,0:T(8,128)(2,1)} %pair_sum.5.rest_1_), channel_id=1, source_target_pairs={{0,2},{1,3},{2,0},{3,1},{4,6},{5,7},{6,4},{7,5},{8,10},{9,11},{10,... | collective-permute-start | bytes 2359304 | tf_op jit(solution)/shard_map/ppermute | solution.py:606
  75.5 2.8 %collective-permute-start.6 = (bf16[512,512]{1,0:T(8,128)(2,1)}, bf16[512,512]{1,0:T(8,128)(2,1)S(1)}, u32[]{:S(2)}, u32[]{:S(2)}) collective-permute-start(bf16[512,512]{1,0:T(8,128)(2,1)} %copy-done.22), channel_id=1, source_target_pairs={{0,1},{1,0},{2,3},{3,2},{4,5},{5,4},{6,7},{7,6},{8,9},{9,8},{10,11... | collective-permute-start | bytes 1572872 | tf_op jit(solution)/shard_map/ppermute | solution.py:603
  75.5 7.8 %collective-permute-start.7 = (bf16[512,512]{1,0:T(8,128)(2,1)S(1)}, bf16[512,512]{1,0:T(8,128)(2,1)S(1)}, u32[]{:S(2)}, u32[]{:S(2)}) collective-permute-start(bf16[512,512]{1,0:T(8,128)(2,1)S(1)} %get-tuple-element.39), channel_id=1, source_target_pairs={{0,1},{1,0},{2,3},{3,2},{4,5},{5,4},{6,7},{7,6},{8,9},{9,8},{10,11... | collective-permute-start | bytes 1572872 | tf_op jit(solution)/shard_map/ppermute | solution.py:603
  78.3 24.3 %collective-permute-start.21 = (bf16[768,512]{1,0:T(8,128)(2,1)}, bf16[768,512]{1,0:T(8,128)(2,1)}, u32[]{:S(2)}, u32[]{:S(2)}) collective-permute-start(bf16[768,512]{1,0:T(8,128)(2,1)} %copy-done.20), channel_id=1, source_target_pairs={{0,1},{1,0},{2,3},{3,2},{4,5},{5,4},{6,7},{7,6},{8,9},{9,8},{10,11... | collective-permute-start | bytes 2359304 | tf_op jit(solution)/shard_map/ppermute | solution.py:603
  79.2 26.6 %collective-permute-start.22 = (bf16[768,512]{1,0:T(8,128)(2,1)}, bf16[768,512]{1,0:T(8,128)(2,1)}, u32[]{:S(2)}, u32[]{:S(2)}) collective-permute-start(bf16[768,512]{1,0:T(8,128)(2,1)} %copy-done.21), channel_id=1, source_target_pairs={{0,1},{1,0},{2,3},{3,2},{4,5},{5,4},{6,7},{7,6},{8,9},{9,8},{10,11... | collective-permute-start | bytes 2359304 | tf_op jit(solution)/shard_map/ppermute | solution.py:603
  86.2 25.6 %collective-permute-start.9 = (bf16[1024,512]{1,0:T(8,128)(2,1)}, bf16[1024,512]{1,0:T(8,128)(2,1)S(1)}, u32[]{:S(2)}, u32[]{:S(2)}) collective-permute-start(bf16[1024,512]{1,0:T(8,128)(2,1)} %pair_sum.6.rest_1_), channel_id=1, source_target_pairs={{0,2},{1,3},{2,0},{3,1},{4,6},{5,7},{6,4},{7,5},{8,10},{9,11},{10,... | collective-permute-start | bytes 3145736 | tf_op jit(solution)/shard_map/ppermute | solution.py:606
  96.5 52.5 %collective-permute-start.17 = (bf16[3,2304,128]{2,1,0:T(8,128)(2,1)}, bf16[3,2304,128]{2,1,0:T(8,128)(2,1)S(1)}, u32[]{:S(2)}, u32[]{:S(2)}) collective-permute-start(bf16[3,2304,128]{2,1,0:T(8,128)(2,1)} %get-tuple-element.45.rest_2_.rest_7_.rest_10_), channel_id=1, source_target_pairs={{4,0},{8,4},{12,8},{5,1},{9,5},{13,9},{6,2},{10,6},{14,10},{7,3},{... | collective-permute-start | bytes 5308424 | tf_op jit(solution)/shard_map/ppermute | solution.py:613
  98.0 51.1 %collective-permute-start.18 = (bf16[3,2304,128]{2,1,0:T(8,128)(2,1)}, bf16[3,2304,128]{2,1,0:T(8,128)(2,1)S(1)}, u32[]{:S(2)}, u32[]{:S(2)}) collective-permute-start(bf16[3,2304,128]{2,1,0:T(8,128)(2,1)} %get-tuple-element.46.rest_4_.rest_9_.rest_5_.rest_13_), channel_id=1, source_target_pairs={{0,4},{4,8},{8,12},{1,5},{5,9},{9,13},{2,6},{6,10},{10,14},{3,7},{... | collective-permute-start | bytes 5308424 | tf_op jit(solution)/shard_map/ppermute | solution.py:616
  102.6 5.2 %collective-permute-start.11 = (bf16[512,512]{1,0:T(8,128)(2,1)S(1)}, bf16[512,512]{1,0:T(8,128)(2,1)S(1)}, u32[]{:S(2)}, u32[]{:S(2)}) collective-permute-start(bf16[512,512]{1,0:T(8,128)(2,1)S(1)} %get-tuple-element.42), channel_id=1, source_target_pairs={{0,1},{1,0},{2,3},{3,2},{4,5},{5,4},{6,7},{7,6},{8,9},{9,8},{10,11... | collective-permute-start | bytes 1572872 | tf_op jit(solution)/shard_map/ppermute | solution.py:603
  105.8 1.6 collective-permute-start.25
  107.4 37.1 %collective-permute-start.5 = (bf16[1024,512]{1,0:T(8,128)(2,1)S(1)}, bf16[1024,512]{1,0:T(8,128)(2,1)S(1)}, u32[]{:S(2)}, u32[]{:S(2)}) collective-permute-start(bf16[1024,512]{1,0:T(8,128)(2,1)S(1)} %copy-done.19), channel_id=1, source_target_pairs={{0,1},{1,0},{2,3},{3,2},{4,5},{5,4},{6,7},{7,6},{8,9},{9,8},{10,11... | collective-permute-start | bytes 3145736 | tf_op jit(solution)/shard_map/ppermute | solution.py:603
  107.8 8.0 %collective-permute-start.23 = (bf16[768,128]{1,0:T(8,128)(2,1)S(1)}, bf16[768,128]{1,0:T(8,128)(2,1)S(1)}, u32[]{:S(2)}, u32[]{:S(2)}) collective-permute-start(bf16[768,128]{1,0:T(8,128)(2,1)S(1)} %rank_products.4.rest_2_), channel_id=1, source_target_pairs={{0,1},{1,0},{2,3},{3,2},{4,5},{5,4},{6,7},{7,6},{8,9},{9,8},{10,11... | collective-permute-start | bytes 589832 | tf_op jit(solution)/shard_map/ppermute | solution.py:603
  111.8 6.2 %collective-permute-start.26 = (bf16[768,128]{1,0:T(8,128)(2,1)S(1)}, bf16[768,128]{1,0:T(8,128)(2,1)S(1)}, u32[]{:S(2)}, u32[]{:S(2)}) collective-permute-start(bf16[768,128]{1,0:T(8,128)(2,1)S(1)} %add_convert_fusion.1.rest_8_), channel_id=1, source_target_pairs={{0,2},{1,3},{2,0},{3,1},{4,6},{5,7},{6,4},{7,5},{8,10},{9,11},{10,... | collective-permute-start | bytes 589832 | tf_op jit(solution)/shard_map/ppermute | solution.py:606
  112.8 22.7 %copy-start.13 = (bf16[768,512]{1,0:T(8,128)(2,1)S(1)}, bf16[768,512]{1,0:T(8,128)(2,1)}, u32[]{:S(2)}) copy-start(bf16[768,512]{1,0:T(8,128)(2,1)} %copy-done.12) | copy-start | bytes 2359300
  115.8 3.2 %collective-permute-start.19 = (bf16[768,128]{1,0:T(8,128)(2,1)S(1)}, bf16[768,128]{1,0:T(8,128)(2,1)S(1)}, u32[]{:S(2)}, u32[]{:S(2)}) collective-permute-start(bf16[768,128]{1,0:T(8,128)(2,1)S(1)} %rank_products.6.rest_1_), channel_id=1, source_target_pairs={{0,1},{1,0},{2,3},{3,2},{4,5},{5,4},{6,7},{7,6},{8,9},{9,8},{10,11... | collective-permute-start | bytes 589832 | tf_op jit(solution)/shard_map/ppermute | solution.py:603
  118.0 31.0 %collective-permute-start.16 = (bf16[512,512]{1,0:T(8,128)(2,1)S(1)}, bf16[512,512]{1,0:T(8,128)(2,1)S(1)}, u32[]{:S(2)}, u32[]{:S(2)}) collective-permute-start(bf16[512,512]{1,0:T(8,128)(2,1)S(1)} %pair_sum.7), channel_id=1, source_target_pairs={{0,2},{1,3},{2,0},{3,1},{4,6},{5,7},{6,4},{7,5},{8,10},{9,11},{10,... | collective-permute-start | bytes 1572872 | tf_op jit(solution)/shard_map/ppermute | solution.py:606
  119.1 15.4 %collective-permute-start.24 = (bf16[768,128]{1,0:T(8,128)(2,1)S(1)}, bf16[768,128]{1,0:T(8,128)(2,1)S(1)}, u32[]{:S(2)}, u32[]{:S(2)}) collective-permute-start(bf16[768,128]{1,0:T(8,128)(2,1)S(1)} %add_convert_fusion.2.rest_6_), channel_id=1, source_target_pairs={{0,2},{1,3},{2,0},{3,1},{4,6},{5,7},{6,4},{7,5},{8,10},{9,11},{10,... | collective-permute-start | bytes 589832 | tf_op jit(solution)/shard_map/ppermute | solution.py:606
  120.2 24.3 %copy-start.5 = (bf16[2,1024,512]{2,1,0:T(8,128)(2,1)S(1)}, bf16[2,1024,512]{2,1,0:T(8,128)(2,1)}, u32[]{:S(2)}) copy-start(bf16[2,1024,512]{2,1,0:T(8,128)(2,1)} %copy-done.3) | copy-start | bytes 6291460
  134.5 10.0 %collective-permute-start.20 = (bf16[768,128]{1,0:T(8,128)(2,1)S(1)}, bf16[768,128]{1,0:T(8,128)(2,1)S(1)}, u32[]{:S(2)}, u32[]{:S(2)}) collective-permute-start(bf16[768,128]{1,0:T(8,128)(2,1)S(1)} %add_convert_fusion.3.rest_3_), channel_id=1, source_target_pairs={{0,2},{1,3},{2,0},{3,1},{4,6},{5,7},{6,4},{7,5},{8,10},{9,11},{10,... | collective-permute-start | bytes 589832 | tf_op jit(solution)/shard_map/ppermute | solution.py:606
  151.3 1.5 collective-permute-start.27
  151.3 2.6 %collective-permute-start.10 = (bf16[512,512]{1,0:T(8,128)(2,1)S(1)}, bf16[512,512]{1,0:T(8,128)(2,1)S(1)}, u32[]{:S(2)}, u32[]{:S(2)}) collective-permute-start(bf16[512,512]{1,0:T(8,128)(2,1)S(1)} %get-tuple-element.41), channel_id=1, source_target_pairs={{0,1},{1,0},{2,3},{3,2},{4,5},{5,4},{6,7},{7,6},{8,9},{9,8},{10,11... | collective-permute-start | bytes 1572872 | tf_op jit(solution)/shard_map/ppermute | solution.py:603
  152.8 7.0 %collective-permute-start.28 = (bf16[768,128]{1,0:T(8,128)(2,1)S(1)}, bf16[768,128]{1,0:T(8,128)(2,1)S(1)}, u32[]{:S(2)}, u32[]{:S(2)}) collective-permute-start(bf16[768,128]{1,0:T(8,128)(2,1)S(1)} %add_convert_fusion.rest_6_), channel_id=1, source_target_pairs={{0,2},{1,3},{2,0},{3,1},{4,6},{5,7},{6,4},{7,5},{8,10},{9,11},{10,... | collective-permute-start | bytes 589832 | tf_op jit(solution)/shard_map/ppermute | solution.py:606
  (26 other events, 226.2 us)

commit v9 on v8

--- a/solution.py
+++ b/solution.py
@@ -716,7 +716,8 @@
         if by_distance:
             part = rank(1, [part])
             part = rank(2, [part, bases[2][2][-1]])
-        send_on(*fourth, [part, bases[2][2][-1]])
+        summed = [pieces[-1] for _, _, pieces in ranks[:2]]
+        send_on(*fourth, [part, bases[2][2][-1]] + summed)
         for chunk in range(len(ranks), 3):
             part = rank(chunk, [pairs[-1]])
         out, _ = write(None, 0, 2)

time: 167 us -> 165 us (0.988)
  Pallas kernels: 85.6 us -> 82.5 us
  starting transfers between devices: 34 us -> 35.9 us
    pallas_call x3, Pallas kernels: 34.5 us -> 32.3 us  [base_products(): pl.pallas_call(body, out_shape=(*[jax.ShapeDtypeStruct((n * prefill, widt...]
    ppermute x8, starting transfers between devices: 9.31 us -> 11.3 us  [chip_shift(): lax.ppermute(a, 'tensor', [(2 * x + c, 2 * ((x + k) % n_x) + c) for x in...]
    unnamed x58 -> x66, local copies, waits for them, and re-layouts: 10.1 us -> 9.19 us
  transfers between devices with their start and end apart: 29 -> 29, of which waited for: 10 -> 12; matrix products, arithmetic and copies ran while one was open for 0% -> 0% of each run, Pallas kernels for 47% -> 46%
where the time goes in v9:
time: 165 us; the launch traced here: 163 us
  Pallas kernels  82.5 us (50%)
  starting transfers between devices  35.9 us (22%)
  waiting for transfers between devices  34.9 us (21%)
  local copies, waits for them, and re-layouts  9.19 us (6%)
    pallas_call x3, Pallas kernels, base_products(): pl.pallas_call(body, out_shape=(*[jax.ShapeDtypeStruct((n * prefill, widt...  32.3 us
    ppermute x8, waiting for transfers between devices, chip_shift(): lax.ppermute(a, 'tensor', [(2 * x + c, 2 * ((x + k) % n_x) + c) for x in...  25.8 us
    pallas_call x3, Pallas kernels, finish(): pl.pallas_call(body, out_shape=(jax.ShapeDtypeStruct((shape[0] * tiles, 2...  18.1 us
    ppermute x3, starting transfers between devices, rightward(): return lax.ppermute(a, 'adapter', [(z - hops, z) for z in range(hops, n_z)])  18 us
    pallas_call x1, Pallas kernels, split_weight(): pl.pallas_call(body, out_shape=(jax.ShapeDtypeStruct((n_t, features, 2 *...  16.9 us
    ppermute x8, starting transfers between devices, chip_shift(): lax.ppermute(a, 'tensor', [(2 * x + c, 2 * ((x + k) % n_x) + c) for x in...  11.3 us
    pallas_call x4, Pallas kernels, rank_products(): pl.pallas_call(body, out_shape=jax.ShapeDtypeStruct((count * prefill, ran...  9.99 us
    unnamed x66, local copies, waits for them, and re-layouts  9.19 us
  transfers between devices with their start and end apart: 29, of which 12 were waited for; matrix products, arithmetic and copies ran while one was open for 0% of the time, Pallas kernels for 46%

profile of v9, /device:TPU:0, one launch (start us, length us, event | category | flops | bytes accessed | tf_op | source)
XLA Modules:
  0.0 163.5 jit_solution(12515674012583134190)
XLA Ops:
  4.1 6.8 %collective-permute-start.13 = (bf16[3,2304,128]{2,1,0:T(8,128)(2,1)S(1)}, bf16[3,2304,128]{2,1,0:T(8,128)(2,1)}, u32[]{:S(2)}, u32[]{:S(2)}) collective-permute-start(bf16[3,2304,128]{2,1,0:T(8,128)(2,1)S(1)} %pack_maps.1.rest_0_.rest_10_.rest_5_.rest_8_), channel_id=1, source_target_pairs={{0,4},{4,8},{8,12},{1,5},{5,9},{9,13},{2,6},{6,10},{10,14},{3,7},{... | collective-permute-start | bytes 5308424 | tf_op jit(solution)/shard_map/ppermute | solution.py:616
  10.9 1.6 plan_requests.1.plan_ref
  13.2 16.9 %split_weight.1 = (bf16[4,2048,512]{2,1,0:T(8,128)(2,1)}, bf16[768,512]{1,0:T(8,128)(2,1)S(1)}, bf16[512,512]{1,0:T(8,128)(2,1)S(1)}, bf16[256,512]{1,0:T(8,128)(2,1)S(1)}, bf16[2,768,512]{2,1,0:T(8,128)(2,1)S(1)}) custom-call(s32[8,128]{1,0:T(8,128)S(1)} %copy-done.15, s32[4]{0:T(128)S(1)} %compare_select_fusion.2.slot_ref, bf16[3072,2048]{1,0:T(8,128)(2,1)} %x_ref.13, ...), custom_call_target="tpu_custom_call" | custom-call | flops 64424508 | bytes 167772 | tf_op jit(solution)/shard_map/split_weight/pallas_call | solution.py:184
  31.1 1.5 collective-permute-done.1.rest_1_
  33.0 2.0 %collective-permute-start.4 = (bf16[768,512]{1,0:T(8,128)(2,1)S(1)}, bf16[768,512]{1,0:T(8,128)(2,1)S(1)}, u32[]{:S(2)}, u32[]{:S(2)}) collective-permute-start(bf16[768,512]{1,0:T(8,128)(2,1)S(1)} %pair_sum.4.rest_1_), channel_id=1, source_target_pairs={{0,2},{1,3},{2,0},{3,1},{4,6},{5,7},{6,4},{7,5},{8,10},{9,11},{10,... | collective-permute-start | bytes 2359304 | tf_op jit(solution)/shard_map/ppermute | solution.py:606
  35.0 10.0 %base_products.3 = (bf16[768,512]{1,0:T(8,128)(2,1)S(1)}, bf16[512,512]{1,0:T(8,128)(2,1)S(1)}, bf16[256,512]{1,0:T(8,128)(2,1)S(1)}, bf16[2,768,512]{2,1,0:T(8,128)(2,1)S(1)}) custom-call(s32[8,128]{1,0:T(8,128)S(1)} %copy-done.15, bf16[3072,2048]{1,0:T(8,128)(2,1)} %x_ref.13, bf16[4,2048,512]{2,1,0:T(8,128)(2,1)} %get-tuple-element.29.rest_0_, ...), custom_call_target="tpu_custom_call" | custom-call | flops 64424508 | bytes 83886 | tf_op jit(solution)/shard_map/base_products/pallas_call | solution.py:260
  45.0 1.4 collective-permute-done.12.refs_0_
  48.8 6.3 %collective-permute-start.15 = (bf16[3,2304,128]{2,1,0:T(8,128)(2,1)}, bf16[3,2304,128]{2,1,0:T(8,128)(2,1)}, u32[]{:S(2)}, u32[]{:S(2)}) collective-permute-start(bf16[3,2304,128]{2,1,0:T(8,128)(2,1)} %get-tuple-element.44.rest_2_.rest_3_.rest_12_.rest_8_.rest_4_), channel_id=1, source_target_pairs={{0,4},{4,8},{8,12},{1,5},{5,9},{9,13},{2,6},{6,10},{10,14},{3,7},{... | collective-permute-start | bytes 5308424 | tf_op jit(solution)/shard_map/ppermute | solution.py:616
  55.7 1.8 %collective-permute-done.3.rest_1_ = bf16[256,512]{1,0:T(8,128)(2,1)S(1)} collective-permute-done((bf16[256,512]{1,0:T(8,128)(2,1)S(1)}, bf16[256,512]{1,0:T(8,128)(2,1)S(1)}, u32[]{:S(2)}, u32[]{:S(2)}) %collective-permute-start.3) | collective-permute-done | bytes 262176 | tf_op jit(solution)/shard_map/ppermute | solution.py:603
  58.7 1.7 %collective-permute-start.8 = (bf16[768,512]{1,0:T(8,128)(2,1)}, bf16[768,512]{1,0:T(8,128)(2,1)S(1)}, u32[]{:S(2)}, u32[]{:S(2)}) collective-permute-start(bf16[768,512]{1,0:T(8,128)(2,1)} %pair_sum.5.rest_1_), channel_id=1, source_target_pairs={{0,2},{1,3},{2,0},{3,1},{4,6},{5,7},{6,4},{7,5},{8,10},{9,11},{10,... | collective-permute-start | bytes 2359304 | tf_op jit(solution)/shard_map/ppermute | solution.py:606
  60.4 14.3 %base_products.4 = (bf16[1024,512]{1,0:T(8,128)(2,1)S(1)}, bf16[512,512]{1,0:T(8,128)(2,1)S(1)}, bf16[512,512]{1,0:T(8,128)(2,1)S(1)}, bf16[2,1024,512]{2,1,0:T(8,128)(2,1)S(1)}) custom-call(s32[8,128]{1,0:T(8,128)S(1)} %copy-done.15, bf16[3072,2048]{1,0:T(8,128)(2,1)} %x_ref.13, bf16[4,2048,512]{2,1,0:T(8,128)(2,1)} %get-tuple-element.29.rest_0_, ...), custom_call_target="tpu_custom_call" | custom-call | flops 85899344 | bytes 83886 | tf_op jit(solution)/shard_map/base_products/pallas_call | solution.py:260
  76.2 2.4 %collective-permute-done.8.rest_2_.rest_3_.rest_5_ = bf16[768,512]{1,0:T(8,128)(2,1)S(1)} collective-permute-done((bf16[768,512]{1,0:T(8,128)(2,1)}, bf16[768,512]{1,0:T(8,128)(2,1)S(1)}, u32[]{:S(2)}, u32[]{:S(2)}) %collective-permute-start.8) | collective-permute-done | bytes 786464 | tf_op jit(solution)/shard_map/ppermute | solution.py:606
  78.6 1.7 %copy-done.1 = bf16[3,2304,128]{2,1,0:T(8,128)(2,1)S(1)} copy-done((bf16[3,2304,128]{2,1,0:T(8,128)(2,1)S(1)}, bf16[3,2304,128]{2,1,0:T(8,128)(2,1)}, u32[]{:S(2)}) %copy-start.1) | copy-done | bytes 1769496
  80.3 2.3 %rank_products.4.rest_2_ = bf16[768,128]{1,0:T(8,128)(2,1)S(1)} custom-call(s32[8,128]{1,0:T(8,128)S(1)} %copy-done.15, bf16[3072,2048]{1,0:T(8,128)(2,1)S(1)} %bitcast.10, bf16[3,2304,128]{2,1,0:T(8,128)(2,1)S(1)} %copy-done.1, bf16[2,1024,512]{2,1,0:T(8,128)(2,1)S(1)} %get-tuple-element.36.rest_1_.a_ref.rest_0_, ...), custom_call_target="tpu_custom_call" | custom-call | flops 4026531 | bytes 47185 | tf_op jit(solution)/shard_map/rank_products/pallas_call | solution.py:413
  82.7 1.6 copy-done.4
  85.7 1.7 %collective-permute-start.9 = (bf16[1024,512]{1,0:T(8,128)(2,1)}, bf16[1024,512]{1,0:T(8,128)(2,1)S(1)}, u32[]{:S(2)}, u32[]{:S(2)}) collective-permute-start(bf16[1024,512]{1,0:T(8,128)(2,1)} %pair_sum.6.rest_1_), channel_id=1, source_target_pairs={{0,2},{1,3},{2,0},{3,1},{4,6},{5,7},{6,4},{7,5},{8,10},{9,11},{10,... | collective-permute-start | bytes 3145736 | tf_op jit(solution)/shard_map/ppermute | solution.py:606
  87.4 8.1 %base_products.5 = (bf16[512,512]{1,0:T(8,128)(2,1)S(1)}, bf16[512,512]{1,0:T(8,128)(2,1)S(1)}, bf16[2,512,512]{2,1,0:T(8,128)(2,1)S(1)}) custom-call(s32[8,128]{1,0:T(8,128)S(1)} %copy-done.15, bf16[3072,2048]{1,0:T(8,128)(2,1)} %x_ref.13, bf16[4,2048,512]{2,1,0:T(8,128)(2,1)} %get-tuple-element.29.rest_0_, bf16[1024,512]{1,0:T(8,128)(2,1)} %pair_sum.6.rest_1_), custom_call_target="tpu_custom_call" | custom-call | flops 42949672 | bytes 83886 | tf_op jit(solution)/shard_map/base_products/pallas_call | solution.py:260
  96.3 2.7 %rank_products.5.rest_5_ = bf16[768,128]{1,0:T(8,128)(2,1)S(1)} custom-call(s32[8,128]{1,0:T(8,128)S(1)} %copy-done.15, bf16[3072,2048]{1,0:T(8,128)(2,1)S(1)} %bitcast.12, bf16[3,2304,128]{2,1,0:T(8,128)(2,1)S(1)} %copy-done.2, bf16[3,2304,128]{2,1,0:T(8,128)(2,1)} %get-tuple-element.43.rest_1_.rest_11_.rest_6_.rest_9_, ...), custom_call_target="tpu_custom_call" | custom-call | flops 4026531 | bytes 47185 | tf_op jit(solution)/shard_map/rank_products/pallas_call | solution.py:413
  99.2 1.4 collective-permute-start.21
  100.7 4.8 %collective-permute-start.22 = (bf16[3,2304,128]{2,1,0:T(8,128)(2,1)}, bf16[3,2304,128]{2,1,0:T(8,128)(2,1)S(1)}, u32[]{:S(2)}, u32[]{:S(2)}) collective-permute-start(bf16[3,2304,128]{2,1,0:T(8,128)(2,1)} %get-tuple-element.46.rest_4_.rest_9_.rest_5_.rest_13_), channel_id=1, source_target_pairs={{0,4},{4,8},{8,12},{1,5},{5,9},{9,13},{2,6},{6,10},{10,14},{3,7},{... | collective-permute-start | bytes 5308424 | tf_op jit(solution)/shard_map/ppermute | solution.py:616
  107.4 1.7 %collective-permute-start.17 = (bf16[768,128]{1,0:T(8,128)(2,1)S(1)}, bf16[768,128]{1,0:T(8,128)(2,1)S(1)}, u32[]{:S(2)}, u32[]{:S(2)}) collective-permute-start(bf16[768,128]{1,0:T(8,128)(2,1)S(1)} %add_convert_fusion.3.rest_6_), channel_id=1, source_target_pairs={{0,2},{1,3},{2,0},{3,1},{4,6},{5,7},{6,4},{7,5},{8,10},{9,11},{10,... | collective-permute-start | bytes 589832 | tf_op jit(solution)/shard_map/ppermute | solution.py:606
  109.2 7.0 %collective-permute-done.19.rest_4_.rest_9_ = bf16[768,128]{1,0:T(8,128)(2,1)S(1)} collective-permute-done((bf16[768,128]{1,0:T(8,128)(2,1)S(1)}, bf16[768,128]{1,0:T(8,128)(2,1)S(1)}, u32[]{:S(2)}, u32[]{:S(2)}) %collective-permute-start.19) | collective-permute-done | bytes 196640 | tf_op jit(solution)/shard_map/ppermute | solution.py:606
  116.1 3.5 %collective-permute-done.17.rest_3_.rest_7_ = bf16[768,128]{1,0:T(8,128)(2,1)S(1)} collective-permute-done((bf16[768,128]{1,0:T(8,128)(2,1)S(1)}, bf16[768,128]{1,0:T(8,128)(2,1)S(1)}, u32[]{:S(2)}, u32[]{:S(2)}) %collective-permute-start.17) | collective-permute-done | bytes 196640 | tf_op jit(solution)/shard_map/ppermute | solution.py:606
  120.2 2.9 %rank_products.6.rest_1_ = bf16[768,128]{1,0:T(8,128)(2,1)S(1)} custom-call(s32[8,128]{1,0:T(8,128)S(1)} %copy-done.16, bf16[3072,2048]{1,0:T(8,128)(2,1)S(1)} %bitcast.12, bf16[3,2304,128]{2,1,0:T(8,128)(2,1)S(1)} %copy-done.2, bf16[3,2304,128]{2,1,0:T(8,128)(2,1)} %get-tuple-element.43.rest_1_.rest_11_.rest_6_.rest_9_, ...), custom_call_target="tpu_custom_call" | custom-call | flops 4026531 | bytes 47185 | tf_op jit(solution)/shard_map/rank_products/pallas_call | solution.py:413
  124.6 1.7 %collective-permute-start.20 = (bf16[512,512]{1,0:T(8,128)(2,1)S(1)}, bf16[512,512]{1,0:T(8,128)(2,1)S(1)}, u32[]{:S(2)}, u32[]{:S(2)}) collective-permute-start(bf16[512,512]{1,0:T(8,128)(2,1)S(1)} %pair_sum.7), channel_id=1, source_target_pairs={{0,2},{1,3},{2,0},{3,1},{4,6},{5,7},{6,4},{7,5},{8,10},{9,11},{10,... | collective-permute-start | bytes 1572872 | tf_op jit(solution)/shard_map/ppermute | solution.py:606
  126.8 8.3 %finish.3 = (bf16[6144,2,128]{2,1,0:T(2,128)(2,1)}, f32[8,128]{1,0:T(8,128)}) custom-call(s32[8,128]{1,0:T(8,128)S(1)} %copy-done.16, bf16[2,768,512]{2,1,0:T(8,128)(2,1)S(1)} %copy-done.11, bf16[768,512]{1,0:T(8,128)(2,1)} %collective-permute-done.25.rest_1_, bf16[768,512]{1,0:T(8,128)(2,1)S(1)} %copy-done.13, bf16[2,768,512]{2,1,0:T(8,128)(2,1)S(1)} %copy-done.7, ...), custom_call_target="tpu_custom_call" | custom-call | flops 24159192 | bytes 78643 | tf_op jit(solution)/shard_map/finish/pallas_call | solution.py:571
  135.1 7.7 %collective-permute-done.24.rest_4_ = bf16[768,128]{1,0:T(8,128)(2,1)S(1)} collective-permute-done((bf16[768,128]{1,0:T(8,128)(2,1)S(1)}, bf16[768,128]{1,0:T(8,128)(2,1)S(1)}, u32[]{:S(2)}, u32[]{:S(2)}) %collective-permute-start.24) | collective-permute-done | bytes 196640 | tf_op jit(solution)/shard_map/ppermute | solution.py:606
  142.8 4.8 %finish.4 = (bf16[6144,2,128]{2,1,0:T(2,128)(2,1)}, f32[8,128]{1,0:T(8,128)S(1)}) custom-call(s32[8,128]{1,0:T(8,128)S(1)} %copy-done.16, bf16[2,1024,512]{2,1,0:T(8,128)(2,1)S(1)} %copy-done.5, bf16[1024,512]{1,0:T(8,128)(2,1)S(1)} %collective-permute-done.5.rest_1_, ...), custom_call_target="tpu_custom_call", output_to_operand_aliasing={{0}: (11, {})} | custom-call | flops 12079595 | bytes 39321 | tf_op jit(solution)/shard_map/finish/pallas_call | solution.py:571
  147.6 2.1 %rank_products.7 = bf16[768,128]{1,0:T(8,128)(2,1)S(1)} custom-call(s32[8,128]{1,0:T(8,128)S(1)} %copy-done.16, bf16[3072,2048]{1,0:T(8,128)(2,1)S(1)} %bitcast.12, bf16[3,2304,128]{2,1,0:T(8,128)(2,1)S(1)} %copy-done.2, bf16[3,2304,128]{2,1,0:T(8,128)(2,1)} %get-tuple-element.43.rest_1_.rest_11_.rest_6_.rest_9_, ...), custom_call_target="tpu_custom_call" | custom-call | flops 4026531 | bytes 47185 | tf_op jit(solution)/shard_map/rank_products/pallas_call | solution.py:413
  151.3 1.7 %collective-permute-start.28 = (bf16[768,128]{1,0:T(8,128)(2,1)S(1)}, bf16[768,128]{1,0:T(8,128)(2,1)S(1)}, u32[]{:S(2)}, u32[]{:S(2)}) collective-permute-start(bf16[768,128]{1,0:T(8,128)(2,1)S(1)} %add_convert_fusion.rest_6_), channel_id=1, source_target_pairs={{0,2},{1,3},{2,0},{3,1},{4,6},{5,7},{6,4},{7,5},{8,10},{9,11},{10,... | collective-permute-start | bytes 589832 | tf_op jit(solution)/shard_map/ppermute | solution.py:606
  153.0 5.3 %collective-permute-done.28.rest_7_ = bf16[768,128]{1,0:T(8,128)(2,1)S(1)} collective-permute-done((bf16[768,128]{1,0:T(8,128)(2,1)S(1)}, bf16[768,128]{1,0:T(8,128)(2,1)S(1)}, u32[]{:S(2)}, u32[]{:S(2)}) %collective-permute-start.28) | collective-permute-done | bytes 196640 | tf_op jit(solution)/shard_map/ppermute | solution.py:606
  158.3 5.0 %finish.5 = (bf16[6144,2,128]{2,1,0:T(2,128)(2,1)}, f32[8,128]{1,0:T(8,128)}) custom-call(s32[8,128]{1,0:T(8,128)S(1)} %copy-done.16, bf16[2,1024,512]{2,1,0:T(8,128)(2,1)S(1)} %copy-done.5, bf16[1024,512]{1,0:T(8,128)(2,1)S(1)} %collective-permute-done.5.rest_1_, ...), custom_call_target="tpu_custom_call", output_to_operand_aliasing={{0}: (16, {})} | custom-call | flops 12079595 | bytes 39321 | tf_op jit(solution)/shard_map/finish/pallas_call | solution.py:571
  (118 shorter events, 20.0 us)
Async XLA Ops:
  2.8 27.3 %copy-start = (bf16[3,2304,128]{2,1,0:T(8,128)(2,1)}, bf16[3,2304,128]{2,1,0:T(8,128)(2,1)S(1)}, u32[]{:S(2)}) copy-start(bf16[3,2304,128]{2,1,0:T(8,128)(2,1)S(1)} %pack_maps.1.rest_0_.rest_10_.rest_5_.rest_8_) | copy-start | bytes 5308420
  2.8 43.6 %collective-permute-start.12 = (bf16[3,2304,128]{2,1,0:T(8,128)(2,1)S(1)}, bf16[3,2304,128]{2,1,0:T(8,128)(2,1)}, u32[]{:S(2)}, u32[]{:S(2)}) collective-permute-start(bf16[3,2304,128]{2,1,0:T(8,128)(2,1)S(1)} %pack_maps.1.rest_0_.rest_10_.rest_5_.rest_8_), channel_id=1, source_target_pairs={{4,0},{8,4},{12,8},{5,1},{9,5},{13,9},{6,2},{10,6},{14,10},{7,3},{... | collective-permute-start | bytes 5308424 | tf_op jit(solution)/shard_map/ppermute | solution.py:613
  4.1 43.4 %collective-permute-start.13 = (bf16[3,2304,128]{2,1,0:T(8,128)(2,1)S(1)}, bf16[3,2304,128]{2,1,0:T(8,128)(2,1)}, u32[]{:S(2)}, u32[]{:S(2)}) collective-permute-start(bf16[3,2304,128]{2,1,0:T(8,128)(2,1)S(1)} %pack_maps.1.rest_0_.rest_10_.rest_5_.rest_8_), channel_id=1, source_target_pairs={{0,4},{4,8},{8,12},{1,5},{5,9},{9,13},{2,6},{6,10},{10,14},{3,7},{... | collective-permute-start | bytes 5308424 | tf_op jit(solution)/shard_map/ppermute | solution.py:616
  30.1 2.5 %collective-permute-start = (bf16[512,512]{1,0:T(8,128)(2,1)S(1)}, bf16[512,512]{1,0:T(8,128)(2,1)S(1)}, u32[]{:S(2)}, u32[]{:S(2)}) collective-permute-start(bf16[512,512]{1,0:T(8,128)(2,1)S(1)} %get-tuple-element.31), channel_id=1, source_target_pairs={{0,1},{1,0},{2,3},{3,2},{4,5},{5,4},{6,7},{7,6},{8,9},{9,8},{10,11... | collective-permute-start | bytes 1572872 | tf_op jit(solution)/shard_map/ppermute | solution.py:603
  31.1 1.5 collective-permute-start.1
  33.0 24.4 %collective-permute-start.4 = (bf16[768,512]{1,0:T(8,128)(2,1)S(1)}, bf16[768,512]{1,0:T(8,128)(2,1)S(1)}, u32[]{:S(2)}, u32[]{:S(2)}) collective-permute-start(bf16[768,512]{1,0:T(8,128)(2,1)S(1)} %pair_sum.4.rest_1_), channel_id=1, source_target_pairs={{0,2},{1,3},{2,0},{3,1},{4,6},{5,7},{6,4},{7,5},{8,10},{9,11},{10,... | collective-permute-start | bytes 2359304 | tf_op jit(solution)/shard_map/ppermute | solution.py:606
  47.5 51.7 %collective-permute-start.14 = (bf16[3,2304,128]{2,1,0:T(8,128)(2,1)}, bf16[3,2304,128]{2,1,0:T(8,128)(2,1)}, u32[]{:S(2)}, u32[]{:S(2)}) collective-permute-start(bf16[3,2304,128]{2,1,0:T(8,128)(2,1)} %get-tuple-element.43.rest_1_.rest_11_.rest_6_.rest_9_), channel_id=1, source_target_pairs={{4,0},{8,4},{12,8},{5,1},{9,5},{13,9},{6,2},{10,6},{14,10},{7,3},{... | collective-permute-start | bytes 5308424 | tf_op jit(solution)/shard_map/ppermute | solution.py:613
  48.8 50.4 %collective-permute-start.15 = (bf16[3,2304,128]{2,1,0:T(8,128)(2,1)}, bf16[3,2304,128]{2,1,0:T(8,128)(2,1)}, u32[]{:S(2)}, u32[]{:S(2)}) collective-permute-start(bf16[3,2304,128]{2,1,0:T(8,128)(2,1)} %get-tuple-element.44.rest_2_.rest_3_.rest_12_.rest_8_.rest_4_), channel_id=1, source_target_pairs={{0,4},{4,8},{8,12},{1,5},{5,9},{9,13},{2,6},{6,10},{10,14},{3,7},{... | collective-permute-start | bytes 5308424 | tf_op jit(solution)/shard_map/ppermute | solution.py:616
  55.2 2.3 %collective-permute-start.2 = (bf16[512,512]{1,0:T(8,128)(2,1)S(1)}, bf16[512,512]{1,0:T(8,128)(2,1)S(1)}, u32[]{:S(2)}, u32[]{:S(2)}) collective-permute-start(bf16[512,512]{1,0:T(8,128)(2,1)S(1)} %get-tuple-element.34), channel_id=1, source_target_pairs={{0,1},{1,0},{2,3},{3,2},{4,5},{5,4},{6,7},{7,6},{8,9},{9,8},{10,11... | collective-permute-start | bytes 1572872 | tf_op jit(solution)/shard_map/ppermute | solution.py:603
  55.2 2.3 %collective-permute-start.3 = (bf16[256,512]{1,0:T(8,128)(2,1)S(1)}, bf16[256,512]{1,0:T(8,128)(2,1)S(1)}, u32[]{:S(2)}, u32[]{:S(2)}) collective-permute-start(bf16[256,512]{1,0:T(8,128)(2,1)S(1)} %get-tuple-element.35), channel_id=1, source_target_pairs={{0,1},{1,0},{2,3},{3,2},{4,5},{5,4},{6,7},{7,6},{8,9},{9,8},{10,11... | collective-permute-start | bytes 786440 | tf_op jit(solution)/shard_map/ppermute | solution.py:603
  57.5 21.1 %slice-start = ((s8[12582912]{0:T(1024)(128)(4,1)}), s8[4194304]{0:T(1024)(128)(4,1)S(1)}, s32[]{:S(2)}) async-start(s8[12582912]{0:T(1024)(128)(4,1)} %bitcast.9), calls=%async_computation | async-start | bytes 8388608
  58.7 19.8 %collective-permute-start.8 = (bf16[768,512]{1,0:T(8,128)(2,1)}, bf16[768,512]{1,0:T(8,128)(2,1)S(1)}, u32[]{:S(2)}, u32[]{:S(2)}) collective-permute-start(bf16[768,512]{1,0:T(8,128)(2,1)} %pair_sum.5.rest_1_), channel_id=1, source_target_pairs={{0,2},{1,3},{2,0},{3,1},{4,6},{5,7},{6,4},{7,5},{8,10},{9,11},{10,... | collective-permute-start | bytes 2359304 | tf_op jit(solution)/shard_map/ppermute | solution.py:606
  75.7 7.0 %collective-permute-start.6 = (bf16[512,512]{1,0:T(8,128)(2,1)S(1)}, bf16[512,512]{1,0:T(8,128)(2,1)S(1)}, u32[]{:S(2)}, u32[]{:S(2)}) collective-permute-start(bf16[512,512]{1,0:T(8,128)(2,1)S(1)} %get-tuple-element.38), channel_id=1, source_target_pairs={{0,1},{1,0},{2,3},{3,2},{4,5},{5,4},{6,7},{7,6},{8,9},{9,8},{10,11... | collective-permute-start | bytes 1572872 | tf_op jit(solution)/shard_map/ppermute | solution.py:603
  75.7 7.0 %collective-permute-start.7 = (bf16[512,512]{1,0:T(8,128)(2,1)S(1)}, bf16[512,512]{1,0:T(8,128)(2,1)S(1)}, u32[]{:S(2)}, u32[]{:S(2)}) collective-permute-start(bf16[512,512]{1,0:T(8,128)(2,1)S(1)} %get-tuple-element.39), channel_id=1, source_target_pairs={{0,1},{1,0},{2,3},{3,2},{4,5},{5,4},{6,7},{7,6},{8,9},{9,8},{10,11... | collective-permute-start | bytes 1572872 | tf_op jit(solution)/shard_map/ppermute | solution.py:603
  78.5 28.9 %collective-permute-start.25 = (bf16[768,512]{1,0:T(8,128)(2,1)}, bf16[768,512]{1,0:T(8,128)(2,1)}, u32[]{:S(2)}, u32[]{:S(2)}) collective-permute-start(bf16[768,512]{1,0:T(8,128)(2,1)} %copy-done.22), channel_id=1, source_target_pairs={{0,1},{1,0},{2,3},{3,2},{4,5},{5,4},{6,7},{7,6},{8,9},{9,8},{10,11... | collective-permute-start | bytes 2359304 | tf_op jit(solution)/shard_map/ppermute | solution.py:603
  85.7 34.0 %collective-permute-start.9 = (bf16[1024,512]{1,0:T(8,128)(2,1)}, bf16[1024,512]{1,0:T(8,128)(2,1)S(1)}, u32[]{:S(2)}, u32[]{:S(2)}) collective-permute-start(bf16[1024,512]{1,0:T(8,128)(2,1)} %pair_sum.6.rest_1_), channel_id=1, source_target_pairs={{0,2},{1,3},{2,0},{3,1},{4,6},{5,7},{6,4},{7,5},{8,10},{9,11},{10,... | collective-permute-start | bytes 3145736 | tf_op jit(solution)/shard_map/ppermute | solution.py:606
  99.1 21.1 %copy-start.16 = (s32[8,128]{1,0:T(8,128)S(1)}, s32[8,128]{1,0:T(8,128)}, u32[]{:S(2)}) copy-start(s32[8,128]{1,0:T(8,128)} %plan_requests.1.plan_ref) | copy-start | bytes 12292
  99.1 6.4 %collective-permute-start.18 = (bf16[768,128]{1,0:T(8,128)(2,1)S(1)}, bf16[768,128]{1,0:T(8,128)(2,1)S(1)}, u32[]{:S(2)}, u32[]{:S(2)}) collective-permute-start(bf16[768,128]{1,0:T(8,128)(2,1)S(1)} %rank_products.5.rest_5_), channel_id=1, source_target_pairs={{0,1},{1,0},{2,3},{3,2},{4,5},{5,4},{6,7},{7,6},{8,9},{9,8},{10,11... | collective-permute-start | bytes 589832 | tf_op jit(solution)/shard_map/ppermute | solution.py:603
  99.2 48.4 %collective-permute-start.21 = (bf16[3,2304,128]{2,1,0:T(8,128)(2,1)}, bf16[3,2304,128]{2,1,0:T(8,128)(2,1)S(1)}, u32[]{:S(2)}, u32[]{:S(2)}) collective-permute-start(bf16[3,2304,128]{2,1,0:T(8,128)(2,1)} %get-tuple-element.45.rest_2_.rest_7_.rest_10_), channel_id=1, source_target_pairs={{4,0},{8,4},{12,8},{5,1},{9,5},{13,9},{6,2},{10,6},{14,10},{7,3},{... | collective-permute-start | bytes 5308424 | tf_op jit(solution)/shard_map/ppermute | solution.py:613
  100.7 46.9 %collective-permute-start.22 = (bf16[3,2304,128]{2,1,0:T(8,128)(2,1)}, bf16[3,2304,128]{2,1,0:T(8,128)(2,1)S(1)}, u32[]{:S(2)}, u32[]{:S(2)}) collective-permute-start(bf16[3,2304,128]{2,1,0:T(8,128)(2,1)} %get-tuple-element.46.rest_4_.rest_9_.rest_5_.rest_13_), channel_id=1, source_target_pairs={{0,4},{4,8},{8,12},{1,5},{5,9},{9,13},{2,6},{6,10},{10,14},{3,7},{... | collective-permute-start | bytes 5308424 | tf_op jit(solution)/shard_map/ppermute | solution.py:616
  105.5 1.5 collective-permute-start.16
  107.0 9.1 %collective-permute-start.19 = (bf16[768,128]{1,0:T(8,128)(2,1)S(1)}, bf16[768,128]{1,0:T(8,128)(2,1)S(1)}, u32[]{:S(2)}, u32[]{:S(2)}) collective-permute-start(bf16[768,128]{1,0:T(8,128)(2,1)S(1)} %add_convert_fusion.2.rest_8_), channel_id=1, source_target_pairs={{0,2},{1,3},{2,0},{3,1},{4,6},{5,7},{6,4},{7,5},{8,10},{9,11},{10,... | collective-permute-start | bytes 589832 | tf_op jit(solution)/shard_map/ppermute | solution.py:606
  107.4 12.2 %collective-permute-start.17 = (bf16[768,128]{1,0:T(8,128)(2,1)S(1)}, bf16[768,128]{1,0:T(8,128)(2,1)S(1)}, u32[]{:S(2)}, u32[]{:S(2)}) collective-permute-start(bf16[768,128]{1,0:T(8,128)(2,1)S(1)} %add_convert_fusion.3.rest_6_), channel_id=1, source_target_pairs={{0,2},{1,3},{2,0},{3,1},{4,6},{5,7},{6,4},{7,5},{8,10},{9,11},{10,... | collective-permute-start | bytes 589832 | tf_op jit(solution)/shard_map/ppermute | solution.py:606
  116.1 6.9 %collective-permute-start.11 = (bf16[512,512]{1,0:T(8,128)(2,1)S(1)}, bf16[512,512]{1,0:T(8,128)(2,1)S(1)}, u32[]{:S(2)}, u32[]{:S(2)}) collective-permute-start(bf16[512,512]{1,0:T(8,128)(2,1)S(1)} %copy-done.26), channel_id=1, source_target_pairs={{0,1},{1,0},{2,3},{3,2},{4,5},{5,4},{6,7},{7,6},{8,9},{9,8},{10,11... | collective-permute-start | bytes 1572872 | tf_op jit(solution)/shard_map/ppermute | solution.py:603
  119.6 15.4 %collective-permute-start.5 = (bf16[1024,512]{1,0:T(8,128)(2,1)S(1)}, bf16[1024,512]{1,0:T(8,128)(2,1)S(1)}, u32[]{:S(2)}, u32[]{:S(2)}) collective-permute-start(bf16[1024,512]{1,0:T(8,128)(2,1)S(1)} %copy-done.19), channel_id=1, source_target_pairs={{0,1},{1,0},{2,3},{3,2},{4,5},{5,4},{6,7},{7,6},{8,9},{9,8},{10,11... | collective-permute-start | bytes 3145736 | tf_op jit(solution)/shard_map/ppermute | solution.py:603
  119.7 6.7 %collective-permute-start.26 = (bf16[768,512]{1,0:T(8,128)(2,1)S(1)}, bf16[768,512]{1,0:T(8,128)(2,1)S(1)}, u32[]{:S(2)}, u32[]{:S(2)}) collective-permute-start(bf16[768,512]{1,0:T(8,128)(2,1)S(1)} %copy-done.21), channel_id=1, source_target_pairs={{0,1},{1,0},{2,3},{3,2},{4,5},{5,4},{6,7},{7,6},{8,9},{9,8},{10,11... | collective-permute-start | bytes 2359304 | tf_op jit(solution)/shard_map/ppermute | solution.py:603
  123.1 1.5 collective-permute-start.23
  124.6 23.0 %collective-permute-start.20 = (bf16[512,512]{1,0:T(8,128)(2,1)S(1)}, bf16[512,512]{1,0:T(8,128)(2,1)S(1)}, u32[]{:S(2)}, u32[]{:S(2)}) collective-permute-start(bf16[512,512]{1,0:T(8,128)(2,1)S(1)} %pair_sum.7), channel_id=1, source_target_pairs={{0,2},{1,3},{2,0},{3,1},{4,6},{5,7},{6,4},{7,5},{8,10},{9,11},{10,... | collective-permute-start | bytes 1572872 | tf_op jit(solution)/shard_map/ppermute | solution.py:606
  126.3 16.4 %collective-permute-start.24 = (bf16[768,128]{1,0:T(8,128)(2,1)S(1)}, bf16[768,128]{1,0:T(8,128)(2,1)S(1)}, u32[]{:S(2)}, u32[]{:S(2)}) collective-permute-start(bf16[768,128]{1,0:T(8,128)(2,1)S(1)} %add_convert_fusion.1.rest_3_), channel_id=1, source_target_pairs={{0,2},{1,3},{2,0},{3,1},{4,6},{5,7},{6,4},{7,5},{8,10},{9,11},{10,... | collective-permute-start | bytes 589832 | tf_op jit(solution)/shard_map/ppermute | solution.py:606
  149.7 1.5 collective-permute-start.27
  149.8 3.2 %collective-permute-start.10 = (bf16[512,512]{1,0:T(8,128)(2,1)S(1)}, bf16[512,512]{1,0:T(8,128)(2,1)S(1)}, u32[]{:S(2)}, u32[]{:S(2)}) collective-permute-start(bf16[512,512]{1,0:T(8,128)(2,1)S(1)} %copy-done.24), channel_id=1, source_target_pairs={{0,1},{1,0},{2,3},{3,2},{4,5},{5,4},{6,7},{7,6},{8,9},{9,8},{10,11... | collective-permute-start | bytes 1572872 | tf_op jit(solution)/shard_map/ppermute | solution.py:603
  151.3 7.0 %collective-permute-start.28 = (bf16[768,128]{1,0:T(8,128)(2,1)S(1)}, bf16[768,128]{1,0:T(8,128)(2,1)S(1)}, u32[]{:S(2)}, u32[]{:S(2)}) collective-permute-start(bf16[768,128]{1,0:T(8,128)(2,1)S(1)} %add_convert_fusion.rest_6_), channel_id=1, source_target_pairs={{0,2},{1,3},{2,0},{3,1},{4,6},{5,7},{6,4},{7,5},{8,10},{9,11},{10,... | collective-permute-start | bytes 589832 | tf_op jit(solution)/shard_map/ppermute | solution.py:606
  (30 other events, 222.5 us)

commit v10 on v9

--- a/solution.py
+++ b/solution.py
@@ -720,9 +720,9 @@
         send_on(*fourth, [part, bases[2][2][-1]] + summed)
         for chunk in range(len(ranks), 3):
             part = rank(chunk, [pairs[-1]])
-        out, _ = write(None, 0, 2)
-        out, written = write(out, 2, 3)
+        out, written = write(None, 0, 2)
         rank(3, [written, bases[3][2][-1]])
+        out, _ = write(out, 2, 3)
         out, _ = write(out, 3, 4)
         tiles = out.shape[0] // shape[0]
         out = out.reshape(shape[0], tiles, 2, columns // tiles)

time: 165 us -> 168 us (1.018)
  waiting for transfers between devices: 34.9 us -> 37.5 us
  starting transfers between devices: 35.9 us -> 34 us
    ppermute x3, waiting for transfers between devices: 1.42 us -> 6.94 us  [leftward(): return lax.ppermute(a, 'adapter', [(z, z - hops) for z in range(hops, n_z)])]
    ppermute x8, waiting for transfers between devices: 25.8 us -> 23.2 us  [chip_shift(): lax.ppermute(a, 'tensor', [(2 * x + c, 2 * ((x + k) % n_x) + c) for x in...]
    ppermute x8, starting transfers between devices: 11.3 us -> 9.57 us  [chip_shift(): lax.ppermute(a, 'tensor', [(2 * x + c, 2 * ((x + k) % n_x) + c) for x in...]
    unnamed x66 -> x68, local copies, waits for them, and re-layouts: 9.19 us -> 9.45 us
  transfers between devices with their start and end apart: 29 -> 29, of which waited for: 12 -> 12; matrix products, arithmetic and copies ran while one was open for 0% -> 0% of each run, Pallas kernels for 46% -> 47%
where the time goes in v10:
time: 168 us; the launch traced here: 165 us
  Pallas kernels  83.3 us (50%)
  waiting for transfers between devices  37.5 us (22%)
  starting transfers between devices  34 us (20%)
  local copies, waits for them, and re-layouts  9.45 us (6%)
    pallas_call x3, Pallas kernels, base_products(): pl.pallas_call(body, out_shape=(*[jax.ShapeDtypeStruct((n * prefill, widt...  33.4 us
    ppermute x8, waiting for transfers between devices, chip_shift(): lax.ppermute(a, 'tensor', [(2 * x + c, 2 * ((x + k) % n_x) + c) for x in...  23.2 us
    pallas_call x3, Pallas kernels, finish(): pl.pallas_call(body, out_shape=(jax.ShapeDtypeStruct((shape[0] * tiles, 2...  17.8 us
    ppermute x3, starting transfers between devices, rightward(): return lax.ppermute(a, 'adapter', [(z - hops, z) for z in range(hops, n_z)])  17.6 us
    pallas_call x1, Pallas kernels, split_weight(): pl.pallas_call(body, out_shape=(jax.ShapeDtypeStruct((n_t, features, 2 *...  17 us
    pallas_call x4, Pallas kernels, rank_products(): pl.pallas_call(body, out_shape=jax.ShapeDtypeStruct((count * prefill, ran...  10 us
    ppermute x8, starting transfers between devices, chip_shift(): lax.ppermute(a, 'tensor', [(2 * x + c, 2 * ((x + k) % n_x) + c) for x in...  9.57 us
    unnamed x68, local copies, waits for them, and re-layouts  9.45 us
  transfers between devices with their start and end apart: 29, of which 12 were waited for; matrix products, arithmetic and copies ran while one was open for 0% of the time, Pallas kernels for 47%

profile of v10, /device:TPU:0, one launch (start us, length us, event | category | flops | bytes accessed | tf_op | source)
XLA Modules:
  0.0 165.3 jit_solution(15863702238994164495)
XLA Ops:
  0.0 1.4 copy-done.14
  4.1 6.8 %collective-permute-start.13 = (bf16[3,2304,128]{2,1,0:T(8,128)(2,1)S(1)}, bf16[3,2304,128]{2,1,0:T(8,128)(2,1)}, u32[]{:S(2)}, u32[]{:S(2)}) collective-permute-start(bf16[3,2304,128]{2,1,0:T(8,128)(2,1)S(1)} %pack_maps.1.rest_0_.rest_10_.rest_5_.rest_8_), channel_id=1, source_target_pairs={{0,4},{4,8},{8,12},{1,5},{5,9},{9,13},{2,6},{6,10},{10,14},{3,7},{... | collective-permute-start | bytes 5308424 | tf_op jit(solution)/shard_map/ppermute | solution.py:616
  10.9 1.6 plan_requests.1.plan_ref
  13.2 17.0 %split_weight.1 = (bf16[4,2048,512]{2,1,0:T(8,128)(2,1)}, bf16[768,512]{1,0:T(8,128)(2,1)S(1)}, bf16[512,512]{1,0:T(8,128)(2,1)S(1)}, bf16[256,512]{1,0:T(8,128)(2,1)S(1)}, bf16[2,768,512]{2,1,0:T(8,128)(2,1)S(1)}) custom-call(s32[8,128]{1,0:T(8,128)S(1)} %copy-done.15, s32[4]{0:T(128)S(1)} %compare_select_fusion.2.slot_ref, bf16[3072,2048]{1,0:T(8,128)(2,1)} %x_ref.13, ...), custom_call_target="tpu_custom_call" | custom-call | flops 64424508 | bytes 167772 | tf_op jit(solution)/shard_map/split_weight/pallas_call | solution.py:184
  31.6 1.8 %collective-permute-done.1.rest_1_ = bf16[256,512]{1,0:T(8,128)(2,1)S(1)} collective-permute-done((bf16[256,512]{1,0:T(8,128)(2,1)S(1)}, bf16[256,512]{1,0:T(8,128)(2,1)S(1)}, u32[]{:S(2)}, u32[]{:S(2)}) %collective-permute-start.1) | collective-permute-done | bytes 262176 | tf_op jit(solution)/shard_map/ppermute | solution.py:603
  33.8 2.0 %collective-permute-start.4 = (bf16[768,512]{1,0:T(8,128)(2,1)S(1)}, bf16[768,512]{1,0:T(8,128)(2,1)S(1)}, u32[]{:S(2)}, u32[]{:S(2)}) collective-permute-start(bf16[768,512]{1,0:T(8,128)(2,1)S(1)} %pair_sum.4.rest_1_), channel_id=1, source_target_pairs={{0,2},{1,3},{2,0},{3,1},{4,6},{5,7},{6,4},{7,5},{8,10},{9,11},{10,... | collective-permute-start | bytes 2359304 | tf_op jit(solution)/shard_map/ppermute | solution.py:606
  35.8 11.0 %base_products.3 = (bf16[768,512]{1,0:T(8,128)(2,1)S(1)}, bf16[512,512]{1,0:T(8,128)(2,1)S(1)}, bf16[256,512]{1,0:T(8,128)(2,1)S(1)}, bf16[2,768,512]{2,1,0:T(8,128)(2,1)S(1)}) custom-call(s32[8,128]{1,0:T(8,128)S(1)} %copy-done.15, bf16[3072,2048]{1,0:T(8,128)(2,1)} %x_ref.13, bf16[4,2048,512]{2,1,0:T(8,128)(2,1)} %get-tuple-element.29.rest_0_, ...), custom_call_target="tpu_custom_call" | custom-call | flops 64424508 | bytes 83886 | tf_op jit(solution)/shard_map/base_products/pallas_call | solution.py:260
  49.0 6.2 %collective-permute-start.15 = (bf16[3,2304,128]{2,1,0:T(8,128)(2,1)}, bf16[3,2304,128]{2,1,0:T(8,128)(2,1)}, u32[]{:S(2)}, u32[]{:S(2)}) collective-permute-start(bf16[3,2304,128]{2,1,0:T(8,128)(2,1)} %get-tuple-element.44.rest_2_.rest_3_.rest_12_.rest_4_.rest_8_), channel_id=1, source_target_pairs={{0,4},{4,8},{8,12},{1,5},{5,9},{9,13},{2,6},{6,10},{10,14},{3,7},{... | collective-permute-start | bytes 5308424 | tf_op jit(solution)/shard_map/ppermute | solution.py:616
  55.7 1.8 %collective-permute-done.3.rest_1_ = bf16[256,512]{1,0:T(8,128)(2,1)S(1)} collective-permute-done((bf16[256,512]{1,0:T(8,128)(2,1)S(1)}, bf16[256,512]{1,0:T(8,128)(2,1)S(1)}, u32[]{:S(2)}, u32[]{:S(2)}) %collective-permute-start.3) | collective-permute-done | bytes 262176 | tf_op jit(solution)/shard_map/ppermute | solution.py:603
  58.7 1.7 %collective-permute-start.8 = (bf16[768,512]{1,0:T(8,128)(2,1)}, bf16[768,512]{1,0:T(8,128)(2,1)S(1)}, u32[]{:S(2)}, u32[]{:S(2)}) collective-permute-start(bf16[768,512]{1,0:T(8,128)(2,1)} %pair_sum.5.rest_1_), channel_id=1, source_target_pairs={{0,2},{1,3},{2,0},{3,1},{4,6},{5,7},{6,4},{7,5},{8,10},{9,11},{10,... | collective-permute-start | bytes 2359304 | tf_op jit(solution)/shard_map/ppermute | solution.py:606
  60.4 13.2 %base_products.4 = (bf16[1024,512]{1,0:T(8,128)(2,1)S(1)}, bf16[512,512]{1,0:T(8,128)(2,1)S(1)}, bf16[512,512]{1,0:T(8,128)(2,1)S(1)}, bf16[2,1024,512]{2,1,0:T(8,128)(2,1)S(1)}) custom-call(s32[8,128]{1,0:T(8,128)S(1)} %copy-done.15, bf16[3072,2048]{1,0:T(8,128)(2,1)} %x_ref.13, bf16[4,2048,512]{2,1,0:T(8,128)(2,1)} %get-tuple-element.29.rest_0_, ...), custom_call_target="tpu_custom_call" | custom-call | flops 85899344 | bytes 83886 | tf_op jit(solution)/shard_map/base_products/pallas_call | solution.py:260
  75.1 3.4 %collective-permute-done.8.rest_2_.rest_3_.rest_5_ = bf16[768,512]{1,0:T(8,128)(2,1)S(1)} collective-permute-done((bf16[768,512]{1,0:T(8,128)(2,1)}, bf16[768,512]{1,0:T(8,128)(2,1)S(1)}, u32[]{:S(2)}, u32[]{:S(2)}) %collective-permute-start.8) | collective-permute-done | bytes 786464 | tf_op jit(solution)/shard_map/ppermute | solution.py:606
  78.6 1.8 %copy-done.1 = bf16[3,2304,128]{2,1,0:T(8,128)(2,1)S(1)} copy-done((bf16[3,2304,128]{2,1,0:T(8,128)(2,1)S(1)}, bf16[3,2304,128]{2,1,0:T(8,128)(2,1)}, u32[]{:S(2)}) %copy-start.1) | copy-done | bytes 1769496
  80.3 2.1 %rank_products.4.rest_2_ = bf16[768,128]{1,0:T(8,128)(2,1)S(1)} custom-call(s32[8,128]{1,0:T(8,128)S(1)} %copy-done.15, bf16[3072,2048]{1,0:T(8,128)(2,1)S(1)} %bitcast.10, bf16[3,2304,128]{2,1,0:T(8,128)(2,1)S(1)} %copy-done.1, bf16[2,1024,512]{2,1,0:T(8,128)(2,1)S(1)} %get-tuple-element.36.rest_1_.a_ref.rest_0_, ...), custom_call_target="tpu_custom_call" | custom-call | flops 4026531 | bytes 47185 | tf_op jit(solution)/shard_map/rank_products/pallas_call | solution.py:413
  82.4 1.6 copy-done.4
  84.0 1.3 pair_sum.6.rest_1_
  85.4 1.7 %collective-permute-start.9 = (bf16[1024,512]{1,0:T(8,128)(2,1)}, bf16[1024,512]{1,0:T(8,128)(2,1)S(1)}, u32[]{:S(2)}, u32[]{:S(2)}) collective-permute-start(bf16[1024,512]{1,0:T(8,128)(2,1)} %pair_sum.6.rest_1_), channel_id=1, source_target_pairs={{0,2},{1,3},{2,0},{3,1},{4,6},{5,7},{6,4},{7,5},{8,10},{9,11},{10,... | collective-permute-start | bytes 3145736 | tf_op jit(solution)/shard_map/ppermute | solution.py:606
  87.1 9.2 %base_products.5 = (bf16[512,512]{1,0:T(8,128)(2,1)S(1)}, bf16[512,512]{1,0:T(8,128)(2,1)S(1)}, bf16[2,512,512]{2,1,0:T(8,128)(2,1)S(1)}) custom-call(s32[8,128]{1,0:T(8,128)S(1)} %copy-done.15, bf16[3072,2048]{1,0:T(8,128)(2,1)} %x_ref.13, bf16[4,2048,512]{2,1,0:T(8,128)(2,1)} %get-tuple-element.29.rest_0_, bf16[1024,512]{1,0:T(8,128)(2,1)} %pair_sum.6.rest_1_), custom_call_target="tpu_custom_call" | custom-call | flops 42949672 | bytes 83886 | tf_op jit(solution)/shard_map/base_products/pallas_call | solution.py:260
  97.1 2.9 %rank_products.5.rest_5_ = bf16[768,128]{1,0:T(8,128)(2,1)S(1)} custom-call(s32[8,128]{1,0:T(8,128)S(1)} %copy-done.15, bf16[3072,2048]{1,0:T(8,128)(2,1)S(1)} %bitcast.12, bf16[3,2304,128]{2,1,0:T(8,128)(2,1)S(1)} %copy-done.2, bf16[3,2304,128]{2,1,0:T(8,128)(2,1)} %get-tuple-element.43.rest_1_.rest_11_.rest_6_.rest_9_, ...), custom_call_target="tpu_custom_call" | custom-call | flops 4026531 | bytes 47185 | tf_op jit(solution)/shard_map/rank_products/pallas_call | solution.py:413
  100.1 1.4 collective-permute-start.21
  101.6 4.7 %collective-permute-start.22 = (bf16[3,2304,128]{2,1,0:T(8,128)(2,1)}, bf16[3,2304,128]{2,1,0:T(8,128)(2,1)S(1)}, u32[]{:S(2)}, u32[]{:S(2)}) collective-permute-start(bf16[3,2304,128]{2,1,0:T(8,128)(2,1)} %get-tuple-element.46.rest_4_.rest_5_.rest_9_.rest_13_), channel_id=1, source_target_pairs={{0,4},{4,8},{8,12},{1,5},{5,9},{9,13},{2,6},{6,10},{10,14},{3,7},{... | collective-permute-start | bytes 5308424 | tf_op jit(solution)/shard_map/ppermute | solution.py:616
  108.6 6.5 %collective-permute-done.19.rest_4_.rest_9_ = bf16[768,128]{1,0:T(8,128)(2,1)S(1)} collective-permute-done((bf16[768,128]{1,0:T(8,128)(2,1)S(1)}, bf16[768,128]{1,0:T(8,128)(2,1)S(1)}, u32[]{:S(2)}, u32[]{:S(2)}) %collective-permute-start.19) | collective-permute-done | bytes 196640 | tf_op jit(solution)/shard_map/ppermute | solution.py:606
  115.1 3.4 %collective-permute-done.17.rest_3_.rest_7_ = bf16[768,128]{1,0:T(8,128)(2,1)S(1)} collective-permute-done((bf16[768,128]{1,0:T(8,128)(2,1)S(1)}, bf16[768,128]{1,0:T(8,128)(2,1)S(1)}, u32[]{:S(2)}, u32[]{:S(2)}) %collective-permute-start.17) | collective-permute-done | bytes 196640 | tf_op jit(solution)/shard_map/ppermute | solution.py:606
  119.1 2.9 %rank_products.6.rest_1_ = bf16[768,128]{1,0:T(8,128)(2,1)S(1)} custom-call(s32[8,128]{1,0:T(8,128)S(1)} %copy-done.16, bf16[3072,2048]{1,0:T(8,128)(2,1)S(1)} %bitcast.12, bf16[3,2304,128]{2,1,0:T(8,128)(2,1)S(1)} %copy-done.2, bf16[3,2304,128]{2,1,0:T(8,128)(2,1)} %get-tuple-element.43.rest_1_.rest_11_.rest_6_.rest_9_, ...), custom_call_target="tpu_custom_call" | custom-call | flops 4026531 | bytes 47185 | tf_op jit(solution)/shard_map/rank_products/pallas_call | solution.py:413
  122.3 1.7 %collective-permute-start.20 = (bf16[512,512]{1,0:T(8,128)(2,1)S(1)}, bf16[512,512]{1,0:T(8,128)(2,1)S(1)}, u32[]{:S(2)}, u32[]{:S(2)}) collective-permute-start(bf16[512,512]{1,0:T(8,128)(2,1)S(1)} %pair_sum.7), channel_id=1, source_target_pairs={{0,2},{1,3},{2,0},{3,1},{4,6},{5,7},{6,4},{7,5},{8,10},{9,11},{10,... | collective-permute-start | bytes 1572872 | tf_op jit(solution)/shard_map/ppermute | solution.py:606
  124.6 7.4 %finish.3 = (bf16[6144,2,128]{2,1,0:T(2,128)(2,1)}, f32[8,128]{1,0:T(8,128)S(1)}) custom-call(s32[8,128]{1,0:T(8,128)S(1)} %copy-done.16, bf16[2,768,512]{2,1,0:T(8,128)(2,1)S(1)} %copy-done.11, bf16[768,512]{1,0:T(8,128)(2,1)S(1)} %collective-permute-done.23.rest_1_, bf16[768,512]{1,0:T(8,128)(2,1)S(1)} %copy-done.13, bf16[2,768,512]{2,1,0:T(8,128)(2,1)S(1)} %copy-done.7, ...), custom_call_target="tpu_custom_call" | custom-call | flops 24159192 | bytes 78643 | tf_op jit(solution)/shard_map/finish/pallas_call | solution.py:571
  132.0 4.2 %collective-permute-done.20.rest_8_.rest_5_ = bf16[512,512]{1,0:T(8,128)(2,1)S(1)} collective-permute-done((bf16[512,512]{1,0:T(8,128)(2,1)S(1)}, bf16[512,512]{1,0:T(8,128)(2,1)S(1)}, u32[]{:S(2)}, u32[]{:S(2)}) %collective-permute-start.20) | collective-permute-done | bytes 524320 | tf_op jit(solution)/shard_map/ppermute | solution.py:606
  136.3 6.9 %collective-permute-done.21.rest_3_.rest_11_ = bf16[3,2304,128]{2,1,0:T(8,128)(2,1)S(1)} collective-permute-done((bf16[3,2304,128]{2,1,0:T(8,128)(2,1)}, bf16[3,2304,128]{2,1,0:T(8,128)(2,1)S(1)}, u32[]{:S(2)}, u32[]{:S(2)}) %collective-permute-start.21) | collective-permute-done | bytes 1769504 | tf_op jit(solution)/shard_map/ppermute | solution.py:613
  144.5 2.2 %rank_products.7 = bf16[768,128]{1,0:T(8,128)(2,1)S(1)} custom-call(s32[8,128]{1,0:T(8,128)S(1)} %copy-done.16, bf16[3072,2048]{1,0:T(8,128)(2,1)S(1)} %bitcast.12, bf16[3,2304,128]{2,1,0:T(8,128)(2,1)S(1)} %copy-done.2, bf16[3,2304,128]{2,1,0:T(8,128)(2,1)} %get-tuple-element.43.rest_1_.rest_11_.rest_6_.rest_9_, ...), custom_call_target="tpu_custom_call" | custom-call | flops 4026531 | bytes 47185 | tf_op jit(solution)/shard_map/rank_products/pallas_call | solution.py:413
  149.1 5.5 %collective-permute-done.28.rest_4_ = bf16[768,128]{1,0:T(8,128)(2,1)S(1)} collective-permute-done((bf16[768,128]{1,0:T(8,128)(2,1)S(1)}, bf16[768,128]{1,0:T(8,128)(2,1)S(1)}, u32[]{:S(2)}, u32[]{:S(2)}) %collective-permute-start.28) | collective-permute-done | bytes 196640 | tf_op jit(solution)/shard_map/ppermute | solution.py:606
  154.6 5.0 %finish.4 = (bf16[6144,2,128]{2,1,0:T(2,128)(2,1)}, f32[8,128]{1,0:T(8,128)}) custom-call(s32[8,128]{1,0:T(8,128)S(1)} %copy-done.16, bf16[2,1024,512]{2,1,0:T(8,128)(2,1)S(1)} %copy-done.5, bf16[1024,512]{1,0:T(8,128)(2,1)S(1)} %collective-permute-done.5.rest_1_, ...), custom_call_target="tpu_custom_call", output_to_operand_aliasing={{0}: (11, {})} | custom-call | flops 12079595 | bytes 39321 | tf_op jit(solution)/shard_map/finish/pallas_call | solution.py:571
  159.7 5.4 %finish.5 = (bf16[6144,2,128]{2,1,0:T(2,128)(2,1)}, f32[8,128]{1,0:T(8,128)}) custom-call(s32[8,128]{1,0:T(8,128)S(1)} %copy-done.16, bf16[2,1024,512]{2,1,0:T(8,128)(2,1)S(1)} %copy-done.5, bf16[1024,512]{1,0:T(8,128)(2,1)S(1)} %collective-permute-done.5.rest_1_, ...), custom_call_target="tpu_custom_call", output_to_operand_aliasing={{0}: (16, {})} | custom-call | flops 12079595 | bytes 39321 | tf_op jit(solution)/shard_map/finish/pallas_call | solution.py:571
  (120 shorter events, 18.9 us)
Async XLA Ops:
  2.8 27.3 %copy-start = (bf16[3,2304,128]{2,1,0:T(8,128)(2,1)}, bf16[3,2304,128]{2,1,0:T(8,128)(2,1)S(1)}, u32[]{:S(2)}) copy-start(bf16[3,2304,128]{2,1,0:T(8,128)(2,1)S(1)} %pack_maps.1.rest_0_.rest_10_.rest_5_.rest_8_) | copy-start | bytes 5308420
  2.8 44.0 %collective-permute-start.12 = (bf16[3,2304,128]{2,1,0:T(8,128)(2,1)S(1)}, bf16[3,2304,128]{2,1,0:T(8,128)(2,1)}, u32[]{:S(2)}, u32[]{:S(2)}) collective-permute-start(bf16[3,2304,128]{2,1,0:T(8,128)(2,1)S(1)} %pack_maps.1.rest_0_.rest_10_.rest_5_.rest_8_), channel_id=1, source_target_pairs={{4,0},{8,4},{12,8},{5,1},{9,5},{13,9},{6,2},{10,6},{14,10},{7,3},{... | collective-permute-start | bytes 5308424 | tf_op jit(solution)/shard_map/ppermute | solution.py:613
  4.1 43.4 %collective-permute-start.13 = (bf16[3,2304,128]{2,1,0:T(8,128)(2,1)S(1)}, bf16[3,2304,128]{2,1,0:T(8,128)(2,1)}, u32[]{:S(2)}, u32[]{:S(2)}) collective-permute-start(bf16[3,2304,128]{2,1,0:T(8,128)(2,1)S(1)} %pack_maps.1.rest_0_.rest_10_.rest_5_.rest_8_), channel_id=1, source_target_pairs={{0,4},{4,8},{8,12},{1,5},{5,9},{9,13},{2,6},{6,10},{10,14},{3,7},{... | collective-permute-start | bytes 5308424 | tf_op jit(solution)/shard_map/ppermute | solution.py:616
  31.1 2.3 %collective-permute-start = (bf16[512,512]{1,0:T(8,128)(2,1)S(1)}, bf16[512,512]{1,0:T(8,128)(2,1)S(1)}, u32[]{:S(2)}, u32[]{:S(2)}) collective-permute-start(bf16[512,512]{1,0:T(8,128)(2,1)S(1)} %get-tuple-element.31), channel_id=1, source_target_pairs={{0,1},{1,0},{2,3},{3,2},{4,5},{5,4},{6,7},{7,6},{8,9},{9,8},{10,11... | collective-permute-start | bytes 1572872 | tf_op jit(solution)/shard_map/ppermute | solution.py:603
  31.1 2.3 %collective-permute-start.1 = (bf16[256,512]{1,0:T(8,128)(2,1)S(1)}, bf16[256,512]{1,0:T(8,128)(2,1)S(1)}, u32[]{:S(2)}, u32[]{:S(2)}) collective-permute-start(bf16[256,512]{1,0:T(8,128)(2,1)S(1)} %get-tuple-element.32), channel_id=1, source_target_pairs={{0,1},{1,0},{2,3},{3,2},{4,5},{5,4},{6,7},{7,6},{8,9},{9,8},{10,11... | collective-permute-start | bytes 786440 | tf_op jit(solution)/shard_map/ppermute | solution.py:603
  33.8 23.6 %collective-permute-start.4 = (bf16[768,512]{1,0:T(8,128)(2,1)S(1)}, bf16[768,512]{1,0:T(8,128)(2,1)S(1)}, u32[]{:S(2)}, u32[]{:S(2)}) collective-permute-start(bf16[768,512]{1,0:T(8,128)(2,1)S(1)} %pair_sum.4.rest_1_), channel_id=1, source_target_pairs={{0,2},{1,3},{2,0},{3,1},{4,6},{5,7},{6,4},{7,5},{8,10},{9,11},{10,... | collective-permute-start | bytes 2359304 | tf_op jit(solution)/shard_map/ppermute | solution.py:606
  47.7 52.4 %collective-permute-start.14 = (bf16[3,2304,128]{2,1,0:T(8,128)(2,1)}, bf16[3,2304,128]{2,1,0:T(8,128)(2,1)}, u32[]{:S(2)}, u32[]{:S(2)}) collective-permute-start(bf16[3,2304,128]{2,1,0:T(8,128)(2,1)} %get-tuple-element.43.rest_1_.rest_11_.rest_6_.rest_9_), channel_id=1, source_target_pairs={{4,0},{8,4},{12,8},{5,1},{9,5},{13,9},{6,2},{10,6},{14,10},{7,3},{... | collective-permute-start | bytes 5308424 | tf_op jit(solution)/shard_map/ppermute | solution.py:613
  49.0 51.1 %collective-permute-start.15 = (bf16[3,2304,128]{2,1,0:T(8,128)(2,1)}, bf16[3,2304,128]{2,1,0:T(8,128)(2,1)}, u32[]{:S(2)}, u32[]{:S(2)}) collective-permute-start(bf16[3,2304,128]{2,1,0:T(8,128)(2,1)} %get-tuple-element.44.rest_2_.rest_3_.rest_12_.rest_4_.rest_8_), channel_id=1, source_target_pairs={{0,4},{4,8},{8,12},{1,5},{5,9},{9,13},{2,6},{6,10},{10,14},{3,7},{... | collective-permute-start | bytes 5308424 | tf_op jit(solution)/shard_map/ppermute | solution.py:616
  55.2 2.3 %collective-permute-start.2 = (bf16[512,512]{1,0:T(8,128)(2,1)S(1)}, bf16[512,512]{1,0:T(8,128)(2,1)S(1)}, u32[]{:S(2)}, u32[]{:S(2)}) collective-permute-start(bf16[512,512]{1,0:T(8,128)(2,1)S(1)} %get-tuple-element.34), channel_id=1, source_target_pairs={{0,1},{1,0},{2,3},{3,2},{4,5},{5,4},{6,7},{7,6},{8,9},{9,8},{10,11... | collective-permute-start | bytes 1572872 | tf_op jit(solution)/shard_map/ppermute | solution.py:603
  55.2 2.3 %collective-permute-start.3 = (bf16[256,512]{1,0:T(8,128)(2,1)S(1)}, bf16[256,512]{1,0:T(8,128)(2,1)S(1)}, u32[]{:S(2)}, u32[]{:S(2)}) collective-permute-start(bf16[256,512]{1,0:T(8,128)(2,1)S(1)} %get-tuple-element.35), channel_id=1, source_target_pairs={{0,1},{1,0},{2,3},{3,2},{4,5},{5,4},{6,7},{7,6},{8,9},{9,8},{10,11... | collective-permute-start | bytes 786440 | tf_op jit(solution)/shard_map/ppermute | solution.py:603
  57.5 21.1 %slice-start = ((s8[12582912]{0:T(1024)(128)(4,1)}), s8[4194304]{0:T(1024)(128)(4,1)S(1)}, s32[]{:S(2)}) async-start(s8[12582912]{0:T(1024)(128)(4,1)} %bitcast.9), calls=%async_computation | async-start | bytes 8388608
  58.7 19.9 %slice-start.2 = ((s8[12582912]{0:T(1024)(128)(4,1)}), s8[4194304]{0:T(1024)(128)(4,1)S(1)}, s32[]{:S(2)}) async-start(s8[12582912]{0:T(1024)(128)(4,1)} %bitcast.9), calls=%async_computation.2 | async-start | bytes 8388608
  58.7 19.8 %collective-permute-start.8 = (bf16[768,512]{1,0:T(8,128)(2,1)}, bf16[768,512]{1,0:T(8,128)(2,1)S(1)}, u32[]{:S(2)}, u32[]{:S(2)}) collective-permute-start(bf16[768,512]{1,0:T(8,128)(2,1)} %pair_sum.5.rest_1_), channel_id=1, source_target_pairs={{0,2},{1,3},{2,0},{3,1},{4,6},{5,7},{6,4},{7,5},{8,10},{9,11},{10,... | collective-permute-start | bytes 2359304 | tf_op jit(solution)/shard_map/ppermute | solution.py:606
  74.6 7.8 %collective-permute-start.6 = (bf16[512,512]{1,0:T(8,128)(2,1)S(1)}, bf16[512,512]{1,0:T(8,128)(2,1)S(1)}, u32[]{:S(2)}, u32[]{:S(2)}) collective-permute-start(bf16[512,512]{1,0:T(8,128)(2,1)S(1)} %get-tuple-element.38), channel_id=1, source_target_pairs={{0,1},{1,0},{2,3},{3,2},{4,5},{5,4},{6,7},{7,6},{8,9},{9,8},{10,11... | collective-permute-start | bytes 1572872 | tf_op jit(solution)/shard_map/ppermute | solution.py:603
  74.6 7.8 %collective-permute-start.7 = (bf16[512,512]{1,0:T(8,128)(2,1)S(1)}, bf16[512,512]{1,0:T(8,128)(2,1)S(1)}, u32[]{:S(2)}, u32[]{:S(2)}) collective-permute-start(bf16[512,512]{1,0:T(8,128)(2,1)S(1)} %get-tuple-element.39), channel_id=1, source_target_pairs={{0,1},{1,0},{2,3},{3,2},{4,5},{5,4},{6,7},{7,6},{8,9},{9,8},{10,11... | collective-permute-start | bytes 1572872 | tf_op jit(solution)/shard_map/ppermute | solution.py:603
  85.4 33.2 %collective-permute-start.9 = (bf16[1024,512]{1,0:T(8,128)(2,1)}, bf16[1024,512]{1,0:T(8,128)(2,1)S(1)}, u32[]{:S(2)}, u32[]{:S(2)}) collective-permute-start(bf16[1024,512]{1,0:T(8,128)(2,1)} %pair_sum.6.rest_1_), channel_id=1, source_target_pairs={{0,2},{1,3},{2,0},{3,1},{4,6},{5,7},{6,4},{7,5},{8,10},{9,11},{10,... | collective-permute-start | bytes 3145736 | tf_op jit(solution)/shard_map/ppermute | solution.py:606
  100.0 6.3 %collective-permute-start.18 = (bf16[768,128]{1,0:T(8,128)(2,1)S(1)}, bf16[768,128]{1,0:T(8,128)(2,1)S(1)}, u32[]{:S(2)}, u32[]{:S(2)}) collective-permute-start(bf16[768,128]{1,0:T(8,128)(2,1)S(1)} %rank_products.5.rest_5_), channel_id=1, source_target_pairs={{0,1},{1,0},{2,3},{3,2},{4,5},{5,4},{6,7},{7,6},{8,9},{9,8},{10,11... | collective-permute-start | bytes 589832 | tf_op jit(solution)/shard_map/ppermute | solution.py:603
  100.1 43.1 %collective-permute-start.21 = (bf16[3,2304,128]{2,1,0:T(8,128)(2,1)}, bf16[3,2304,128]{2,1,0:T(8,128)(2,1)S(1)}, u32[]{:S(2)}, u32[]{:S(2)}) collective-permute-start(bf16[3,2304,128]{2,1,0:T(8,128)(2,1)} %get-tuple-element.45.rest_2_.rest_7_.rest_10_), channel_id=1, source_target_pairs={{4,0},{8,4},{12,8},{5,1},{9,5},{13,9},{6,2},{10,6},{14,10},{7,3},{... | collective-permute-start | bytes 5308424 | tf_op jit(solution)/shard_map/ppermute | solution.py:613
  101.6 42.9 %collective-permute-start.22 = (bf16[3,2304,128]{2,1,0:T(8,128)(2,1)}, bf16[3,2304,128]{2,1,0:T(8,128)(2,1)S(1)}, u32[]{:S(2)}, u32[]{:S(2)}) collective-permute-start(bf16[3,2304,128]{2,1,0:T(8,128)(2,1)} %get-tuple-element.46.rest_4_.rest_5_.rest_9_.rest_13_), channel_id=1, source_target_pairs={{0,4},{4,8},{8,12},{1,5},{5,9},{9,13},{2,6},{6,10},{10,14},{3,7},{... | collective-permute-start | bytes 5308424 | tf_op jit(solution)/shard_map/ppermute | solution.py:616
  106.2 1.5 collective-permute-start.16
  106.4 8.7 %collective-permute-start.19 = (bf16[768,128]{1,0:T(8,128)(2,1)S(1)}, bf16[768,128]{1,0:T(8,128)(2,1)S(1)}, u32[]{:S(2)}, u32[]{:S(2)}) collective-permute-start(bf16[768,128]{1,0:T(8,128)(2,1)S(1)} %add_convert_fusion.2.rest_8_), channel_id=1, source_target_pairs={{0,2},{1,3},{2,0},{3,1},{4,6},{5,7},{6,4},{7,5},{8,10},{9,11},{10,... | collective-permute-start | bytes 589832 | tf_op jit(solution)/shard_map/ppermute | solution.py:606
  107.8 10.8 %collective-permute-start.17 = (bf16[768,128]{1,0:T(8,128)(2,1)S(1)}, bf16[768,128]{1,0:T(8,128)(2,1)S(1)}, u32[]{:S(2)}, u32[]{:S(2)}) collective-permute-start(bf16[768,128]{1,0:T(8,128)(2,1)S(1)} %add_convert_fusion.3.rest_6_), channel_id=1, source_target_pairs={{0,2},{1,3},{2,0},{3,1},{4,6},{5,7},{6,4},{7,5},{8,10},{9,11},{10,... | collective-permute-start | bytes 589832 | tf_op jit(solution)/shard_map/ppermute | solution.py:606
  115.1 8.9 %collective-permute-start.23 = (bf16[768,512]{1,0:T(8,128)(2,1)S(1)}, bf16[768,512]{1,0:T(8,128)(2,1)S(1)}, u32[]{:S(2)}, u32[]{:S(2)}) collective-permute-start(bf16[768,512]{1,0:T(8,128)(2,1)S(1)} %copy-done.21), channel_id=1, source_target_pairs={{0,1},{1,0},{2,3},{3,2},{4,5},{5,4},{6,7},{7,6},{8,9},{9,8},{10,11... | collective-permute-start | bytes 2359304 | tf_op jit(solution)/shard_map/ppermute | solution.py:603
  118.6 3.5 %collective-permute-start.11 = (bf16[512,512]{1,0:T(8,128)(2,1)S(1)}, bf16[512,512]{1,0:T(8,128)(2,1)S(1)}, u32[]{:S(2)}, u32[]{:S(2)}) collective-permute-start(bf16[512,512]{1,0:T(8,128)(2,1)S(1)} %copy-done.27), channel_id=1, source_target_pairs={{0,1},{1,0},{2,3},{3,2},{4,5},{5,4},{6,7},{7,6},{8,9},{9,8},{10,11... | collective-permute-start | bytes 1572872 | tf_op jit(solution)/shard_map/ppermute | solution.py:603
  118.6 5.5 %collective-permute-start.24 = (bf16[768,512]{1,0:T(8,128)(2,1)S(1)}, bf16[768,512]{1,0:T(8,128)(2,1)S(1)}, u32[]{:S(2)}, u32[]{:S(2)}) collective-permute-start(bf16[768,512]{1,0:T(8,128)(2,1)S(1)} %copy-done.23), channel_id=1, source_target_pairs={{0,1},{1,0},{2,3},{3,2},{4,5},{5,4},{6,7},{7,6},{8,9},{9,8},{10,11... | collective-permute-start | bytes 2359304 | tf_op jit(solution)/shard_map/ppermute | solution.py:603
  122.3 14.0 %collective-permute-start.20 = (bf16[512,512]{1,0:T(8,128)(2,1)S(1)}, bf16[512,512]{1,0:T(8,128)(2,1)S(1)}, u32[]{:S(2)}, u32[]{:S(2)}) collective-permute-start(bf16[512,512]{1,0:T(8,128)(2,1)S(1)} %pair_sum.7), channel_id=1, source_target_pairs={{0,2},{1,3},{2,0},{3,1},{4,6},{5,7},{6,4},{7,5},{8,10},{9,11},{10,... | collective-permute-start | bytes 1572872 | tf_op jit(solution)/shard_map/ppermute | solution.py:606
  124.0 25.1 %collective-permute-start.5 = (bf16[1024,512]{1,0:T(8,128)(2,1)S(1)}, bf16[1024,512]{1,0:T(8,128)(2,1)S(1)}, u32[]{:S(2)}, u32[]{:S(2)}) collective-permute-start(bf16[1024,512]{1,0:T(8,128)(2,1)S(1)} %copy-done.19), channel_id=1, source_target_pairs={{0,1},{1,0},{2,3},{3,2},{4,5},{5,4},{6,7},{7,6},{8,9},{9,8},{10,11... | collective-permute-start | bytes 3145736 | tf_op jit(solution)/shard_map/ppermute | solution.py:603
  124.1 22.7 %collective-permute-start.27 = (bf16[768,128]{1,0:T(8,128)(2,1)S(1)}, bf16[768,128]{1,0:T(8,128)(2,1)S(1)}, u32[]{:S(2)}, u32[]{:S(2)}) collective-permute-start(bf16[768,128]{1,0:T(8,128)(2,1)S(1)} %rank_products.6.rest_1_), channel_id=1, source_target_pairs={{0,1},{1,0},{2,3},{3,2},{4,5},{5,4},{6,7},{7,6},{8,9},{9,8},{10,11... | collective-permute-start | bytes 589832 | tf_op jit(solution)/shard_map/ppermute | solution.py:603
  136.3 23.4 %collective-permute-start.10 = (bf16[512,512]{1,0:T(8,128)(2,1)S(1)}, bf16[512,512]{1,0:T(8,128)(2,1)S(1)}, u32[]{:S(2)}, u32[]{:S(2)}) collective-permute-start(bf16[512,512]{1,0:T(8,128)(2,1)S(1)} %copy-done.25), channel_id=1, source_target_pairs={{0,1},{1,0},{2,3},{3,2},{4,5},{5,4},{6,7},{7,6},{8,9},{9,8},{10,11... | collective-permute-start | bytes 1572872 | tf_op jit(solution)/shard_map/ppermute | solution.py:603
  146.7 1.5 collective-permute-start.25
  146.9 7.8 %collective-permute-start.28 = (bf16[768,128]{1,0:T(8,128)(2,1)S(1)}, bf16[768,128]{1,0:T(8,128)(2,1)S(1)}, u32[]{:S(2)}, u32[]{:S(2)}) collective-permute-start(bf16[768,128]{1,0:T(8,128)(2,1)S(1)} %add_convert_fusion.rest_3_), channel_id=1, source_target_pairs={{0,2},{1,3},{2,0},{3,1},{4,6},{5,7},{6,4},{7,5},{8,10},{9,11},{10,... | collective-permute-start | bytes 589832 | tf_op jit(solution)/shard_map/ppermute | solution.py:606
  148.3 11.4 %collective-permute-start.26 = (bf16[768,128]{1,0:T(8,128)(2,1)S(1)}, bf16[768,128]{1,0:T(8,128)(2,1)S(1)}, u32[]{:S(2)}, u32[]{:S(2)}) collective-permute-start(bf16[768,128]{1,0:T(8,128)(2,1)S(1)} %add_convert_fusion.1.rest_6_), channel_id=1, source_target_pairs={{0,2},{1,3},{2,0},{3,1},{4,6},{5,7},{6,4},{7,5},{8,10},{9,11},{10,... | collective-permute-start | bytes 589832 | tf_op jit(solution)/shard_map/ppermute | solution.py:606
  (31 other events, 221.3 us)

commit v11 on v9

--- a/solution.py
+++ b/solution.py
@@ -716,7 +716,7 @@
         if by_distance:
             part = rank(1, [part])
             part = rank(2, [part, bases[2][2][-1]])
-        summed = [pieces[-1] for _, _, pieces in ranks[:2]]
+        summed = [pieces[-1] for _, _, pieces in ranks[:3]]
         send_on(*fourth, [part, bases[2][2][-1]] + summed)
         for chunk in range(len(ranks), 3):
             part = rank(chunk, [pairs[-1]])

time: 165 us -> 163 us (0.988)
  waiting for transfers between devices: 34.9 us -> 31.2 us
    ppermute x8, waiting for transfers between devices: 25.8 us -> 20 us  [chip_shift(): lax.ppermute(a, 'tensor', [(2 * x + c, 2 * ((x + k) % n_x) + c) for x in...]
    ppermute x3, waiting for transfers between devices: 1.42 us -> 4.02 us  [leftward(): return lax.ppermute(a, 'adapter', [(z, z - hops) for z in range(hops, n_z)])]
    ppermute x15, waiting for transfers between devices: 6.56 us -> 4.79 us  [core_swap(): return lax.ppermute(a, 'tensor', [(t, t ^ 1) for t in range(n_t)])]
    unnamed x66 -> x68, local copies, waits for them, and re-layouts: 9.19 us -> 9.18 us
  transfers between devices with their start and end apart: 29 -> 29, of which waited for: 12 -> 14; matrix products, arithmetic and copies ran while one was open for 0% -> 0% of each run, Pallas kernels for 46% -> 47%
where the time goes in v11:
time: 163 us; the launch traced here: 161 us
  Pallas kernels  83.1 us (51%)
  starting transfers between devices  36.9 us (23%)
  waiting for transfers between devices  31.2 us (19%)
  local copies, waits for them, and re-layouts  9.18 us (6%)
    pallas_call x3, Pallas kernels, base_products(): pl.pallas_call(body, out_shape=(*[jax.ShapeDtypeStruct((n * prefill, widt...  32.3 us
    ppermute x8, waiting for transfers between devices, chip_shift(): lax.ppermute(a, 'tensor', [(2 * x + c, 2 * ((x + k) % n_x) + c) for x in...  20 us
    pallas_call x3, Pallas kernels, finish(): pl.pallas_call(body, out_shape=(jax.ShapeDtypeStruct((shape[0] * tiles, 2...  18.5 us
    ppermute x3, starting transfers between devices, rightward(): return lax.ppermute(a, 'adapter', [(z - hops, z) for z in range(hops, n_z)])  18 us
    pallas_call x1, Pallas kernels, split_weight(): pl.pallas_call(body, out_shape=(jax.ShapeDtypeStruct((n_t, features, 2 *...  17 us
    ppermute x8, starting transfers between devices, chip_shift(): lax.ppermute(a, 'tensor', [(2 * x + c, 2 * ((x + k) % n_x) + c) for x in...  12 us
    pallas_call x4, Pallas kernels, rank_products(): pl.pallas_call(body, out_shape=jax.ShapeDtypeStruct((count * prefill, ran...  10.1 us
    unnamed x68, local copies, waits for them, and re-layouts  9.18 us
  transfers between devices with their start and end apart: 29, of which 14 were waited for; matrix products, arithmetic and copies ran while one was open for 0% of the time, Pallas kernels for 47%

profile of v11, /device:TPU:0, one launch (start us, length us, event | category | flops | bytes accessed | tf_op | source)
XLA Modules:
  0.0 161.3 jit_solution(1163872566569191432)
XLA Ops:
  4.1 6.8 %collective-permute-start.13 = (bf16[3,2304,128]{2,1,0:T(8,128)(2,1)S(1)}, bf16[3,2304,128]{2,1,0:T(8,128)(2,1)}, u32[]{:S(2)}, u32[]{:S(2)}) collective-permute-start(bf16[3,2304,128]{2,1,0:T(8,128)(2,1)S(1)} %pack_maps.1.rest_0_.rest_10_.rest_5_.rest_8_), channel_id=1, source_target_pairs={{0,4},{4,8},{8,12},{1,5},{5,9},{9,13},{2,6},{6,10},{10,14},{3,7},{... | collective-permute-start | bytes 5308424 | tf_op jit(solution)/shard_map/ppermute | solution.py:616
  10.9 1.6 plan_requests.1.plan_ref
  13.2 17.0 %split_weight.1 = (bf16[4,2048,512]{2,1,0:T(8,128)(2,1)}, bf16[768,512]{1,0:T(8,128)(2,1)S(1)}, bf16[512,512]{1,0:T(8,128)(2,1)S(1)}, bf16[256,512]{1,0:T(8,128)(2,1)S(1)}, bf16[2,768,512]{2,1,0:T(8,128)(2,1)S(1)}) custom-call(s32[8,128]{1,0:T(8,128)S(1)} %copy-done.15, s32[4]{0:T(128)S(1)} %compare_select_fusion.2.slot_ref, bf16[3072,2048]{1,0:T(8,128)(2,1)} %x_ref.13, ...), custom_call_target="tpu_custom_call" | custom-call | flops 64424508 | bytes 167772 | tf_op jit(solution)/shard_map/split_weight/pallas_call | solution.py:184
  31.5 1.8 %collective-permute-done.1.rest_1_ = bf16[256,512]{1,0:T(8,128)(2,1)S(1)} collective-permute-done((bf16[256,512]{1,0:T(8,128)(2,1)S(1)}, bf16[256,512]{1,0:T(8,128)(2,1)S(1)}, u32[]{:S(2)}, u32[]{:S(2)}) %collective-permute-start.1) | collective-permute-done | bytes 262176 | tf_op jit(solution)/shard_map/ppermute | solution.py:603
  33.7 2.0 %collective-permute-start.4 = (bf16[768,512]{1,0:T(8,128)(2,1)S(1)}, bf16[768,512]{1,0:T(8,128)(2,1)S(1)}, u32[]{:S(2)}, u32[]{:S(2)}) collective-permute-start(bf16[768,512]{1,0:T(8,128)(2,1)S(1)} %pair_sum.4.rest_1_), channel_id=1, source_target_pairs={{0,2},{1,3},{2,0},{3,1},{4,6},{5,7},{6,4},{7,5},{8,10},{9,11},{10,... | collective-permute-start | bytes 2359304 | tf_op jit(solution)/shard_map/ppermute | solution.py:606
  35.7 8.9 %base_products.3 = (bf16[768,512]{1,0:T(8,128)(2,1)S(1)}, bf16[512,512]{1,0:T(8,128)(2,1)S(1)}, bf16[256,512]{1,0:T(8,128)(2,1)S(1)}, bf16[2,768,512]{2,1,0:T(8,128)(2,1)S(1)}) custom-call(s32[8,128]{1,0:T(8,128)S(1)} %copy-done.15, bf16[3072,2048]{1,0:T(8,128)(2,1)} %x_ref.13, bf16[4,2048,512]{2,1,0:T(8,128)(2,1)} %get-tuple-element.29.rest_0_, ...), custom_call_target="tpu_custom_call" | custom-call | flops 64424508 | bytes 83886 | tf_op jit(solution)/shard_map/base_products/pallas_call | solution.py:260
  44.7 1.8 %collective-permute-done.12.refs_0_ = bf16[3,2304,128]{2,1,0:T(8,128)(2,1)} collective-permute-done((bf16[3,2304,128]{2,1,0:T(8,128)(2,1)S(1)}, bf16[3,2304,128]{2,1,0:T(8,128)(2,1)}, u32[]{:S(2)}, u32[]{:S(2)}) %collective-permute-start.12) | collective-permute-done | bytes 1769504 | tf_op jit(solution)/shard_map/ppermute | solution.py:613
  48.8 6.3 %collective-permute-start.15 = (bf16[3,2304,128]{2,1,0:T(8,128)(2,1)}, bf16[3,2304,128]{2,1,0:T(8,128)(2,1)}, u32[]{:S(2)}, u32[]{:S(2)}) collective-permute-start(bf16[3,2304,128]{2,1,0:T(8,128)(2,1)} %get-tuple-element.44.rest_2_.rest_3_.rest_12_.rest_8_.rest_4_), channel_id=1, source_target_pairs={{0,4},{4,8},{8,12},{1,5},{5,9},{9,13},{2,6},{6,10},{10,14},{3,7},{... | collective-permute-start | bytes 5308424 | tf_op jit(solution)/shard_map/ppermute | solution.py:616
  55.2 1.5 collective-permute-done.3.rest_1_
  57.9 1.7 %collective-permute-start.8 = (bf16[768,512]{1,0:T(8,128)(2,1)}, bf16[768,512]{1,0:T(8,128)(2,1)S(1)}, u32[]{:S(2)}, u32[]{:S(2)}) collective-permute-start(bf16[768,512]{1,0:T(8,128)(2,1)} %pair_sum.5.rest_1_), channel_id=1, source_target_pairs={{0,2},{1,3},{2,0},{3,1},{4,6},{5,7},{6,4},{7,5},{8,10},{9,11},{10,... | collective-permute-start | bytes 2359304 | tf_op jit(solution)/shard_map/ppermute | solution.py:606
  59.6 14.2 %base_products.4 = (bf16[1024,512]{1,0:T(8,128)(2,1)S(1)}, bf16[512,512]{1,0:T(8,128)(2,1)S(1)}, bf16[512,512]{1,0:T(8,128)(2,1)S(1)}, bf16[2,1024,512]{2,1,0:T(8,128)(2,1)S(1)}) custom-call(s32[8,128]{1,0:T(8,128)S(1)} %copy-done.15, bf16[3072,2048]{1,0:T(8,128)(2,1)} %x_ref.13, bf16[4,2048,512]{2,1,0:T(8,128)(2,1)} %get-tuple-element.29.rest_0_, ...), custom_call_target="tpu_custom_call" | custom-call | flops 85899344 | bytes 83886 | tf_op jit(solution)/shard_map/base_products/pallas_call | solution.py:260
  75.4 2.4 %collective-permute-done.8.rest_2_.rest_3_.rest_5_ = bf16[768,512]{1,0:T(8,128)(2,1)S(1)} collective-permute-done((bf16[768,512]{1,0:T(8,128)(2,1)}, bf16[768,512]{1,0:T(8,128)(2,1)S(1)}, u32[]{:S(2)}, u32[]{:S(2)}) %collective-permute-start.8) | collective-permute-done | bytes 786464 | tf_op jit(solution)/shard_map/ppermute | solution.py:606
  77.8 1.8 %copy-done.1 = bf16[3,2304,128]{2,1,0:T(8,128)(2,1)S(1)} copy-done((bf16[3,2304,128]{2,1,0:T(8,128)(2,1)S(1)}, bf16[3,2304,128]{2,1,0:T(8,128)(2,1)}, u32[]{:S(2)}) %copy-start.1) | copy-done | bytes 1769496
  79.6 2.5 %rank_products.4.rest_2_ = bf16[768,128]{1,0:T(8,128)(2,1)S(1)} custom-call(s32[8,128]{1,0:T(8,128)S(1)} %copy-done.15, bf16[3072,2048]{1,0:T(8,128)(2,1)S(1)} %bitcast.10, bf16[3,2304,128]{2,1,0:T(8,128)(2,1)S(1)} %copy-done.1, bf16[2,1024,512]{2,1,0:T(8,128)(2,1)S(1)} %get-tuple-element.36.rest_1_.a_ref.rest_0_, ...), custom_call_target="tpu_custom_call" | custom-call | flops 4026531 | bytes 47185 | tf_op jit(solution)/shard_map/rank_products/pallas_call | solution.py:413
  82.1 1.6 copy-done.4
  85.0 1.7 %collective-permute-start.9 = (bf16[1024,512]{1,0:T(8,128)(2,1)}, bf16[1024,512]{1,0:T(8,128)(2,1)S(1)}, u32[]{:S(2)}, u32[]{:S(2)}) collective-permute-start(bf16[1024,512]{1,0:T(8,128)(2,1)} %pair_sum.6.rest_1_), channel_id=1, source_target_pairs={{0,2},{1,3},{2,0},{3,1},{4,6},{5,7},{6,4},{7,5},{8,10},{9,11},{10,... | collective-permute-start | bytes 3145736 | tf_op jit(solution)/shard_map/ppermute | solution.py:606
  86.7 9.2 %base_products.5 = (bf16[512,512]{1,0:T(8,128)(2,1)S(1)}, bf16[512,512]{1,0:T(8,128)(2,1)S(1)}, bf16[2,512,512]{2,1,0:T(8,128)(2,1)S(1)}) custom-call(s32[8,128]{1,0:T(8,128)S(1)} %copy-done.15, bf16[3072,2048]{1,0:T(8,128)(2,1)} %x_ref.13, bf16[4,2048,512]{2,1,0:T(8,128)(2,1)} %get-tuple-element.29.rest_0_, bf16[1024,512]{1,0:T(8,128)(2,1)} %pair_sum.6.rest_1_), custom_call_target="tpu_custom_call" | custom-call | flops 42949672 | bytes 83886 | tf_op jit(solution)/shard_map/base_products/pallas_call | solution.py:260
  96.8 2.6 %rank_products.5.rest_5_ = bf16[768,128]{1,0:T(8,128)(2,1)S(1)} custom-call(s32[8,128]{1,0:T(8,128)S(1)} %copy-done.15, bf16[3072,2048]{1,0:T(8,128)(2,1)S(1)} %bitcast.12, bf16[3,2304,128]{2,1,0:T(8,128)(2,1)S(1)} %copy-done.2, bf16[3,2304,128]{2,1,0:T(8,128)(2,1)} %get-tuple-element.43.rest_1_.rest_11_.rest_6_.rest_9_, ...), custom_call_target="tpu_custom_call" | custom-call | flops 4026531 | bytes 47185 | tf_op jit(solution)/shard_map/rank_products/pallas_call | solution.py:413
  101.4 4.8 %collective-permute-start.24 = (bf16[3,2304,128]{2,1,0:T(8,128)(2,1)}, bf16[3,2304,128]{2,1,0:T(8,128)(2,1)S(1)}, u32[]{:S(2)}, u32[]{:S(2)}) collective-permute-start(bf16[3,2304,128]{2,1,0:T(8,128)(2,1)} %get-tuple-element.46.rest_4_.rest_9_.rest_5_.rest_13_), channel_id=1, source_target_pairs={{0,4},{4,8},{8,12},{1,5},{5,9},{9,13},{2,6},{6,10},{10,14},{3,7},{... | collective-permute-start | bytes 5308424 | tf_op jit(solution)/shard_map/ppermute | solution.py:616
  106.8 3.8 %collective-permute-done.9.rest_6_.rest_2_ = bf16[1024,512]{1,0:T(8,128)(2,1)S(1)} collective-permute-done((bf16[1024,512]{1,0:T(8,128)(2,1)}, bf16[1024,512]{1,0:T(8,128)(2,1)S(1)}, u32[]{:S(2)}, u32[]{:S(2)}) %collective-permute-start.9) | collective-permute-done | bytes 1048608 | tf_op jit(solution)/shard_map/ppermute | solution.py:606
  110.7 2.4 %collective-permute-start.17 = (bf16[768,128]{1,0:T(8,128)(2,1)S(1)}, bf16[768,128]{1,0:T(8,128)(2,1)S(1)}, u32[]{:S(2)}, u32[]{:S(2)}) collective-permute-start(bf16[768,128]{1,0:T(8,128)(2,1)S(1)} %add_convert_fusion.3.rest_6_), channel_id=1, source_target_pairs={{0,2},{1,3},{2,0},{3,1},{4,6},{5,7},{6,4},{7,5},{8,10},{9,11},{10,... | collective-permute-start | bytes 589832 | tf_op jit(solution)/shard_map/ppermute | solution.py:606
  113.1 2.9 %rank_products.6.rest_1_ = bf16[768,128]{1,0:T(8,128)(2,1)S(1)} custom-call(s32[8,128]{1,0:T(8,128)S(1)} %copy-done.16, bf16[3072,2048]{1,0:T(8,128)(2,1)S(1)} %bitcast.12, bf16[3,2304,128]{2,1,0:T(8,128)(2,1)S(1)} %copy-done.2, bf16[3,2304,128]{2,1,0:T(8,128)(2,1)} %get-tuple-element.43.rest_1_.rest_11_.rest_6_.rest_9_, ...), custom_call_target="tpu_custom_call" | custom-call | flops 4026531 | bytes 47185 | tf_op jit(solution)/shard_map/rank_products/pallas_call | solution.py:413
  116.0 2.2 %collective-permute-done.17.rest_3_.rest_7_ = bf16[768,128]{1,0:T(8,128)(2,1)S(1)} collective-permute-done((bf16[768,128]{1,0:T(8,128)(2,1)S(1)}, bf16[768,128]{1,0:T(8,128)(2,1)S(1)}, u32[]{:S(2)}, u32[]{:S(2)}) %collective-permute-start.17) | collective-permute-done | bytes 196640 | tf_op jit(solution)/shard_map/ppermute | solution.py:606
  118.8 1.7 %collective-permute-start.21 = (bf16[768,128]{1,0:T(8,128)(2,1)S(1)}, bf16[768,128]{1,0:T(8,128)(2,1)S(1)}, u32[]{:S(2)}, u32[]{:S(2)}) collective-permute-start(bf16[768,128]{1,0:T(8,128)(2,1)S(1)} %add_convert_fusion.1.rest_3_), channel_id=1, source_target_pairs={{0,2},{1,3},{2,0},{3,1},{4,6},{5,7},{6,4},{7,5},{8,10},{9,11},{10,... | collective-permute-start | bytes 589832 | tf_op jit(solution)/shard_map/ppermute | solution.py:606
  120.5 5.2 %collective-permute-done.21.rest_5_.rest_4_ = bf16[768,128]{1,0:T(8,128)(2,1)S(1)} collective-permute-done((bf16[768,128]{1,0:T(8,128)(2,1)S(1)}, bf16[768,128]{1,0:T(8,128)(2,1)S(1)}, u32[]{:S(2)}, u32[]{:S(2)}) %collective-permute-start.21) | collective-permute-done | bytes 196640 | tf_op jit(solution)/shard_map/ppermute | solution.py:606
  126.1 1.7 %collective-permute-start.22 = (bf16[512,512]{1,0:T(8,128)(2,1)S(1)}, bf16[512,512]{1,0:T(8,128)(2,1)S(1)}, u32[]{:S(2)}, u32[]{:S(2)}) collective-permute-start(bf16[512,512]{1,0:T(8,128)(2,1)S(1)} %pair_sum.7), channel_id=1, source_target_pairs={{0,2},{1,3},{2,0},{3,1},{4,6},{5,7},{6,4},{7,5},{8,10},{9,11},{10,... | collective-permute-start | bytes 1572872 | tf_op jit(solution)/shard_map/ppermute | solution.py:606
  128.1 8.4 %finish.3 = (bf16[6144,2,128]{2,1,0:T(2,128)(2,1)}, f32[8,128]{1,0:T(8,128)}) custom-call(s32[8,128]{1,0:T(8,128)S(1)} %copy-done.16, bf16[2,768,512]{2,1,0:T(8,128)(2,1)S(1)} %copy-done.11, bf16[768,512]{1,0:T(8,128)(2,1)S(1)} %collective-permute-done.25.rest_1_, bf16[768,512]{1,0:T(8,128)(2,1)S(1)} %copy-done.13, bf16[2,768,512]{2,1,0:T(8,128)(2,1)S(1)} %copy-done.7, ...), custom_call_target="tpu_custom_call" | custom-call | flops 24159192 | bytes 78643 | tf_op jit(solution)/shard_map/finish/pallas_call | solution.py:571
  136.5 4.8 %finish.4 = (bf16[6144,2,128]{2,1,0:T(2,128)(2,1)}, f32[8,128]{1,0:T(8,128)S(1)}) custom-call(s32[8,128]{1,0:T(8,128)S(1)} %copy-done.16, bf16[2,1024,512]{2,1,0:T(8,128)(2,1)S(1)} %copy-done.5, bf16[1024,512]{1,0:T(8,128)(2,1)S(1)} %collective-permute-done.5.rest_1_, ...), custom_call_target="tpu_custom_call", output_to_operand_aliasing={{0}: (11, {})} | custom-call | flops 12079595 | bytes 39321 | tf_op jit(solution)/shard_map/finish/pallas_call | solution.py:571
  141.3 2.3 %collective-permute-done.23.rest_3_.rest_11_ = bf16[3,2304,128]{2,1,0:T(8,128)(2,1)S(1)} collective-permute-done((bf16[3,2304,128]{2,1,0:T(8,128)(2,1)}, bf16[3,2304,128]{2,1,0:T(8,128)(2,1)S(1)}, u32[]{:S(2)}, u32[]{:S(2)}) %collective-permute-start.23) | collective-permute-done | bytes 1769504 | tf_op jit(solution)/shard_map/ppermute | solution.py:613
  144.9 2.2 %rank_products.7 = bf16[768,128]{1,0:T(8,128)(2,1)S(1)} custom-call(s32[8,128]{1,0:T(8,128)S(1)} %copy-done.16, bf16[3072,2048]{1,0:T(8,128)(2,1)S(1)} %bitcast.12, bf16[3,2304,128]{2,1,0:T(8,128)(2,1)S(1)} %copy-done.2, bf16[3,2304,128]{2,1,0:T(8,128)(2,1)} %get-tuple-element.43.rest_1_.rest_11_.rest_6_.rest_9_, ...), custom_call_target="tpu_custom_call" | custom-call | flops 4026531 | bytes 47185 | tf_op jit(solution)/shard_map/rank_products/pallas_call | solution.py:413
  149.4 6.3 %collective-permute-done.28.rest_7_ = bf16[768,128]{1,0:T(8,128)(2,1)S(1)} collective-permute-done((bf16[768,128]{1,0:T(8,128)(2,1)S(1)}, bf16[768,128]{1,0:T(8,128)(2,1)S(1)}, u32[]{:S(2)}, u32[]{:S(2)}) %collective-permute-start.28) | collective-permute-done | bytes 196640 | tf_op jit(solution)/shard_map/ppermute | solution.py:606
  155.7 5.4 %finish.5 = (bf16[6144,2,128]{2,1,0:T(2,128)(2,1)}, f32[8,128]{1,0:T(8,128)}) custom-call(s32[8,128]{1,0:T(8,128)S(1)} %copy-done.16, bf16[2,1024,512]{2,1,0:T(8,128)(2,1)S(1)} %copy-done.5, bf16[1024,512]{1,0:T(8,128)(2,1)S(1)} %collective-permute-done.5.rest_1_, ...), custom_call_target="tpu_custom_call", output_to_operand_aliasing={{0}: (16, {})} | custom-call | flops 12079595 | bytes 39321 | tf_op jit(solution)/shard_map/finish/pallas_call | solution.py:571
  (120 shorter events, 21.3 us)
Async XLA Ops:
  2.8 27.3 %copy-start = (bf16[3,2304,128]{2,1,0:T(8,128)(2,1)}, bf16[3,2304,128]{2,1,0:T(8,128)(2,1)S(1)}, u32[]{:S(2)}) copy-start(bf16[3,2304,128]{2,1,0:T(8,128)(2,1)S(1)} %pack_maps.1.rest_0_.rest_10_.rest_5_.rest_8_) | copy-start | bytes 5308420
  2.8 43.6 %collective-permute-start.12 = (bf16[3,2304,128]{2,1,0:T(8,128)(2,1)S(1)}, bf16[3,2304,128]{2,1,0:T(8,128)(2,1)}, u32[]{:S(2)}, u32[]{:S(2)}) collective-permute-start(bf16[3,2304,128]{2,1,0:T(8,128)(2,1)S(1)} %pack_maps.1.rest_0_.rest_10_.rest_5_.rest_8_), channel_id=1, source_target_pairs={{4,0},{8,4},{12,8},{5,1},{9,5},{13,9},{6,2},{10,6},{14,10},{7,3},{... | collective-permute-start | bytes 5308424 | tf_op jit(solution)/shard_map/ppermute | solution.py:613
  4.1 43.4 %collective-permute-start.13 = (bf16[3,2304,128]{2,1,0:T(8,128)(2,1)S(1)}, bf16[3,2304,128]{2,1,0:T(8,128)(2,1)}, u32[]{:S(2)}, u32[]{:S(2)}) collective-permute-start(bf16[3,2304,128]{2,1,0:T(8,128)(2,1)S(1)} %pack_maps.1.rest_0_.rest_10_.rest_5_.rest_8_), channel_id=1, source_target_pairs={{0,4},{4,8},{8,12},{1,5},{5,9},{9,13},{2,6},{6,10},{10,14},{3,7},{... | collective-permute-start | bytes 5308424 | tf_op jit(solution)/shard_map/ppermute | solution.py:616
  31.0 2.3 %collective-permute-start = (bf16[512,512]{1,0:T(8,128)(2,1)S(1)}, bf16[512,512]{1,0:T(8,128)(2,1)S(1)}, u32[]{:S(2)}, u32[]{:S(2)}) collective-permute-start(bf16[512,512]{1,0:T(8,128)(2,1)S(1)} %get-tuple-element.31), channel_id=1, source_target_pairs={{0,1},{1,0},{2,3},{3,2},{4,5},{5,4},{6,7},{7,6},{8,9},{9,8},{10,11... | collective-permute-start | bytes 1572872 | tf_op jit(solution)/shard_map/ppermute | solution.py:603
  31.0 2.3 %collective-permute-start.1 = (bf16[256,512]{1,0:T(8,128)(2,1)S(1)}, bf16[256,512]{1,0:T(8,128)(2,1)S(1)}, u32[]{:S(2)}, u32[]{:S(2)}) collective-permute-start(bf16[256,512]{1,0:T(8,128)(2,1)S(1)} %get-tuple-element.32), channel_id=1, source_target_pairs={{0,1},{1,0},{2,3},{3,2},{4,5},{5,4},{6,7},{7,6},{8,9},{9,8},{10,11... | collective-permute-start | bytes 786440 | tf_op jit(solution)/shard_map/ppermute | solution.py:603
  33.7 23.0 %collective-permute-start.4 = (bf16[768,512]{1,0:T(8,128)(2,1)S(1)}, bf16[768,512]{1,0:T(8,128)(2,1)S(1)}, u32[]{:S(2)}, u32[]{:S(2)}) collective-permute-start(bf16[768,512]{1,0:T(8,128)(2,1)S(1)} %pair_sum.4.rest_1_), channel_id=1, source_target_pairs={{0,2},{1,3},{2,0},{3,1},{4,6},{5,7},{6,4},{7,5},{8,10},{9,11},{10,... | collective-permute-start | bytes 2359304 | tf_op jit(solution)/shard_map/ppermute | solution.py:606
  44.6 12.1 %collective-permute-start.2 = (bf16[512,512]{1,0:T(8,128)(2,1)S(1)}, bf16[512,512]{1,0:T(8,128)(2,1)S(1)}, u32[]{:S(2)}, u32[]{:S(2)}) collective-permute-start(bf16[512,512]{1,0:T(8,128)(2,1)S(1)} %get-tuple-element.34), channel_id=1, source_target_pairs={{0,1},{1,0},{2,3},{3,2},{4,5},{5,4},{6,7},{7,6},{8,9},{9,8},{10,11... | collective-permute-start | bytes 1572872 | tf_op jit(solution)/shard_map/ppermute | solution.py:603
  47.5 52.4 %collective-permute-start.14 = (bf16[3,2304,128]{2,1,0:T(8,128)(2,1)}, bf16[3,2304,128]{2,1,0:T(8,128)(2,1)}, u32[]{:S(2)}, u32[]{:S(2)}) collective-permute-start(bf16[3,2304,128]{2,1,0:T(8,128)(2,1)} %get-tuple-element.43.rest_1_.rest_11_.rest_6_.rest_9_), channel_id=1, source_target_pairs={{4,0},{8,4},{12,8},{5,1},{9,5},{13,9},{6,2},{10,6},{14,10},{7,3},{... | collective-permute-start | bytes 5308424 | tf_op jit(solution)/shard_map/ppermute | solution.py:613
  48.8 51.3 %collective-permute-start.15 = (bf16[3,2304,128]{2,1,0:T(8,128)(2,1)}, bf16[3,2304,128]{2,1,0:T(8,128)(2,1)}, u32[]{:S(2)}, u32[]{:S(2)}) collective-permute-start(bf16[3,2304,128]{2,1,0:T(8,128)(2,1)} %get-tuple-element.44.rest_2_.rest_3_.rest_12_.rest_8_.rest_4_), channel_id=1, source_target_pairs={{0,4},{4,8},{8,12},{1,5},{5,9},{9,13},{2,6},{6,10},{10,14},{3,7},{... | collective-permute-start | bytes 5308424 | tf_op jit(solution)/shard_map/ppermute | solution.py:616
  55.2 1.5 collective-permute-start.3
  56.7 21.1 %slice-start = ((s8[12582912]{0:T(1024)(128)(4,1)}), s8[4194304]{0:T(1024)(128)(4,1)S(1)}, s32[]{:S(2)}) async-start(s8[12582912]{0:T(1024)(128)(4,1)} %bitcast.9), calls=%async_computation | async-start | bytes 8388608
  57.9 19.9 %slice-start.2 = ((s8[12582912]{0:T(1024)(128)(4,1)}), s8[4194304]{0:T(1024)(128)(4,1)S(1)}, s32[]{:S(2)}) async-start(s8[12582912]{0:T(1024)(128)(4,1)} %bitcast.9), calls=%async_computation.2 | async-start | bytes 8388608
  57.9 19.8 %collective-permute-start.8 = (bf16[768,512]{1,0:T(8,128)(2,1)}, bf16[768,512]{1,0:T(8,128)(2,1)S(1)}, u32[]{:S(2)}, u32[]{:S(2)}) collective-permute-start(bf16[768,512]{1,0:T(8,128)(2,1)} %pair_sum.5.rest_1_), channel_id=1, source_target_pairs={{0,2},{1,3},{2,0},{3,1},{4,6},{5,7},{6,4},{7,5},{8,10},{9,11},{10,... | collective-permute-start | bytes 2359304 | tf_op jit(solution)/shard_map/ppermute | solution.py:606
  74.9 7.1 %collective-permute-start.6 = (bf16[512,512]{1,0:T(8,128)(2,1)S(1)}, bf16[512,512]{1,0:T(8,128)(2,1)S(1)}, u32[]{:S(2)}, u32[]{:S(2)}) collective-permute-start(bf16[512,512]{1,0:T(8,128)(2,1)S(1)} %get-tuple-element.38), channel_id=1, source_target_pairs={{0,1},{1,0},{2,3},{3,2},{4,5},{5,4},{6,7},{7,6},{8,9},{9,8},{10,11... | collective-permute-start | bytes 1572872 | tf_op jit(solution)/shard_map/ppermute | solution.py:603
  74.9 7.2 %collective-permute-start.7 = (bf16[512,512]{1,0:T(8,128)(2,1)S(1)}, bf16[512,512]{1,0:T(8,128)(2,1)S(1)}, u32[]{:S(2)}, u32[]{:S(2)}) collective-permute-start(bf16[512,512]{1,0:T(8,128)(2,1)S(1)} %get-tuple-element.39), channel_id=1, source_target_pairs={{0,1},{1,0},{2,3},{3,2},{4,5},{5,4},{6,7},{7,6},{8,9},{9,8},{10,11... | collective-permute-start | bytes 1572872 | tf_op jit(solution)/shard_map/ppermute | solution.py:603
  85.0 25.6 %collective-permute-start.9 = (bf16[1024,512]{1,0:T(8,128)(2,1)}, bf16[1024,512]{1,0:T(8,128)(2,1)S(1)}, u32[]{:S(2)}, u32[]{:S(2)}) collective-permute-start(bf16[1024,512]{1,0:T(8,128)(2,1)} %pair_sum.6.rest_1_), channel_id=1, source_target_pairs={{0,2},{1,3},{2,0},{3,1},{4,6},{5,7},{6,4},{7,5},{8,10},{9,11},{10,... | collective-permute-start | bytes 3145736 | tf_op jit(solution)/shard_map/ppermute | solution.py:606
  99.4 2.0 %collective-permute-start.18 = (bf16[768,128]{1,0:T(8,128)(2,1)S(1)}, bf16[768,128]{1,0:T(8,128)(2,1)S(1)}, u32[]{:S(2)}, u32[]{:S(2)}) collective-permute-start(bf16[768,128]{1,0:T(8,128)(2,1)S(1)} %rank_products.5.rest_5_), channel_id=1, source_target_pairs={{0,1},{1,0},{2,3},{3,2},{4,5},{5,4},{6,7},{7,6},{8,9},{9,8},{10,11... | collective-permute-start | bytes 589832 | tf_op jit(solution)/shard_map/ppermute | solution.py:603
  99.5 6.9 %collective-permute-start.16 = (bf16[768,128]{1,0:T(8,128)(2,1)S(1)}, bf16[768,128]{1,0:T(8,128)(2,1)S(1)}, u32[]{:S(2)}, u32[]{:S(2)}) collective-permute-start(bf16[768,128]{1,0:T(8,128)(2,1)S(1)} %rank_products.4.rest_2_), channel_id=1, source_target_pairs={{0,1},{1,0},{2,3},{3,2},{4,5},{5,4},{6,7},{7,6},{8,9},{9,8},{10,11... | collective-permute-start | bytes 589832 | tf_op jit(solution)/shard_map/ppermute | solution.py:603
  100.0 18.8 %collective-permute-start.11 = (bf16[512,512]{1,0:T(8,128)(2,1)S(1)}, bf16[512,512]{1,0:T(8,128)(2,1)S(1)}, u32[]{:S(2)}, u32[]{:S(2)}) collective-permute-start(bf16[512,512]{1,0:T(8,128)(2,1)S(1)} %copy-done.27), channel_id=1, source_target_pairs={{0,1},{1,0},{2,3},{3,2},{4,5},{5,4},{6,7},{7,6},{8,9},{9,8},{10,11... | collective-permute-start | bytes 1572872 | tf_op jit(solution)/shard_map/ppermute | solution.py:603
  100.1 43.5 %collective-permute-start.23 = (bf16[3,2304,128]{2,1,0:T(8,128)(2,1)}, bf16[3,2304,128]{2,1,0:T(8,128)(2,1)S(1)}, u32[]{:S(2)}, u32[]{:S(2)}) collective-permute-start(bf16[3,2304,128]{2,1,0:T(8,128)(2,1)} %get-tuple-element.45.rest_2_.rest_7_.rest_10_), channel_id=1, source_target_pairs={{4,0},{8,4},{12,8},{5,1},{9,5},{13,9},{6,2},{10,6},{14,10},{7,3},{... | collective-permute-start | bytes 5308424 | tf_op jit(solution)/shard_map/ppermute | solution.py:613
  101.4 43.5 %collective-permute-start.24 = (bf16[3,2304,128]{2,1,0:T(8,128)(2,1)}, bf16[3,2304,128]{2,1,0:T(8,128)(2,1)S(1)}, u32[]{:S(2)}, u32[]{:S(2)}) collective-permute-start(bf16[3,2304,128]{2,1,0:T(8,128)(2,1)} %get-tuple-element.46.rest_4_.rest_9_.rest_5_.rest_13_), channel_id=1, source_target_pairs={{0,4},{4,8},{8,12},{1,5},{5,9},{9,13},{2,6},{6,10},{10,14},{3,7},{... | collective-permute-start | bytes 5308424 | tf_op jit(solution)/shard_map/ppermute | solution.py:616
  106.3 9.6 %collective-permute-start.19 = (bf16[768,128]{1,0:T(8,128)(2,1)S(1)}, bf16[768,128]{1,0:T(8,128)(2,1)S(1)}, u32[]{:S(2)}, u32[]{:S(2)}) collective-permute-start(bf16[768,128]{1,0:T(8,128)(2,1)S(1)} %add_convert_fusion.2.rest_8_), channel_id=1, source_target_pairs={{0,2},{1,3},{2,0},{3,1},{4,6},{5,7},{6,4},{7,5},{8,10},{9,11},{10,... | collective-permute-start | bytes 589832 | tf_op jit(solution)/shard_map/ppermute | solution.py:606
  110.7 7.5 %collective-permute-start.17 = (bf16[768,128]{1,0:T(8,128)(2,1)S(1)}, bf16[768,128]{1,0:T(8,128)(2,1)S(1)}, u32[]{:S(2)}, u32[]{:S(2)}) collective-permute-start(bf16[768,128]{1,0:T(8,128)(2,1)S(1)} %add_convert_fusion.3.rest_6_), channel_id=1, source_target_pairs={{0,2},{1,3},{2,0},{3,1},{4,6},{5,7},{6,4},{7,5},{8,10},{9,11},{10,... | collective-permute-start | bytes 589832 | tf_op jit(solution)/shard_map/ppermute | solution.py:606
  115.9 2.3 %collective-permute-start.20 = (bf16[768,128]{1,0:T(8,128)(2,1)S(1)}, bf16[768,128]{1,0:T(8,128)(2,1)S(1)}, u32[]{:S(2)}, u32[]{:S(2)}) collective-permute-start(bf16[768,128]{1,0:T(8,128)(2,1)S(1)} %rank_products.6.rest_1_), channel_id=1, source_target_pairs={{0,1},{1,0},{2,3},{3,2},{4,5},{5,4},{6,7},{7,6},{8,9},{9,8},{10,11... | collective-permute-start | bytes 589832 | tf_op jit(solution)/shard_map/ppermute | solution.py:603
  118.2 7.9 %collective-permute-start.25 = (bf16[768,512]{1,0:T(8,128)(2,1)S(1)}, bf16[768,512]{1,0:T(8,128)(2,1)S(1)}, u32[]{:S(2)}, u32[]{:S(2)}) collective-permute-start(bf16[768,512]{1,0:T(8,128)(2,1)S(1)} %copy-done.21), channel_id=1, source_target_pairs={{0,1},{1,0},{2,3},{3,2},{4,5},{5,4},{6,7},{7,6},{8,9},{9,8},{10,11... | collective-permute-start | bytes 2359304 | tf_op jit(solution)/shard_map/ppermute | solution.py:603
  118.2 18.3 %collective-permute-start.5 = (bf16[1024,512]{1,0:T(8,128)(2,1)S(1)}, bf16[1024,512]{1,0:T(8,128)(2,1)S(1)}, u32[]{:S(2)}, u32[]{:S(2)}) collective-permute-start(bf16[1024,512]{1,0:T(8,128)(2,1)S(1)} %copy-done.19), channel_id=1, source_target_pairs={{0,1},{1,0},{2,3},{3,2},{4,5},{5,4},{6,7},{7,6},{8,9},{9,8},{10,11... | collective-permute-start | bytes 3145736 | tf_op jit(solution)/shard_map/ppermute | solution.py:603
  118.8 6.9 %collective-permute-start.21 = (bf16[768,128]{1,0:T(8,128)(2,1)S(1)}, bf16[768,128]{1,0:T(8,128)(2,1)S(1)}, u32[]{:S(2)}, u32[]{:S(2)}) collective-permute-start(bf16[768,128]{1,0:T(8,128)(2,1)S(1)} %add_convert_fusion.1.rest_3_), channel_id=1, source_target_pairs={{0,2},{1,3},{2,0},{3,1},{4,6},{5,7},{6,4},{7,5},{8,10},{9,11},{10,... | collective-permute-start | bytes 589832 | tf_op jit(solution)/shard_map/ppermute | solution.py:606
  125.8 2.4 %collective-permute-start.26 = (bf16[768,512]{1,0:T(8,128)(2,1)S(1)}, bf16[768,512]{1,0:T(8,128)(2,1)S(1)}, u32[]{:S(2)}, u32[]{:S(2)}) collective-permute-start(bf16[768,512]{1,0:T(8,128)(2,1)S(1)} %copy-done.23), channel_id=1, source_target_pairs={{0,1},{1,0},{2,3},{3,2},{4,5},{5,4},{6,7},{7,6},{8,9},{9,8},{10,11... | collective-permute-start | bytes 2359304 | tf_op jit(solution)/shard_map/ppermute | solution.py:603
  126.1 15.2 %collective-permute-start.22 = (bf16[512,512]{1,0:T(8,128)(2,1)S(1)}, bf16[512,512]{1,0:T(8,128)(2,1)S(1)}, u32[]{:S(2)}, u32[]{:S(2)}) collective-permute-start(bf16[512,512]{1,0:T(8,128)(2,1)S(1)} %pair_sum.7), channel_id=1, source_target_pairs={{0,2},{1,3},{2,0},{3,1},{4,6},{5,7},{6,4},{7,5},{8,10},{9,11},{10,... | collective-permute-start | bytes 1572872 | tf_op jit(solution)/shard_map/ppermute | solution.py:606
  147.1 1.5 collective-permute-start.27
  147.2 2.2 %collective-permute-start.10 = (bf16[512,512]{1,0:T(8,128)(2,1)S(1)}, bf16[512,512]{1,0:T(8,128)(2,1)S(1)}, u32[]{:S(2)}, u32[]{:S(2)}) collective-permute-start(bf16[512,512]{1,0:T(8,128)(2,1)S(1)} %copy-done.25), channel_id=1, source_target_pairs={{0,1},{1,0},{2,3},{3,2},{4,5},{5,4},{6,7},{7,6},{8,9},{9,8},{10,11... | collective-permute-start | bytes 1572872 | tf_op jit(solution)/shard_map/ppermute | solution.py:603
  148.7 7.0 %collective-permute-start.28 = (bf16[768,128]{1,0:T(8,128)(2,1)S(1)}, bf16[768,128]{1,0:T(8,128)(2,1)S(1)}, u32[]{:S(2)}, u32[]{:S(2)}) collective-permute-start(bf16[768,128]{1,0:T(8,128)(2,1)S(1)} %add_convert_fusion.rest_6_), channel_id=1, source_target_pairs={{0,2},{1,3},{2,0},{3,1},{4,6},{5,7},{6,4},{7,5},{8,10},{9,11},{10,... | collective-permute-start | bytes 589832 | tf_op jit(solution)/shard_map/ppermute | solution.py:606
  (31 other events, 205.1 us)
